TPU v7x, 256 devices: a whole 4x4x8 slice. The times are simulated.
256 devices in a mesh: batch: 2 (over z_hi), narrow: 8 (over x, core), wide: 16 (over z_lo, y).
Axes of the slice: x: 4, y: 4, z: 8 (z_hi: 2, z_lo: 4; z = z_hi * 4 + z_lo), core: 2. Of those that a mesh axis runs over, the one named last changes fastest.
Arguments:
- inputs: bfloat16 [2, 16384, 256], P('batch', ('narrow', 'wide')), may hold values from -6 to 6
- in_weight: bfloat16 [256, 768], replicated, may hold values from -0.375 to 0.375
- short_kernel: float32 [3, 768], replicated, may hold values from -3 to 3
- filter_one: float32 [16384, 256], P(('narrow', 'wide')), as said below
- filter_two: float32 [16384, 256], P(('narrow', 'wide')), as said below
- out_weight: bfloat16 [256, 256], replicated, may hold values from -0.375 to 0.375
- out_grad: bfloat16 [2, 16384, 256], P('batch', ('narrow', 'wide')), may hold values from -6 to 6
Outputs:
- outputs: bfloat16 [2, 16384, 256], P('batch', ('narrow', 'wide'))
- grad_inputs: bfloat16 [2, 16384, 256], P('batch', ('narrow', 'wide'))
- grad_in_weight: float32 [256, 768], replicated
- grad_short: float32 [3, 768], replicated
- grad_filter_one: float32 [16384, 256], P(('narrow', 'wide'))
- grad_filter_two: float32 [16384, 256], P(('narrow', 'wide'))
- grad_out_weight: float32 [256, 256], replicated
Inputs may be any that keep to these rules, and one draw needn't show every extreme that they name: `filter_one`: A long filter's value at each position and channel. `filter_two`: A long filter's value at each position and channel.
All inputs are finite; a program needn't handle non-finite values.
Results may differ from a plain program's by a relative error of at most 0.005.
Values may be sent and summed in bfloat16 or wider, within the bound.
No kernel may reach another device: no remote copies, remote signals or barrier semaphores. Data moves between devices by JAX's collectives and lax.ppermute only.
A program may use at most 64 MiB of HBM per device.

v0:
```python
import math

import jax
import jax.numpy as jnp
from jax import lax
from jax.sharding import PartitionSpec as P

precise = lax.Precision.HIGHEST


def from_behind(block, axis, distance):
    devices = range(lax.axis_size(axis))
    route = [(i - distance, i) for i in devices if i - distance in devices]
    return lax.ppermute(block, axis, route)


def phase_table(first_index, second_index, period):
    product = first_index[:, None] * second_index[None, :] % period
    angles = product.astype(jnp.float32) * (2.0 * math.pi / period)
    return (jnp.cos(angles), jnp.sin(angles))


def local_dft(real_in, imag_in, sign):
    planes, pairs, length, chans = real_in.shape
    first = math.gcd(length, 16)
    second = length // first
    first_index = jnp.arange(first, dtype=jnp.int32)
    second_index = jnp.arange(second, dtype=jnp.int32)
    first_cos, first_sin = phase_table(first_index, first_index, first)
    second_cos, second_sin = phase_table(second_index, second_index, second)
    twist_cos, twist_sin = phase_table(first_index, second_index, length)
    twist_cos = twist_cos[:, :, None]
    twist_sin = twist_sin[:, :, None]
    real_grid = real_in.reshape(planes, pairs, first, second, chans)
    imag_grid = imag_in.reshape(planes, pairs, first, second, chans)
    section_real = jnp.einsum(
        "kp,nmpqd->nmkqd", first_cos, real_grid, precision=precise
    ) - sign * jnp.einsum("kp,nmpqd->nmkqd", first_sin, imag_grid, precision=precise)
    section_imag = jnp.einsum(
        "kp,nmpqd->nmkqd", first_cos, imag_grid, precision=precise
    ) + sign * jnp.einsum("kp,nmpqd->nmkqd", first_sin, real_grid, precision=precise)
    turned_real = section_real * twist_cos - sign * section_imag * twist_sin
    turned_imag = section_imag * twist_cos + sign * section_real * twist_sin
    final_real = jnp.einsum(
        "jq,nmkqd->nmjkd", second_cos, turned_real, precision=precise
    ) - sign * jnp.einsum("jq,nmkqd->nmjkd", second_sin, turned_imag, precision=precise)
    final_imag = jnp.einsum(
        "jq,nmkqd->nmjkd", second_cos, turned_imag, precision=precise
    ) + sign * jnp.einsum("jq,nmkqd->nmjkd", second_sin, turned_real, precision=precise)
    return (
        final_real.reshape(planes, pairs, length, chans),
        final_imag.reshape(planes, pairs, length, chans),
    )


def build_tables(seq_rows, seq_parts, position):
    columns = seq_rows // seq_parts
    length = 2 * seq_parts * seq_rows
    outer_index = jnp.arange(2 * seq_parts, dtype=jnp.int32)
    inner_index = jnp.arange(seq_parts, dtype=jnp.int32)
    all_rows = jnp.arange(seq_rows, dtype=jnp.int32)
    step_cos, step_sin = phase_table(outer_index, inner_index, 2 * seq_parts)
    back_cos, back_sin = phase_table(inner_index, outer_index, 2 * seq_parts)
    own_columns = position * columns + jnp.arange(columns, dtype=jnp.int32)
    turn_cos, turn_sin = phase_table(outer_index, own_columns, length)
    own_pairs = position * 2 + jnp.arange(2, dtype=jnp.int32)
    undo_cos, undo_sin = phase_table(own_pairs, all_rows, length)
    return (
        step_cos,
        step_sin,
        back_cos / length,
        back_sin / length,
        turn_cos[:, :, None],
        turn_sin[:, :, None],
        undo_cos[:, :, None],
        undo_sin[:, :, None],
    )


def spectrum(columns_in, tables):
    step_cos, step_sin, back_cos, back_sin, turn_cos, turn_sin, undo_cos, undo_sin = tables
    real_part = jnp.einsum("kq,nqrd->nkrd", step_cos, columns_in, precision=precise)
    imag_part = -jnp.einsum("kq,nqrd->nkrd", step_sin, columns_in, precision=precise)
    packed = jnp.stack(
        [real_part * turn_cos + imag_part * turn_sin, imag_part * turn_cos - real_part * turn_sin],
        1,
    )
    received = lax.all_to_all(packed, ("narrow", "wide"), split_axis=2, concat_axis=3, tiled=True)
    return local_dft(received[:, 0], received[:, 1], -1.0)


def signal(spectrum_pair, tables):
    step_cos, step_sin, back_cos, back_sin, turn_cos, turn_sin, undo_cos, undo_sin = tables
    spec_real, spec_imag = spectrum_pair
    time_real, time_imag = local_dft(spec_real, spec_imag, 1.0)
    packed = jnp.stack(
        [time_real * undo_cos - time_imag * undo_sin, time_real * undo_sin + time_imag * undo_cos],
        1,
    )
    received = lax.all_to_all(packed, ("narrow", "wide"), split_axis=3, concat_axis=2, tiled=True)
    return jnp.einsum("qk,nkrd->nqrd", back_cos, received[:, 0], precision=precise) - jnp.einsum(
        "qk,nkrd->nqrd", back_sin, received[:, 1], precision=precise
    )


def multiply(first_pair, second_pair):
    return (
        first_pair[0] * second_pair[0] - first_pair[1] * second_pair[1],
        first_pair[0] * second_pair[1] + first_pair[1] * second_pair[0],
    )


def multiply_conj(first_pair, second_pair):
    return (
        first_pair[0] * second_pair[0] + first_pair[1] * second_pair[1],
        first_pair[0] * second_pair[1] - first_pair[1] * second_pair[0],
    )


def join_pairs(first_pair, second_pair):
    return (
        jnp.concatenate([first_pair[0], second_pair[0]], 0),
        jnp.concatenate([first_pair[1], second_pair[1]], 0),
    )


def per_device(inputs, in_weight, short_kernel, filter_one, filter_two, out_weight, out_grad):
    model_width = out_weight.shape[0]
    sequence = inputs[0]
    seq_rows = sequence.shape[0]
    seq_parts = lax.axis_size(("narrow", "wide"))
    position = lax.axis_index(("narrow", "wide"))
    columns = seq_rows // seq_parts
    grad_scale = 1.0 / math.sqrt(lax.axis_size("batch") * seq_parts * seq_rows)
    projected = jnp.dot(sequence, in_weight, preferred_element_type=jnp.float32)
    before_rows = from_behind(projected[seq_rows - 2 :], ("narrow", "wide"), 1)
    extended = jnp.concatenate([before_rows, projected], 0)
    lagged_one = extended[1 : seq_rows + 1]
    lagged_two = extended[:seq_rows]
    mixed_all = (
        short_kernel[0] * projected + short_kernel[1] * lagged_one + short_kernel[2] * lagged_two
    )
    value_part = mixed_all[:, :model_width]
    gate_one = mixed_all[:, model_width : 2 * model_width]
    gate_two = mixed_all[:, 2 * model_width :]
    cotangent = out_grad[0]
    grad_pre = jnp.dot(cotangent, out_weight.T, preferred_element_type=jnp.float32)
    tables = build_tables(seq_rows, seq_parts, position)

    def stacked_cols(stacked):
        shaped = stacked.reshape(stacked.shape[0], seq_parts, columns, stacked.shape[2])
        return lax.all_to_all(shaped, ("narrow", "wide"), split_axis=1, concat_axis=1, tiled=True)

    def stacked_rows(stacked):
        received = lax.all_to_all(
            stacked, ("narrow", "wide"), split_axis=1, concat_axis=2, tiled=True
        )
        return received.reshape(stacked.shape[0], seq_rows, stacked.shape[3])

    def forward(stacked):
        return spectrum(stacked_cols(stacked), tables)

    def inverse(spectrum_pair):
        return stacked_rows(signal(spectrum_pair, tables))

    held_all = jnp.stack([value_part, gate_one, gate_two, filter_one, filter_two])
    value_held = held_all[0]
    one_held = held_all[1]
    two_held = held_all[2]
    spec_real, spec_imag = forward(jnp.stack([held_all[3], held_all[4], value_held]))
    one_spec = (spec_real[0:1], spec_imag[0:1])
    two_spec = (spec_real[1:2], spec_imag[1:2])
    value_spec = (spec_real[2:3], spec_imag[2:3])
    conv_one = inverse(multiply(one_spec, value_spec))[0]
    gated_one = one_held * conv_one
    gated_spec = forward(gated_one[None])
    conv_two = inverse(multiply(two_spec, gated_spec))[0]
    pre_held = two_held * conv_two
    pre_out = pre_held.astype(jnp.bfloat16)
    grad_pre_held = grad_pre[None][0]
    grad_two = grad_pre_held * conv_two
    grad_conv_two = grad_pre_held * two_held
    conv_two_spec = forward(grad_conv_two[None])
    back_pair = inverse(
        join_pairs(multiply_conj(two_spec, conv_two_spec), multiply_conj(gated_spec, conv_two_spec))
    )
    grad_gated = back_pair[0]
    grad_one = grad_gated * conv_one
    grad_conv_one = grad_gated * one_held
    conv_one_spec = forward(grad_conv_one[None])
    last_pair = inverse(
        join_pairs(multiply_conj(one_spec, conv_one_spec), multiply_conj(value_spec, conv_one_spec))
    )
    back_home = jnp.stack([last_pair[0], grad_one, grad_two, last_pair[1], back_pair[1]])
    outputs = jnp.dot(pre_out, out_weight, preferred_element_type=jnp.float32).astype(jnp.bfloat16)
    part_out_weight = jnp.dot(pre_out.T, cotangent, preferred_element_type=jnp.float32)
    grad_mixed = jnp.concatenate([back_home[0], back_home[1], back_home[2]], 1)
    after_rows = from_behind(grad_mixed[:2], ("narrow", "wide"), -1)
    ahead_rows = jnp.concatenate([grad_mixed, after_rows], 0)
    grad_proj = (
        short_kernel[0] * grad_mixed
        + short_kernel[1] * ahead_rows[1 : seq_rows + 1]
        + short_kernel[2] * ahead_rows[2:]
    ).astype(jnp.bfloat16)
    part_kernel = jnp.stack(
        [
            jnp.sum(grad_mixed * projected, 0),
            jnp.sum(grad_mixed * lagged_one, 0),
            jnp.sum(grad_mixed * lagged_two, 0),
        ]
    )
    part_in_weight = jnp.dot(sequence.T, grad_proj, preferred_element_type=jnp.float32)
    grad_inputs = jnp.dot(grad_proj, in_weight.T, preferred_element_type=jnp.float32).astype(
        jnp.bfloat16
    )
    sum_in, sum_out, sum_kernel = lax.psum(
        (part_in_weight, part_out_weight, part_kernel), ("batch", "narrow", "wide")
    )
    sum_one, sum_two = lax.psum((back_home[3], back_home[4]), "batch")
    return (
        outputs[None],
        grad_inputs[None],
        sum_in * grad_scale,
        sum_kernel * grad_scale,
        sum_one * grad_scale,
        sum_two * grad_scale,
        sum_out * grad_scale,
    )


def solution(mesh):
    return jax.shard_map(
        per_device,
        mesh=mesh,
        in_specs=(
            P("batch", ("narrow", "wide"), None),
            P(),
            P(),
            P(("narrow", "wide"), None),
            P(("narrow", "wide"), None),
            P(),
            P("batch", ("narrow", "wide"), None),
        ),
        out_specs=(
            P("batch", ("narrow", "wide"), None),
            P("batch", ("narrow", "wide"), None),
            P(),
            P(),
            P(("narrow", "wide"), None),
            P(("narrow", "wide"), None),
            P(),
        ),
        check_vma=False,
    )
```

profile of v0, /device:TPU:1, one launch (start us, length us, event | category | flops | bytes accessed | tf_op | source)
XLA Modules:
  0.0 830.9 jit_solution(17139280486663566265)
XLA Ops:
  22.2 8.0 all-to-all-start.8
  31.4 9.5 %all-to-all-done.8 = f32[1,128,1,256]{3,2,0,1:T(1,128)S(1)} async-done(((f32[1,128,1,256]{3,2,0,1:T(1,128)}), f32[1,128,1,256]{3,2,0,1:T(1,128)S(1)}, u32[]{:S(2)}, u32[]{:S(2)}) %all-to-all-start.8) | async-done | bytes 131104 | tf_op jit(solution)/shard_map/all_to_all | solution.py:152
  49.8 12.7 %all-to-all-done = f32[3,128,1,256]{3,2,0,1:T(1,128)S(1)} async-done(((f32[3,128,1,256]{3,2,0,1:T(1,128)}), f32[3,128,1,256]{3,2,0,1:T(1,128)S(1)}, u32[]{:S(2)}, u32[]{:S(2)}) %all-to-all-start) | async-done | bytes 393248 | tf_op jit(solution)/shard_map/all_to_all | solution.py:152
  62.5 18.4 %all-to-all-start.9 = ((f32[1,2,256,1,256]{4,3,1,0,2:T(1,128)}), f32[1,2,256,1,256]{4,3,1,0,2:T(1,128)S(1)}, u32[]{:S(2)}, u32[]{:S(2)}) async-start(f32[1,2,256,1,256]{4,3,1,0,2:T(1,128)} %copy.353), calls=%async_computation.9 | async-start | bytes 1048576 | tf_op jit(solution)/shard_map/all_to_all | solution.py:88
  86.4 12.7 %all-to-all-done.9 = f32[1,2,256,1,256]{4,3,1,0,2:T(1,128)S(1)} async-done(((f32[1,2,256,1,256]{4,3,1,0,2:T(1,128)}), f32[1,2,256,1,256]{4,3,1,0,2:T(1,128)S(1)}, u32[]{:S(2)}, u32[]{:S(2)}) %all-to-all-start.9) | async-done | bytes 524320 | tf_op jit(solution)/shard_map/all_to_all | solution.py:88
  99.1 6.6 all-to-all-start.1
  110.6 35.1 %all-to-all-done.1 = f32[3,2,256,1,256]{4,1,3,0,2:T(2,128)S(1)} async-done(((f32[3,2,256,1,256]{4,1,3,0,2:T(2,128)}), f32[3,2,256,1,256]{4,1,3,0,2:T(2,128)S(1)}, u32[]{:S(2)}, u32[]{:S(2)}) %all-to-all-start.1) | async-done | bytes 1572896 | tf_op jit(solution)/shard_map/all_to_all | solution.py:88
  163.8 24.8 %all_to_all.200 = f32[1,2,2,128,256]{4,2,1,0,3:T(2,128)S(1)} all-to-all(f32[1,2,2,128,256]{4,2,1,0,3:T(2,128)S(1)} %copy.322), channel_id=1, replica_groups=mesh['batch'=2,'narrow'=8,'wide'=16] {'narrow','wide'}, dimensions={3} | all-to-all | bytes 1048576 | tf_op jit(solution)/shard_map/all_to_all | solution.py:100
  191.4 16.7 %all_to_all.201 = f32[1,128,1,256]{3,2,0,1:T(1,128)S(1)} all-to-all(f32[1,128,1,256]{3,2,0,1:T(1,128)S(1)} %copy.324), channel_id=1, replica_groups=mesh['batch'=2,'narrow'=8,'wide'=16] {'narrow','wide'}, dimensions={1} | all-to-all | bytes 262144 | tf_op jit(solution)/shard_map/all_to_all | solution.py:155
  208.3 16.5 %all_to_all.202 = f32[1,128,1,256]{3,2,0,1:T(1,128)S(1)} all-to-all(f32[1,128,1,256]{3,2,0,1:T(1,128)S(1)} %copy.325), channel_id=1, replica_groups=mesh['batch'=2,'narrow'=8,'wide'=16] {'narrow','wide'}, dimensions={1} | all-to-all | bytes 262144 | tf_op jit(solution)/shard_map/all_to_all | solution.py:152
  227.6 6.3 all-to-all-start.5
  234.3 17.5 %all-to-all-done.5 = f32[1,2,256,1,256]{4,3,1,0,2:T(1,128)S(1)} async-done(((f32[1,2,256,1,256]{4,3,1,0,2:T(1,128)}), f32[1,2,256,1,256]{4,3,1,0,2:T(1,128)S(1)}, u32[]{:S(2)}, u32[]{:S(2)}) %all-to-all-start.5) | async-done | bytes 524320 | tf_op jit(solution)/shard_map/all_to_all | solution.py:88
  265.5 35.2 %all_to_all.203 = f32[2,2,2,128,256]{4,2,0,1,3:T(2,128)S(1)} all-to-all(f32[2,2,2,128,256]{4,2,0,1,3:T(2,128)S(1)} %copy.378), channel_id=1, replica_groups=mesh['batch'=2,'narrow'=8,'wide'=16] {'narrow','wide'}, dimensions={3} | all-to-all | bytes 2097152 | tf_op jit(solution)/shard_map/all_to_all | solution.py:100
  305.1 19.0 %all_to_all.204 = f32[2,128,1,256]{3,2,0,1:T(1,128)S(1)} all-to-all(f32[2,128,1,256]{3,2,0,1:T(1,128)S(1)} %copy.382), channel_id=1, replica_groups=mesh['batch'=2,'narrow'=8,'wide'=16] {'narrow','wide'}, dimensions={1} | all-to-all | bytes 524288 | tf_op jit(solution)/shard_map/all_to_all | solution.py:155
  325.1 16.8 %all_to_all.205 = f32[1,128,1,256]{3,2,0,1:T(1,128)S(1)} all-to-all(f32[1,128,1,256]{3,2,0,1:T(1,128)S(1)} %copy.384), channel_id=1, replica_groups=mesh['batch'=2,'narrow'=8,'wide'=16] {'narrow','wide'}, dimensions={1} | all-to-all | bytes 262144 | tf_op jit(solution)/shard_map/all_to_all | solution.py:152
  344.3 24.3 %all_to_all.206 = f32[1,2,256,1,256]{4,3,1,0,2:T(1,128)S(1)} all-to-all(f32[1,2,256,1,256]{4,3,1,0,2:T(1,128)S(1)} %copy.385), channel_id=1, replica_groups=mesh['batch'=2,'narrow'=8,'wide'=16] {'narrow','wide'}, dimensions={2} | all-to-all | bytes 1048576 | tf_op jit(solution)/shard_map/all_to_all | solution.py:88
  382.5 7.2 all-to-all-start.6
  399.4 8.5 %all-to-all-done.6 = f32[1,2,2,128,256]{4,2,1,0,3:T(2,128)S(1)} async-done(((f32[1,2,2,128,256]{4,2,1,0,3:T(2,128)}), f32[1,2,2,128,256]{4,2,1,0,3:T(2,128)S(1)}, u32[]{:S(2)}, u32[]{:S(2)}) %all-to-all-start.6) | async-done | bytes 524320 | tf_op jit(solution)/shard_map/all_to_all | solution.py:100
  407.9 6.8 all-to-all-start.14
  418.1 25.7 %all-to-all-done.14 = f32[2,2,2,128,256]{4,2,0,1,3:T(2,128)S(1)} async-done(((f32[2,2,2,128,256]{4,2,0,1,3:T(2,128)}), f32[2,2,2,128,256]{4,2,0,1,3:T(2,128)S(1)}, u32[]{:S(2)}, u32[]{:S(2)}) %all-to-all-start.14) | async-done | bytes 1048608 | tf_op jit(solution)/shard_map/all_to_all | solution.py:100
  443.8 6.7 all-to-all-start.7
  469.1 11.2 %all-to-all-done.15 = f32[2,128,1,256]{3,2,0,1:T(1,128)S(1)} async-done(((f32[2,128,1,256]{3,2,0,1:T(1,128)}), f32[2,128,1,256]{3,2,0,1:T(1,128)S(1)}, u32[]{:S(2)}, u32[]{:S(2)}) %all-to-all-start.15) | async-done | bytes 262176 | tf_op jit(solution)/shard_map/all_to_all | solution.py:155
  487.2 80.1 %psum.36 = f32[3,768]{1,0:T(4,128)S(1)} all-reduce(f32[3,768]{1,0:T(4,128)S(1)} %pad_maximum_fusion.11), channel_id=1, replica_groups=mesh['batch'=2,'narrow'=8,'wide'=16] {'batch','narrow','wide'}, use_global_device_ids=true, to_apply=%region_4.5 | all-reduce | flops 2304 | bytes 18432 | tf_op jit(solution)/shard_map/psum | solution.py:216
  573.2 247.6 %all-reduce.5.cloned.1.call-done = (f32[256,768]{0,1:T(8,128)}, f32[256,256]{1,0:T(8,128)}) async-done(((f32[256,768]{0,1:T(8,128)}, f32[256,256]{1,0:T(8,128)}), (f32[256,768]{0,1:T(8,128)}, f32[256,256]{1,0:T(8,128)})) %all-reduce.5.cloned.1.call-update) | async-done | bytes 1048592 | tf_op jit(solution)/shard_map/psum | solution.py:216
  (285 shorter events, 141.3 us)
Async XLA Ops:
  7.2 23.0 %copy-start.15 = (f32[128,256]{1,0:T(8,128)S(1)}, f32[128,256]{1,0:T(8,128)}, u32[]{:S(2)}) copy-start(f32[128,256]{1,0:T(8,128)} %param.11) | copy-start | bytes 393220
  8.2 22.0 %copy-start.16 = (f32[128,256]{1,0:T(8,128)S(1)}, f32[128,256]{1,0:T(8,128)}, u32[]{:S(2)}) copy-start(f32[128,256]{1,0:T(8,128)} %param.10) | copy-start | bytes 393220
  9.3 11.4 %collective-permute-start = (f32[2,768]{1,0:T(2,128)S(1)}, f32[2,768]{1,0:T(2,128)S(1)}, u32[]{:S(2)}, u32[]{:S(2)}) collective-permute-start(f32[2,768]{1,0:T(2,128)S(1)} %slice.167), channel_id=1, source_target_pairs={{0,1},{1,2},{2,3},{3,4},{4,5},{5,6},{6,7},{7,8},{8,9},{9,10},{10,1... | collective-permute-start | bytes 18440 | tf_op jit(solution)/shard_map/ppermute | solution.py:14
  22.2 18.7 %all-to-all-start.8 = ((f32[1,128,1,256]{3,2,0,1:T(1,128)}), f32[1,128,1,256]{3,2,0,1:T(1,128)S(1)}, u32[]{:S(2)}, u32[]{:S(2)}) async-start(f32[1,128,1,256]{3,2,0,1:T(1,128)} %copy.352), calls=%async_computation.8 | async-start | bytes 262144 | tf_op jit(solution)/shard_map/all_to_all | solution.py:152
  40.9 21.5 %all-to-all-start = ((f32[3,128,1,256]{3,2,0,1:T(1,128)}), f32[3,128,1,256]{3,2,0,1:T(1,128)S(1)}, u32[]{:S(2)}, u32[]{:S(2)}) async-start(f32[3,128,1,256]{3,2,0,1:T(1,128)} %copy.296), calls=%async_computation | async-start | bytes 786432 | tf_op jit(solution)/shard_map/all_to_all | solution.py:152
  46.9 35.8 %copy-start.29 = (f32[256]{0:T(256)}, f32[256]{0:T(256)S(1)}, u32[]{:S(2)}) copy-start(f32[256]{0:T(256)S(1)} %get-tuple-element.122) | copy-start | bytes 3076
  46.9 35.8 %copy-start.32 = (f32[256]{0:T(256)}, f32[256]{0:T(256)S(1)}, u32[]{:S(2)}) copy-start(f32[256]{0:T(256)S(1)} %get-tuple-element.123) | copy-start | bytes 3076
  62.5 36.6 %all-to-all-start.9 = ((f32[1,2,256,1,256]{4,3,1,0,2:T(1,128)}), f32[1,2,256,1,256]{4,3,1,0,2:T(1,128)S(1)}, u32[]{:S(2)}, u32[]{:S(2)}) async-start(f32[1,2,256,1,256]{4,3,1,0,2:T(1,128)} %copy.353), calls=%async_computation.9 | async-start | bytes 1048576 | tf_op jit(solution)/shard_map/all_to_all | solution.py:88
  99.1 46.7 %all-to-all-start.1 = ((f32[3,2,256,1,256]{4,1,3,0,2:T(2,128)}), f32[3,2,256,1,256]{4,1,3,0,2:T(2,128)S(1)}, u32[]{:S(2)}, u32[]{:S(2)}) async-start(f32[3,2,256,1,256]{4,1,3,0,2:T(2,128)} %copy.298), calls=%async_computation.1 | async-start | bytes 3145728 | tf_op jit(solution)/shard_map/all_to_all | solution.py:88
  189.3 36.3 %copy-start.30 = (f32[256]{0:T(256)S(1)}, f32[256]{0:T(256)}, u32[]{:S(2)}) copy-start(f32[256]{0:T(256)} %copy-done.29) | copy-start | bytes 3076
  189.3 36.3 %copy-start.33 = (f32[256]{0:T(256)S(1)}, f32[256]{0:T(256)}, u32[]{:S(2)}) copy-start(f32[256]{0:T(256)} %copy-done.32) | copy-start | bytes 3076
  227.6 24.3 %all-to-all-start.5 = ((f32[1,2,256,1,256]{4,3,1,0,2:T(1,128)}), f32[1,2,256,1,256]{4,3,1,0,2:T(1,128)S(1)}, u32[]{:S(2)}, u32[]{:S(2)}) async-start(f32[1,2,256,1,256]{4,3,1,0,2:T(1,128)} %copy.326), calls=%async_computation.5 | async-start | bytes 1048576 | tf_op jit(solution)/shard_map/all_to_all | solution.py:88
  304.9 37.9 %copy-start.31 = (f32[256]{0:T(256)S(1)}, f32[256]{0:T(256)}, u32[]{:S(2)}) copy-start(f32[256]{0:T(256)} %copy-done.29) | copy-start | bytes 3076
  304.9 37.9 %copy-start.34 = (f32[256]{0:T(256)S(1)}, f32[256]{0:T(256)}, u32[]{:S(2)}) copy-start(f32[256]{0:T(256)} %copy-done.32) | copy-start | bytes 3076
  382.5 25.4 %all-to-all-start.6 = ((f32[1,2,2,128,256]{4,2,1,0,3:T(2,128)}), f32[1,2,2,128,256]{4,2,1,0,3:T(2,128)S(1)}, u32[]{:S(2)}, u32[]{:S(2)}) async-start(f32[1,2,2,128,256]{4,2,1,0,3:T(2,128)} %copy.349), calls=%async_computation.6 | async-start | bytes 1048576 | tf_op jit(solution)/shard_map/all_to_all | solution.py:100
  407.9 35.9 %all-to-all-start.14 = ((f32[2,2,2,128,256]{4,2,0,1,3:T(2,128)}), f32[2,2,2,128,256]{4,2,0,1,3:T(2,128)S(1)}, u32[]{:S(2)}, u32[]{:S(2)}) async-start(f32[2,2,2,128,256]{4,2,0,1,3:T(2,128)} %copy.410), calls=%async_computation.14 | async-start | bytes 2097152 | tf_op jit(solution)/shard_map/all_to_all | solution.py:100
  443.8 17.5 %all-to-all-start.7 = ((f32[1,128,1,256]{3,2,0,1:T(1,128)}), f32[1,128,1,256]{3,2,0,1:T(1,128)S(1)}, u32[]{:S(2)}, u32[]{:S(2)}) async-start(f32[1,128,1,256]{3,2,0,1:T(1,128)} %copy.351), calls=%async_computation.7 | async-start | bytes 262144 | tf_op jit(solution)/shard_map/all_to_all | solution.py:155
  455.6 29.6 %copy-start.10 = (bf16[256,256]{1,0:T(8,128)(2,1)S(1)}, bf16[256,256]{1,0:T(8,128)(2,1)}, u32[]{:S(2)}) copy-start(bf16[256,256]{1,0:T(8,128)(2,1)} %param.12) | copy-start | bytes 393220
  461.2 19.0 %all-to-all-start.15 = ((f32[2,128,1,256]{3,2,0,1:T(1,128)}), f32[2,128,1,256]{3,2,0,1:T(1,128)S(1)}, u32[]{:S(2)}, u32[]{:S(2)}) async-start(f32[2,128,1,256]{3,2,0,1:T(1,128)} %copy.414), calls=%async_computation.15 | async-start | bytes 524288 | tf_op jit(solution)/shard_map/all_to_all | solution.py:155
  467.4 102.6 %all-reduce.7.cloned.1.call-start = ((), (), s32[]{:S(2)}) async-start(), calls=%async_computation.17 | async-start | bytes 524288 | tf_op jit(solution)/shard_map/psum | solution.py:219
  469.1 17.7 %copy-start.28 = (f32[2,768]{1,0:T(2,128)S(1)}, f32[2,768]{1,0:T(2,128)}, u32[]{:S(2)}) copy-start(f32[2,768]{1,0:T(2,128)} %copy-done.27) | copy-start | bytes 18436
  480.5 6.3 collective-permute-start.1
  486.1 81.9 %copy-start.14 = (bf16[1,128,256]{2,1,0:T(8,128)(2,1)S(1)}, bf16[1,128,256]{2,1,0:T(8,128)(2,1)}, u32[]{:S(2)}) copy-start(bf16[1,128,256]{2,1,0:T(8,128)(2,1)} %param.7) | copy-start | bytes 196612
  486.7 334.0 %all-reduce.5.cloned.1.call-start = ((), (), s32[]{:S(2)}) async-start(), calls=%async_computation.16 | async-start | bytes 2097152 | tf_op jit(solution)/shard_map/psum | solution.py:216
  (24 other events, 151.4 us)
Sparse Core Ops, SparseCore 0:
  486.9 40.3 all-reduce.6
  569.2 251.4 all-reduce.4
where the time goes:
time: 839 us; the launch traced here: 831 us
  waiting for transfers between devices  391 us (47%)
  blocking collectives  233 us (28%)
  starting transfers between devices  80.9 us (10%)
  matrix products  66.6 us (8%)
  local copies, waits for them, and re-layouts  34.4 us (4%)
  between operations  16 us (2%)
    psum x1, waiting for transfers between devices, per_device(): lax.psum((part_in_weight, part_out_weight, part_kernel), ('batch', 'narro...  248 us
    psum x1, blocking collectives, per_device(): lax.psum((part_in_weight, part_out_weight, part_kernel), ('batch', 'narro...  80.1 us
    all_to_all x3, waiting for transfers between devices, spectrum(): lax.all_to_all(packed, ('narrow', 'wide'), split_axis=2, concat_axis=3, t...  65.3 us
    all_to_all x2, blocking collectives, signal(): lax.all_to_all(packed, ('narrow', 'wide'), split_axis=3, concat_axis=2, t...  60 us
    all_to_all x2, blocking collectives, stacked_rows(): lax.all_to_all(stacked, ('narrow', 'wide'), split_axis=1, concat_axis=2,...  35.7 us
    all_to_all x2, waiting for transfers between devices, signal(): lax.all_to_all(packed, ('narrow', 'wide'), split_axis=3, concat_axis=2, t...  34.2 us
    all_to_all x2, blocking collectives, stacked_cols(): lax.all_to_all(shaped, ('narrow', 'wide'), split_axis=1, concat_axis=1, t...  33.3 us
    all_to_all x3, starting transfers between devices, spectrum(): lax.all_to_all(packed, ('narrow', 'wide'), split_axis=2, concat_axis=3, t...  31.3 us
  transfers between devices with their start and end apart: 13, of which 11 were waited for; matrix products, arithmetic and copies ran while one was open for 5% of the time, Pallas kernels for 0%

commit v1 on v0

v1 whole, which is shorter than its diff:
```python
import math

import jax
import jax.numpy as jnp
import numpy as np
from jax import lax
from jax.experimental import pallas as pl
from jax.experimental.pallas import tpu as pltpu
from jax.sharding import PartitionSpec as P

everyone = ("batch", "narrow", "wide")
vmem_limit = 56 * 1024 * 1024


def two_terms(table):
    high = table.astype(np.float32).astype(jnp.bfloat16)
    low = (table - high.astype(np.float64)).astype(np.float32).astype(jnp.bfloat16)
    return high, low


def transform_tables(blocks, rows):
    length = 2 * blocks * rows
    outer = np.arange(blocks) + 0.5
    step = 2.0 * math.pi * np.outer(outer, np.arange(blocks)) / (2 * blocks)
    turn = 2.0 * math.pi * np.outer(outer, np.arange(rows)) / length
    inner = 2.0 * math.pi * np.outer(np.arange(rows), np.arange(rows)) / rows
    first = np.concatenate([np.cos(step), -np.sin(step)], 0)
    c, s = np.cos(inner), np.sin(inner)
    second = np.block([[c, -s], [s, c]])
    second_back = np.block([[c, s], [-s, c]])
    first_back = np.concatenate([np.cos(step).T, -np.sin(step).T], 1) * (2.0 / length)
    tables = []
    for table in (first, second, second_back, first_back):
        tables.extend(two_terms(table))
    tables.append(np.cos(turn).astype(np.float32))
    tables.append(np.sin(turn).astype(np.float32))
    return tables


def bf16_dot(a, b):
    return jnp.dot(a, b, preferred_element_type=jnp.float32)


def split(x):
    high = x.astype(jnp.bfloat16)
    low = (x - high.astype(jnp.float32)).astype(jnp.bfloat16)
    return high, low


def table_left(high, low, x):
    x_high, x_low = split(x)
    return bf16_dot(high, x_high) + bf16_dot(low, x_high) + bf16_dot(high, x_low)


def table_right(x, high, low):
    x_high, x_low = split(x)
    return bf16_dot(x_high, high) + bf16_dot(x_high, low) + bf16_dot(x_low, high)


def pack_kernel(seq_ref, in_weight_ref, one_ref, two_ref, out_weight_ref, grad_ref, out_ref, rows_ref):
    width = out_weight_ref.shape[0]
    slots = rows_ref.shape[0] // width
    contract_first = (((0,), (1,)), ((), ()))
    contract_last = (((1,), (1,)), ((), ()))
    seq = seq_ref[0]

    def put(index, x):
        rows_ref[pl.ds(index, width, stride=slots), :] = x

    def put_two(index, x):
        high = x.astype(jnp.bfloat16).astype(jnp.float32)
        put(index, high)
        put(index + 1, x - high)

    projected = [
        lax.dot_general(
            in_weight_ref[:, group * width : (group + 1) * width],
            seq,
            contract_first,
            preferred_element_type=jnp.float32,
        )
        for group in range(3)
    ]
    put(0, projected[0])
    put_two(1, projected[1])
    put_two(3, projected[2])
    put(
        5,
        lax.dot_general(
            out_weight_ref[...], grad_ref[0], contract_last, preferred_element_type=jnp.float32
        ),
    )
    chosen = jnp.where(lax.axis_index("batch") == 0, one_ref[...], two_ref[...])
    put_two(6, chosen.T)
    out_ref[...] = rows_ref[...].reshape(out_ref.shape).astype(jnp.bfloat16)


def convolve_kernel(
    in_ref,
    short_ref,
    first_high,
    first_low,
    second_high,
    second_low,
    second_back_high,
    second_back_low,
    first_back_high,
    first_back_low,
    turn_cos_ref,
    turn_sin_ref,
    out_ref,
    rows_ref,
    send_ref,
):
    sources, slots, rows = in_ref.shape
    blocks = sources // 2
    width = short_ref.shape[1] // 3
    scale = 1.0 / math.sqrt(sources * rows)
    turn_cos = turn_cos_ref[...]
    turn_sin = turn_sin_ref[...]
    lane = lax.broadcasted_iota(jnp.int32, (blocks, rows), 1)
    block = lax.broadcasted_iota(jnp.int32, (blocks, rows), 0)

    rows_ref[...] = in_ref[...].astype(jnp.float32).reshape(sources * slots, rows)

    def row(member, index):
        return rows_ref[pl.ds(member * blocks * slots + index, blocks, stride=slots), :]

    def later(x, distance):
        moved = pltpu.roll(x, distance, 1)
        carried = jnp.where(block == 0, 0.0, pltpu.roll(moved, 1, 0))
        return jnp.where(lane < distance, carried, moved)

    def earlier(x, distance):
        moved = pltpu.roll(x, rows - distance, 1)
        carried = jnp.where(block == blocks - 1, 0.0, pltpu.roll(moved, blocks - 1, 0))
        return jnp.where(lane >= rows - distance, carried, moved)

    def forward(signals):
        outer = table_left(first_high[...], first_low[...], jnp.concatenate(signals, 1))
        turned = []
        for i in range(len(signals)):
            re = outer[:blocks, i * rows : (i + 1) * rows]
            im = outer[blocks:, i * rows : (i + 1) * rows]
            turned.append(
                jnp.concatenate(
                    [re * turn_cos + im * turn_sin, im * turn_cos - re * turn_sin], 1
                )
            )
        inner = table_right(jnp.concatenate(turned, 0), second_high[...], second_low[...])
        return [
            (inner[i * blocks : (i + 1) * blocks, :rows], inner[i * blocks : (i + 1) * blocks, rows:])
            for i in range(len(signals))
        ]

    def backward(spectra):
        stacked = jnp.concatenate([jnp.concatenate(pair, 1) for pair in spectra], 0)
        inner = table_right(stacked, second_back_high[...], second_back_low[...])
        turned = []
        for i in range(len(spectra)):
            re = inner[i * blocks : (i + 1) * blocks, :rows]
            im = inner[i * blocks : (i + 1) * blocks, rows:]
            turned.append(
                jnp.concatenate(
                    [re * turn_cos - im * turn_sin, im * turn_cos + re * turn_sin], 0
                )
            )
        outer = table_left(first_back_high[...], first_back_low[...], jnp.concatenate(turned, 1))
        return [outer[:, i * rows : (i + 1) * rows] for i in range(len(spectra))]

    def times(a, b):
        return a[0] * b[0] - a[1] * b[1], a[0] * b[1] + a[1] * b[0]

    def conj_times(a, b):
        return a[0] * b[0] + a[1] * b[1], a[0] * b[1] - a[1] * b[0]

    def added(a, b):
        return a[0] + b[0], a[1] + b[1]

    mesh_place = (
        lax.axis_index("batch") * lax.axis_size("narrow") + lax.axis_index("narrow")
    ) * lax.axis_size("wide") + lax.axis_index("wide")
    short = short_ref[...]
    short_lane = lax.broadcasted_iota(jnp.int32, short.shape, 1)
    taps = []
    for group in range(3):
        column = jnp.sum(
            jnp.where(short_lane == mesh_place + group * width, short, 0.0), axis=1, keepdims=True
        )
        taps.append([column[tap : tap + 1, :] for tap in range(3)])

    projected, lagged_one, lagged_two, mixed, pre = [], [], [], [], []
    for member in range(2):
        now = [
            row(member, 0),
            row(member, 1) + row(member, 2),
            row(member, 3) + row(member, 4),
        ]
        one = [later(x, 1) for x in now]
        two = [later(x, 2) for x in now]
        projected.append(now)
        lagged_one.append(one)
        lagged_two.append(two)
        mixed.append(
            [
                taps[g][0] * now[g] + taps[g][1] * one[g] + taps[g][2] * two[g]
                for g in range(3)
            ]
        )
        pre.append(row(member, 5))
    members = range(2)
    grad_conv_two = [pre[m] * mixed[m][2] for m in members]
    spectra = forward(
        [row(m, 6) + row(m, 7) for m in members] + [mixed[m][0] for m in members] + grad_conv_two
    )
    one_spec, two_spec = spectra[0], spectra[1]
    value_spec, conv_two_spec = spectra[2:4], spectra[4:6]
    found = backward(
        [times(one_spec, value_spec[m]) for m in members]
        + [conj_times(two_spec, conv_two_spec[m]) for m in members]
    )
    conv_one, grad_gated = found[:2], found[2:]
    spectra = forward(
        [mixed[m][1] * conv_one[m] for m in members]
        + [mixed[m][1] * grad_gated[m] for m in members]
    )
    gated_spec, conv_one_spec = spectra[:2], spectra[2:]
    found = backward(
        [times(two_spec, gated_spec[m]) for m in members]
        + [conj_times(one_spec, conv_one_spec[m]) for m in members]
        + [
            added(*[conj_times(value_spec[m], conv_one_spec[m]) for m in members]),
            added(*[conj_times(gated_spec[m], conv_two_spec[m]) for m in members]),
        ]
    )
    conv_two, grad_value = found[:2], found[2:4]
    grad_filters = [found[4] * scale, found[5] * scale]

    def put(member, index, x):
        send_ref[pl.ds(member * blocks * slots + index, blocks, stride=slots), :] = x

    sums = [[0.0] * 3 for _ in range(3)]
    for m in members:
        put(m, 0, mixed[m][2] * conv_two[m])
        grads = [grad_value[m], grad_gated[m] * conv_one[m], pre[m] * conv_two[m]]
        for g in range(3):
            put(
                m,
                1 + g,
                taps[g][0] * grads[g]
                + taps[g][1] * earlier(grads[g], 1)
                + taps[g][2] * earlier(grads[g], 2),
            )
            for tap, lagged in enumerate((projected, lagged_one, lagged_two)):
                sums[g][tap] = sums[g][tap] + jnp.sum(
                    jnp.sum(grads[g] * lagged[m][g], axis=0, keepdims=True), axis=1, keepdims=True
                )
        put(m, 4, grad_filters[0])
        put(m, 5, grad_filters[1])
    sum_lane = lax.broadcasted_iota(jnp.int32, (1, rows), 1)
    line = jnp.zeros((1, rows), jnp.float32)
    for g in range(3):
        for tap in range(3):
            total = sums[g][tap] * scale
            high = total.astype(jnp.bfloat16).astype(jnp.float32)
            line = jnp.where(sum_lane == g * 3 + tap, high, line)
            line = jnp.where(sum_lane == 16 + g * 3 + tap, total - high, line)
    line = jnp.broadcast_to(line, (blocks, rows))
    for m in members:
        put(m, 6, line)
        put(m, 7, jnp.zeros((blocks, rows), jnp.float32))
    out_ref[...] = send_ref[...].reshape(out_ref.shape).astype(jnp.bfloat16)


def finish_kernel(
    in_ref,
    seq_ref,
    in_weight_ref,
    out_weight_ref,
    grad_ref,
    outputs_ref,
    grad_inputs_ref,
    short_ref,
    one_ref,
    two_ref,
    part_ref,
    rows_ref,
):
    width, slots, rows = in_ref.shape
    contract_last = (((1,), (1,)), ((), ()))
    rows_ref[...] = in_ref[...].astype(jnp.float32).reshape(width * slots, rows)

    def column(index):
        return rows_ref[pl.ds(index, width, stride=slots), :]

    pre_out = column(0)
    outputs_ref[0] = bf16_dot(pre_out.T.astype(jnp.bfloat16), out_weight_ref[...]).astype(
        jnp.bfloat16
    )
    parts = []
    seq_turned = seq_ref[0].astype(jnp.float32).T.astype(jnp.bfloat16)
    total = None
    for group in range(3):
        grad = column(1 + group).T.astype(jnp.bfloat16)
        term = lax.dot_general(
            grad,
            in_weight_ref[:, group * width : (group + 1) * width],
            contract_last,
            preferred_element_type=jnp.float32,
        )
        total = term if total is None else total + term
        parts.append(bf16_dot(seq_turned, grad))
    grad_inputs_ref[0] = total.astype(jnp.bfloat16)
    parts.append(bf16_dot(pre_out.astype(jnp.bfloat16), grad_ref[0]))
    for index, part in enumerate(parts):
        for half in range(2):
            place = (index * 2 + half) * width
            part_ref[place : place + width, :] = part[
                :, half * rows : (half + 1) * rows
            ].astype(jnp.bfloat16)
    one_ref[...] = column(4).T
    two_ref[...] = column(5).T
    sums = column(6).T
    for group in range(3):
        short_ref[:, group * width : (group + 1) * width] = (
            sums[group * 3 : group * 3 + 3, :] + sums[16 + group * 3 : 19 + group * 3, :]
        )


def add_kernel(in_ref, out_ref):
    scale = 1.0 / math.sqrt(in_ref.shape[0] * 128)
    total = jnp.sum(in_ref[...].astype(jnp.float32), axis=0) * scale
    out_ref[...] = jnp.broadcast_to(total[None], out_ref.shape).astype(jnp.bfloat16)


def place_kernel(in_ref, in_weight_ref, out_weight_ref):
    width, lanes = out_weight_ref.shape[0], in_ref.shape[1]
    for index in range(8):
        block = in_ref[index * width : (index + 1) * width, :].astype(jnp.float32)
        if index < 6:
            in_weight_ref[:, index * lanes : (index + 1) * lanes] = block
        else:
            out_weight_ref[:, (index - 6) * lanes : (index - 5) * lanes] = block


def call(kernel, out_shape, scratch=()):
    return pl.pallas_call(
        kernel,
        out_shape=out_shape,
        scratch_shapes=list(scratch),
        compiler_params=pltpu.CompilerParams(vmem_limit_bytes=vmem_limit),
    )


def exchange(x):
    return lax.all_to_all(x, everyone, split_axis=0, concat_axis=0, tiled=True)


def per_device(inputs, in_weight, short_kernel, filter_one, filter_two, out_weight, out_grad):
    width = out_weight.shape[0]
    rows = inputs.shape[1]
    devices = lax.axis_size(everyone)
    shape = jax.ShapeDtypeStruct
    f32, bf16 = jnp.float32, jnp.bfloat16
    scratch = pltpu.VMEM((devices * 8, rows), f32)
    packed = call(pack_kernel, shape((width, 8, rows), bf16), [scratch])(
        inputs, in_weight, filter_one, filter_two, out_weight, out_grad
    )
    received = exchange(packed)
    tables = [jnp.asarray(t) for t in transform_tables(devices // 2, rows)]
    back = call(convolve_kernel, shape((devices, 8, rows), bf16), [scratch, scratch])(
        received, short_kernel, *tables
    )
    home = exchange(back)
    outputs, grad_inputs, grad_short, grad_one, grad_two, part = call(
        finish_kernel,
        (
            shape((1, rows, width), bf16),
            shape((1, rows, width), bf16),
            shape((3, 3 * width), f32),
            shape((rows, width), f32),
            shape((rows, width), f32),
            shape((8 * width, rows), bf16),
        ),
        [scratch],
    )(home, inputs, in_weight, out_weight, out_grad)
    part = exchange(part.reshape(devices, 8 * width // devices, rows))
    whole = exchange(call(add_kernel, shape(part.shape, bf16))(part))
    grad_in_weight, grad_out_weight = call(
        place_kernel, (shape((width, 3 * width), f32), shape((width, width), f32))
    )(whole.reshape(8 * width, rows))
    return (
        outputs,
        grad_inputs,
        grad_in_weight,
        grad_short,
        grad_one,
        grad_two,
        grad_out_weight,
    )


def solution(mesh):
    split_rows = P("batch", ("narrow", "wide"), None)
    split_filter = P(("narrow", "wide"), None)
    return jax.shard_map(
        per_device,
        mesh=mesh,
        in_specs=(split_rows, P(), P(), split_filter, split_filter, P(), split_rows),
        out_specs=(split_rows, split_rows, P(), P(), split_filter, split_filter, P()),
        check_vma=False,
    )
```

time: 839 us -> 138 us (0.16)
  waiting for transfers between devices: 391 us -> 0 us
  blocking collectives: 233 us -> 122 us
  starting transfers between devices: 80.9 us -> 0 us
  matrix products: 66.6 us -> 0 us
  local copies, waits for them, and re-layouts: 34.4 us -> 0 us
  Pallas kernels: 0 us -> 15.4 us
  between operations: 16 us -> 0.64 us
    psum x2 -> x0, waiting for transfers between devices: 248 us -> none  [the longest x1 248 us: per_device(): lax.psum((part_in_weight, part_out_weight, part_kernel), ('batch', 'narro...]
    all_to_all x9 -> x0, waiting for transfers between devices: 138 us -> none  [the longest x3 65.3 us: spectrum(): lax.all_to_all(packed, ('narrow', 'wide'), split_axis=2, concat_axis=3, t...]
    psum x1 -> x0, blocking collectives: 80.1 us -> none  [per_device(): lax.psum((part_in_weight, part_out_weight, part_kernel), ('batch', 'narro...]
    all_to_all x9 -> x0, starting transfers between devices: 72 us -> none  [the longest x3 31.3 us: spectrum(): lax.all_to_all(packed, ('narrow', 'wide'), split_axis=2, concat_axis=3, t...]
    dot_general x86 -> x0, matrix products: 66.6 us -> none  [the longest x8 8.11 us: local_dft(): jnp.einsum('jq,nmkqd->nmjkd', second_sin, turned_imag, precision=precise)]
    all_to_all x7 -> x4, blocking collectives: 153 us -> 122 us  [exchange(): return lax.all_to_all(x, everyone, split_axis=0, concat_axis=0, tiled=True)]
    pallas_call x0 -> x5, Pallas kernels: none -> 15.4 us  [the longest x1 6.18 us: per_device(): call(convolve_kernel, shape((devices, 8, rows), bf16), [scratch, scratch])]
    another operation x14 -> x0, local copies, waits for them, and re-layouts: 10.2 us -> none  [the longest x4 4.73 us: spectrum(): jnp.stack([real_part * turn_cos + imag_part * turn_sin, imag_part * turn_...]
  transfers between devices with their start and end apart: 13 -> 0, of which waited for: 11 -> 0; matrix products, arithmetic and copies ran while one was open for 5% -> 0% of each run, Pallas kernels for 0% -> 0%
where the time goes in v1:
time: 138 us
  blocking collectives  122 us (88%)
  Pallas kernels  15.4 us (11%)
    all_to_all x4, blocking collectives, exchange(): return lax.all_to_all(x, everyone, split_axis=0, concat_axis=0, tiled=True)  122 us
    pallas_call x1, Pallas kernels, per_device(): call(convolve_kernel, shape((devices, 8, rows), bf16), [scratch, scratch])  6.18 us

profile of v1, /device:TPU:1, one launch (start us, length us, event | category | flops | bytes accessed | tf_op | source)
XLA Modules:
  0.0 137.6 jit_solution(16449189868754232683)
XLA Ops:
  0.6 2.4 %shard_map.216 = bf16[256,8,128]{2,1,0:T(8,128)(2,1)} custom-call(bf16[1,128,256]{2,1,0:T(8,128)(2,1)} %seq_ref.3, bf16[256,768]{1,0:T(8,128)(2,1)} %in_weight_ref.3, f32[128,256]{1,0:T(8,128)} %one_ref.1, f32[128,256]{1,0:T(8,128)} %two_ref.1, bf16[256,256]{1,0:T(8,128)(2,1)} %out_weight_ref.3, bf16[1,128,256]{2,1,0:T(8,128)(2,1)} %grad_ref.3), custom_call_target="tpu_custom_call" | custom-call | tf_op jit(solution)/shard_map/pallas_call | solution.py:366
  3.0 36.7 %all_to_all.20.in_ref = bf16[256,8,128]{2,1,0:T(8,128)(2,1)} all-to-all(bf16[256,8,128]{2,1,0:T(8,128)(2,1)} %shard_map.216), channel_id=1, replica_groups=mesh['batch'=2,'narrow'=8,'wide'=16] {'batch','narrow','wide'}, dimensions={0} | all-to-all | bytes 1048576 | tf_op jit(solution)/shard_map/all_to_all | solution.py:356
  39.6 6.2 %shard_map.217 = bf16[256,8,128]{2,1,0:T(8,128)(2,1)} custom-call(bf16[256,8,128]{2,1,0:T(8,128)(2,1)} %all_to_all.20.in_ref, f32[3,768]{1,0:T(4,128)} %short_ref.1, bf16[256,128]{1,0:T(8,128)(2,1)} %constant.20.clone.first_high, bf16[256,128]{1,0:T(8,128)(2,1)} %constant.21.clone.first_low, bf16[256,256]{1,0:T(8,128)(2,1)} %constant.22.clone.second_high, ...), custom_call_target="tpu_custom_call" | custom-call | tf_op jit(solution)/shard_map/pallas_call | solution.py:371
  45.8 28.3 %all_to_all.21.in_ref = bf16[256,8,128]{2,1,0:T(8,128)(2,1)} all-to-all(bf16[256,8,128]{2,1,0:T(8,128)(2,1)} %shard_map.217), channel_id=1, replica_groups=mesh['batch'=2,'narrow'=8,'wide'=16] {'batch','narrow','wide'}, dimensions={0} | all-to-all | bytes 1048576 | tf_op jit(solution)/shard_map/all_to_all | solution.py:356
  74.1 2.6 %shard_map.218 = (bf16[1,128,256]{2,1,0:T(8,128)(2,1)}, bf16[1,128,256]{2,1,0:T(8,128)(2,1)}, f32[3,768]{1,0:T(4,128)}, f32[128,256]{1,0:T(8,128)}, f32[128,256]{1,0:T(8,128)}, /*index=5*/bf16[2048,128]{1,0:T(8,128)(2,1)}) custom-call(bf16[256,8,128]{2,1,0:T(8,128)(2,1)} %all_to_all.21.in_ref, bf16[1,128,256]{2,1,0:T(8,128)(2,1)} %seq_ref.3, ...), custom_call_target="tpu_custom_call" | custom-call | tf_op jit(solution)/shard_map/pallas_call | solution.py:375
  76.8 28.3 %all_to_all.22.in_ref = bf16[256,8,128]{2,1,0:T(8,128)(2,1)} all-to-all(bf16[256,8,128]{2,1,0:T(8,128)(2,1)} %bitcast.3), channel_id=1, replica_groups=mesh['batch'=2,'narrow'=8,'wide'=16] {'batch','narrow','wide'}, dimensions={0} | all-to-all | bytes 1048576 | tf_op jit(solution)/shard_map/all_to_all | solution.py:356
  105.1 2.1 %shard_map.219 = bf16[256,8,128]{2,1,0:T(8,128)(2,1)} custom-call(bf16[256,8,128]{2,1,0:T(8,128)(2,1)} %all_to_all.22.in_ref), custom_call_target="tpu_custom_call" | custom-call | tf_op jit(solution)/shard_map/pallas_call | solution.py:388
  107.2 28.3 %all_to_all.23 = bf16[256,8,128]{2,1,0:T(8,128)(2,1)} all-to-all(bf16[256,8,128]{2,1,0:T(8,128)(2,1)} %shard_map.219), channel_id=1, replica_groups=mesh['batch'=2,'narrow'=8,'wide'=16] {'batch','narrow','wide'}, dimensions={0} | all-to-all | bytes 1048576 | tf_op jit(solution)/shard_map/all_to_all | solution.py:356
  135.5 2.1 %shard_map.220 = (f32[256,768]{1,0:T(8,128)}, f32[256,256]{1,0:T(8,128)}) custom-call(bf16[2048,128]{1,0:T(8,128)(2,1)} %bitcast.2), custom_call_target="tpu_custom_call" | custom-call | tf_op jit(solution)/shard_map/pallas_call | solution.py:389

commit v2 on v1

--- a/solution.py
+++ b/solution.py
@@ -1,3 +1,4 @@
+import functools
 import math
 
 import jax
@@ -6,9 +7,10 @@
 from jax import lax
 from jax.experimental import pallas as pl
 from jax.experimental.pallas import tpu as pltpu
+from jax.sharding import Mesh
 from jax.sharding import PartitionSpec as P
 
-everyone = ("batch", "narrow", "wide")
+everyone = ("zh", "x", "core", "zl", "y")
 vmem_limit = 56 * 1024 * 1024
 
 
@@ -57,7 +59,7 @@
     return bf16_dot(x_high, high) + bf16_dot(x_high, low) + bf16_dot(x_low, high)
 
 
-def pack_kernel(seq_ref, in_weight_ref, one_ref, two_ref, out_weight_ref, grad_ref, out_ref, rows_ref):
+def pack_kernel(seq_ref, in_weight_ref, one_ref, two_ref, out_weight_ref, grad_ref, out_ref, both_ref, rows_ref):
     width = out_weight_ref.shape[0]
     slots = rows_ref.shape[0] // width
     contract_first = (((0,), (1,)), ((), ()))
@@ -90,8 +92,10 @@
             out_weight_ref[...], grad_ref[0], contract_last, preferred_element_type=jnp.float32
         ),
     )
-    chosen = jnp.where(lax.axis_index("batch") == 0, one_ref[...], two_ref[...])
+    chosen = jnp.where(lax.axis_index("zh") == 0, one_ref[...], two_ref[...])
     put_two(6, chosen.T)
+    both_ref[:, :width] = seq
+    both_ref[:, width:] = grad_ref[0]
     out_ref[...] = rows_ref[...].reshape(out_ref.shape).astype(jnp.bfloat16)
 
 
@@ -109,8 +113,8 @@
     turn_cos_ref,
     turn_sin_ref,
     out_ref,
+    sums_ref,
     rows_ref,
-    send_ref,
 ):
     sources, slots, rows = in_ref.shape
     blocks = sources // 2
@@ -177,9 +181,7 @@
     def added(a, b):
         return a[0] + b[0], a[1] + b[1]
 
-    mesh_place = (
-        lax.axis_index("batch") * lax.axis_size("narrow") + lax.axis_index("narrow")
-    ) * lax.axis_size("wide") + lax.axis_index("wide")
+    mesh_place = lax.axis_index(everyone)
     short = short_ref[...]
     short_lane = lax.broadcasted_iota(jnp.int32, short.shape, 1)
     taps = []
@@ -236,111 +238,175 @@
     conv_two, grad_value = found[:2], found[2:4]
     grad_filters = [found[4] * scale, found[5] * scale]
 
-    def put(member, index, x):
-        send_ref[pl.ds(member * blocks * slots + index, blocks, stride=slots), :] = x
-
+    new = lax.broadcasted_iota(jnp.int32, (blocks, blocks), 0)
+    old = lax.broadcasted_iota(jnp.int32, (blocks, blocks), 1)
+    wanted = (new & 99) | (((new >> 2) & 1) << 4) | (((new >> 3) & 3) << 2)
+    reorder = jnp.where(old == wanted, 1.0, 0.0).astype(jnp.bfloat16)
     sums = [[0.0] * 3 for _ in range(3)]
     for m in members:
-        put(m, 0, mixed[m][2] * conv_two[m])
+        sent = [mixed[m][2] * conv_two[m]]
         grads = [grad_value[m], grad_gated[m] * conv_one[m], pre[m] * conv_two[m]]
         for g in range(3):
-            put(
-                m,
-                1 + g,
+            sent.append(
                 taps[g][0] * grads[g]
                 + taps[g][1] * earlier(grads[g], 1)
-                + taps[g][2] * earlier(grads[g], 2),
+                + taps[g][2] * earlier(grads[g], 2)
             )
             for tap, lagged in enumerate((projected, lagged_one, lagged_two)):
                 sums[g][tap] = sums[g][tap] + jnp.sum(
                     jnp.sum(grads[g] * lagged[m][g], axis=0, keepdims=True), axis=1, keepdims=True
                 )
-        put(m, 4, grad_filters[0])
-        put(m, 5, grad_filters[1])
-    sum_lane = lax.broadcasted_iota(jnp.int32, (1, rows), 1)
-    line = jnp.zeros((1, rows), jnp.float32)
+        sent.extend(grad_filters)
+        turned = bf16_dot(reorder, jnp.concatenate(sent, 1).astype(jnp.bfloat16))
+        half = out_ref.shape[0] // 2
+        for index in range(len(sent)):
+            out_ref[m * half : (m + 1) * half, index] = (
+                turned[:, index * rows : (index + 1) * rows]
+                .reshape(half, blocks // half, rows)
+                .astype(jnp.bfloat16)
+            )
+    shape = sums_ref.shape
+    sum_lane = lax.broadcasted_iota(jnp.int32, shape, 1)
+    line = jnp.zeros(shape, jnp.float32)
     for g in range(3):
         for tap in range(3):
             total = sums[g][tap] * scale
             high = total.astype(jnp.bfloat16).astype(jnp.float32)
             line = jnp.where(sum_lane == g * 3 + tap, high, line)
             line = jnp.where(sum_lane == 16 + g * 3 + tap, total - high, line)
-    line = jnp.broadcast_to(line, (blocks, rows))
-    for m in members:
-        put(m, 6, line)
-        put(m, 7, jnp.zeros((blocks, rows), jnp.float32))
-    out_ref[...] = send_ref[...].reshape(out_ref.shape).astype(jnp.bfloat16)
-
-
-def finish_kernel(
-    in_ref,
-    seq_ref,
-    in_weight_ref,
-    out_weight_ref,
-    grad_ref,
-    outputs_ref,
-    grad_inputs_ref,
-    short_ref,
-    one_ref,
-    two_ref,
-    part_ref,
-    rows_ref,
-):
-    width, slots, rows = in_ref.shape
+    own_row = lax.broadcasted_iota(jnp.int32, shape, 0) == lax.axis_index(("zh", "zl"))
+    sums_ref[...] = jnp.where(own_row, line, 0.0)
+
+
+def channel_order(place_of):
+    channel = lax.broadcasted_iota(jnp.int32, (256, 256), 0)
+    row = lax.broadcasted_iota(jnp.int32, (256, 256), 1)
+    zh, x, core = channel >> 7, (channel >> 5) & 3, (channel >> 4) & 1
+    zl, y = (channel >> 2) & 3, channel & 3
+    return jnp.where(row == place_of(zh, x, core, zl, y), 1.0, 0.0).astype(jnp.bfloat16)
+
+
+def part_kernel(in_ref, *refs):
+    both_refs, part_ref, send_refs, rows_ref = refs[:8], refs[8], refs[9:13], refs[13]
+    sources, kinds, blocks, rows = in_ref.shape
+    width = both_refs[0].shape[1] // 2
+    core, y = lax.axis_index("core"), lax.axis_index("y")
+    rows_ref[...] = in_ref[...].astype(jnp.float32).reshape(sources * kinds * blocks, rows)
+    out_part = jnp.zeros((sources, width), jnp.float32)
+    in_part = jnp.zeros((3 * sources, width), jnp.float32)
+    for other in range(2):
+        for ahead in range(4):
+            block = (core ^ other) * 4 + ((y + ahead) & 3)
+            kept = jnp.concatenate(
+                [
+                    rows_ref[pl.ds(kind * blocks + block, sources, stride=kinds * blocks), :]
+                    for kind in range(kinds)
+                ],
+                0,
+            ).astype(jnp.bfloat16)
+            send_refs[ahead][other] = kept
+            both_ref = both_refs[other * 4 + (4 - ahead) % 4]
+            out_part += bf16_dot(kept[:sources], both_ref[:, width:])
+            in_part += bf16_dot(kept[sources : 4 * sources], both_ref[:, :width])
+    part_ref[0] = out_part
+    for group in range(3):
+        part_ref[1 + group] = in_part[group * sources : (group + 1) * sources]
+
+
+def finish_kernel(*refs):
+    held = refs[:8]
+    in_weight_ref, out_weight_ref, outputs_ref, grad_inputs_ref, one_ref, two_ref = refs[8:]
+    width = out_weight_ref.shape[0]
+    count = width // 8
+    core, y = lax.axis_index("core"), lax.axis_index("y")
+    order = channel_order(
+        lambda zh, x, c, zl, v: (
+            (((c ^ core) * 4 + ((y - v) & 3)) * 32) + (zh * 16 + x * 4 + zl)
+        )
+    )
+    contract_first = (((0,), (1,)), ((), ()))
     contract_last = (((1,), (1,)), ((), ()))
-    rows_ref[...] = in_ref[...].astype(jnp.float32).reshape(width * slots, rows)
-
-    def column(index):
-        return rows_ref[pl.ds(index, width, stride=slots), :]
-
-    pre_out = column(0)
-    outputs_ref[0] = bf16_dot(pre_out.T.astype(jnp.bfloat16), out_weight_ref[...]).astype(
+
+    def natural(kind):
+        stacked = jnp.concatenate(
+            [held[i][i // 4, kind * count : (kind + 1) * count, :] for i in range(8)], 0
+        )
+        return lax.dot_general(
+            stacked, order, contract_first, preferred_element_type=jnp.float32
+        )
+
+    outputs_ref[0] = bf16_dot(natural(0).astype(jnp.bfloat16), out_weight_ref[...]).astype(
         jnp.bfloat16
     )
-    parts = []
-    seq_turned = seq_ref[0].astype(jnp.float32).T.astype(jnp.bfloat16)
     total = None
     for group in range(3):
-        grad = column(1 + group).T.astype(jnp.bfloat16)
         term = lax.dot_general(
-            grad,
+            natural(1 + group).astype(jnp.bfloat16),
             in_weight_ref[:, group * width : (group + 1) * width],
             contract_last,
             preferred_element_type=jnp.float32,
         )
         total = term if total is None else total + term
-        parts.append(bf16_dot(seq_turned, grad))
     grad_inputs_ref[0] = total.astype(jnp.bfloat16)
-    parts.append(bf16_dot(pre_out.astype(jnp.bfloat16), grad_ref[0]))
-    for index, part in enumerate(parts):
+    one_ref[...] = natural(4)
+    two_ref[...] = natural(5)
+
+
+def add_x_kernel(in_ref, sums_ref, out_ref):
+    total = jnp.sum(in_ref[...], axis=0)
+    count, lanes = total.shape[0], out_ref.shape[2]
+    rows = jnp.concatenate([total[:, :lanes], total[:, lanes:], sums_ref[...]], 0)
+    out_ref[...] = jnp.broadcast_to(rows.astype(jnp.bfloat16)[None], out_ref.shape)
+
+
+def add_z_kernel(scale, in_ref, out_ref):
+    total = jnp.sum(in_ref[...].astype(jnp.float32), axis=0)
+    row = lax.broadcasted_iota(jnp.int32, total.shape, 0)
+    total = total * jnp.where(row < 64, scale, 1.0)
+    out_ref[...] = jnp.broadcast_to(total.astype(jnp.bfloat16)[None], out_ref.shape)
+
+
+def place_kernel(own_ref, other_ref, in_weight_ref, out_weight_ref, short_ref):
+    width, lanes = out_weight_ref.shape[0], own_ref.shape[2]
+    core = lax.axis_index("core")
+    order = channel_order(
+        lambda zh, x, c, zl, y: ((c ^ core) * 4 + y) * 32 + (zh * 16 + x * 4 + zl)
+    )
+    contract_first = (((0,), (1,)), ((), ()))
+    for kind in range(4):
         for half in range(2):
-            place = (index * 2 + half) * width
-            part_ref[place : place + width, :] = part[
-                :, half * rows : (half + 1) * rows
-            ].astype(jnp.bfloat16)
-    one_ref[...] = column(4).T
-    two_ref[...] = column(5).T
-    sums = column(6).T
+            stacked = jnp.concatenate(
+                [
+                    ref[kind * 4 + y, half * 32 : (half + 1) * 32, :]
+                    for ref in (own_ref, other_ref)
+                    for y in range(4)
+                ],
+                0,
+            )
+            if kind == 0:
+                out_weight_ref[:, half * lanes : (half + 1) * lanes] = bf16_dot(order, stacked)
+            else:
+                in_weight_ref[
+                    half * lanes : (half + 1) * lanes, (kind - 1) * width : kind * width
+                ] = lax.dot_general(
+                    stacked, order, contract_first, preferred_element_type=jnp.float32
+                )
+    sums = jnp.concatenate(
+        [
+            ref[i, 64:80, :].astype(jnp.float32)[:8]
+            for ref in (own_ref, other_ref)
+            for i in range(16)
+        ],
+        0,
+    ).astype(jnp.bfloat16)
+    order = channel_order(
+        lambda zh, x, c, zl, y: ((c ^ core) * 16 + x * 4 + y) * 8 + zh * 4 + zl
+    )
+    sums = lax.dot_general(sums, order, contract_first, preferred_element_type=jnp.float32)
     for group in range(3):
         short_ref[:, group * width : (group + 1) * width] = (
             sums[group * 3 : group * 3 + 3, :] + sums[16 + group * 3 : 19 + group * 3, :]
         )
-
-
-def add_kernel(in_ref, out_ref):
-    scale = 1.0 / math.sqrt(in_ref.shape[0] * 128)
-    total = jnp.sum(in_ref[...].astype(jnp.float32), axis=0) * scale
-    out_ref[...] = jnp.broadcast_to(total[None], out_ref.shape).astype(jnp.bfloat16)
-
-
-def place_kernel(in_ref, in_weight_ref, out_weight_ref):
-    width, lanes = out_weight_ref.shape[0], in_ref.shape[1]
-    for index in range(8):
-        block = in_ref[index * width : (index + 1) * width, :].astype(jnp.float32)
-        if index < 6:
-            in_weight_ref[:, index * lanes : (index + 1) * lanes] = block
-        else:
-            out_weight_ref[:, (index - 6) * lanes : (index - 5) * lanes] = block
 
 
 def call(kernel, out_shape, scratch=()):
@@ -352,43 +418,65 @@
     )
 
 
-def exchange(x):
-    return lax.all_to_all(x, everyone, split_axis=0, concat_axis=0, tiled=True)
+def exchange(x, axes):
+    return lax.all_to_all(x, axes, split_axis=0, concat_axis=0, tiled=True)
+
+
+def swap_core(x):
+    return lax.ppermute(x, "core", [(0, 1), (1, 0)])
+
+
+def ring(x, distance):
+    return lax.ppermute(x, "y", [(i, (i + distance) % 4) for i in range(4)])
 
 
 def per_device(inputs, in_weight, short_kernel, filter_one, filter_two, out_weight, out_grad):
     width = out_weight.shape[0]
     rows = inputs.shape[1]
     devices = lax.axis_size(everyone)
+    scale = 1.0 / math.sqrt(devices * rows)
     shape = jax.ShapeDtypeStruct
     f32, bf16 = jnp.float32, jnp.bfloat16
-    scratch = pltpu.VMEM((devices * 8, rows), f32)
-    packed = call(pack_kernel, shape((width, 8, rows), bf16), [scratch])(
-        inputs, in_weight, filter_one, filter_two, out_weight, out_grad
-    )
-    received = exchange(packed)
+    packed, both = call(
+        pack_kernel,
+        (shape((width, 8, rows), bf16), shape((rows, 2 * width), bf16)),
+        [pltpu.VMEM((width * 8, rows), f32)],
+    )(inputs, in_weight, filter_one, filter_two, out_weight, out_grad)
+    received = exchange(packed, everyone)
+    gathered = [both] + [ring(both, distance) for distance in (1, 2, 3)]
+    gathered += [swap_core(x) for x in gathered]
     tables = [jnp.asarray(t) for t in transform_tables(devices // 2, rows)]
-    back = call(convolve_kernel, shape((devices, 8, rows), bf16), [scratch, scratch])(
-        received, short_kernel, *tables
-    )
-    home = exchange(back)
-    outputs, grad_inputs, grad_short, grad_one, grad_two, part = call(
+    back, sums = call(
+        convolve_kernel,
+        (shape((32, 6, 8, rows), bf16), shape((16, rows), f32)),
+        [pltpu.VMEM((devices * 8, rows), f32)],
+    )(received, short_kernel, *tables)
+    halfway = exchange(back, ("zh", "x", "zl"))
+    part, *leaving = call(
+        part_kernel,
+        (shape((4, 32, width), f32),) + (shape((2, 6 * 32, rows), bf16),) * 4,
+        [pltpu.VMEM((32 * 6 * 8, rows), f32)],
+    )(halfway, *gathered)
+    arrived = [leaving[0]] + [ring(leaving[distance], distance) for distance in (1, 2, 3)]
+    arrived += [swap_core(x) for x in arrived]
+    part = exchange(part, "x")
+    part = call(add_x_kernel, shape((8, 80, rows), bf16))(part, sums)
+    part = exchange(part, ("zh", "zl"))
+    part = call(functools.partial(add_z_kernel, scale), shape((16, 80, rows), bf16))(part)
+    part = exchange(part, ("x", "y"))
+    grad_in_weight, grad_out_weight, grad_short = call(
+        place_kernel,
+        (shape((width, 3 * width), f32), shape((width, width), f32), shape((3, 3 * width), f32)),
+    )(part, swap_core(part))
+    outputs, grad_inputs, grad_one, grad_two = call(
         finish_kernel,
         (
             shape((1, rows, width), bf16),
             shape((1, rows, width), bf16),
-            shape((3, 3 * width), f32),
             shape((rows, width), f32),
             shape((rows, width), f32),
-            shape((8 * width, rows), bf16),
         ),
-        [scratch],
-    )(home, inputs, in_weight, out_weight, out_grad)
-    part = exchange(part.reshape(devices, 8 * width // devices, rows))
-    whole = exchange(call(add_kernel, shape(part.shape, bf16))(part))
-    grad_in_weight, grad_out_weight = call(
-        place_kernel, (shape((width, 3 * width), f32), shape((width, width), f32))
-    )(whole.reshape(8 * width, rows))
+    )(*arrived, in_weight, out_weight)
     return (
         outputs,
         grad_inputs,
@@ -401,8 +489,9 @@
 
 
 def solution(mesh):
-    split_rows = P("batch", ("narrow", "wide"), None)
-    split_filter = P(("narrow", "wide"), None)
+    mesh = Mesh(mesh.devices.reshape(2, 4, 2, 4, 4), everyone)
+    positions = ("x", "core", "zl", "y")
+    split_rows, split_filter = P("zh", positions, None), P(positions, None)
     return jax.shard_map(
         per_device,
         mesh=mesh,

time: 138 us -> 127 us (0.920)
  blocking collectives: 122 us -> 71.1 us
  starting transfers between devices: 0 us -> 24.4 us
  waiting for transfers between devices: 0 us -> 8.09 us
  Pallas kernels: 15.4 us -> 19.4 us
  local copies, waits for them, and re-layouts: 0 us -> 2.57 us
    all_to_all x4, blocking collectives: 122 us -> 71.1 us  [exchange(): return lax.all_to_all(x, axes, split_axis=0, concat_axis=0, tiled=True)]
    ppermute x0 -> x15, starting transfers between devices: none -> 20.4 us  [the longest x9 14.7 us: swap_core(): return lax.ppermute(x, 'core', [(0, 1), (1, 0)])]
    ppermute x0 -> x15, waiting for transfers between devices: none -> 6.55 us  [the longest x6 4.66 us: ring(): return lax.ppermute(x, 'y', [(i, (i + distance) % 4) for i in range(4)])]
    all_to_all x0 -> x1, starting transfers between devices: none -> 4.01 us  [exchange(): return lax.all_to_all(x, axes, split_axis=0, concat_axis=0, tiled=True)]
    pallas_call x3 -> x5, Pallas kernels: 10.7 us -> 14.2 us  [the longest x1 6.12 us: per_device(): call(convolve_kernel, (shape((32, 6, 8, rows), bf16), shape((16, rows), f...]
    unnamed x0 -> x44, local copies, waits for them, and re-layouts: none -> 2.57 us
    all_to_all x0 -> x1, waiting for transfers between devices: none -> 1.54 us  [exchange(): return lax.all_to_all(x, axes, split_axis=0, concat_axis=0, tiled=True)]
  transfers between devices with their start and end apart: 0 -> 16, of which waited for: 0 -> 8; matrix products, arithmetic and copies ran while one was open for 0% -> 0% of each run, Pallas kernels for 0% -> 2%
where the time goes in v2:
time: 127 us; the launch traced here: 126 us
  blocking collectives  71.1 us (56%)
  starting transfers between devices  24.4 us (19%)
  Pallas kernels  19.4 us (15%)
  waiting for transfers between devices  8.09 us (6%)
  local copies, waits for them, and re-layouts  2.57 us (2%)
    all_to_all x4, blocking collectives, exchange(): return lax.all_to_all(x, axes, split_axis=0, concat_axis=0, tiled=True)  71.1 us
    ppermute x9, starting transfers between devices, swap_core(): return lax.ppermute(x, 'core', [(0, 1), (1, 0)])  14.7 us
    pallas_call x1, Pallas kernels, per_device(): call(convolve_kernel, (shape((32, 6, 8, rows), bf16), shape((16, rows), f...  6.12 us
    ppermute x6, starting transfers between devices, ring(): return lax.ppermute(x, 'y', [(i, (i + distance) % 4) for i in range(4)])  5.66 us
    ppermute x6, waiting for transfers between devices, ring(): return lax.ppermute(x, 'y', [(i, (i + distance) % 4) for i in range(4)])  4.66 us
    all_to_all x1, starting transfers between devices, exchange(): return lax.all_to_all(x, axes, split_axis=0, concat_axis=0, tiled=True)  4.01 us
    pallas_call x1, Pallas kernels, per_device(): call(finish_kernel, (shape((1, rows, width), bf16), shape((1, rows, width...  2.73 us
    unnamed x44, local copies, waits for them, and re-layouts  2.57 us
  transfers between devices with their start and end apart: 16, of which 8 were waited for; matrix products, arithmetic and copies ran while one was open for 0% of the time, Pallas kernels for 2%

profile of v2, /device:TPU:1, one launch (start us, length us, event | category | flops | bytes accessed | tf_op | source)
XLA Modules:
  0.0 126.3 jit_solution(1880046507453663258)
XLA Ops:
  0.6 2.4 %shard_map.216 = (bf16[256,8,128]{2,1,0:T(8,128)(2,1)}, bf16[128,512]{1,0:T(8,128)(2,1)}) custom-call(bf16[1,128,256]{2,1,0:T(8,128)(2,1)} %seq_ref.1, bf16[256,768]{1,0:T(8,128)(2,1)} %refs_8_.1, f32[128,256]{1,0:T(8,128)} %one_ref.1, f32[128,256]{1,0:T(8,128)} %two_ref.1, bf16[256,256]{1,0:T(8,128)(2,1)} %refs_9_.1, bf16[1,128,256]{2,1,0:T(8,128)(2,1)} %grad_ref.1), custom_call_target="tpu_custom_call" | custom-call | tf_op jit(solution)/shard_map/pallas_call | solution.py:440
  3.0 36.7 %all_to_all.25.in_ref = bf16[256,8,128]{2,1,0:T(8,128)(2,1)} all-to-all(bf16[256,8,128]{2,1,0:T(8,128)(2,1)} %get-tuple-element.23), channel_id=1, replica_groups=mesh['zh'=2,'x'=4,'core'=2,'zl'=4,'y'=4] {'zh','x','core','zl','y'}, dimensions={0} | all-to-all | bytes 1048576 | tf_op jit(solution)/shard_map/all_to_all | solution.py:422
  39.7 6.1 %shard_map.217 = (bf16[32,6,8,128]{3,2,1,0:T(8,128)(2,1)}, f32[16,128]{1,0:T(8,128)}) custom-call(bf16[256,8,128]{2,1,0:T(8,128)(2,1)} %all_to_all.25.in_ref, f32[3,768]{1,0:T(4,128)} %short_ref.1, bf16[256,128]{1,0:T(8,128)(2,1)} %constant.20.clone.first_high, bf16[256,128]{1,0:T(8,128)(2,1)} %constant.21.clone.first_low, ...), custom_call_target="tpu_custom_call" | custom-call | tf_op jit(solution)/shard_map/pallas_call | solution.py:449
  45.8 4.0 %all-to-all-start.1 = ((bf16[32,6,8,128]{3,2,1,0:T(8,128)(2,1)}), bf16[32,6,8,128]{3,2,1,0:T(8,128)(2,1)S(1)}, u32[]{:S(2)}, u32[]{:S(2)}) async-start(bf16[32,6,8,128]{3,2,1,0:T(8,128)(2,1)} %get-tuple-element.24), calls=%async_computation.1 | async-start | bytes 786432 | tf_op jit(solution)/shard_map/all_to_all | solution.py:422
  49.8 1.3 %collective-permute-start.2 = (bf16[128,512]{1,0:T(8,128)(2,1)S(1)}, bf16[128,512]{1,0:T(8,128)(2,1)S(1)}, u32[]{:S(2)}, u32[]{:S(2)}) collective-permute-start(bf16[128,512]{1,0:T(8,128)(2,1)S(1)} %copy-done.3), channel_id=1, source_target_pairs={{0,3},{1,0},{2,1},{3,2},{4,7},{5,4},{6,5},{7,6},{8,11},{9,8},{10,9... | collective-permute-start | bytes 393224 | tf_op jit(solution)/shard_map/ppermute | solution.py:430
  52.2 1.4 %collective-permute-start.3 = (bf16[128,512]{1,0:T(8,128)(2,1)S(1)}, bf16[128,512]{1,0:T(8,128)(2,1)S(1)}, u32[]{:S(2)}, u32[]{:S(2)}) collective-permute-start(bf16[128,512]{1,0:T(8,128)(2,1)S(1)} %copy-done.3), channel_id=1, source_target_pairs={{0,16},{16,0},{1,17},{17,1},{2,18},{18,2},{3,19},{19,3},{4,20},{20... | collective-permute-start | bytes 393224 | tf_op jit(solution)/shard_map/ppermute | solution.py:426
  54.2 3.0 %collective-permute-start.6 = (bf16[128,512]{1,0:T(8,128)(2,1)S(1)}, bf16[128,512]{1,0:T(8,128)(2,1)S(1)}, u32[]{:S(2)}, u32[]{:S(2)}) collective-permute-start(bf16[128,512]{1,0:T(8,128)(2,1)S(1)} %collective-permute-done.2.refs_3_), channel_id=1, source_target_pairs={{0,16},{16,0},{1,17},{17,1},{2,18},{18,2},{3,19},{19,3},{4,20},{20... | collective-permute-start | bytes 393224 | tf_op jit(solution)/shard_map/ppermute | solution.py:426
  57.2 2.3 %collective-permute-start.5 = (bf16[128,512]{1,0:T(8,128)(2,1)S(1)}, bf16[128,512]{1,0:T(8,128)(2,1)S(1)}, u32[]{:S(2)}, u32[]{:S(2)}) collective-permute-start(bf16[128,512]{1,0:T(8,128)(2,1)S(1)} %collective-permute-done.1.refs_2_), channel_id=1, source_target_pairs={{0,16},{16,0},{1,17},{17,1},{2,18},{18,2},{3,19},{19,3},{4,20},{20... | collective-permute-start | bytes 393224 | tf_op jit(solution)/shard_map/ppermute | solution.py:426
  61.4 0.9 collective-permute-done.4.refs_5_
  62.3 1.5 %all-to-all-done.1.in_ref = bf16[32,6,8,128]{3,2,1,0:T(8,128)(2,1)S(1)} async-done(((bf16[32,6,8,128]{3,2,1,0:T(8,128)(2,1)}), bf16[32,6,8,128]{3,2,1,0:T(8,128)(2,1)S(1)}, u32[]{:S(2)}, u32[]{:S(2)}) %all-to-all-start.1) | async-done | bytes 393248 | tf_op jit(solution)/shard_map/all_to_all | solution.py:422
  64.7 2.5 %shard_map.218 = (f32[4,32,256]{2,1,0:T(8,128)}, bf16[2,192,128]{2,1,0:T(8,128)(2,1)}, bf16[2,192,128]{2,1,0:T(8,128)(2,1)}, bf16[2,192,128]{2,1,0:T(8,128)(2,1)}, bf16[2,192,128]{2,1,0:T(8,128)(2,1)}) custom-call(bf16[32,6,8,128]{3,2,1,0:T(8,128)(2,1)} %copy-done, bf16[128,512]{1,0:T(8,128)(2,1)} %get-tuple-element.25.refs_0_, bf16[128,512]{1,0:T(8,128)(2,1)} %copy-done.6, ...), custom_call_target="tpu_custom_call" | custom-call | tf_op jit(solution)/shard_map/pallas_call | solution.py:455
  67.2 8.8 %all_to_all.26.in_ref = f32[4,32,256]{2,1,0:T(8,128)} all-to-all(f32[4,32,256]{2,1,0:T(8,128)} %get-tuple-element.32), channel_id=1, replica_groups=mesh['zh'=2,'x'=4,'core'=2,'zl'=4,'y'=4] {'x'}, dimensions={0} | all-to-all | bytes 262144 | tf_op jit(solution)/shard_map/all_to_all | solution.py:422
  76.0 1.6 %shard_map.220 = bf16[8,80,128]{2,1,0:T(8,128)(2,1)} custom-call(f32[4,32,256]{2,1,0:T(8,128)} %all_to_all.26.in_ref, f32[16,128]{1,0:T(8,128)} %get-tuple-element.33.sums_ref), custom_call_target="tpu_custom_call" | custom-call | tf_op jit(solution)/shard_map/pallas_call | solution.py:463
  77.6 14.1 %all_to_all.27.in_ref = bf16[8,80,128]{2,1,0:T(8,128)(2,1)} all-to-all(bf16[8,80,128]{2,1,0:T(8,128)(2,1)} %shard_map.220), channel_id=1, replica_groups=mesh['zh'=2,'x'=4,'core'=2,'zl'=4,'y'=4] {'zh','zl'}, dimensions={0} | all-to-all | bytes 327680 | tf_op jit(solution)/shard_map/all_to_all | solution.py:422
  91.7 1.7 %shard_map.221 = bf16[16,80,128]{2,1,0:T(8,128)(2,1)} custom-call(bf16[8,80,128]{2,1,0:T(8,128)(2,1)} %all_to_all.27.in_ref), custom_call_target="tpu_custom_call" | custom-call | tf_op jit(solution)/shard_map/pallas_call | solution.py:465
  93.3 11.6 %all_to_all.28.own_ref = bf16[16,80,128]{2,1,0:T(8,128)(2,1)S(1)} all-to-all(bf16[16,80,128]{2,1,0:T(8,128)(2,1)} %shard_map.221), channel_id=1, replica_groups=mesh['zh'=2,'x'=4,'core'=2,'zl'=4,'y'=4] {'x','y'}, dimensions={0} | all-to-all | bytes 655360 | tf_op jit(solution)/shard_map/all_to_all | solution.py:422
  104.9 4.4 %collective-permute-start.14 = (bf16[16,80,128]{2,1,0:T(8,128)(2,1)S(1)}, bf16[16,80,128]{2,1,0:T(8,128)(2,1)S(1)}, u32[]{:S(2)}, u32[]{:S(2)}) collective-permute-start(bf16[16,80,128]{2,1,0:T(8,128)(2,1)S(1)} %all_to_all.28.own_ref), channel_id=1, source_target_pairs={{0,16},{16,0},{1,17},{17,1},{2,18},{18,2},{3,19},{19,3},{4,20},{20... | collective-permute-start | bytes 983048 | tf_op jit(solution)/shard_map/ppermute | solution.py:426
  109.4 1.8 %collective-permute-start.8 = (bf16[2,192,128]{2,1,0:T(8,128)(2,1)S(1)}, bf16[2,192,128]{2,1,0:T(8,128)(2,1)S(1)}, u32[]{:S(2)}, u32[]{:S(2)}) collective-permute-start(bf16[2,192,128]{2,1,0:T(8,128)(2,1)S(1)} %copy-done.20), channel_id=1, source_target_pairs={{0,2},{1,3},{2,0},{3,1},{4,6},{5,7},{6,4},{7,5},{8,10},{9,11},{10,... | collective-permute-start | bytes 294920 | tf_op jit(solution)/shard_map/ppermute | solution.py:430
  111.2 1.4 %collective-permute-start.9 = (bf16[2,192,128]{2,1,0:T(8,128)(2,1)S(1)}, bf16[2,192,128]{2,1,0:T(8,128)(2,1)S(1)}, u32[]{:S(2)}, u32[]{:S(2)}) collective-permute-start(bf16[2,192,128]{2,1,0:T(8,128)(2,1)S(1)} %copy-done.19), channel_id=1, source_target_pairs={{0,3},{1,0},{2,1},{3,2},{4,7},{5,4},{6,5},{7,6},{8,11},{9,8},{10,9... | collective-permute-start | bytes 294920 | tf_op jit(solution)/shard_map/ppermute | solution.py:430
  112.6 1.1 collective-permute-start.10
  113.7 3.1 %collective-permute-done.7.refs_1_ = bf16[2,192,128]{2,1,0:T(8,128)(2,1)S(1)} collective-permute-done((bf16[2,192,128]{2,1,0:T(8,128)(2,1)S(1)}, bf16[2,192,128]{2,1,0:T(8,128)(2,1)S(1)}, u32[]{:S(2)}, u32[]{:S(2)}) %collective-permute-start.7) | collective-permute-done | bytes 98336 | tf_op jit(solution)/shard_map/ppermute | solution.py:430
  116.8 1.0 collective-permute-start.11
  120.4 2.7 %shard_map.219 = (bf16[1,128,256]{2,1,0:T(8,128)(2,1)}, bf16[1,128,256]{2,1,0:T(8,128)(2,1)}, f32[128,256]{1,0:T(8,128)}, f32[128,256]{1,0:T(8,128)}) custom-call(bf16[2,192,128]{2,1,0:T(8,128)(2,1)} %get-tuple-element.26.refs_0_, bf16[2,192,128]{2,1,0:T(8,128)(2,1)} %copy-done.12, bf16[2,192,128]{2,1,0:T(8,128)(2,1)} %copy-done.13, ...), custom_call_target="tpu_custom_call" | custom-call | tf_op jit(solution)/shard_map/pallas_call | solution.py:471
  123.9 2.4 %shard_map.222 = (f32[256,768]{1,0:T(8,128)}, f32[256,256]{1,0:T(8,128)}, f32[3,768]{1,0:T(4,128)}) custom-call(bf16[16,80,128]{2,1,0:T(8,128)(2,1)} %copy-done.1, bf16[16,80,128]{2,1,0:T(8,128)(2,1)} %copy-done.2), custom_call_target="tpu_custom_call" | custom-call | tf_op jit(solution)/shard_map/pallas_call | solution.py:467
  (63 shorter events, 7.7 us)
Async XLA Ops:
  45.8 4.0 %copy-start.3 = (bf16[128,512]{1,0:T(8,128)(2,1)S(1)}, bf16[128,512]{1,0:T(8,128)(2,1)}, u32[]{:S(2)}) copy-start(bf16[128,512]{1,0:T(8,128)(2,1)} %get-tuple-element.25.refs_0_) | copy-start | bytes 393220
  45.8 18.1 %all-to-all-start.1 = ((bf16[32,6,8,128]{3,2,1,0:T(8,128)(2,1)}), bf16[32,6,8,128]{3,2,1,0:T(8,128)(2,1)S(1)}, u32[]{:S(2)}, u32[]{:S(2)}) async-start(bf16[32,6,8,128]{3,2,1,0:T(8,128)(2,1)} %get-tuple-element.24), calls=%async_computation.1 | async-start | bytes 786432 | tf_op jit(solution)/shard_map/all_to_all | solution.py:422
  49.8 4.4 %collective-permute-start.2 = (bf16[128,512]{1,0:T(8,128)(2,1)S(1)}, bf16[128,512]{1,0:T(8,128)(2,1)S(1)}, u32[]{:S(2)}, u32[]{:S(2)}) collective-permute-start(bf16[128,512]{1,0:T(8,128)(2,1)S(1)} %copy-done.3), channel_id=1, source_target_pairs={{0,3},{1,0},{2,1},{3,2},{4,7},{5,4},{6,5},{7,6},{8,11},{9,8},{10,9... | collective-permute-start | bytes 393224 | tf_op jit(solution)/shard_map/ppermute | solution.py:430
  51.1 6.1 %collective-permute-start.1 = (bf16[128,512]{1,0:T(8,128)(2,1)S(1)}, bf16[128,512]{1,0:T(8,128)(2,1)S(1)}, u32[]{:S(2)}, u32[]{:S(2)}) collective-permute-start(bf16[128,512]{1,0:T(8,128)(2,1)S(1)} %copy-done.3), channel_id=1, source_target_pairs={{0,2},{1,3},{2,0},{3,1},{4,6},{5,7},{6,4},{7,5},{8,10},{9,11},{10,... | collective-permute-start | bytes 393224 | tf_op jit(solution)/shard_map/ppermute | solution.py:430
  52.0 8.4 %collective-permute-start = (bf16[128,512]{1,0:T(8,128)(2,1)S(1)}, bf16[128,512]{1,0:T(8,128)(2,1)S(1)}, u32[]{:S(2)}, u32[]{:S(2)}) collective-permute-start(bf16[128,512]{1,0:T(8,128)(2,1)S(1)} %copy-done.3), channel_id=1, source_target_pairs={{0,1},{1,2},{2,3},{3,0},{4,5},{5,6},{6,7},{7,4},{8,9},{9,10},{10,1... | collective-permute-start | bytes 393224 | tf_op jit(solution)/shard_map/ppermute | solution.py:430
  52.2 9.1 %collective-permute-start.3 = (bf16[128,512]{1,0:T(8,128)(2,1)S(1)}, bf16[128,512]{1,0:T(8,128)(2,1)S(1)}, u32[]{:S(2)}, u32[]{:S(2)}) collective-permute-start(bf16[128,512]{1,0:T(8,128)(2,1)S(1)} %copy-done.3), channel_id=1, source_target_pairs={{0,16},{16,0},{1,17},{17,1},{2,18},{18,2},{3,19},{19,3},{4,20},{20... | collective-permute-start | bytes 393224 | tf_op jit(solution)/shard_map/ppermute | solution.py:426
  54.2 9.7 %copy-start.4 = (bf16[128,512]{1,0:T(8,128)(2,1)}, bf16[128,512]{1,0:T(8,128)(2,1)S(1)}, u32[]{:S(2)}) copy-start(bf16[128,512]{1,0:T(8,128)(2,1)S(1)} %collective-permute-done.2.refs_3_) | copy-start | bytes 393220
  54.2 7.1 %collective-permute-start.6 = (bf16[128,512]{1,0:T(8,128)(2,1)S(1)}, bf16[128,512]{1,0:T(8,128)(2,1)S(1)}, u32[]{:S(2)}, u32[]{:S(2)}) collective-permute-start(bf16[128,512]{1,0:T(8,128)(2,1)S(1)} %collective-permute-done.2.refs_3_), channel_id=1, source_target_pairs={{0,16},{16,0},{1,17},{17,1},{2,18},{18,2},{3,19},{19,3},{4,20},{20... | collective-permute-start | bytes 393224 | tf_op jit(solution)/shard_map/ppermute | solution.py:426
  57.2 6.7 %copy-start.5 = (bf16[128,512]{1,0:T(8,128)(2,1)}, bf16[128,512]{1,0:T(8,128)(2,1)S(1)}, u32[]{:S(2)}) copy-start(bf16[128,512]{1,0:T(8,128)(2,1)S(1)} %collective-permute-done.1.refs_2_) | copy-start | bytes 393220
  57.2 4.2 %collective-permute-start.5 = (bf16[128,512]{1,0:T(8,128)(2,1)S(1)}, bf16[128,512]{1,0:T(8,128)(2,1)S(1)}, u32[]{:S(2)}, u32[]{:S(2)}) collective-permute-start(bf16[128,512]{1,0:T(8,128)(2,1)S(1)} %collective-permute-done.1.refs_2_), channel_id=1, source_target_pairs={{0,16},{16,0},{1,17},{17,1},{2,18},{18,2},{3,19},{19,3},{4,20},{20... | collective-permute-start | bytes 393224 | tf_op jit(solution)/shard_map/ppermute | solution.py:426
  60.5 1.9 %collective-permute-start.4 = (bf16[128,512]{1,0:T(8,128)(2,1)S(1)}, bf16[128,512]{1,0:T(8,128)(2,1)S(1)}, u32[]{:S(2)}, u32[]{:S(2)}) collective-permute-start(bf16[128,512]{1,0:T(8,128)(2,1)S(1)} %collective-permute-done.refs_1_), channel_id=1, source_target_pairs={{0,16},{16,0},{1,17},{17,1},{2,18},{18,2},{3,19},{19,3},{4,20},{20... | collective-permute-start | bytes 393224 | tf_op jit(solution)/shard_map/ppermute | solution.py:426
  93.3 16.0 %copy-start.21 = (bf16[2,192,128]{2,1,0:T(8,128)(2,1)S(1)}, bf16[2,192,128]{2,1,0:T(8,128)(2,1)}, u32[]{:S(2)}) copy-start(bf16[2,192,128]{2,1,0:T(8,128)(2,1)} %get-tuple-element.27) | copy-start | bytes 294916
  93.3 16.1 %copy-start.20 = (bf16[2,192,128]{2,1,0:T(8,128)(2,1)S(1)}, bf16[2,192,128]{2,1,0:T(8,128)(2,1)}, u32[]{:S(2)}) copy-start(bf16[2,192,128]{2,1,0:T(8,128)(2,1)} %get-tuple-element.28) | copy-start | bytes 294916
  93.3 17.9 %copy-start.19 = (bf16[2,192,128]{2,1,0:T(8,128)(2,1)S(1)}, bf16[2,192,128]{2,1,0:T(8,128)(2,1)}, u32[]{:S(2)}) copy-start(bf16[2,192,128]{2,1,0:T(8,128)(2,1)} %get-tuple-element.29) | copy-start | bytes 294916
  93.3 19.3 %copy-start.11 = (bf16[2,192,128]{2,1,0:T(8,128)(2,1)S(1)}, bf16[2,192,128]{2,1,0:T(8,128)(2,1)}, u32[]{:S(2)}) copy-start(bf16[2,192,128]{2,1,0:T(8,128)(2,1)} %get-tuple-element.26.refs_0_) | copy-start | bytes 294916
  104.9 18.3 %copy-start.1 = (bf16[16,80,128]{2,1,0:T(8,128)(2,1)}, bf16[16,80,128]{2,1,0:T(8,128)(2,1)S(1)}, u32[]{:S(2)}) copy-start(bf16[16,80,128]{2,1,0:T(8,128)(2,1)S(1)} %all_to_all.28.own_ref) | copy-start | bytes 983044
  104.9 18.3 %collective-permute-start.14 = (bf16[16,80,128]{2,1,0:T(8,128)(2,1)S(1)}, bf16[16,80,128]{2,1,0:T(8,128)(2,1)S(1)}, u32[]{:S(2)}, u32[]{:S(2)}) collective-permute-start(bf16[16,80,128]{2,1,0:T(8,128)(2,1)S(1)} %all_to_all.28.own_ref), channel_id=1, source_target_pairs={{0,16},{16,0},{1,17},{17,1},{2,18},{18,2},{3,19},{19,3},{4,20},{20... | collective-permute-start | bytes 983048 | tf_op jit(solution)/shard_map/ppermute | solution.py:426
  109.3 7.5 %collective-permute-start.7 = (bf16[2,192,128]{2,1,0:T(8,128)(2,1)S(1)}, bf16[2,192,128]{2,1,0:T(8,128)(2,1)S(1)}, u32[]{:S(2)}, u32[]{:S(2)}) collective-permute-start(bf16[2,192,128]{2,1,0:T(8,128)(2,1)S(1)} %copy-done.21), channel_id=1, source_target_pairs={{0,1},{1,2},{2,3},{3,0},{4,5},{5,6},{6,7},{7,4},{8,9},{9,10},{10,1... | collective-permute-start | bytes 294920 | tf_op jit(solution)/shard_map/ppermute | solution.py:430
  109.4 8.4 %collective-permute-start.8 = (bf16[2,192,128]{2,1,0:T(8,128)(2,1)S(1)}, bf16[2,192,128]{2,1,0:T(8,128)(2,1)S(1)}, u32[]{:S(2)}, u32[]{:S(2)}) collective-permute-start(bf16[2,192,128]{2,1,0:T(8,128)(2,1)S(1)} %copy-done.20), channel_id=1, source_target_pairs={{0,2},{1,3},{2,0},{3,1},{4,6},{5,7},{6,4},{7,5},{8,10},{9,11},{10,... | collective-permute-start | bytes 294920 | tf_op jit(solution)/shard_map/ppermute | solution.py:430
  111.2 6.8 %collective-permute-start.9 = (bf16[2,192,128]{2,1,0:T(8,128)(2,1)S(1)}, bf16[2,192,128]{2,1,0:T(8,128)(2,1)S(1)}, u32[]{:S(2)}, u32[]{:S(2)}) collective-permute-start(bf16[2,192,128]{2,1,0:T(8,128)(2,1)S(1)} %copy-done.19), channel_id=1, source_target_pairs={{0,3},{1,0},{2,1},{3,2},{4,7},{5,4},{6,5},{7,6},{8,11},{9,8},{10,9... | collective-permute-start | bytes 294920 | tf_op jit(solution)/shard_map/ppermute | solution.py:430
  112.6 5.9 %collective-permute-start.10 = (bf16[2,192,128]{2,1,0:T(8,128)(2,1)S(1)}, bf16[2,192,128]{2,1,0:T(8,128)(2,1)S(1)}, u32[]{:S(2)}, u32[]{:S(2)}) collective-permute-start(bf16[2,192,128]{2,1,0:T(8,128)(2,1)S(1)} %copy-done.11), channel_id=1, source_target_pairs={{0,16},{16,0},{1,17},{17,1},{2,18},{18,2},{3,19},{19,3},{4,20},{20... | collective-permute-start | bytes 294920 | tf_op jit(solution)/shard_map/ppermute | solution.py:426
  116.8 2.0 %collective-permute-start.11 = (bf16[2,192,128]{2,1,0:T(8,128)(2,1)S(1)}, bf16[2,192,128]{2,1,0:T(8,128)(2,1)S(1)}, u32[]{:S(2)}, u32[]{:S(2)}) collective-permute-start(bf16[2,192,128]{2,1,0:T(8,128)(2,1)S(1)} %collective-permute-done.7.refs_1_), channel_id=1, source_target_pairs={{0,16},{16,0},{1,17},{17,1},{2,18},{18,2},{3,19},{19,3},{4,20},{20... | collective-permute-start | bytes 294920 | tf_op jit(solution)/shard_map/ppermute | solution.py:426
  117.9 1.3 %collective-permute-start.12 = (bf16[2,192,128]{2,1,0:T(8,128)(2,1)S(1)}, bf16[2,192,128]{2,1,0:T(8,128)(2,1)S(1)}, u32[]{:S(2)}, u32[]{:S(2)}) collective-permute-start(bf16[2,192,128]{2,1,0:T(8,128)(2,1)S(1)} %collective-permute-done.8.refs_2_), channel_id=1, source_target_pairs={{0,16},{16,0},{1,17},{17,1},{2,18},{18,2},{3,19},{19,3},{4,20},{20... | collective-permute-start | bytes 294920 | tf_op jit(solution)/shard_map/ppermute | solution.py:426
  118.0 1.4 %collective-permute-start.13 = (bf16[2,192,128]{2,1,0:T(8,128)(2,1)S(1)}, bf16[2,192,128]{2,1,0:T(8,128)(2,1)S(1)}, u32[]{:S(2)}, u32[]{:S(2)}) collective-permute-start(bf16[2,192,128]{2,1,0:T(8,128)(2,1)S(1)} %collective-permute-done.9.refs_3_), channel_id=1, source_target_pairs={{0,16},{16,0},{1,17},{17,1},{2,18},{18,2},{3,19},{19,3},{4,20},{20... | collective-permute-start | bytes 294920 | tf_op jit(solution)/shard_map/ppermute | solution.py:426
  (14 other events, 22.5 us)

commit v3 on v2

--- a/solution.py
+++ b/solution.py
@@ -11,7 +11,7 @@
 from jax.sharding import PartitionSpec as P
 
 everyone = ("zh", "x", "core", "zl", "y")
-vmem_limit = 56 * 1024 * 1024
+vmem_limit = 16 * 1024 * 1024
 
 
 def two_terms(table):
@@ -113,7 +113,6 @@
     turn_cos_ref,
     turn_sin_ref,
     out_ref,
-    sums_ref,
     rows_ref,
 ):
     sources, slots, rows = in_ref.shape
@@ -265,7 +264,7 @@
                 .reshape(half, blocks // half, rows)
                 .astype(jnp.bfloat16)
             )
-    shape = sums_ref.shape
+    shape = (blocks // half, rows)
     sum_lane = lax.broadcasted_iota(jnp.int32, shape, 1)
     line = jnp.zeros(shape, jnp.float32)
     for g in range(3):
@@ -274,8 +273,7 @@
             high = total.astype(jnp.bfloat16).astype(jnp.float32)
             line = jnp.where(sum_lane == g * 3 + tap, high, line)
             line = jnp.where(sum_lane == 16 + g * 3 + tap, total - high, line)
-    own_row = lax.broadcasted_iota(jnp.int32, shape, 0) == lax.axis_index(("zh", "zl"))
-    sums_ref[...] = jnp.where(own_row, line, 0.0)
+    out_ref[:, 6] = jnp.broadcast_to(line[None], (2 * half,) + shape).astype(jnp.bfloat16)
 
 
 def channel_order(place_of):
@@ -315,7 +313,8 @@
 
 def finish_kernel(*refs):
     held = refs[:8]
-    in_weight_ref, out_weight_ref, outputs_ref, grad_inputs_ref, one_ref, two_ref = refs[8:]
+    in_weight_ref, out_weight_ref, outputs_ref, grad_inputs_ref, short_ref = refs[8:13]
+    one_ref, two_ref = refs[13:]
     width = out_weight_ref.shape[0]
     count = width // 8
     core, y = lax.axis_index("core"), lax.axis_index("y")
@@ -327,10 +326,13 @@
     contract_first = (((0,), (1,)), ((), ()))
     contract_last = (((1,), (1,)), ((), ()))
 
+    def stacked_rows(kind):
+        return jnp.concatenate(
+            [held[i][i // 4, kind * count : (kind + 1) * count, :] for i in range(8)], 0
+        )
+
     def natural(kind):
-        stacked = jnp.concatenate(
-            [held[i][i // 4, kind * count : (kind + 1) * count, :] for i in range(8)], 0
-        )
+        stacked = stacked_rows(kind)
         return lax.dot_general(
             stacked, order, contract_first, preferred_element_type=jnp.float32
         )
@@ -350,23 +352,30 @@
     grad_inputs_ref[0] = total.astype(jnp.bfloat16)
     one_ref[...] = natural(4)
     two_ref[...] = natural(5)
-
-
-def add_x_kernel(in_ref, sums_ref, out_ref):
+    sums = lax.dot_general(
+        stacked_rows(6), order, contract_first, preferred_element_type=jnp.float32
+    )
+    for group in range(3):
+        short_ref[:, group * width : (group + 1) * width] = (
+            sums[group * 3 : group * 3 + 3, :] + sums[16 + group * 3 : 19 + group * 3, :]
+        )
+
+
+def add_x_kernel(in_ref, *refs):
+    out_ref = refs[-1]
     total = jnp.sum(in_ref[...], axis=0)
-    count, lanes = total.shape[0], out_ref.shape[2]
-    rows = jnp.concatenate([total[:, :lanes], total[:, lanes:], sums_ref[...]], 0)
+    lanes = out_ref.shape[2]
+    rows = jnp.concatenate([total[:, :lanes], total[:, lanes:]], 0)
     out_ref[...] = jnp.broadcast_to(rows.astype(jnp.bfloat16)[None], out_ref.shape)
 
 
-def add_z_kernel(scale, in_ref, out_ref):
-    total = jnp.sum(in_ref[...].astype(jnp.float32), axis=0)
-    row = lax.broadcasted_iota(jnp.int32, total.shape, 0)
-    total = total * jnp.where(row < 64, scale, 1.0)
+def add_z_kernel(scale, in_ref, *refs):
+    out_ref = refs[-1]
+    total = jnp.sum(in_ref[...].astype(jnp.float32), axis=0) * scale
     out_ref[...] = jnp.broadcast_to(total.astype(jnp.bfloat16)[None], out_ref.shape)
 
 
-def place_kernel(own_ref, other_ref, in_weight_ref, out_weight_ref, short_ref):
+def place_kernel(own_ref, other_ref, in_weight_ref, out_weight_ref):
     width, lanes = out_weight_ref.shape[0], own_ref.shape[2]
     core = lax.axis_index("core")
     order = channel_order(
@@ -391,30 +400,20 @@
                 ] = lax.dot_general(
                     stacked, order, contract_first, preferred_element_type=jnp.float32
                 )
-    sums = jnp.concatenate(
-        [
-            ref[i, 64:80, :].astype(jnp.float32)[:8]
-            for ref in (own_ref, other_ref)
-            for i in range(16)
-        ],
-        0,
-    ).astype(jnp.bfloat16)
-    order = channel_order(
-        lambda zh, x, c, zl, y: ((c ^ core) * 16 + x * 4 + y) * 8 + zh * 4 + zl
-    )
-    sums = lax.dot_general(sums, order, contract_first, preferred_element_type=jnp.float32)
-    for group in range(3):
-        short_ref[:, group * width : (group + 1) * width] = (
-            sums[group * 3 : group * 3 + 3, :] + sums[16 + group * 3 : 19 + group * 3, :]
-        )
-
-
-def call(kernel, out_shape, scratch=()):
+
+
+def call(kernel, out_shape, scratch=(), whole=0, waited=0):
+    specs = {}
+    if waited:
+        specs["in_specs"] = [pl.BlockSpec(memory_space=pltpu.VMEM)] * whole + [
+            pl.BlockSpec(memory_space=pl.ANY)
+        ] * waited
     return pl.pallas_call(
         kernel,
         out_shape=out_shape,
         scratch_shapes=list(scratch),
         compiler_params=pltpu.CompilerParams(vmem_limit_bytes=vmem_limit),
+        **specs,
     )
 
 
@@ -446,37 +445,39 @@
     gathered = [both] + [ring(both, distance) for distance in (1, 2, 3)]
     gathered += [swap_core(x) for x in gathered]
     tables = [jnp.asarray(t) for t in transform_tables(devices // 2, rows)]
-    back, sums = call(
+    back = call(
         convolve_kernel,
-        (shape((32, 6, 8, rows), bf16), shape((16, rows), f32)),
+        shape((32, 7, 8, rows), bf16),
         [pltpu.VMEM((devices * 8, rows), f32)],
     )(received, short_kernel, *tables)
     halfway = exchange(back, ("zh", "x", "zl"))
     part, *leaving = call(
         part_kernel,
-        (shape((4, 32, width), f32),) + (shape((2, 6 * 32, rows), bf16),) * 4,
-        [pltpu.VMEM((32 * 6 * 8, rows), f32)],
+        (shape((4, 32, width), f32),) + (shape((2, 7 * 32, rows), bf16),) * 4,
+        [pltpu.VMEM((32 * 7 * 8, rows), f32)],
     )(halfway, *gathered)
     arrived = [leaving[0]] + [ring(leaving[distance], distance) for distance in (1, 2, 3)]
+    part = exchange(part, "x")
+    part = call(add_x_kernel, shape((8, 64, rows), bf16), whole=1, waited=3)(part, *arrived[1:])
     arrived += [swap_core(x) for x in arrived]
-    part = exchange(part, "x")
-    part = call(add_x_kernel, shape((8, 80, rows), bf16))(part, sums)
     part = exchange(part, ("zh", "zl"))
-    part = call(functools.partial(add_z_kernel, scale), shape((16, 80, rows), bf16))(part)
-    part = exchange(part, ("x", "y"))
-    grad_in_weight, grad_out_weight, grad_short = call(
-        place_kernel,
-        (shape((width, 3 * width), f32), shape((width, width), f32), shape((3, 3 * width), f32)),
-    )(part, swap_core(part))
-    outputs, grad_inputs, grad_one, grad_two = call(
+    outputs, grad_inputs, grad_short, grad_one, grad_two = call(
         finish_kernel,
         (
             shape((1, rows, width), bf16),
             shape((1, rows, width), bf16),
+            shape((3, 3 * width), f32),
             shape((rows, width), f32),
             shape((rows, width), f32),
         ),
     )(*arrived, in_weight, out_weight)
+    part = call(
+        functools.partial(add_z_kernel, scale), shape((16, 64, rows), bf16), whole=1, waited=1
+    )(part, grad_short)
+    part = exchange(part, ("x", "y"))
+    grad_in_weight, grad_out_weight = call(
+        place_kernel, (shape((width, 3 * width), f32), shape((width, width), f32))
+    )(part, swap_core(part))
     return (
         outputs,
         grad_inputs,

time: 127 us -> 112 us (0.88)
  blocking collectives: 71.1 us -> 54.1 us
  Pallas kernels: 19.4 us -> 9.14 us
  starting transfers between devices: 24.4 us -> 31.6 us
  local copies, waits for them, and re-layouts: 2.57 us -> 6.17 us
  waiting for transfers between devices: 8.09 us -> 10 us
    all_to_all x4 -> x3, blocking collectives: 71.1 us -> 54.1 us  [exchange(): return lax.all_to_all(x, axes, split_axis=0, concat_axis=0, tiled=True)]
    pallas_call x4, Pallas kernels: 11.9 us -> 6.07 us  [the longest x1 4.84 us: per_device(): call(convolve_kernel, shape((32, 7, 8, rows), bf16), [pltpu.VMEM((devices...]
    unnamed x44 -> x40, local copies, waits for them, and re-layouts: 2.57 us -> 6.17 us
    all_to_all x1 -> x2, waiting for transfers between devices: 1.54 us -> 5.11 us  [exchange(): return lax.all_to_all(x, axes, split_axis=0, concat_axis=0, tiled=True)]
    all_to_all x1 -> x2, starting transfers between devices: 4.01 us -> 7.39 us  [exchange(): return lax.all_to_all(x, axes, split_axis=0, concat_axis=0, tiled=True)]
    ppermute x6, waiting for transfers between devices: 4.66 us -> 1.54 us  [ring(): return lax.ppermute(x, 'y', [(i, (i + distance) % 4) for i in range(4)])]
    ppermute x6, starting transfers between devices: 5.66 us -> 7.67 us  [ring(): return lax.ppermute(x, 'y', [(i, (i + distance) % 4) for i in range(4)])]
    pallas_call x1, Pallas kernels: 2.36 us -> 0.4 us  [per_device(): call(pack_kernel, (shape((width, 8, rows), bf16), shape((rows, 2 * width)...]
  transfers between devices with their start and end apart: 16 -> 17, of which waited for: 8 -> 10; matrix products, arithmetic and copies ran while one was open for 0% -> 0% of each run, Pallas kernels for 2% -> 1%
where the time goes in v3:
time: 112 us
  blocking collectives  54.1 us (48%)
  starting transfers between devices  31.6 us (28%)
  waiting for transfers between devices  10 us (9%)
  Pallas kernels  9.14 us (8%)
  local copies, waits for them, and re-layouts  6.17 us (6%)
    all_to_all x3, blocking collectives, exchange(): return lax.all_to_all(x, axes, split_axis=0, concat_axis=0, tiled=True)  54.1 us
    ppermute x9, starting transfers between devices, swap_core(): return lax.ppermute(x, 'core', [(0, 1), (1, 0)])  16.5 us
    ppermute x6, starting transfers between devices, ring(): return lax.ppermute(x, 'y', [(i, (i + distance) % 4) for i in range(4)])  7.67 us
    all_to_all x2, starting transfers between devices, exchange(): return lax.all_to_all(x, axes, split_axis=0, concat_axis=0, tiled=True)  7.39 us
    unnamed x40, local copies, waits for them, and re-layouts  6.17 us
    all_to_all x2, waiting for transfers between devices, exchange(): return lax.all_to_all(x, axes, split_axis=0, concat_axis=0, tiled=True)  5.11 us
    pallas_call x1, Pallas kernels, per_device(): call(convolve_kernel, shape((32, 7, 8, rows), bf16), [pltpu.VMEM((devices...  4.84 us
    ppermute x9, waiting for transfers between devices, swap_core(): return lax.ppermute(x, 'core', [(0, 1), (1, 0)])  3.37 us
  transfers between devices with their start and end apart: 17, of which 10 were waited for; matrix products, arithmetic and copies ran while one was open for 0% of the time, Pallas kernels for 1%

profile of v3, /device:TPU:1, one launch (start us, length us, event | category | flops | bytes accessed | tf_op | source)
XLA Modules:
  0.0 111.8 jit_solution(4993463779982885245)
XLA Ops:
  0.6 1.0 copy-done
  1.6 0.9 copy-done.2
  6.6 36.4 %all_to_all.25.in_ref = bf16[256,8,128]{2,1,0:T(8,128)(2,1)S(1)} all-to-all(bf16[256,8,128]{2,1,0:T(8,128)(2,1)S(1)} %get-tuple-element.21), channel_id=1, replica_groups=mesh['zh'=2,'x'=4,'core'=2,'zl'=4,'y'=4] {'zh','x','core','zl','y'}, dimensions={0} | all-to-all | bytes 1048576 | tf_op jit(solution)/shard_map/all_to_all | solution.py:421
  43.0 4.8 %shard_map.217 = bf16[32,7,8,128]{3,2,1,0:T(8,128)(2,1)} custom-call(bf16[256,8,128]{2,1,0:T(8,128)(2,1)S(1)} %all_to_all.25.in_ref, f32[3,768]{1,0:T(4,128)S(1)} %copy-done.18, bf16[256,128]{1,0:T(8,128)(2,1)S(1)} %copy-done.17, bf16[256,128]{1,0:T(8,128)(2,1)S(1)} %copy-done.16, bf16[256,256]{1,0:T(8,128)(2,1)S(1)} %copy-done.9, ...), custom_call_target="tpu_custom_call" | custom-call | tf_op jit(solution)/shard_map/pallas_call | solution.py:448
  47.9 3.9 %all-to-all-start.1 = ((bf16[32,7,8,128]{3,2,1,0:T(8,128)(2,1)}), bf16[32,7,8,128]{3,2,1,0:T(8,128)(2,1)S(1)}, u32[]{:S(2)}, u32[]{:S(2)}) async-start(bf16[32,7,8,128]{3,2,1,0:T(8,128)(2,1)} %shard_map.217), calls=%async_computation.1 | async-start | bytes 917504 | tf_op jit(solution)/shard_map/all_to_all | solution.py:421
  51.8 1.3 %collective-permute-start.2 = (bf16[128,512]{1,0:T(8,128)(2,1)S(1)}, bf16[128,512]{1,0:T(8,128)(2,1)S(1)}, u32[]{:S(2)}, u32[]{:S(2)}) collective-permute-start(bf16[128,512]{1,0:T(8,128)(2,1)S(1)} %get-tuple-element.22.refs_0_), channel_id=1, source_target_pairs={{0,3},{1,0},{2,1},{3,2},{4,7},{5,4},{6,5},{7,6},{8,11},{9,8},{10,9... | collective-permute-start | bytes 393224 | tf_op jit(solution)/shard_map/ppermute | solution.py:429
  53.1 0.9 collective-permute-start.1
  54.2 1.4 %collective-permute-start.3 = (bf16[128,512]{1,0:T(8,128)(2,1)S(1)}, bf16[128,512]{1,0:T(8,128)(2,1)S(1)}, u32[]{:S(2)}, u32[]{:S(2)}) collective-permute-start(bf16[128,512]{1,0:T(8,128)(2,1)S(1)} %get-tuple-element.22.refs_0_), channel_id=1, source_target_pairs={{0,16},{16,0},{1,17},{17,1},{2,18},{18,2},{3,19},{19,3},{4,20},{20... | collective-permute-start | bytes 393224 | tf_op jit(solution)/shard_map/ppermute | solution.py:425
  56.2 3.0 %collective-permute-start.6 = (bf16[128,512]{1,0:T(8,128)(2,1)S(1)}, bf16[128,512]{1,0:T(8,128)(2,1)S(1)}, u32[]{:S(2)}, u32[]{:S(2)}) collective-permute-start(bf16[128,512]{1,0:T(8,128)(2,1)S(1)} %collective-permute-done.2.refs_3_), channel_id=1, source_target_pairs={{0,16},{16,0},{1,17},{17,1},{2,18},{18,2},{3,19},{19,3},{4,20},{20... | collective-permute-start | bytes 393224 | tf_op jit(solution)/shard_map/ppermute | solution.py:425
  59.2 2.3 %collective-permute-start.5 = (bf16[128,512]{1,0:T(8,128)(2,1)S(1)}, bf16[128,512]{1,0:T(8,128)(2,1)S(1)}, u32[]{:S(2)}, u32[]{:S(2)}) collective-permute-start(bf16[128,512]{1,0:T(8,128)(2,1)S(1)} %collective-permute-done.1.refs_2_), channel_id=1, source_target_pairs={{0,16},{16,0},{1,17},{17,1},{2,18},{18,2},{3,19},{19,3},{4,20},{20... | collective-permute-start | bytes 393224 | tf_op jit(solution)/shard_map/ppermute | solution.py:425
  61.5 0.9 collective-permute-done.refs_1_
  63.3 1.0 collective-permute-done.4.refs_5_
  64.3 3.1 %all-to-all-done.1.in_ref = bf16[32,7,8,128]{3,2,1,0:T(8,128)(2,1)S(1)} async-done(((bf16[32,7,8,128]{3,2,1,0:T(8,128)(2,1)}), bf16[32,7,8,128]{3,2,1,0:T(8,128)(2,1)S(1)}, u32[]{:S(2)}, u32[]{:S(2)}) %all-to-all-start.1) | async-done | bytes 458784 | tf_op jit(solution)/shard_map/all_to_all | solution.py:421
  68.3 3.1 %collective-permute-start.8 = (bf16[2,224,128]{2,1,0:T(8,128)(2,1)S(1)}, bf16[2,224,128]{2,1,0:T(8,128)(2,1)S(1)}, u32[]{:S(2)}, u32[]{:S(2)}) collective-permute-start(bf16[2,224,128]{2,1,0:T(8,128)(2,1)S(1)} %get-tuple-element.25), channel_id=1, source_target_pairs={{0,2},{1,3},{2,0},{3,1},{4,6},{5,7},{6,4},{7,5},{8,10},{9,11},{10,... | collective-permute-start | bytes 344072 | tf_op jit(solution)/shard_map/ppermute | solution.py:429
  71.5 1.7 %collective-permute-start.9 = (bf16[2,224,128]{2,1,0:T(8,128)(2,1)S(1)}, bf16[2,224,128]{2,1,0:T(8,128)(2,1)S(1)}, u32[]{:S(2)}, u32[]{:S(2)}) collective-permute-start(bf16[2,224,128]{2,1,0:T(8,128)(2,1)S(1)} %get-tuple-element.26), channel_id=1, source_target_pairs={{0,3},{1,0},{2,1},{3,2},{4,7},{5,4},{6,5},{7,6},{8,11},{9,8},{10,9... | collective-permute-start | bytes 344072 | tf_op jit(solution)/shard_map/ppermute | solution.py:429
  73.2 7.2 %all_to_all.26.in_ref = f32[4,32,256]{2,1,0:T(8,128)S(1)} all-to-all(f32[4,32,256]{2,1,0:T(8,128)S(1)} %get-tuple-element.29), channel_id=1, replica_groups=mesh['zh'=2,'x'=4,'core'=2,'zl'=4,'y'=4] {'x'}, dimensions={0} | all-to-all | bytes 262144 | tf_op jit(solution)/shard_map/all_to_all | solution.py:421
  81.1 3.5 %all-to-all-start.3 = ((bf16[8,64,128]{2,1,0:T(8,128)(2,1)}), bf16[8,64,128]{2,1,0:T(8,128)(2,1)S(1)}, u32[]{:S(2)}, u32[]{:S(2)}) async-start(bf16[8,64,128]{2,1,0:T(8,128)(2,1)} %shard_map.220), calls=%async_computation.3 | async-start | bytes 262144 | tf_op jit(solution)/shard_map/all_to_all | solution.py:421
  84.6 2.7 %collective-permute-start.10 = (bf16[2,224,128]{2,1,0:T(8,128)(2,1)S(1)}, bf16[2,224,128]{2,1,0:T(8,128)(2,1)S(1)}, u32[]{:S(2)}, u32[]{:S(2)}) collective-permute-start(bf16[2,224,128]{2,1,0:T(8,128)(2,1)S(1)} %get-tuple-element.23.refs_0_), channel_id=1, source_target_pairs={{0,16},{16,0},{1,17},{17,1},{2,18},{18,2},{3,19},{19,3},{4,20},{20... | collective-permute-start | bytes 344072 | tf_op jit(solution)/shard_map/ppermute | solution.py:425
  89.1 1.4 %shard_map.219 = (bf16[1,128,256]{2,1,0:T(8,128)(2,1)}, bf16[1,128,256]{2,1,0:T(8,128)(2,1)}, f32[3,768]{1,0:T(4,128)}, f32[128,256]{1,0:T(8,128)}, f32[128,256]{1,0:T(8,128)}) custom-call(bf16[2,224,128]{2,1,0:T(8,128)(2,1)S(1)} %get-tuple-element.23.refs_0_, bf16[2,224,128]{2,1,0:T(8,128)(2,1)S(1)} %collective-permute-done.7.refs_1_.refs_0_, ...), custom_call_target="tpu_custom_call" | custom-call | tf_op jit(solution)/shard_map/pallas_call | solution.py:464
  90.5 2.0 %all-to-all-done.3.in_ref = bf16[8,64,128]{2,1,0:T(8,128)(2,1)S(1)} async-done(((bf16[8,64,128]{2,1,0:T(8,128)(2,1)}), bf16[8,64,128]{2,1,0:T(8,128)(2,1)S(1)}, u32[]{:S(2)}, u32[]{:S(2)}) %all-to-all-start.3) | async-done | bytes 131104 | tf_op jit(solution)/shard_map/all_to_all | solution.py:421
  93.2 10.5 %all_to_all.27.own_ref = bf16[16,64,128]{2,1,0:T(8,128)(2,1)S(1)} all-to-all(bf16[16,64,128]{2,1,0:T(8,128)(2,1)S(1)} %shard_map.221), channel_id=1, replica_groups=mesh['zh'=2,'x'=4,'core'=2,'zl'=4,'y'=4] {'x','y'}, dimensions={0} | all-to-all | bytes 524288 | tf_op jit(solution)/shard_map/all_to_all | solution.py:421
  103.7 5.7 %collective-permute-start.14 = (bf16[16,64,128]{2,1,0:T(8,128)(2,1)S(1)}, bf16[16,64,128]{2,1,0:T(8,128)(2,1)S(1)}, u32[]{:S(2)}, u32[]{:S(2)}) collective-permute-start(bf16[16,64,128]{2,1,0:T(8,128)(2,1)S(1)} %all_to_all.27.own_ref), channel_id=1, source_target_pairs={{0,16},{16,0},{1,17},{17,1},{2,18},{18,2},{3,19},{19,3},{4,20},{20... | collective-permute-start | bytes 786440 | tf_op jit(solution)/shard_map/ppermute | solution.py:425
  109.4 1.2 %collective-permute-done.14.other_ref = bf16[16,64,128]{2,1,0:T(8,128)(2,1)S(1)} collective-permute-done((bf16[16,64,128]{2,1,0:T(8,128)(2,1)S(1)}, bf16[16,64,128]{2,1,0:T(8,128)(2,1)S(1)}, u32[]{:S(2)}, u32[]{:S(2)}) %collective-permute-start.14) | collective-permute-done | bytes 262176 | tf_op jit(solution)/shard_map/ppermute | solution.py:425
  110.5 1.3 %shard_map.222 = (f32[256,768]{1,0:T(8,128)}, f32[256,256]{1,0:T(8,128)}) custom-call(bf16[16,64,128]{2,1,0:T(8,128)(2,1)S(1)} %all_to_all.27.own_ref, bf16[16,64,128]{2,1,0:T(8,128)(2,1)S(1)} %collective-permute-done.14.other_ref), custom_call_target="tpu_custom_call" | custom-call | tf_op jit(solution)/shard_map/pallas_call | solution.py:478
  (60 shorter events, 9.8 us)
Async XLA Ops:
  6.4 36.5 %copy-start.6 = (bf16[256,256]{1,0:T(8,128)(2,1)S(1)}, bf16[256,256]{1,0:T(8,128)(2,1)}, u32[]{:S(2)}) copy-start(bf16[256,256]{1,0:T(8,128)(2,1)} %constant.25.clone.second_back_low) | copy-start | bytes 393220
  6.4 36.5 %copy-start.7 = (bf16[256,256]{1,0:T(8,128)(2,1)S(1)}, bf16[256,256]{1,0:T(8,128)(2,1)}, u32[]{:S(2)}) copy-start(bf16[256,256]{1,0:T(8,128)(2,1)} %constant.24.clone.second_back_high) | copy-start | bytes 393220
  6.5 36.5 %copy-start.8 = (bf16[256,256]{1,0:T(8,128)(2,1)S(1)}, bf16[256,256]{1,0:T(8,128)(2,1)}, u32[]{:S(2)}) copy-start(bf16[256,256]{1,0:T(8,128)(2,1)} %constant.23.clone.second_low) | copy-start | bytes 393220
  6.5 36.5 %copy-start.9 = (bf16[256,256]{1,0:T(8,128)(2,1)S(1)}, bf16[256,256]{1,0:T(8,128)(2,1)}, u32[]{:S(2)}) copy-start(bf16[256,256]{1,0:T(8,128)(2,1)} %constant.22.clone.second_high) | copy-start | bytes 393220
  6.5 36.5 %copy-start.12 = (f32[128,128]{1,0:T(8,128)S(1)}, f32[128,128]{1,0:T(8,128)}, u32[]{:S(2)}) copy-start(f32[128,128]{1,0:T(8,128)} %constant.29.clone.turn_sin_ref) | copy-start | bytes 196612
  6.5 36.5 %copy-start.13 = (f32[128,128]{1,0:T(8,128)S(1)}, f32[128,128]{1,0:T(8,128)}, u32[]{:S(2)}) copy-start(f32[128,128]{1,0:T(8,128)} %constant.28.clone.turn_cos_ref) | copy-start | bytes 196612
  6.5 36.5 %copy-start.14 = (bf16[128,256]{1,0:T(8,128)(2,1)S(1)}, bf16[128,256]{1,0:T(8,128)(2,1)}, u32[]{:S(2)}) copy-start(bf16[128,256]{1,0:T(8,128)(2,1)} %constant.27.clone.first_back_low) | copy-start | bytes 196612
  47.9 19.5 %all-to-all-start.1 = ((bf16[32,7,8,128]{3,2,1,0:T(8,128)(2,1)}), bf16[32,7,8,128]{3,2,1,0:T(8,128)(2,1)S(1)}, u32[]{:S(2)}, u32[]{:S(2)}) async-start(bf16[32,7,8,128]{3,2,1,0:T(8,128)(2,1)} %shard_map.217), calls=%async_computation.1 | async-start | bytes 917504 | tf_op jit(solution)/shard_map/all_to_all | solution.py:421
  51.8 4.4 %collective-permute-start.2 = (bf16[128,512]{1,0:T(8,128)(2,1)S(1)}, bf16[128,512]{1,0:T(8,128)(2,1)S(1)}, u32[]{:S(2)}, u32[]{:S(2)}) collective-permute-start(bf16[128,512]{1,0:T(8,128)(2,1)S(1)} %get-tuple-element.22.refs_0_), channel_id=1, source_target_pairs={{0,3},{1,0},{2,1},{3,2},{4,7},{5,4},{6,5},{7,6},{8,11},{9,8},{10,9... | collective-permute-start | bytes 393224 | tf_op jit(solution)/shard_map/ppermute | solution.py:429
  53.1 6.1 %collective-permute-start.1 = (bf16[128,512]{1,0:T(8,128)(2,1)S(1)}, bf16[128,512]{1,0:T(8,128)(2,1)S(1)}, u32[]{:S(2)}, u32[]{:S(2)}) collective-permute-start(bf16[128,512]{1,0:T(8,128)(2,1)S(1)} %get-tuple-element.22.refs_0_), channel_id=1, source_target_pairs={{0,2},{1,3},{2,0},{3,1},{4,6},{5,7},{6,4},{7,5},{8,10},{9,11},{10,... | collective-permute-start | bytes 393224 | tf_op jit(solution)/shard_map/ppermute | solution.py:429
  54.0 8.4 %collective-permute-start = (bf16[128,512]{1,0:T(8,128)(2,1)S(1)}, bf16[128,512]{1,0:T(8,128)(2,1)S(1)}, u32[]{:S(2)}, u32[]{:S(2)}) collective-permute-start(bf16[128,512]{1,0:T(8,128)(2,1)S(1)} %get-tuple-element.22.refs_0_), channel_id=1, source_target_pairs={{0,1},{1,2},{2,3},{3,0},{4,5},{5,6},{6,7},{7,4},{8,9},{9,10},{10,1... | collective-permute-start | bytes 393224 | tf_op jit(solution)/shard_map/ppermute | solution.py:429
  54.2 9.1 %collective-permute-start.3 = (bf16[128,512]{1,0:T(8,128)(2,1)S(1)}, bf16[128,512]{1,0:T(8,128)(2,1)S(1)}, u32[]{:S(2)}, u32[]{:S(2)}) collective-permute-start(bf16[128,512]{1,0:T(8,128)(2,1)S(1)} %get-tuple-element.22.refs_0_), channel_id=1, source_target_pairs={{0,16},{16,0},{1,17},{17,1},{2,18},{18,2},{3,19},{19,3},{4,20},{20... | collective-permute-start | bytes 393224 | tf_op jit(solution)/shard_map/ppermute | solution.py:425
  56.2 7.1 %collective-permute-start.6 = (bf16[128,512]{1,0:T(8,128)(2,1)S(1)}, bf16[128,512]{1,0:T(8,128)(2,1)S(1)}, u32[]{:S(2)}, u32[]{:S(2)}) collective-permute-start(bf16[128,512]{1,0:T(8,128)(2,1)S(1)} %collective-permute-done.2.refs_3_), channel_id=1, source_target_pairs={{0,16},{16,0},{1,17},{17,1},{2,18},{18,2},{3,19},{19,3},{4,20},{20... | collective-permute-start | bytes 393224 | tf_op jit(solution)/shard_map/ppermute | solution.py:425
  59.2 4.1 %collective-permute-start.5 = (bf16[128,512]{1,0:T(8,128)(2,1)S(1)}, bf16[128,512]{1,0:T(8,128)(2,1)S(1)}, u32[]{:S(2)}, u32[]{:S(2)}) collective-permute-start(bf16[128,512]{1,0:T(8,128)(2,1)S(1)} %collective-permute-done.1.refs_2_), channel_id=1, source_target_pairs={{0,16},{16,0},{1,17},{17,1},{2,18},{18,2},{3,19},{19,3},{4,20},{20... | collective-permute-start | bytes 393224 | tf_op jit(solution)/shard_map/ppermute | solution.py:425
  62.4 1.9 %collective-permute-start.4 = (bf16[128,512]{1,0:T(8,128)(2,1)S(1)}, bf16[128,512]{1,0:T(8,128)(2,1)S(1)}, u32[]{:S(2)}, u32[]{:S(2)}) collective-permute-start(bf16[128,512]{1,0:T(8,128)(2,1)S(1)} %collective-permute-done.refs_1_), channel_id=1, source_target_pairs={{0,16},{16,0},{1,17},{17,1},{2,18},{18,2},{3,19},{19,3},{4,20},{20... | collective-permute-start | bytes 393224 | tf_op jit(solution)/shard_map/ppermute | solution.py:425
  67.9 12.5 %collective-permute-start.7 = (bf16[2,224,128]{2,1,0:T(8,128)(2,1)S(1)}, bf16[2,224,128]{2,1,0:T(8,128)(2,1)S(1)}, u32[]{:S(2)}, u32[]{:S(2)}) collective-permute-start(bf16[2,224,128]{2,1,0:T(8,128)(2,1)S(1)} %get-tuple-element.24), channel_id=1, source_target_pairs={{0,1},{1,2},{2,3},{3,0},{4,5},{5,6},{6,7},{7,4},{8,9},{9,10},{10,1... | collective-permute-start | bytes 344072 | tf_op jit(solution)/shard_map/ppermute | solution.py:429
  68.3 12.1 %collective-permute-start.8 = (bf16[2,224,128]{2,1,0:T(8,128)(2,1)S(1)}, bf16[2,224,128]{2,1,0:T(8,128)(2,1)S(1)}, u32[]{:S(2)}, u32[]{:S(2)}) collective-permute-start(bf16[2,224,128]{2,1,0:T(8,128)(2,1)S(1)} %get-tuple-element.25), channel_id=1, source_target_pairs={{0,2},{1,3},{2,0},{3,1},{4,6},{5,7},{6,4},{7,5},{8,10},{9,11},{10,... | collective-permute-start | bytes 344072 | tf_op jit(solution)/shard_map/ppermute | solution.py:429
  71.5 9.0 %collective-permute-start.9 = (bf16[2,224,128]{2,1,0:T(8,128)(2,1)S(1)}, bf16[2,224,128]{2,1,0:T(8,128)(2,1)S(1)}, u32[]{:S(2)}, u32[]{:S(2)}) collective-permute-start(bf16[2,224,128]{2,1,0:T(8,128)(2,1)S(1)} %get-tuple-element.26), channel_id=1, source_target_pairs={{0,3},{1,0},{2,1},{3,2},{4,7},{5,4},{6,5},{7,6},{8,11},{9,8},{10,9... | collective-permute-start | bytes 344072 | tf_op jit(solution)/shard_map/ppermute | solution.py:429
  81.1 11.4 %all-to-all-start.3 = ((bf16[8,64,128]{2,1,0:T(8,128)(2,1)}), bf16[8,64,128]{2,1,0:T(8,128)(2,1)S(1)}, u32[]{:S(2)}, u32[]{:S(2)}) async-start(bf16[8,64,128]{2,1,0:T(8,128)(2,1)} %shard_map.220), calls=%async_computation.3 | async-start | bytes 262144 | tf_op jit(solution)/shard_map/all_to_all | solution.py:421
  84.6 3.6 %collective-permute-start.10 = (bf16[2,224,128]{2,1,0:T(8,128)(2,1)S(1)}, bf16[2,224,128]{2,1,0:T(8,128)(2,1)S(1)}, u32[]{:S(2)}, u32[]{:S(2)}) collective-permute-start(bf16[2,224,128]{2,1,0:T(8,128)(2,1)S(1)} %get-tuple-element.23.refs_0_), channel_id=1, source_target_pairs={{0,16},{16,0},{1,17},{17,1},{2,18},{18,2},{3,19},{19,3},{4,20},{20... | collective-permute-start | bytes 344072 | tf_op jit(solution)/shard_map/ppermute | solution.py:425
  87.3 1.3 %collective-permute-start.11 = (bf16[2,224,128]{2,1,0:T(8,128)(2,1)S(1)}, bf16[2,224,128]{2,1,0:T(8,128)(2,1)S(1)}, u32[]{:S(2)}, u32[]{:S(2)}) collective-permute-start(bf16[2,224,128]{2,1,0:T(8,128)(2,1)S(1)} %collective-permute-done.7.refs_1_.refs_0_), channel_id=1, source_target_pairs={{0,16},{16,0},{1,17},{17,1},{2,18},{18,2},{3,19},{19,3},{4,20},{20... | collective-permute-start | bytes 344072 | tf_op jit(solution)/shard_map/ppermute | solution.py:425
  87.4 1.4 %collective-permute-start.12 = (bf16[2,224,128]{2,1,0:T(8,128)(2,1)S(1)}, bf16[2,224,128]{2,1,0:T(8,128)(2,1)S(1)}, u32[]{:S(2)}, u32[]{:S(2)}) collective-permute-start(bf16[2,224,128]{2,1,0:T(8,128)(2,1)S(1)} %collective-permute-done.8.refs_2_.refs_1_), channel_id=1, source_target_pairs={{0,16},{16,0},{1,17},{17,1},{2,18},{18,2},{3,19},{19,3},{4,20},{20... | collective-permute-start | bytes 344072 | tf_op jit(solution)/shard_map/ppermute | solution.py:425
  87.8 1.3 %collective-permute-start.13 = (bf16[2,224,128]{2,1,0:T(8,128)(2,1)S(1)}, bf16[2,224,128]{2,1,0:T(8,128)(2,1)S(1)}, u32[]{:S(2)}, u32[]{:S(2)}) collective-permute-start(bf16[2,224,128]{2,1,0:T(8,128)(2,1)S(1)} %collective-permute-done.9.refs_3_.refs_2_), channel_id=1, source_target_pairs={{0,16},{16,0},{1,17},{17,1},{2,18},{18,2},{3,19},{19,3},{4,20},{20... | collective-permute-start | bytes 344072 | tf_op jit(solution)/shard_map/ppermute | solution.py:425
  103.7 6.8 %collective-permute-start.14 = (bf16[16,64,128]{2,1,0:T(8,128)(2,1)S(1)}, bf16[16,64,128]{2,1,0:T(8,128)(2,1)S(1)}, u32[]{:S(2)}, u32[]{:S(2)}) collective-permute-start(bf16[16,64,128]{2,1,0:T(8,128)(2,1)S(1)} %all_to_all.27.own_ref), channel_id=1, source_target_pairs={{0,16},{16,0},{1,17},{17,1},{2,18},{18,2},{3,19},{19,3},{4,20},{20... | collective-permute-start | bytes 786440 | tf_op jit(solution)/shard_map/ppermute | solution.py:425
  (13 other events, 168.6 us)

commit v4 on v3

--- a/solution.py
+++ b/solution.py
@@ -285,10 +285,11 @@
 
 
 def part_kernel(in_ref, *refs):
-    both_refs, part_ref, send_refs, rows_ref = refs[:8], refs[8], refs[9:13], refs[13]
+    both_refs, part_refs, send_refs = refs[:8], refs[8:12], refs[12:16]
+    rows_ref, sums_ref = refs[16:]
     sources, kinds, blocks, rows = in_ref.shape
     width = both_refs[0].shape[1] // 2
-    core, y = lax.axis_index("core"), lax.axis_index("y")
+    x, core, y = lax.axis_index("x"), lax.axis_index("core"), lax.axis_index("y")
     rows_ref[...] = in_ref[...].astype(jnp.float32).reshape(sources * kinds * blocks, rows)
     out_part = jnp.zeros((sources, width), jnp.float32)
     in_part = jnp.zeros((3 * sources, width), jnp.float32)
@@ -306,9 +307,11 @@
             both_ref = both_refs[other * 4 + (4 - ahead) % 4]
             out_part += bf16_dot(kept[:sources], both_ref[:, width:])
             in_part += bf16_dot(kept[sources : 4 * sources], both_ref[:, :width])
-    part_ref[0] = out_part
+    sums_ref[0] = out_part
     for group in range(3):
-        part_ref[1 + group] = in_part[group * sources : (group + 1) * sources]
+        sums_ref[1 + group] = in_part[group * sources : (group + 1) * sources]
+    for ahead in range(4):
+        part_refs[ahead][...] = sums_ref[(x + ahead) & 3]
 
 
 def finish_kernel(*refs):
@@ -361,9 +364,9 @@
         )
 
 
-def add_x_kernel(in_ref, *refs):
+def add_x_kernel(*refs):
     out_ref = refs[-1]
-    total = jnp.sum(in_ref[...], axis=0)
+    total = refs[0][...] + refs[1][...] + refs[2][...] + refs[3][...]
     lanes = out_ref.shape[2]
     rows = jnp.concatenate([total[:, :lanes], total[:, lanes:]], 0)
     out_ref[...] = jnp.broadcast_to(rows.astype(jnp.bfloat16)[None], out_ref.shape)
@@ -402,7 +405,7 @@
                 )
 
 
-def call(kernel, out_shape, scratch=(), whole=0, waited=0):
+def call(kernel, out_shape, scratch=(), whole=0, waited=0, limit=vmem_limit):
     specs = {}
     if waited:
         specs["in_specs"] = [pl.BlockSpec(memory_space=pltpu.VMEM)] * whole + [
@@ -412,7 +415,7 @@
         kernel,
         out_shape=out_shape,
         scratch_shapes=list(scratch),
-        compiler_params=pltpu.CompilerParams(vmem_limit_bytes=vmem_limit),
+        compiler_params=pltpu.CompilerParams(vmem_limit_bytes=limit),
         **specs,
     )
 
@@ -425,8 +428,8 @@
     return lax.ppermute(x, "core", [(0, 1), (1, 0)])
 
 
-def ring(x, distance):
-    return lax.ppermute(x, "y", [(i, (i + distance) % 4) for i in range(4)])
+def ring(x, axis, distance):
+    return lax.ppermute(x, axis, [(i, (i + distance) % 4) for i in range(4)])
 
 
 def per_device(inputs, in_weight, short_kernel, filter_one, filter_two, out_weight, out_grad):
@@ -440,9 +443,10 @@
         pack_kernel,
         (shape((width, 8, rows), bf16), shape((rows, 2 * width), bf16)),
         [pltpu.VMEM((width * 8, rows), f32)],
+        limit=56 * 1024 * 1024,
     )(inputs, in_weight, filter_one, filter_two, out_weight, out_grad)
     received = exchange(packed, everyone)
-    gathered = [both] + [ring(both, distance) for distance in (1, 2, 3)]
+    gathered = [both] + [ring(both, "y", distance) for distance in (1, 2, 3)]
     gathered += [swap_core(x) for x in gathered]
     tables = [jnp.asarray(t) for t in transform_tables(devices // 2, rows)]
     back = call(
@@ -451,16 +455,20 @@
         [pltpu.VMEM((devices * 8, rows), f32)],
     )(received, short_kernel, *tables)
     halfway = exchange(back, ("zh", "x", "zl"))
-    part, *leaving = call(
+    found = call(
         part_kernel,
-        (shape((4, 32, width), f32),) + (shape((2, 7 * 32, rows), bf16),) * 4,
-        [pltpu.VMEM((32 * 7 * 8, rows), f32)],
+        (shape((32, width), f32),) * 4 + (shape((2, 7 * 32, rows), bf16),) * 4,
+        [pltpu.VMEM((32 * 7 * 8, rows), f32), pltpu.VMEM((4, 32, width), f32)],
     )(halfway, *gathered)
-    arrived = [leaving[0]] + [ring(leaving[distance], distance) for distance in (1, 2, 3)]
-    part = exchange(part, "x")
-    part = call(add_x_kernel, shape((8, 64, rows), bf16), whole=1, waited=3)(part, *arrived[1:])
+    part = [found[0]] + [ring(found[distance], "x", distance) for distance in (1, 2, 3)]
+    arrived = [found[4]] + [ring(found[4 + distance], "y", distance) for distance in (1, 2, 3)]
     arrived += [swap_core(x) for x in arrived]
+    part = call(add_x_kernel, shape((8, 64, rows), bf16))(*part)
     part = exchange(part, ("zh", "zl"))
+    part = call(
+        functools.partial(add_z_kernel, scale), shape((16, 64, rows), bf16), whole=1, waited=4
+    )(part, *arrived[4:])
+    part = exchange(part, ("x", "y"))
     outputs, grad_inputs, grad_short, grad_one, grad_two = call(
         finish_kernel,
         (
@@ -471,10 +479,7 @@
             shape((rows, width), f32),
         ),
     )(*arrived, in_weight, out_weight)
-    part = call(
-        functools.partial(add_z_kernel, scale), shape((16, 64, rows), bf16), whole=1, waited=1
-    )(part, grad_short)
-    part = exchange(part, ("x", "y"))
+    part, grad_short = lax.optimization_barrier((part, grad_short))
     grad_in_weight, grad_out_weight = call(
         place_kernel, (shape((width, 3 * width), f32), shape((width, width), f32))
     )(part, swap_core(part))

time: 112 us -> 106 us (0.946)
  blocking collectives: 54.1 us -> 36.6 us
  waiting for transfers between devices: 10 us -> 17.8 us
  starting transfers between devices: 31.6 us -> 38.5 us
  local copies, waits for them, and re-layouts: 6.17 us -> 0.08 us
  Pallas kernels: 9.14 us -> 11.8 us
    all_to_all x3 -> x1, blocking collectives: 54.1 us -> 36.6 us  [exchange(): return lax.all_to_all(x, axes, split_axis=0, concat_axis=0, tiled=True)]
    all_to_all x2 -> x3, waiting for transfers between devices: 5.11 us -> 12.9 us  [exchange(): return lax.all_to_all(x, axes, split_axis=0, concat_axis=0, tiled=True)]
    unnamed x40 -> x28, local copies, waits for them, and re-layouts: 6.17 us -> 0.08 us
    all_to_all x2 -> x3, starting transfers between devices: 7.39 us -> 11.1 us  [exchange(): return lax.all_to_all(x, axes, split_axis=0, concat_axis=0, tiled=True)]
    ppermute x6 -> x9, starting transfers between devices: 7.67 us -> 10.9 us  [ring(): return lax.ppermute(x, axis, [(i, (i + distance) % 4) for i in range(4)])]
    pallas_call x1, Pallas kernels: 0.4 us -> 2.36 us  [per_device(): call(pack_kernel, (shape((width, 8, rows), bf16), shape((rows, 2 * width)...]
  transfers between devices with their start and end apart: 17 -> 21, of which waited for: 10 -> 11; matrix products, arithmetic and copies ran while one was open for 0% -> 0% of each run, Pallas kernels for 1% -> 2%
where the time goes in v4:
time: 106 us
  starting transfers between devices  38.5 us (36%)
  blocking collectives  36.6 us (35%)
  waiting for transfers between devices  17.8 us (17%)
  Pallas kernels  11.8 us (11%)
    all_to_all x1, blocking collectives, exchange(): return lax.all_to_all(x, axes, split_axis=0, concat_axis=0, tiled=True)  36.6 us
    ppermute x9, starting transfers between devices, swap_core(): return lax.ppermute(x, 'core', [(0, 1), (1, 0)])  16.5 us
    all_to_all x3, waiting for transfers between devices, exchange(): return lax.all_to_all(x, axes, split_axis=0, concat_axis=0, tiled=True)  12.9 us
    all_to_all x3, starting transfers between devices, exchange(): return lax.all_to_all(x, axes, split_axis=0, concat_axis=0, tiled=True)  11.1 us
    ppermute x9, starting transfers between devices, ring(): return lax.ppermute(x, axis, [(i, (i + distance) % 4) for i in range(4)])  10.9 us
    pallas_call x1, Pallas kernels, per_device(): call(convolve_kernel, shape((32, 7, 8, rows), bf16), [pltpu.VMEM((devices...  4.84 us
    ppermute x9, waiting for transfers between devices, swap_core(): return lax.ppermute(x, 'core', [(0, 1), (1, 0)])  3.36 us
    pallas_call x1, Pallas kernels, per_device(): call(pack_kernel, (shape((width, 8, rows), bf16), shape((rows, 2 * width)...  2.36 us
  transfers between devices with their start and end apart: 21, of which 11 were waited for; matrix products, arithmetic and copies ran while one was open for 0% of the time, Pallas kernels for 2%

profile of v4, /device:TPU:1, one launch (start us, length us, event | category | flops | bytes accessed | tf_op | source)
XLA Modules:
  0.0 105.6 jit_solution(18065097818964242467)
XLA Ops:
  0.6 2.4 %shard_map.216 = (bf16[256,8,128]{2,1,0:T(8,128)(2,1)}, bf16[128,512]{1,0:T(8,128)(2,1)}) custom-call(bf16[1,128,256]{2,1,0:T(8,128)(2,1)} %seq_ref.1, bf16[256,768]{1,0:T(8,128)(2,1)} %refs_8_.1, f32[128,256]{1,0:T(8,128)} %one_ref.1, f32[128,256]{1,0:T(8,128)} %two_ref.1, bf16[256,256]{1,0:T(8,128)(2,1)} %refs_9_.1, bf16[1,128,256]{2,1,0:T(8,128)(2,1)} %grad_ref.1), custom_call_target="tpu_custom_call" | custom-call | tf_op jit(solution)/shard_map/pallas_call | solution.py:442
  3.1 36.6 %all_to_all.20.in_ref = bf16[256,8,128]{2,1,0:T(8,128)(2,1)S(1)} all-to-all(bf16[256,8,128]{2,1,0:T(8,128)(2,1)} %get-tuple-element.26), channel_id=1, replica_groups=mesh['zh'=2,'x'=4,'core'=2,'zl'=4,'y'=4] {'zh','x','core','zl','y'}, dimensions={0} | all-to-all | bytes 1048576 | tf_op jit(solution)/shard_map/all_to_all | solution.py:424
  39.8 4.8 %shard_map.217 = bf16[32,7,8,128]{3,2,1,0:T(8,128)(2,1)} custom-call(bf16[256,8,128]{2,1,0:T(8,128)(2,1)S(1)} %all_to_all.20.in_ref, f32[3,768]{1,0:T(4,128)S(1)} %copy-done.13, bf16[256,128]{1,0:T(8,128)(2,1)S(1)} %copy-done.12, bf16[256,128]{1,0:T(8,128)(2,1)S(1)} %copy-done.11, bf16[256,256]{1,0:T(8,128)(2,1)S(1)} %copy-done.6, ...), custom_call_target="tpu_custom_call" | custom-call | tf_op jit(solution)/shard_map/pallas_call | solution.py:452
  44.6 4.0 %all-to-all-start.1 = ((bf16[32,7,8,128]{3,2,1,0:T(8,128)(2,1)}), bf16[32,7,8,128]{3,2,1,0:T(8,128)(2,1)S(1)}, u32[]{:S(2)}, u32[]{:S(2)}) async-start(bf16[32,7,8,128]{3,2,1,0:T(8,128)(2,1)} %shard_map.217), calls=%async_computation.1 | async-start | bytes 917504 | tf_op jit(solution)/shard_map/all_to_all | solution.py:424
  48.6 1.3 %collective-permute-start.2 = (bf16[128,512]{1,0:T(8,128)(2,1)S(1)}, bf16[128,512]{1,0:T(8,128)(2,1)S(1)}, u32[]{:S(2)}, u32[]{:S(2)}) collective-permute-start(bf16[128,512]{1,0:T(8,128)(2,1)S(1)} %copy-done.2), channel_id=1, source_target_pairs={{0,3},{1,0},{2,1},{3,2},{4,7},{5,4},{6,5},{7,6},{8,11},{9,8},{10,9... | collective-permute-start | bytes 393224 | tf_op jit(solution)/shard_map/ppermute | solution.py:432
  51.0 1.4 %collective-permute-start.3 = (bf16[128,512]{1,0:T(8,128)(2,1)S(1)}, bf16[128,512]{1,0:T(8,128)(2,1)S(1)}, u32[]{:S(2)}, u32[]{:S(2)}) collective-permute-start(bf16[128,512]{1,0:T(8,128)(2,1)S(1)} %copy-done.2), channel_id=1, source_target_pairs={{0,16},{16,0},{1,17},{17,1},{2,18},{18,2},{3,19},{19,3},{4,20},{20... | collective-permute-start | bytes 393224 | tf_op jit(solution)/shard_map/ppermute | solution.py:428
  53.1 3.0 %collective-permute-start.6 = (bf16[128,512]{1,0:T(8,128)(2,1)S(1)}, bf16[128,512]{1,0:T(8,128)(2,1)S(1)}, u32[]{:S(2)}, u32[]{:S(2)}) collective-permute-start(bf16[128,512]{1,0:T(8,128)(2,1)S(1)} %collective-permute-done.2.refs_3_), channel_id=1, source_target_pairs={{0,16},{16,0},{1,17},{17,1},{2,18},{18,2},{3,19},{19,3},{4,20},{20... | collective-permute-start | bytes 393224 | tf_op jit(solution)/shard_map/ppermute | solution.py:428
  56.0 2.3 %collective-permute-start.5 = (bf16[128,512]{1,0:T(8,128)(2,1)S(1)}, bf16[128,512]{1,0:T(8,128)(2,1)S(1)}, u32[]{:S(2)}, u32[]{:S(2)}) collective-permute-start(bf16[128,512]{1,0:T(8,128)(2,1)S(1)} %collective-permute-done.1.refs_2_), channel_id=1, source_target_pairs={{0,16},{16,0},{1,17},{17,1},{2,18},{18,2},{3,19},{19,3},{4,20},{20... | collective-permute-start | bytes 393224 | tf_op jit(solution)/shard_map/ppermute | solution.py:428
  58.3 0.9 collective-permute-done.refs_1_
  60.2 1.0 collective-permute-done.4.refs_5_
  61.2 3.1 %all-to-all-done.1.in_ref = bf16[32,7,8,128]{3,2,1,0:T(8,128)(2,1)S(1)} async-done(((bf16[32,7,8,128]{3,2,1,0:T(8,128)(2,1)}), bf16[32,7,8,128]{3,2,1,0:T(8,128)(2,1)S(1)}, u32[]{:S(2)}, u32[]{:S(2)}) %all-to-all-start.1) | async-done | bytes 458784 | tf_op jit(solution)/shard_map/all_to_all | solution.py:424
  65.1 1.8 %collective-permute-start.15 = (f32[32,256]{1,0:T(8,128)S(1)}, f32[32,256]{1,0:T(8,128)S(1)}, u32[]{:S(2)}, u32[]{:S(2)}) collective-permute-start(f32[32,256]{1,0:T(8,128)S(1)} %get-tuple-element.36), channel_id=1, source_target_pairs={{0,64},{32,96},{64,0},{96,32},{1,65},{33,97},{65,1},{97,33},{2,66}... | collective-permute-start | bytes 98312 | tf_op jit(solution)/shard_map/ppermute | solution.py:432
  66.9 1.6 %collective-permute-start.16 = (f32[32,256]{1,0:T(8,128)S(1)}, f32[32,256]{1,0:T(8,128)S(1)}, u32[]{:S(2)}, u32[]{:S(2)}) collective-permute-start(f32[32,256]{1,0:T(8,128)S(1)} %get-tuple-element.37), channel_id=1, source_target_pairs={{0,96},{32,0},{64,32},{96,64},{1,97},{33,1},{65,33},{97,65},{2,98}... | collective-permute-start | bytes 98312 | tf_op jit(solution)/shard_map/ppermute | solution.py:432
  68.9 2.5 %collective-permute-start.8 = (bf16[2,224,128]{2,1,0:T(8,128)(2,1)S(1)}, bf16[2,224,128]{2,1,0:T(8,128)(2,1)S(1)}, u32[]{:S(2)}, u32[]{:S(2)}) collective-permute-start(bf16[2,224,128]{2,1,0:T(8,128)(2,1)S(1)} %get-tuple-element.30), channel_id=1, source_target_pairs={{0,2},{1,3},{2,0},{3,1},{4,6},{5,7},{6,4},{7,5},{8,10},{9,11},{10,... | collective-permute-start | bytes 344072 | tf_op jit(solution)/shard_map/ppermute | solution.py:432
  71.4 1.9 %collective-permute-start.9 = (bf16[2,224,128]{2,1,0:T(8,128)(2,1)S(1)}, bf16[2,224,128]{2,1,0:T(8,128)(2,1)S(1)}, u32[]{:S(2)}, u32[]{:S(2)}) collective-permute-start(bf16[2,224,128]{2,1,0:T(8,128)(2,1)S(1)} %get-tuple-element.31), channel_id=1, source_target_pairs={{0,3},{1,0},{2,1},{3,2},{4,7},{5,4},{6,5},{7,6},{8,11},{9,8},{10,9... | collective-permute-start | bytes 344072 | tf_op jit(solution)/shard_map/ppermute | solution.py:432
  74.0 3.4 %all-to-all-start.2 = ((bf16[8,64,128]{2,1,0:T(8,128)(2,1)}), bf16[8,64,128]{2,1,0:T(8,128)(2,1)S(1)}, u32[]{:S(2)}, u32[]{:S(2)}) async-start(bf16[8,64,128]{2,1,0:T(8,128)(2,1)} %shard_map.220), calls=%async_computation.2 | async-start | bytes 262144 | tf_op jit(solution)/shard_map/all_to_all | solution.py:424
  77.4 2.2 %collective-permute-start.10 = (bf16[2,224,128]{2,1,0:T(8,128)(2,1)S(1)}, bf16[2,224,128]{2,1,0:T(8,128)(2,1)S(1)}, u32[]{:S(2)}, u32[]{:S(2)}) collective-permute-start(bf16[2,224,128]{2,1,0:T(8,128)(2,1)S(1)} %get-tuple-element.28.refs_0_), channel_id=1, source_target_pairs={{0,16},{16,0},{1,17},{17,1},{2,18},{18,2},{3,19},{19,3},{4,20},{20... | collective-permute-start | bytes 344072 | tf_op jit(solution)/shard_map/ppermute | solution.py:428
  81.5 3.9 %all-to-all-done.2.in_ref = bf16[8,64,128]{2,1,0:T(8,128)(2,1)S(1)} async-done(((bf16[8,64,128]{2,1,0:T(8,128)(2,1)}), bf16[8,64,128]{2,1,0:T(8,128)(2,1)S(1)}, u32[]{:S(2)}, u32[]{:S(2)}) %all-to-all-start.2) | async-done | bytes 131104 | tf_op jit(solution)/shard_map/all_to_all | solution.py:424
  86.1 3.7 %all-to-all-start.3 = ((bf16[16,64,128]{2,1,0:T(8,128)(2,1)}), bf16[16,64,128]{2,1,0:T(8,128)(2,1)S(1)}, u32[]{:S(2)}, u32[]{:S(2)}) async-start(bf16[16,64,128]{2,1,0:T(8,128)(2,1)} %shard_map.221), calls=%async_computation.3 | async-start | bytes 524288 | tf_op jit(solution)/shard_map/all_to_all | solution.py:424
  89.8 1.4 %shard_map.219 = (bf16[1,128,256]{2,1,0:T(8,128)(2,1)}, bf16[1,128,256]{2,1,0:T(8,128)(2,1)}, f32[3,768]{1,0:T(4,128)}, f32[128,256]{1,0:T(8,128)}, f32[128,256]{1,0:T(8,128)}) custom-call(bf16[2,224,128]{2,1,0:T(8,128)(2,1)S(1)} %get-tuple-element.28.refs_0_, bf16[2,224,128]{2,1,0:T(8,128)(2,1)S(1)} %collective-permute-done.7.refs_1_, ...), custom_call_target="tpu_custom_call" | custom-call | tf_op jit(solution)/shard_map/pallas_call | solution.py:472
  91.1 5.9 %all-to-all-done.3.own_ref = bf16[16,64,128]{2,1,0:T(8,128)(2,1)S(1)} async-done(((bf16[16,64,128]{2,1,0:T(8,128)(2,1)}), bf16[16,64,128]{2,1,0:T(8,128)(2,1)S(1)}, u32[]{:S(2)}, u32[]{:S(2)}) %all-to-all-start.3) | async-done | bytes 262176 | tf_op jit(solution)/shard_map/all_to_all | solution.py:424
  97.0 6.1 %collective-permute-start.17 = (bf16[16,64,128]{2,1,0:T(8,128)(2,1)S(1)}, bf16[16,64,128]{2,1,0:T(8,128)(2,1)S(1)}, u32[]{:S(2)}, u32[]{:S(2)}) collective-permute-start(bf16[16,64,128]{2,1,0:T(8,128)(2,1)S(1)} %all-to-all-done.3.own_ref), channel_id=1, source_target_pairs={{0,16},{16,0},{1,17},{17,1},{2,18},{18,2},{3,19},{19,3},{4,20},{20... | collective-permute-start | bytes 786440 | tf_op jit(solution)/shard_map/ppermute | solution.py:428
  103.1 1.2 %collective-permute-done.17.other_ref = bf16[16,64,128]{2,1,0:T(8,128)(2,1)S(1)} collective-permute-done((bf16[16,64,128]{2,1,0:T(8,128)(2,1)S(1)}, bf16[16,64,128]{2,1,0:T(8,128)(2,1)S(1)}, u32[]{:S(2)}, u32[]{:S(2)}) %collective-permute-start.17) | collective-permute-done | bytes 262176 | tf_op jit(solution)/shard_map/ppermute | solution.py:428
  104.3 1.3 %shard_map.222 = (f32[256,768]{1,0:T(8,128)}, f32[256,256]{1,0:T(8,128)}) custom-call(bf16[16,64,128]{2,1,0:T(8,128)(2,1)S(1)} %all-to-all-done.3.own_ref, bf16[16,64,128]{2,1,0:T(8,128)(2,1)S(1)} %collective-permute-done.17.other_ref), custom_call_target="tpu_custom_call" | custom-call | tf_op jit(solution)/shard_map/pallas_call | solution.py:483
  (54 shorter events, 7.1 us)
Async XLA Ops:
  3.0 36.7 %copy-start.3 = (bf16[256,256]{1,0:T(8,128)(2,1)S(1)}, bf16[256,256]{1,0:T(8,128)(2,1)}, u32[]{:S(2)}) copy-start(bf16[256,256]{1,0:T(8,128)(2,1)} %constant.25.clone.second_back_low) | copy-start | bytes 393220
  3.0 36.7 %copy-start.4 = (bf16[256,256]{1,0:T(8,128)(2,1)S(1)}, bf16[256,256]{1,0:T(8,128)(2,1)}, u32[]{:S(2)}) copy-start(bf16[256,256]{1,0:T(8,128)(2,1)} %constant.24.clone.second_back_high) | copy-start | bytes 393220
  3.0 36.7 %copy-start.5 = (bf16[256,256]{1,0:T(8,128)(2,1)S(1)}, bf16[256,256]{1,0:T(8,128)(2,1)}, u32[]{:S(2)}) copy-start(bf16[256,256]{1,0:T(8,128)(2,1)} %constant.23.clone.second_low) | copy-start | bytes 393220
  44.6 19.7 %all-to-all-start.1 = ((bf16[32,7,8,128]{3,2,1,0:T(8,128)(2,1)}), bf16[32,7,8,128]{3,2,1,0:T(8,128)(2,1)S(1)}, u32[]{:S(2)}, u32[]{:S(2)}) async-start(bf16[32,7,8,128]{3,2,1,0:T(8,128)(2,1)} %shard_map.217), calls=%async_computation.1 | async-start | bytes 917504 | tf_op jit(solution)/shard_map/all_to_all | solution.py:424
  48.6 4.4 %collective-permute-start.2 = (bf16[128,512]{1,0:T(8,128)(2,1)S(1)}, bf16[128,512]{1,0:T(8,128)(2,1)S(1)}, u32[]{:S(2)}, u32[]{:S(2)}) collective-permute-start(bf16[128,512]{1,0:T(8,128)(2,1)S(1)} %copy-done.2), channel_id=1, source_target_pairs={{0,3},{1,0},{2,1},{3,2},{4,7},{5,4},{6,5},{7,6},{8,11},{9,8},{10,9... | collective-permute-start | bytes 393224 | tf_op jit(solution)/shard_map/ppermute | solution.py:432
  49.9 6.1 %collective-permute-start.1 = (bf16[128,512]{1,0:T(8,128)(2,1)S(1)}, bf16[128,512]{1,0:T(8,128)(2,1)S(1)}, u32[]{:S(2)}, u32[]{:S(2)}) collective-permute-start(bf16[128,512]{1,0:T(8,128)(2,1)S(1)} %copy-done.2), channel_id=1, source_target_pairs={{0,2},{1,3},{2,0},{3,1},{4,6},{5,7},{6,4},{7,5},{8,10},{9,11},{10,... | collective-permute-start | bytes 393224 | tf_op jit(solution)/shard_map/ppermute | solution.py:432
  50.9 8.4 %collective-permute-start = (bf16[128,512]{1,0:T(8,128)(2,1)S(1)}, bf16[128,512]{1,0:T(8,128)(2,1)S(1)}, u32[]{:S(2)}, u32[]{:S(2)}) collective-permute-start(bf16[128,512]{1,0:T(8,128)(2,1)S(1)} %copy-done.2), channel_id=1, source_target_pairs={{0,1},{1,2},{2,3},{3,0},{4,5},{5,6},{6,7},{7,4},{8,9},{9,10},{10,1... | collective-permute-start | bytes 393224 | tf_op jit(solution)/shard_map/ppermute | solution.py:432
  51.0 9.1 %collective-permute-start.3 = (bf16[128,512]{1,0:T(8,128)(2,1)S(1)}, bf16[128,512]{1,0:T(8,128)(2,1)S(1)}, u32[]{:S(2)}, u32[]{:S(2)}) collective-permute-start(bf16[128,512]{1,0:T(8,128)(2,1)S(1)} %copy-done.2), channel_id=1, source_target_pairs={{0,16},{16,0},{1,17},{17,1},{2,18},{18,2},{3,19},{19,3},{4,20},{20... | collective-permute-start | bytes 393224 | tf_op jit(solution)/shard_map/ppermute | solution.py:428
  53.1 7.1 %collective-permute-start.6 = (bf16[128,512]{1,0:T(8,128)(2,1)S(1)}, bf16[128,512]{1,0:T(8,128)(2,1)S(1)}, u32[]{:S(2)}, u32[]{:S(2)}) collective-permute-start(bf16[128,512]{1,0:T(8,128)(2,1)S(1)} %collective-permute-done.2.refs_3_), channel_id=1, source_target_pairs={{0,16},{16,0},{1,17},{17,1},{2,18},{18,2},{3,19},{19,3},{4,20},{20... | collective-permute-start | bytes 393224 | tf_op jit(solution)/shard_map/ppermute | solution.py:428
  56.0 4.1 %collective-permute-start.5 = (bf16[128,512]{1,0:T(8,128)(2,1)S(1)}, bf16[128,512]{1,0:T(8,128)(2,1)S(1)}, u32[]{:S(2)}, u32[]{:S(2)}) collective-permute-start(bf16[128,512]{1,0:T(8,128)(2,1)S(1)} %collective-permute-done.1.refs_2_), channel_id=1, source_target_pairs={{0,16},{16,0},{1,17},{17,1},{2,18},{18,2},{3,19},{19,3},{4,20},{20... | collective-permute-start | bytes 393224 | tf_op jit(solution)/shard_map/ppermute | solution.py:428
  59.3 1.9 %collective-permute-start.4 = (bf16[128,512]{1,0:T(8,128)(2,1)S(1)}, bf16[128,512]{1,0:T(8,128)(2,1)S(1)}, u32[]{:S(2)}, u32[]{:S(2)}) collective-permute-start(bf16[128,512]{1,0:T(8,128)(2,1)S(1)} %collective-permute-done.refs_1_), channel_id=1, source_target_pairs={{0,16},{16,0},{1,17},{17,1},{2,18},{18,2},{3,19},{19,3},{4,20},{20... | collective-permute-start | bytes 393224 | tf_op jit(solution)/shard_map/ppermute | solution.py:428
  64.8 6.6 %collective-permute-start.14 = (f32[32,256]{1,0:T(8,128)S(1)}, f32[32,256]{1,0:T(8,128)S(1)}, u32[]{:S(2)}, u32[]{:S(2)}) collective-permute-start(f32[32,256]{1,0:T(8,128)S(1)} %get-tuple-element.35), channel_id=1, source_target_pairs={{0,32},{32,64},{64,96},{96,0},{1,33},{33,65},{65,97},{97,1},{2,34}... | collective-permute-start | bytes 98312 | tf_op jit(solution)/shard_map/ppermute | solution.py:432
  65.1 8.3 %collective-permute-start.15 = (f32[32,256]{1,0:T(8,128)S(1)}, f32[32,256]{1,0:T(8,128)S(1)}, u32[]{:S(2)}, u32[]{:S(2)}) collective-permute-start(f32[32,256]{1,0:T(8,128)S(1)} %get-tuple-element.36), channel_id=1, source_target_pairs={{0,64},{32,96},{64,0},{96,32},{1,65},{33,97},{65,1},{97,33},{2,66}... | collective-permute-start | bytes 98312 | tf_op jit(solution)/shard_map/ppermute | solution.py:432
  66.9 6.4 %collective-permute-start.16 = (f32[32,256]{1,0:T(8,128)S(1)}, f32[32,256]{1,0:T(8,128)S(1)}, u32[]{:S(2)}, u32[]{:S(2)}) collective-permute-start(f32[32,256]{1,0:T(8,128)S(1)} %get-tuple-element.37), channel_id=1, source_target_pairs={{0,96},{32,0},{64,32},{96,64},{1,97},{33,1},{65,33},{97,65},{2,98}... | collective-permute-start | bytes 98312 | tf_op jit(solution)/shard_map/ppermute | solution.py:432
  68.5 11.1 %collective-permute-start.7 = (bf16[2,224,128]{2,1,0:T(8,128)(2,1)S(1)}, bf16[2,224,128]{2,1,0:T(8,128)(2,1)S(1)}, u32[]{:S(2)}, u32[]{:S(2)}) collective-permute-start(bf16[2,224,128]{2,1,0:T(8,128)(2,1)S(1)} %get-tuple-element.29), channel_id=1, source_target_pairs={{0,1},{1,2},{2,3},{3,0},{4,5},{5,6},{6,7},{7,4},{8,9},{9,10},{10,1... | collective-permute-start | bytes 344072 | tf_op jit(solution)/shard_map/ppermute | solution.py:432
  68.9 10.8 %collective-permute-start.8 = (bf16[2,224,128]{2,1,0:T(8,128)(2,1)S(1)}, bf16[2,224,128]{2,1,0:T(8,128)(2,1)S(1)}, u32[]{:S(2)}, u32[]{:S(2)}) collective-permute-start(bf16[2,224,128]{2,1,0:T(8,128)(2,1)S(1)} %get-tuple-element.30), channel_id=1, source_target_pairs={{0,2},{1,3},{2,0},{3,1},{4,6},{5,7},{6,4},{7,5},{8,10},{9,11},{10,... | collective-permute-start | bytes 344072 | tf_op jit(solution)/shard_map/ppermute | solution.py:432
  71.4 8.7 %collective-permute-start.9 = (bf16[2,224,128]{2,1,0:T(8,128)(2,1)S(1)}, bf16[2,224,128]{2,1,0:T(8,128)(2,1)S(1)}, u32[]{:S(2)}, u32[]{:S(2)}) collective-permute-start(bf16[2,224,128]{2,1,0:T(8,128)(2,1)S(1)} %get-tuple-element.31), channel_id=1, source_target_pairs={{0,3},{1,0},{2,1},{3,2},{4,7},{5,4},{6,5},{7,6},{8,11},{9,8},{10,9... | collective-permute-start | bytes 344072 | tf_op jit(solution)/shard_map/ppermute | solution.py:432
  74.0 11.3 %all-to-all-start.2 = ((bf16[8,64,128]{2,1,0:T(8,128)(2,1)}), bf16[8,64,128]{2,1,0:T(8,128)(2,1)S(1)}, u32[]{:S(2)}, u32[]{:S(2)}) async-start(bf16[8,64,128]{2,1,0:T(8,128)(2,1)} %shard_map.220), calls=%async_computation.2 | async-start | bytes 262144 | tf_op jit(solution)/shard_map/all_to_all | solution.py:424
  77.4 3.2 %collective-permute-start.10 = (bf16[2,224,128]{2,1,0:T(8,128)(2,1)S(1)}, bf16[2,224,128]{2,1,0:T(8,128)(2,1)S(1)}, u32[]{:S(2)}, u32[]{:S(2)}) collective-permute-start(bf16[2,224,128]{2,1,0:T(8,128)(2,1)S(1)} %get-tuple-element.28.refs_0_), channel_id=1, source_target_pairs={{0,16},{16,0},{1,17},{17,1},{2,18},{18,2},{3,19},{19,3},{4,20},{20... | collective-permute-start | bytes 344072 | tf_op jit(solution)/shard_map/ppermute | solution.py:428
  79.6 1.3 %collective-permute-start.11 = (bf16[2,224,128]{2,1,0:T(8,128)(2,1)S(1)}, bf16[2,224,128]{2,1,0:T(8,128)(2,1)S(1)}, u32[]{:S(2)}, u32[]{:S(2)}) collective-permute-start(bf16[2,224,128]{2,1,0:T(8,128)(2,1)S(1)} %collective-permute-done.7.refs_1_), channel_id=1, source_target_pairs={{0,16},{16,0},{1,17},{17,1},{2,18},{18,2},{3,19},{19,3},{4,20},{20... | collective-permute-start | bytes 344072 | tf_op jit(solution)/shard_map/ppermute | solution.py:428
  79.7 1.4 %collective-permute-start.12 = (bf16[2,224,128]{2,1,0:T(8,128)(2,1)S(1)}, bf16[2,224,128]{2,1,0:T(8,128)(2,1)S(1)}, u32[]{:S(2)}, u32[]{:S(2)}) collective-permute-start(bf16[2,224,128]{2,1,0:T(8,128)(2,1)S(1)} %collective-permute-done.8.refs_2_), channel_id=1, source_target_pairs={{0,16},{16,0},{1,17},{17,1},{2,18},{18,2},{3,19},{19,3},{4,20},{20... | collective-permute-start | bytes 344072 | tf_op jit(solution)/shard_map/ppermute | solution.py:428
  80.1 1.3 %collective-permute-start.13 = (bf16[2,224,128]{2,1,0:T(8,128)(2,1)S(1)}, bf16[2,224,128]{2,1,0:T(8,128)(2,1)S(1)}, u32[]{:S(2)}, u32[]{:S(2)}) collective-permute-start(bf16[2,224,128]{2,1,0:T(8,128)(2,1)S(1)} %collective-permute-done.9.refs_3_), channel_id=1, source_target_pairs={{0,16},{16,0},{1,17},{17,1},{2,18},{18,2},{3,19},{19,3},{4,20},{20... | collective-permute-start | bytes 344072 | tf_op jit(solution)/shard_map/ppermute | solution.py:428
  86.1 11.0 %all-to-all-start.3 = ((bf16[16,64,128]{2,1,0:T(8,128)(2,1)}), bf16[16,64,128]{2,1,0:T(8,128)(2,1)S(1)}, u32[]{:S(2)}, u32[]{:S(2)}) async-start(bf16[16,64,128]{2,1,0:T(8,128)(2,1)} %shard_map.221), calls=%async_computation.3 | async-start | bytes 524288 | tf_op jit(solution)/shard_map/all_to_all | solution.py:424
  97.0 7.2 %collective-permute-start.17 = (bf16[16,64,128]{2,1,0:T(8,128)(2,1)S(1)}, bf16[16,64,128]{2,1,0:T(8,128)(2,1)S(1)}, u32[]{:S(2)}, u32[]{:S(2)}) collective-permute-start(bf16[16,64,128]{2,1,0:T(8,128)(2,1)S(1)} %all-to-all-done.3.own_ref), channel_id=1, source_target_pairs={{0,16},{16,0},{1,17},{17,1},{2,18},{18,2},{3,19},{19,3},{4,20},{20... | collective-permute-start | bytes 786440 | tf_op jit(solution)/shard_map/ppermute | solution.py:428
  (11 other events, 304.7 us)

commit v5 on v4

--- a/solution.py
+++ b/solution.py
@@ -112,9 +112,9 @@
     first_back_low,
     turn_cos_ref,
     turn_sin_ref,
-    out_ref,
-    rows_ref,
+    *rest,
 ):
+    out_ref, rows_ref = rest[-2:]
     sources, slots, rows = in_ref.shape
     blocks = sources // 2
     width = short_ref.shape[1] // 3
@@ -365,7 +365,7 @@
 
 
 def add_x_kernel(*refs):
-    out_ref = refs[-1]
+    out_ref = refs[7]
     total = refs[0][...] + refs[1][...] + refs[2][...] + refs[3][...]
     lanes = out_ref.shape[2]
     rows = jnp.concatenate([total[:, :lanes], total[:, lanes:]], 0)
@@ -405,19 +405,18 @@
                 )
 
 
-def call(kernel, out_shape, scratch=(), whole=0, waited=0, limit=vmem_limit):
-    specs = {}
-    if waited:
-        specs["in_specs"] = [pl.BlockSpec(memory_space=pltpu.VMEM)] * whole + [
-            pl.BlockSpec(memory_space=pl.ANY)
-        ] * waited
+def call(kernel, out_shape, scratch=(), limit=vmem_limit, **options):
     return pl.pallas_call(
         kernel,
         out_shape=out_shape,
         scratch_shapes=list(scratch),
         compiler_params=pltpu.CompilerParams(vmem_limit_bytes=limit),
-        **specs,
-    )
+        **options,
+    )
+
+
+def specs(*spaces):
+    return [pl.BlockSpec(memory_space=space) for space in spaces]
 
 
 def exchange(x, axes):
@@ -453,7 +452,8 @@
         convolve_kernel,
         shape((32, 7, 8, rows), bf16),
         [pltpu.VMEM((devices * 8, rows), f32)],
-    )(received, short_kernel, *tables)
+        in_specs=specs(*[pltpu.VMEM] * (2 + len(tables)), *[pl.ANY] * 3),
+    )(received, short_kernel, *tables, *gathered[1:4])
     halfway = exchange(back, ("zh", "x", "zl"))
     found = call(
         part_kernel,
@@ -461,13 +461,22 @@
         [pltpu.VMEM((32 * 7 * 8, rows), f32), pltpu.VMEM((4, 32, width), f32)],
     )(halfway, *gathered)
     part = [found[0]] + [ring(found[distance], "x", distance) for distance in (1, 2, 3)]
-    arrived = [found[4]] + [ring(found[4 + distance], "y", distance) for distance in (1, 2, 3)]
-    arrived += [swap_core(x) for x in arrived]
-    part = call(add_x_kernel, shape((8, 64, rows), bf16))(*part)
+    leaving = found[5:]
+    part, *leaving = call(
+        add_x_kernel,
+        (shape((8, 64, rows), bf16),) + (shape(leaving[0].shape, bf16),) * 3,
+        in_specs=specs(*[pltpu.VMEM] * 4, *[pl.ANY] * 3),
+        out_specs=specs(pltpu.VMEM, *[pl.ANY] * 3),
+        input_output_aliases={4: 1, 5: 2, 6: 3},
+    )(*part, *leaving)
+    arrived = [found[4]] + [ring(x, "y", 1 + i) for i, x in enumerate(leaving)]
     part = exchange(part, ("zh", "zl"))
     part = call(
-        functools.partial(add_z_kernel, scale), shape((16, 64, rows), bf16), whole=1, waited=4
-    )(part, *arrived[4:])
+        functools.partial(add_z_kernel, scale),
+        shape((16, 64, rows), bf16),
+        in_specs=specs(pltpu.VMEM, *[pl.ANY] * 3),
+    )(part, *arrived[1:])
+    arrived += [swap_core(x) for x in arrived]
     part = exchange(part, ("x", "y"))
     outputs, grad_inputs, grad_short, grad_one, grad_two = call(
         finish_kernel,

time: 106 us -> 105 us (level)
  blocking collectives: 36.6 us -> 0 us
  waiting for transfers between devices: 17.8 us -> 40.6 us
  starting transfers between devices: 38.5 us -> 51.3 us
    all_to_all x1 -> x0, blocking collectives: 36.6 us -> none  [exchange(): return lax.all_to_all(x, axes, split_axis=0, concat_axis=0, tiled=True)]
    all_to_all x3 -> x4, starting transfers between devices: 11.1 us -> 28.9 us  [exchange(): return lax.all_to_all(x, axes, split_axis=0, concat_axis=0, tiled=True)]
    ppermute x9, waiting for transfers between devices: 1.54 us -> 17.6 us  [ring(): return lax.ppermute(x, axis, [(i, (i + distance) % 4) for i in range(4)])]
    all_to_all x3 -> x4, waiting for transfers between devices: 12.9 us -> 19.4 us  [exchange(): return lax.all_to_all(x, axes, split_axis=0, concat_axis=0, tiled=True)]
    ppermute x9, starting transfers between devices: 16.5 us -> 12.1 us  [swap_core(): return lax.ppermute(x, 'core', [(0, 1), (1, 0)])]
  transfers between devices with their start and end apart: 21 -> 22, of which waited for: 11 -> 20; matrix products, arithmetic and copies ran while one was open for 0% -> 0% of each run, Pallas kernels for 2% -> 1%
where the time goes in v5:
time: 105 us
  starting transfers between devices  51.3 us (49%)
  waiting for transfers between devices  40.6 us (39%)
  Pallas kernels  11.8 us (11%)
    all_to_all x4, starting transfers between devices, exchange(): return lax.all_to_all(x, axes, split_axis=0, concat_axis=0, tiled=True)  28.9 us
    all_to_all x4, waiting for transfers between devices, exchange(): return lax.all_to_all(x, axes, split_axis=0, concat_axis=0, tiled=True)  19.4 us
    ppermute x9, waiting for transfers between devices, ring(): return lax.ppermute(x, axis, [(i, (i + distance) % 4) for i in range(4)])  17.6 us
    ppermute x9, starting transfers between devices, swap_core(): return lax.ppermute(x, 'core', [(0, 1), (1, 0)])  12.1 us
    ppermute x9, starting transfers between devices, ring(): return lax.ppermute(x, axis, [(i, (i + distance) % 4) for i in range(4)])  10.3 us
    pallas_call x1, Pallas kernels, per_device(): call(convolve_kernel, shape((32, 7, 8, rows), bf16), [pltpu.VMEM((devices...  4.82 us
    ppermute x9, waiting for transfers between devices, swap_core(): return lax.ppermute(x, 'core', [(0, 1), (1, 0)])  3.63 us
    pallas_call x1, Pallas kernels, per_device(): call(pack_kernel, (shape((width, 8, rows), bf16), shape((rows, 2 * width)...  2.36 us
  transfers between devices with their start and end apart: 22, of which 20 were waited for; matrix products, arithmetic and copies ran while one was open for 0% of the time, Pallas kernels for 1%

profile of v5, /device:TPU:1, one launch (start us, length us, event | category | flops | bytes accessed | tf_op | source)
XLA Modules:
  0.0 104.6 jit_solution(11715284823059272052)
XLA Ops:
  0.6 2.4 %shard_map.216 = (bf16[256,8,128]{2,1,0:T(8,128)(2,1)}, bf16[128,512]{1,0:T(8,128)(2,1)}) custom-call(bf16[1,128,256]{2,1,0:T(8,128)(2,1)} %seq_ref.1, bf16[256,768]{1,0:T(8,128)(2,1)} %refs_8_.1, f32[128,256]{1,0:T(8,128)} %one_ref.1, f32[128,256]{1,0:T(8,128)} %two_ref.1, bf16[256,256]{1,0:T(8,128)(2,1)} %refs_9_.1, bf16[1,128,256]{2,1,0:T(8,128)(2,1)} %grad_ref.1), custom_call_target="tpu_custom_call" | custom-call | tf_op jit(solution)/shard_map/pallas_call | solution.py:441
  3.1 15.7 %all-to-all-start = ((bf16[256,8,128]{2,1,0:T(8,128)(2,1)}), bf16[256,8,128]{2,1,0:T(8,128)(2,1)S(1)}, u32[]{:S(2)}, u32[]{:S(2)}) async-start(bf16[256,8,128]{2,1,0:T(8,128)(2,1)} %get-tuple-element.30), calls=%async_computation | async-start | bytes 1048576 | tf_op jit(solution)/shard_map/all_to_all | solution.py:423
  18.8 2.7 %collective-permute-start.2 = (bf16[128,512]{1,0:T(8,128)(2,1)S(1)}, bf16[128,512]{1,0:T(8,128)(2,1)S(1)}, u32[]{:S(2)}, u32[]{:S(2)}) collective-permute-start(bf16[128,512]{1,0:T(8,128)(2,1)S(1)} %copy-done.2), channel_id=1, source_target_pairs={{0,3},{1,0},{2,1},{3,2},{4,7},{5,4},{6,5},{7,6},{8,11},{9,8},{10,9... | collective-permute-start | bytes 393224 | tf_op jit(solution)/shard_map/ppermute | solution.py:431
  22.6 5.3 %collective-permute-done.2.rest_2_.refs_3_ = bf16[128,512]{1,0:T(8,128)(2,1)S(1)} collective-permute-done((bf16[128,512]{1,0:T(8,128)(2,1)S(1)}, bf16[128,512]{1,0:T(8,128)(2,1)S(1)}, u32[]{:S(2)}, u32[]{:S(2)}) %collective-permute-start.2) | collective-permute-done | bytes 131104 | tf_op jit(solution)/shard_map/ppermute | solution.py:431
  28.4 6.4 %collective-permute-done.rest_0_.refs_1_ = bf16[128,512]{1,0:T(8,128)(2,1)S(1)} collective-permute-done((bf16[128,512]{1,0:T(8,128)(2,1)S(1)}, bf16[128,512]{1,0:T(8,128)(2,1)S(1)}, u32[]{:S(2)}, u32[]{:S(2)}) %collective-permute-start) | collective-permute-done | bytes 131104 | tf_op jit(solution)/shard_map/ppermute | solution.py:431
  34.8 4.9 %all-to-all-done.in_ref = bf16[256,8,128]{2,1,0:T(8,128)(2,1)S(1)} async-done(((bf16[256,8,128]{2,1,0:T(8,128)(2,1)}), bf16[256,8,128]{2,1,0:T(8,128)(2,1)S(1)}, u32[]{:S(2)}, u32[]{:S(2)}) %all-to-all-start) | async-done | bytes 524320 | tf_op jit(solution)/shard_map/all_to_all | solution.py:423
  39.8 4.8 %shard_map.217 = bf16[32,7,8,128]{3,2,1,0:T(8,128)(2,1)} custom-call(bf16[256,8,128]{2,1,0:T(8,128)(2,1)S(1)} %all-to-all-done.in_ref, f32[3,768]{1,0:T(4,128)S(1)} %copy-done.13, bf16[256,128]{1,0:T(8,128)(2,1)S(1)} %copy-done.12, bf16[256,128]{1,0:T(8,128)(2,1)S(1)} %copy-done.11, bf16[256,256]{1,0:T(8,128)(2,1)S(1)} %copy-done.6, ...), custom_call_target="tpu_custom_call" | custom-call | tf_op jit(solution)/shard_map/pallas_call | solution.py:451
  44.6 4.7 %all-to-all-start.1 = ((bf16[32,7,8,128]{3,2,1,0:T(8,128)(2,1)}), bf16[32,7,8,128]{3,2,1,0:T(8,128)(2,1)S(1)}, u32[]{:S(2)}, u32[]{:S(2)}) async-start(bf16[32,7,8,128]{3,2,1,0:T(8,128)(2,1)} %shard_map.217), calls=%async_computation.1 | async-start | bytes 917504 | tf_op jit(solution)/shard_map/all_to_all | solution.py:423
  49.3 0.8 collective-permute-start.3
  51.9 13.6 %all-to-all-done.1.in_ref = bf16[32,7,8,128]{3,2,1,0:T(8,128)(2,1)S(1)} async-done(((bf16[32,7,8,128]{3,2,1,0:T(8,128)(2,1)}), bf16[32,7,8,128]{3,2,1,0:T(8,128)(2,1)S(1)}, u32[]{:S(2)}, u32[]{:S(2)}) %all-to-all-start.1) | async-done | bytes 458784 | tf_op jit(solution)/shard_map/all_to_all | solution.py:423
  66.2 1.7 %collective-permute-start.8 = (f32[32,256]{1,0:T(8,128)S(1)}, f32[32,256]{1,0:T(8,128)S(1)}, u32[]{:S(2)}, u32[]{:S(2)}) collective-permute-start(f32[32,256]{1,0:T(8,128)S(1)} %get-tuple-element.35), channel_id=1, source_target_pairs={{0,64},{32,96},{64,0},{96,32},{1,65},{33,97},{65,1},{97,33},{2,66}... | collective-permute-start | bytes 98312 | tf_op jit(solution)/shard_map/ppermute | solution.py:431
  67.8 1.7 %collective-permute-start.9 = (f32[32,256]{1,0:T(8,128)S(1)}, f32[32,256]{1,0:T(8,128)S(1)}, u32[]{:S(2)}, u32[]{:S(2)}) collective-permute-start(f32[32,256]{1,0:T(8,128)S(1)} %get-tuple-element.36), channel_id=1, source_target_pairs={{0,96},{32,0},{64,32},{96,64},{1,97},{33,1},{65,33},{97,65},{2,98}... | collective-permute-start | bytes 98312 | tf_op jit(solution)/shard_map/ppermute | solution.py:431
  71.7 3.4 %all-to-all-start.2 = ((bf16[8,64,128]{2,1,0:T(8,128)(2,1)}), bf16[8,64,128]{2,1,0:T(8,128)(2,1)S(1)}, u32[]{:S(2)}, u32[]{:S(2)}) async-start(bf16[8,64,128]{2,1,0:T(8,128)(2,1)} %get-tuple-element.45), calls=%async_computation.2 | async-start | bytes 262144 | tf_op jit(solution)/shard_map/all_to_all | solution.py:423
  75.2 1.7 %collective-permute-start.11 = (bf16[2,224,128]{2,1,0:T(8,128)(2,1)S(1)}, bf16[2,224,128]{2,1,0:T(8,128)(2,1)S(1)}, u32[]{:S(2)}, u32[]{:S(2)}) collective-permute-start(bf16[2,224,128]{2,1,0:T(8,128)(2,1)S(1)} %get-tuple-element.41), channel_id=1, source_target_pairs={{0,2},{1,3},{2,0},{3,1},{4,6},{5,7},{6,4},{7,5},{8,10},{9,11},{10,... | collective-permute-start | bytes 344072 | tf_op jit(solution)/shard_map/ppermute | solution.py:431
  76.9 1.2 %collective-permute-start.12 = (bf16[2,224,128]{2,1,0:T(8,128)(2,1)S(1)}, bf16[2,224,128]{2,1,0:T(8,128)(2,1)S(1)}, u32[]{:S(2)}, u32[]{:S(2)}) collective-permute-start(bf16[2,224,128]{2,1,0:T(8,128)(2,1)S(1)} %get-tuple-element.42), channel_id=1, source_target_pairs={{0,3},{1,0},{2,1},{3,2},{4,7},{5,4},{6,5},{7,6},{8,11},{9,8},{10,9... | collective-permute-start | bytes 344072 | tf_op jit(solution)/shard_map/ppermute | solution.py:431
  78.1 3.2 %collective-permute-done.10.refs_1_.refs_0_ = bf16[2,224,128]{2,1,0:T(8,128)(2,1)S(1)} collective-permute-done((bf16[2,224,128]{2,1,0:T(8,128)(2,1)S(1)}, bf16[2,224,128]{2,1,0:T(8,128)(2,1)S(1)}, u32[]{:S(2)}, u32[]{:S(2)}) %collective-permute-start.10) | collective-permute-done | bytes 114720 | tf_op jit(solution)/shard_map/ppermute | solution.py:431
  81.3 0.8 collective-permute-done.12.refs_3_.refs_2_
  82.0 0.9 all-to-all-done.2.in_ref
  83.7 5.2 %all-to-all-start.3 = ((bf16[16,64,128]{2,1,0:T(8,128)(2,1)}), bf16[16,64,128]{2,1,0:T(8,128)(2,1)S(1)}, u32[]{:S(2)}, u32[]{:S(2)}) async-start(bf16[16,64,128]{2,1,0:T(8,128)(2,1)} %shard_map.221), calls=%async_computation.3 | async-start | bytes 524288 | tf_op jit(solution)/shard_map/all_to_all | solution.py:423
  88.8 4.9 %collective-permute-start.13 = (bf16[2,224,128]{2,1,0:T(8,128)(2,1)S(1)}, bf16[2,224,128]{2,1,0:T(8,128)(2,1)S(1)}, u32[]{:S(2)}, u32[]{:S(2)}) collective-permute-start(bf16[2,224,128]{2,1,0:T(8,128)(2,1)S(1)} %get-tuple-element.32.refs_0_), channel_id=1, source_target_pairs={{0,16},{16,0},{1,17},{17,1},{2,18},{18,2},{3,19},{19,3},{4,20},{20... | collective-permute-start | bytes 344072 | tf_op jit(solution)/shard_map/ppermute | solution.py:427
  95.6 1.4 %shard_map.220 = (bf16[1,128,256]{2,1,0:T(8,128)(2,1)}, bf16[1,128,256]{2,1,0:T(8,128)(2,1)}, f32[3,768]{1,0:T(4,128)}, f32[128,256]{1,0:T(8,128)}, f32[128,256]{1,0:T(8,128)}) custom-call(bf16[2,224,128]{2,1,0:T(8,128)(2,1)S(1)} %get-tuple-element.32.refs_0_, bf16[2,224,128]{2,1,0:T(8,128)(2,1)S(1)} %collective-permute-done.10.refs_1_.refs_0_, ...), custom_call_target="tpu_custom_call" | custom-call | tf_op jit(solution)/shard_map/pallas_call | solution.py:481
  97.0 5.2 %collective-permute-start.17 = (bf16[16,64,128]{2,1,0:T(8,128)(2,1)S(1)}, bf16[16,64,128]{2,1,0:T(8,128)(2,1)S(1)}, u32[]{:S(2)}, u32[]{:S(2)}) collective-permute-start(bf16[16,64,128]{2,1,0:T(8,128)(2,1)S(1)} %all-to-all-done.3.own_ref), channel_id=1, source_target_pairs={{0,16},{16,0},{1,17},{17,1},{2,18},{18,2},{3,19},{19,3},{4,20},{20... | collective-permute-start | bytes 786440 | tf_op jit(solution)/shard_map/ppermute | solution.py:427
  102.2 1.2 %collective-permute-done.17.other_ref = bf16[16,64,128]{2,1,0:T(8,128)(2,1)S(1)} collective-permute-done((bf16[16,64,128]{2,1,0:T(8,128)(2,1)S(1)}, bf16[16,64,128]{2,1,0:T(8,128)(2,1)S(1)}, u32[]{:S(2)}, u32[]{:S(2)}) %collective-permute-start.17) | collective-permute-done | bytes 262176 | tf_op jit(solution)/shard_map/ppermute | solution.py:427
  103.3 1.3 %shard_map.222 = (f32[256,768]{1,0:T(8,128)}, f32[256,256]{1,0:T(8,128)}) custom-call(bf16[16,64,128]{2,1,0:T(8,128)(2,1)S(1)} %all-to-all-done.3.own_ref, bf16[16,64,128]{2,1,0:T(8,128)(2,1)S(1)} %collective-permute-done.17.other_ref), custom_call_target="tpu_custom_call" | custom-call | tf_op jit(solution)/shard_map/pallas_call | solution.py:492
  (55 shorter events, 9.0 us)
Async XLA Ops:
  0.6 39.0 %copy-start.13 = (f32[3,768]{1,0:T(4,128)S(1)}, f32[3,768]{1,0:T(4,128)}, u32[]{:S(2)}) copy-start(f32[3,768]{1,0:T(4,128)} %short_ref.1) | copy-start | bytes 27652
  3.0 36.7 %copy-start.4 = (bf16[256,256]{1,0:T(8,128)(2,1)S(1)}, bf16[256,256]{1,0:T(8,128)(2,1)}, u32[]{:S(2)}) copy-start(bf16[256,256]{1,0:T(8,128)(2,1)} %constant.24.clone.second_back_high) | copy-start | bytes 393220
  3.1 36.6 %all-to-all-start = ((bf16[256,8,128]{2,1,0:T(8,128)(2,1)}), bf16[256,8,128]{2,1,0:T(8,128)(2,1)S(1)}, u32[]{:S(2)}, u32[]{:S(2)}) async-start(bf16[256,8,128]{2,1,0:T(8,128)(2,1)} %get-tuple-element.30), calls=%async_computation | async-start | bytes 1048576 | tf_op jit(solution)/shard_map/all_to_all | solution.py:423
  18.8 9.2 %collective-permute-start.2 = (bf16[128,512]{1,0:T(8,128)(2,1)S(1)}, bf16[128,512]{1,0:T(8,128)(2,1)S(1)}, u32[]{:S(2)}, u32[]{:S(2)}) collective-permute-start(bf16[128,512]{1,0:T(8,128)(2,1)S(1)} %copy-done.2), channel_id=1, source_target_pairs={{0,3},{1,0},{2,1},{3,2},{4,7},{5,4},{6,5},{7,6},{8,11},{9,8},{10,9... | collective-permute-start | bytes 393224 | tf_op jit(solution)/shard_map/ppermute | solution.py:431
  21.5 6.9 %collective-permute-start.1 = (bf16[128,512]{1,0:T(8,128)(2,1)S(1)}, bf16[128,512]{1,0:T(8,128)(2,1)S(1)}, u32[]{:S(2)}, u32[]{:S(2)}) collective-permute-start(bf16[128,512]{1,0:T(8,128)(2,1)S(1)} %copy-done.2), channel_id=1, source_target_pairs={{0,2},{1,3},{2,0},{3,1},{4,6},{5,7},{6,4},{7,5},{8,10},{9,11},{10,... | collective-permute-start | bytes 393224 | tf_op jit(solution)/shard_map/ppermute | solution.py:431
  22.1 12.7 %collective-permute-start = (bf16[128,512]{1,0:T(8,128)(2,1)S(1)}, bf16[128,512]{1,0:T(8,128)(2,1)S(1)}, u32[]{:S(2)}, u32[]{:S(2)}) collective-permute-start(bf16[128,512]{1,0:T(8,128)(2,1)S(1)} %copy-done.2), channel_id=1, source_target_pairs={{0,1},{1,2},{2,3},{3,0},{4,5},{5,6},{6,7},{7,4},{8,9},{9,10},{10,1... | collective-permute-start | bytes 393224 | tf_op jit(solution)/shard_map/ppermute | solution.py:431
  44.6 20.9 %all-to-all-start.1 = ((bf16[32,7,8,128]{3,2,1,0:T(8,128)(2,1)}), bf16[32,7,8,128]{3,2,1,0:T(8,128)(2,1)S(1)}, u32[]{:S(2)}, u32[]{:S(2)}) async-start(bf16[32,7,8,128]{3,2,1,0:T(8,128)(2,1)} %shard_map.217), calls=%async_computation.1 | async-start | bytes 917504 | tf_op jit(solution)/shard_map/all_to_all | solution.py:423
  49.3 1.8 %collective-permute-start.3 = (bf16[128,512]{1,0:T(8,128)(2,1)S(1)}, bf16[128,512]{1,0:T(8,128)(2,1)S(1)}, u32[]{:S(2)}, u32[]{:S(2)}) collective-permute-start(bf16[128,512]{1,0:T(8,128)(2,1)S(1)} %copy-done.2), channel_id=1, source_target_pairs={{0,16},{16,0},{1,17},{17,1},{2,18},{18,2},{3,19},{19,3},{4,20},{20... | collective-permute-start | bytes 393224 | tf_op jit(solution)/shard_map/ppermute | solution.py:427
  50.1 1.3 %collective-permute-start.6 = (bf16[128,512]{1,0:T(8,128)(2,1)S(1)}, bf16[128,512]{1,0:T(8,128)(2,1)S(1)}, u32[]{:S(2)}, u32[]{:S(2)}) collective-permute-start(bf16[128,512]{1,0:T(8,128)(2,1)S(1)} %collective-permute-done.2.rest_2_.refs_3_), channel_id=1, source_target_pairs={{0,16},{16,0},{1,17},{17,1},{2,18},{18,2},{3,19},{19,3},{4,20},{20... | collective-permute-start | bytes 393224 | tf_op jit(solution)/shard_map/ppermute | solution.py:427
  50.2 1.4 %collective-permute-start.5 = (bf16[128,512]{1,0:T(8,128)(2,1)S(1)}, bf16[128,512]{1,0:T(8,128)(2,1)S(1)}, u32[]{:S(2)}, u32[]{:S(2)}) collective-permute-start(bf16[128,512]{1,0:T(8,128)(2,1)S(1)} %collective-permute-done.1.rest_1_.refs_2_), channel_id=1, source_target_pairs={{0,16},{16,0},{1,17},{17,1},{2,18},{18,2},{3,19},{19,3},{4,20},{20... | collective-permute-start | bytes 393224 | tf_op jit(solution)/shard_map/ppermute | solution.py:427
  50.6 1.3 %collective-permute-start.4 = (bf16[128,512]{1,0:T(8,128)(2,1)S(1)}, bf16[128,512]{1,0:T(8,128)(2,1)S(1)}, u32[]{:S(2)}, u32[]{:S(2)}) collective-permute-start(bf16[128,512]{1,0:T(8,128)(2,1)S(1)} %collective-permute-done.rest_0_.refs_1_), channel_id=1, source_target_pairs={{0,16},{16,0},{1,17},{17,1},{2,18},{18,2},{3,19},{19,3},{4,20},{20... | collective-permute-start | bytes 393224 | tf_op jit(solution)/shard_map/ppermute | solution.py:427
  66.1 4.1 %collective-permute-start.7 = (f32[32,256]{1,0:T(8,128)S(1)}, f32[32,256]{1,0:T(8,128)S(1)}, u32[]{:S(2)}, u32[]{:S(2)}) collective-permute-start(f32[32,256]{1,0:T(8,128)S(1)} %get-tuple-element.34), channel_id=1, source_target_pairs={{0,32},{32,64},{64,96},{96,0},{1,33},{33,65},{65,97},{97,1},{2,34}... | collective-permute-start | bytes 98312 | tf_op jit(solution)/shard_map/ppermute | solution.py:431
  66.2 4.3 %collective-permute-start.8 = (f32[32,256]{1,0:T(8,128)S(1)}, f32[32,256]{1,0:T(8,128)S(1)}, u32[]{:S(2)}, u32[]{:S(2)}) collective-permute-start(f32[32,256]{1,0:T(8,128)S(1)} %get-tuple-element.35), channel_id=1, source_target_pairs={{0,64},{32,96},{64,0},{96,32},{1,65},{33,97},{65,1},{97,33},{2,66}... | collective-permute-start | bytes 98312 | tf_op jit(solution)/shard_map/ppermute | solution.py:431
  67.8 3.2 %collective-permute-start.9 = (f32[32,256]{1,0:T(8,128)S(1)}, f32[32,256]{1,0:T(8,128)S(1)}, u32[]{:S(2)}, u32[]{:S(2)}) collective-permute-start(f32[32,256]{1,0:T(8,128)S(1)} %get-tuple-element.36), channel_id=1, source_target_pairs={{0,96},{32,0},{64,32},{96,64},{1,97},{33,1},{65,33},{97,65},{2,98}... | collective-permute-start | bytes 98312 | tf_op jit(solution)/shard_map/ppermute | solution.py:431
  71.7 11.2 %all-to-all-start.2 = ((bf16[8,64,128]{2,1,0:T(8,128)(2,1)}), bf16[8,64,128]{2,1,0:T(8,128)(2,1)S(1)}, u32[]{:S(2)}, u32[]{:S(2)}) async-start(bf16[8,64,128]{2,1,0:T(8,128)(2,1)} %get-tuple-element.45), calls=%async_computation.2 | async-start | bytes 262144 | tf_op jit(solution)/shard_map/all_to_all | solution.py:423
  75.1 6.2 %collective-permute-start.10 = (bf16[2,224,128]{2,1,0:T(8,128)(2,1)S(1)}, bf16[2,224,128]{2,1,0:T(8,128)(2,1)S(1)}, u32[]{:S(2)}, u32[]{:S(2)}) collective-permute-start(bf16[2,224,128]{2,1,0:T(8,128)(2,1)S(1)} %get-tuple-element.40), channel_id=1, source_target_pairs={{0,1},{1,2},{2,3},{3,0},{4,5},{5,6},{6,7},{7,4},{8,9},{9,10},{10,1... | collective-permute-start | bytes 344072 | tf_op jit(solution)/shard_map/ppermute | solution.py:431
  75.2 6.1 %collective-permute-start.11 = (bf16[2,224,128]{2,1,0:T(8,128)(2,1)S(1)}, bf16[2,224,128]{2,1,0:T(8,128)(2,1)S(1)}, u32[]{:S(2)}, u32[]{:S(2)}) collective-permute-start(bf16[2,224,128]{2,1,0:T(8,128)(2,1)S(1)} %get-tuple-element.41), channel_id=1, source_target_pairs={{0,2},{1,3},{2,0},{3,1},{4,6},{5,7},{6,4},{7,5},{8,10},{9,11},{10,... | collective-permute-start | bytes 344072 | tf_op jit(solution)/shard_map/ppermute | solution.py:431
  76.9 5.1 %collective-permute-start.12 = (bf16[2,224,128]{2,1,0:T(8,128)(2,1)S(1)}, bf16[2,224,128]{2,1,0:T(8,128)(2,1)S(1)}, u32[]{:S(2)}, u32[]{:S(2)}) collective-permute-start(bf16[2,224,128]{2,1,0:T(8,128)(2,1)S(1)} %get-tuple-element.42), channel_id=1, source_target_pairs={{0,3},{1,0},{2,1},{3,2},{4,7},{5,4},{6,5},{7,6},{8,11},{9,8},{10,9... | collective-permute-start | bytes 344072 | tf_op jit(solution)/shard_map/ppermute | solution.py:431
  83.7 13.3 %all-to-all-start.3 = ((bf16[16,64,128]{2,1,0:T(8,128)(2,1)}), bf16[16,64,128]{2,1,0:T(8,128)(2,1)S(1)}, u32[]{:S(2)}, u32[]{:S(2)}) async-start(bf16[16,64,128]{2,1,0:T(8,128)(2,1)} %shard_map.221), calls=%async_computation.3 | async-start | bytes 524288 | tf_op jit(solution)/shard_map/all_to_all | solution.py:423
  88.8 5.9 %collective-permute-start.13 = (bf16[2,224,128]{2,1,0:T(8,128)(2,1)S(1)}, bf16[2,224,128]{2,1,0:T(8,128)(2,1)S(1)}, u32[]{:S(2)}, u32[]{:S(2)}) collective-permute-start(bf16[2,224,128]{2,1,0:T(8,128)(2,1)S(1)} %get-tuple-element.32.refs_0_), channel_id=1, source_target_pairs={{0,16},{16,0},{1,17},{17,1},{2,18},{18,2},{3,19},{19,3},{4,20},{20... | collective-permute-start | bytes 344072 | tf_op jit(solution)/shard_map/ppermute | solution.py:427
  93.8 1.3 %collective-permute-start.14 = (bf16[2,224,128]{2,1,0:T(8,128)(2,1)S(1)}, bf16[2,224,128]{2,1,0:T(8,128)(2,1)S(1)}, u32[]{:S(2)}, u32[]{:S(2)}) collective-permute-start(bf16[2,224,128]{2,1,0:T(8,128)(2,1)S(1)} %collective-permute-done.10.refs_1_.refs_0_), channel_id=1, source_target_pairs={{0,16},{16,0},{1,17},{17,1},{2,18},{18,2},{3,19},{19,3},{4,20},{20... | collective-permute-start | bytes 344072 | tf_op jit(solution)/shard_map/ppermute | solution.py:427
  93.9 1.4 %collective-permute-start.15 = (bf16[2,224,128]{2,1,0:T(8,128)(2,1)S(1)}, bf16[2,224,128]{2,1,0:T(8,128)(2,1)S(1)}, u32[]{:S(2)}, u32[]{:S(2)}) collective-permute-start(bf16[2,224,128]{2,1,0:T(8,128)(2,1)S(1)} %collective-permute-done.11.refs_2_.refs_1_), channel_id=1, source_target_pairs={{0,16},{16,0},{1,17},{17,1},{2,18},{18,2},{3,19},{19,3},{4,20},{20... | collective-permute-start | bytes 344072 | tf_op jit(solution)/shard_map/ppermute | solution.py:427
  94.3 1.3 %collective-permute-start.16 = (bf16[2,224,128]{2,1,0:T(8,128)(2,1)S(1)}, bf16[2,224,128]{2,1,0:T(8,128)(2,1)S(1)}, u32[]{:S(2)}, u32[]{:S(2)}) collective-permute-start(bf16[2,224,128]{2,1,0:T(8,128)(2,1)S(1)} %collective-permute-done.12.refs_3_.refs_2_), channel_id=1, source_target_pairs={{0,16},{16,0},{1,17},{17,1},{2,18},{18,2},{3,19},{19,3},{4,20},{20... | collective-permute-start | bytes 344072 | tf_op jit(solution)/shard_map/ppermute | solution.py:427
  97.0 6.3 %collective-permute-start.17 = (bf16[16,64,128]{2,1,0:T(8,128)(2,1)S(1)}, bf16[16,64,128]{2,1,0:T(8,128)(2,1)S(1)}, u32[]{:S(2)}, u32[]{:S(2)}) collective-permute-start(bf16[16,64,128]{2,1,0:T(8,128)(2,1)S(1)} %all-to-all-done.3.own_ref), channel_id=1, source_target_pairs={{0,16},{16,0},{1,17},{17,1},{2,18},{18,2},{3,19},{19,3},{4,20},{20... | collective-permute-start | bytes 786440 | tf_op jit(solution)/shard_map/ppermute | solution.py:427
  (12 other events, 369.6 us)

commit v6 on v5

--- a/solution.py
+++ b/solution.py
@@ -18,6 +18,16 @@
     high = table.astype(np.float32).astype(jnp.bfloat16)
     low = (table - high.astype(np.float64)).astype(np.float32).astype(jnp.bfloat16)
     return high, low
+
+
+def left_table(table):
+    high, low = two_terms(table)
+    return np.concatenate([high, low, high], 1)
+
+
+def right_table(table):
+    high, low = two_terms(table)
+    return np.concatenate([high, low, high], 0)
 
 
 def transform_tables(blocks, rows):
@@ -31,12 +41,14 @@
     second = np.block([[c, -s], [s, c]])
     second_back = np.block([[c, s], [-s, c]])
     first_back = np.concatenate([np.cos(step).T, -np.sin(step).T], 1) * (2.0 / length)
-    tables = []
-    for table in (first, second, second_back, first_back):
-        tables.extend(two_terms(table))
-    tables.append(np.cos(turn).astype(np.float32))
-    tables.append(np.sin(turn).astype(np.float32))
-    return tables
+    return [
+        left_table(first),
+        right_table(second),
+        right_table(second_back),
+        left_table(first_back),
+        np.cos(turn).astype(np.float32),
+        np.sin(turn).astype(np.float32),
+    ]
 
 
 def bf16_dot(a, b):
@@ -49,14 +61,14 @@
     return high, low
 
 
-def table_left(high, low, x):
+def table_left(table, x):
     x_high, x_low = split(x)
-    return bf16_dot(high, x_high) + bf16_dot(low, x_high) + bf16_dot(high, x_low)
-
-
-def table_right(x, high, low):
+    return bf16_dot(table, jnp.concatenate([x_high, x_high, x_low], 0))
+
+
+def table_right(x, table):
     x_high, x_low = split(x)
-    return bf16_dot(x_high, high) + bf16_dot(x_high, low) + bf16_dot(x_low, high)
+    return bf16_dot(jnp.concatenate([x_high, x_high, x_low], 1), table)
 
 
 def pack_kernel(seq_ref, in_weight_ref, one_ref, two_ref, out_weight_ref, grad_ref, out_ref, both_ref, rows_ref):
@@ -102,14 +114,10 @@
 def convolve_kernel(
     in_ref,
     short_ref,
-    first_high,
-    first_low,
-    second_high,
-    second_low,
-    second_back_high,
-    second_back_low,
-    first_back_high,
-    first_back_low,
+    first_ref,
+    second_ref,
+    second_back_ref,
+    first_back_ref,
     turn_cos_ref,
     turn_sin_ref,
     *rest,
@@ -140,7 +148,7 @@
         return jnp.where(lane >= rows - distance, carried, moved)
 
     def forward(signals):
-        outer = table_left(first_high[...], first_low[...], jnp.concatenate(signals, 1))
+        outer = table_left(first_ref[...], jnp.concatenate(signals, 1))
         turned = []
         for i in range(len(signals)):
             re = outer[:blocks, i * rows : (i + 1) * rows]
@@ -150,7 +158,7 @@
                     [re * turn_cos + im * turn_sin, im * turn_cos - re * turn_sin], 1
                 )
             )
-        inner = table_right(jnp.concatenate(turned, 0), second_high[...], second_low[...])
+        inner = table_right(jnp.concatenate(turned, 0), second_ref[...])
         return [
             (inner[i * blocks : (i + 1) * blocks, :rows], inner[i * blocks : (i + 1) * blocks, rows:])
             for i in range(len(signals))
@@ -158,7 +166,7 @@
 
     def backward(spectra):
         stacked = jnp.concatenate([jnp.concatenate(pair, 1) for pair in spectra], 0)
-        inner = table_right(stacked, second_back_high[...], second_back_low[...])
+        inner = table_right(stacked, second_back_ref[...])
         turned = []
         for i in range(len(spectra)):
             re = inner[i * blocks : (i + 1) * blocks, :rows]
@@ -168,7 +176,7 @@
                     [re * turn_cos - im * turn_sin, im * turn_cos + re * turn_sin], 0
                 )
             )
-        outer = table_left(first_back_high[...], first_back_low[...], jnp.concatenate(turned, 1))
+        outer = table_left(first_back_ref[...], jnp.concatenate(turned, 1))
         return [outer[:, i * rows : (i + 1) * rows] for i in range(len(spectra))]
 
     def times(a, b):
@@ -373,7 +381,7 @@
 
 
 def add_z_kernel(scale, in_ref, *refs):
-    out_ref = refs[-1]
+    out_ref = refs[3]
     total = jnp.sum(in_ref[...].astype(jnp.float32), axis=0) * scale
     out_ref[...] = jnp.broadcast_to(total.astype(jnp.bfloat16)[None], out_ref.shape)
 
@@ -469,13 +477,16 @@
         out_specs=specs(pltpu.VMEM, *[pl.ANY] * 3),
         input_output_aliases={4: 1, 5: 2, 6: 3},
     )(*part, *leaving)
-    arrived = [found[4]] + [ring(x, "y", 1 + i) for i, x in enumerate(leaving)]
+    near = [ring(leaving[0], "y", 1), ring(leaving[2], "y", 3)]
     part = exchange(part, ("zh", "zl"))
-    part = call(
+    part, far = call(
         functools.partial(add_z_kernel, scale),
-        shape((16, 64, rows), bf16),
+        (shape((16, 64, rows), bf16), shape(leaving[1].shape, bf16)),
         in_specs=specs(pltpu.VMEM, *[pl.ANY] * 3),
-    )(part, *arrived[1:])
+        out_specs=specs(pltpu.VMEM, pl.ANY),
+        input_output_aliases={3: 1},
+    )(part, *near, leaving[1])
+    arrived = [found[4], near[0], ring(far, "y", 2), near[1]]
     arrived += [swap_core(x) for x in arrived]
     part = exchange(part, ("x", "y"))
     outputs, grad_inputs, grad_short, grad_one, grad_two = call(

time: 105 us -> 105 us (level)
    ppermute x9, starting transfers between devices: 10.3 us -> 12.9 us  [ring(): return lax.ppermute(x, axis, [(i, (i + distance) % 4) for i in range(4)])]
    all_to_all x4, waiting for transfers between devices: 19.4 us -> 21.2 us  [exchange(): return lax.all_to_all(x, axes, split_axis=0, concat_axis=0, tiled=True)]
    ppermute x9, waiting for transfers between devices: 17.6 us -> 16 us  [ring(): return lax.ppermute(x, axis, [(i, (i + distance) % 4) for i in range(4)])]
    ppermute x9, starting transfers between devices: 12.1 us -> 10.6 us  [swap_core(): return lax.ppermute(x, 'core', [(0, 1), (1, 0)])]
  transfers between devices with their start and end apart: 22 -> 22, of which waited for: 20 -> 16; matrix products, arithmetic and copies ran while one was open for 0% -> 0% of each run, Pallas kernels for 1% -> 1%
where the time goes in v6:
time: 105 us
  starting transfers between devices  52 us (50%)
  waiting for transfers between devices  40.6 us (39%)
  Pallas kernels  11.5 us (11%)
    all_to_all x4, starting transfers between devices, exchange(): return lax.all_to_all(x, axes, split_axis=0, concat_axis=0, tiled=True)  28.4 us
    all_to_all x4, waiting for transfers between devices, exchange(): return lax.all_to_all(x, axes, split_axis=0, concat_axis=0, tiled=True)  21.2 us
    ppermute x9, waiting for transfers between devices, ring(): return lax.ppermute(x, axis, [(i, (i + distance) % 4) for i in range(4)])  16 us
    ppermute x9, starting transfers between devices, ring(): return lax.ppermute(x, axis, [(i, (i + distance) % 4) for i in range(4)])  12.9 us
    ppermute x9, starting transfers between devices, swap_core(): return lax.ppermute(x, 'core', [(0, 1), (1, 0)])  10.6 us
    pallas_call x1, Pallas kernels, per_device(): call(convolve_kernel, shape((32, 7, 8, rows), bf16), [pltpu.VMEM((devices...  4.47 us
    ppermute x9, waiting for transfers between devices, swap_core(): return lax.ppermute(x, 'core', [(0, 1), (1, 0)])  3.38 us
    pallas_call x1, Pallas kernels, per_device(): call(pack_kernel, (shape((width, 8, rows), bf16), shape((rows, 2 * width)...  2.41 us
  transfers between devices with their start and end apart: 22, of which 16 were waited for; matrix products, arithmetic and copies ran while one was open for 0% of the time, Pallas kernels for 1%

profile of v6, /device:TPU:1, one launch (start us, length us, event | category | flops | bytes accessed | tf_op | source)
XLA Modules:
  0.0 104.9 jit_solution(1054630271477763851)
XLA Ops:
  0.7 2.4 %shard_map.180 = (bf16[256,8,128]{2,1,0:T(8,128)(2,1)}, bf16[128,512]{1,0:T(8,128)(2,1)}) custom-call(bf16[1,128,256]{2,1,0:T(8,128)(2,1)} %seq_ref.1, bf16[256,768]{1,0:T(8,128)(2,1)} %refs_8_.1, f32[128,256]{1,0:T(8,128)} %one_ref.1, f32[128,256]{1,0:T(8,128)} %two_ref.1, bf16[256,256]{1,0:T(8,128)(2,1)} %refs_9_.1, bf16[1,128,256]{2,1,0:T(8,128)(2,1)} %grad_ref.1), custom_call_target="tpu_custom_call" | custom-call | tf_op jit(solution)/shard_map/pallas_call | solution.py:449
  3.1 15.7 %all-to-all-start = ((bf16[256,8,128]{2,1,0:T(8,128)(2,1)}), bf16[256,8,128]{2,1,0:T(8,128)(2,1)S(1)}, u32[]{:S(2)}, u32[]{:S(2)}) async-start(bf16[256,8,128]{2,1,0:T(8,128)(2,1)} %get-tuple-element.32), calls=%async_computation | async-start | bytes 1048576 | tf_op jit(solution)/shard_map/all_to_all | solution.py:431
  18.8 2.7 %collective-permute-start.2 = (bf16[128,512]{1,0:T(8,128)(2,1)}, bf16[128,512]{1,0:T(8,128)(2,1)S(1)}, u32[]{:S(2)}, u32[]{:S(2)}) collective-permute-start(bf16[128,512]{1,0:T(8,128)(2,1)} %get-tuple-element.33.refs_0_), channel_id=1, source_target_pairs={{0,3},{1,0},{2,1},{3,2},{4,7},{5,4},{6,5},{7,6},{8,11},{9,8},{10,9... | collective-permute-start | bytes 393224 | tf_op jit(solution)/shard_map/ppermute | solution.py:439
  22.6 5.5 %collective-permute-done.2.rest_2_.refs_3_ = bf16[128,512]{1,0:T(8,128)(2,1)S(1)} collective-permute-done((bf16[128,512]{1,0:T(8,128)(2,1)}, bf16[128,512]{1,0:T(8,128)(2,1)S(1)}, u32[]{:S(2)}, u32[]{:S(2)}) %collective-permute-start.2) | collective-permute-done | bytes 131104 | tf_op jit(solution)/shard_map/ppermute | solution.py:439
  28.1 0.9 collective-permute-done.1.rest_1_.refs_2_
  29.0 6.0 %collective-permute-done.rest_0_.refs_1_ = bf16[128,512]{1,0:T(8,128)(2,1)S(1)} collective-permute-done((bf16[128,512]{1,0:T(8,128)(2,1)}, bf16[128,512]{1,0:T(8,128)(2,1)S(1)}, u32[]{:S(2)}, u32[]{:S(2)}) %collective-permute-start) | collective-permute-done | bytes 131104 | tf_op jit(solution)/shard_map/ppermute | solution.py:439
  35.0 4.7 %all-to-all-done.in_ref = bf16[256,8,128]{2,1,0:T(8,128)(2,1)S(1)} async-done(((bf16[256,8,128]{2,1,0:T(8,128)(2,1)}), bf16[256,8,128]{2,1,0:T(8,128)(2,1)S(1)}, u32[]{:S(2)}, u32[]{:S(2)}) %all-to-all-start) | async-done | bytes 524320 | tf_op jit(solution)/shard_map/all_to_all | solution.py:431
  39.7 4.5 %shard_map.181 = bf16[32,7,8,128]{3,2,1,0:T(8,128)(2,1)} custom-call(bf16[256,8,128]{2,1,0:T(8,128)(2,1)S(1)} %all-to-all-done.in_ref, f32[3,768]{1,0:T(4,128)S(1)} %copy-done.9, bf16[256,384]{1,0:T(8,128)(2,1)S(1)} %copy-done.5, bf16[768,256]{1,0:T(8,128)(2,1)S(1)} %copy-done.3, bf16[768,256]{1,0:T(8,128)(2,1)S(1)} %copy-done.2, ...), custom_call_target="tpu_custom_call" | custom-call | tf_op jit(solution)/shard_map/pallas_call | solution.py:459
  44.2 4.9 %all-to-all-start.1 = ((bf16[32,7,8,128]{3,2,1,0:T(8,128)(2,1)}), bf16[32,7,8,128]{3,2,1,0:T(8,128)(2,1)S(1)}, u32[]{:S(2)}, u32[]{:S(2)}) async-start(bf16[32,7,8,128]{3,2,1,0:T(8,128)(2,1)} %shard_map.181), calls=%async_computation.1 | async-start | bytes 917504 | tf_op jit(solution)/shard_map/all_to_all | solution.py:431
  51.7 13.5 %all-to-all-done.1.in_ref = bf16[32,7,8,128]{3,2,1,0:T(8,128)(2,1)S(1)} async-done(((bf16[32,7,8,128]{3,2,1,0:T(8,128)(2,1)}), bf16[32,7,8,128]{3,2,1,0:T(8,128)(2,1)S(1)}, u32[]{:S(2)}, u32[]{:S(2)}) %all-to-all-start.1) | async-done | bytes 458784 | tf_op jit(solution)/shard_map/all_to_all | solution.py:431
  65.9 1.7 %collective-permute-start.8 = (f32[32,256]{1,0:T(8,128)S(1)}, f32[32,256]{1,0:T(8,128)S(1)}, u32[]{:S(2)}, u32[]{:S(2)}) collective-permute-start(f32[32,256]{1,0:T(8,128)S(1)} %get-tuple-element.37), channel_id=1, source_target_pairs={{0,64},{32,96},{64,0},{96,32},{1,65},{33,97},{65,1},{97,33},{2,66}... | collective-permute-start | bytes 98312 | tf_op jit(solution)/shard_map/ppermute | solution.py:439
  67.7 1.6 %collective-permute-start.9 = (f32[32,256]{1,0:T(8,128)S(1)}, f32[32,256]{1,0:T(8,128)S(1)}, u32[]{:S(2)}, u32[]{:S(2)}) collective-permute-start(f32[32,256]{1,0:T(8,128)S(1)} %get-tuple-element.38), channel_id=1, source_target_pairs={{0,96},{32,0},{64,32},{96,64},{1,97},{33,1},{65,33},{97,65},{2,98}... | collective-permute-start | bytes 98312 | tf_op jit(solution)/shard_map/ppermute | solution.py:439
  71.5 3.6 %all-to-all-start.2 = ((bf16[8,64,128]{2,1,0:T(8,128)(2,1)}), bf16[8,64,128]{2,1,0:T(8,128)(2,1)S(1)}, u32[]{:S(2)}, u32[]{:S(2)}) async-start(bf16[8,64,128]{2,1,0:T(8,128)(2,1)} %get-tuple-element.43), calls=%async_computation.2 | async-start | bytes 262144 | tf_op jit(solution)/shard_map/all_to_all | solution.py:431
  75.1 2.7 %collective-permute-start.11 = (bf16[2,224,128]{2,1,0:T(8,128)(2,1)S(1)}, bf16[2,224,128]{2,1,0:T(8,128)(2,1)S(1)}, u32[]{:S(2)}, u32[]{:S(2)}) collective-permute-start(bf16[2,224,128]{2,1,0:T(8,128)(2,1)S(1)} %get-tuple-element.44), channel_id=1, source_target_pairs={{0,3},{1,0},{2,1},{3,2},{4,7},{5,4},{6,5},{7,6},{8,11},{9,8},{10,9... | collective-permute-start | bytes 344072 | tf_op jit(solution)/shard_map/ppermute | solution.py:439
  77.8 2.2 %collective-permute-done.10.refs_0_.refs_1_ = bf16[2,224,128]{2,1,0:T(8,128)(2,1)S(1)} collective-permute-done((bf16[2,224,128]{2,1,0:T(8,128)(2,1)S(1)}, bf16[2,224,128]{2,1,0:T(8,128)(2,1)S(1)}, u32[]{:S(2)}, u32[]{:S(2)}) %collective-permute-start.10) | collective-permute-done | bytes 114720 | tf_op jit(solution)/shard_map/ppermute | solution.py:439
  80.0 2.9 %all-to-all-done.2.in_ref = bf16[8,64,128]{2,1,0:T(8,128)(2,1)S(1)} async-done(((bf16[8,64,128]{2,1,0:T(8,128)(2,1)}), bf16[8,64,128]{2,1,0:T(8,128)(2,1)S(1)}, u32[]{:S(2)}, u32[]{:S(2)}) %all-to-all-start.2) | async-done | bytes 131104 | tf_op jit(solution)/shard_map/all_to_all | solution.py:431
  83.6 4.4 %all-to-all-start.3 = ((bf16[16,64,128]{2,1,0:T(8,128)(2,1)}), bf16[16,64,128]{2,1,0:T(8,128)(2,1)S(1)}, u32[]{:S(2)}, u32[]{:S(2)}) async-start(bf16[16,64,128]{2,1,0:T(8,128)(2,1)} %get-tuple-element.49), calls=%async_computation.3 | async-start | bytes 524288 | tf_op jit(solution)/shard_map/all_to_all | solution.py:431
  88.0 2.9 %collective-permute-start.12 = (bf16[2,224,128]{2,1,0:T(8,128)(2,1)S(1)}, bf16[2,224,128]{2,1,0:T(8,128)(2,1)S(1)}, u32[]{:S(2)}, u32[]{:S(2)}) collective-permute-start(bf16[2,224,128]{2,1,0:T(8,128)(2,1)S(1)} %get-tuple-element.46), channel_id=1, source_target_pairs={{0,2},{1,3},{2,0},{3,1},{4,6},{5,7},{6,4},{7,5},{8,10},{9,11},{10,... | collective-permute-start | bytes 344072 | tf_op jit(solution)/shard_map/ppermute | solution.py:439
  90.9 5.2 %collective-permute-start.13 = (bf16[2,224,128]{2,1,0:T(8,128)(2,1)S(1)}, bf16[2,224,128]{2,1,0:T(8,128)(2,1)S(1)}, u32[]{:S(2)}, u32[]{:S(2)}) collective-permute-start(bf16[2,224,128]{2,1,0:T(8,128)(2,1)S(1)} %get-tuple-element.34.refs_0_), channel_id=1, source_target_pairs={{0,16},{16,0},{1,17},{17,1},{2,18},{18,2},{3,19},{19,3},{4,20},{20... | collective-permute-start | bytes 344072 | tf_op jit(solution)/shard_map/ppermute | solution.py:435
  96.6 3.1 %collective-permute-start.15 = (bf16[2,224,128]{2,1,0:T(8,128)(2,1)S(1)}, bf16[2,224,128]{2,1,0:T(8,128)(2,1)S(1)}, u32[]{:S(2)}, u32[]{:S(2)}) collective-permute-start(bf16[2,224,128]{2,1,0:T(8,128)(2,1)S(1)} %collective-permute-done.12.refs_2_), channel_id=1, source_target_pairs={{0,16},{16,0},{1,17},{17,1},{2,18},{18,2},{3,19},{19,3},{4,20},{20... | collective-permute-start | bytes 344072 | tf_op jit(solution)/shard_map/ppermute | solution.py:435
  99.7 1.0 collective-permute-done.15.refs_6_
  100.6 1.4 %shard_map.185 = (bf16[1,128,256]{2,1,0:T(8,128)(2,1)}, bf16[1,128,256]{2,1,0:T(8,128)(2,1)}, f32[3,768]{1,0:T(4,128)}, f32[128,256]{1,0:T(8,128)}, f32[128,256]{1,0:T(8,128)}) custom-call(bf16[2,224,128]{2,1,0:T(8,128)(2,1)S(1)} %get-tuple-element.34.refs_0_, bf16[2,224,128]{2,1,0:T(8,128)(2,1)S(1)} %collective-permute-done.10.refs_0_.refs_1_, ...), custom_call_target="tpu_custom_call" | custom-call | tf_op jit(solution)/shard_map/pallas_call | solution.py:492
  102.4 1.2 %collective-permute-done.17.other_ref = bf16[16,64,128]{2,1,0:T(8,128)(2,1)S(1)} collective-permute-done((bf16[16,64,128]{2,1,0:T(8,128)(2,1)S(1)}, bf16[16,64,128]{2,1,0:T(8,128)(2,1)S(1)}, u32[]{:S(2)}, u32[]{:S(2)}) %collective-permute-start.17) | collective-permute-done | bytes 262176 | tf_op jit(solution)/shard_map/ppermute | solution.py:435
  103.5 1.3 %shard_map.186 = (f32[256,768]{1,0:T(8,128)}, f32[256,256]{1,0:T(8,128)}) custom-call(bf16[16,64,128]{2,1,0:T(8,128)(2,1)S(1)} %all-to-all-done.3.own_ref, bf16[16,64,128]{2,1,0:T(8,128)(2,1)S(1)} %collective-permute-done.17.other_ref), custom_call_target="tpu_custom_call" | custom-call | tf_op jit(solution)/shard_map/pallas_call | solution.py:503
  (47 shorter events, 8.4 us)
Async XLA Ops:
  0.6 39.0 %copy-start.5 = (bf16[256,384]{1,0:T(8,128)(2,1)S(1)}, bf16[256,384]{1,0:T(8,128)(2,1)}, u32[]{:S(2)}) copy-start(bf16[256,384]{1,0:T(8,128)(2,1)} %constant.12.clone.first_ref) | copy-start | bytes 589828
  0.6 39.0 %copy-start.8 = (f32[128,128]{1,0:T(8,128)S(1)}, f32[128,128]{1,0:T(8,128)}, u32[]{:S(2)}) copy-start(f32[128,128]{1,0:T(8,128)} %constant.16.clone.turn_cos_ref) | copy-start | bytes 196612
  3.1 36.6 %all-to-all-start = ((bf16[256,8,128]{2,1,0:T(8,128)(2,1)}), bf16[256,8,128]{2,1,0:T(8,128)(2,1)S(1)}, u32[]{:S(2)}, u32[]{:S(2)}) async-start(bf16[256,8,128]{2,1,0:T(8,128)(2,1)} %get-tuple-element.32), calls=%async_computation | async-start | bytes 1048576 | tf_op jit(solution)/shard_map/all_to_all | solution.py:431
  18.8 9.3 %collective-permute-start.2 = (bf16[128,512]{1,0:T(8,128)(2,1)}, bf16[128,512]{1,0:T(8,128)(2,1)S(1)}, u32[]{:S(2)}, u32[]{:S(2)}) collective-permute-start(bf16[128,512]{1,0:T(8,128)(2,1)} %get-tuple-element.33.refs_0_), channel_id=1, source_target_pairs={{0,3},{1,0},{2,1},{3,2},{4,7},{5,4},{6,5},{7,6},{8,11},{9,8},{10,9... | collective-permute-start | bytes 393224 | tf_op jit(solution)/shard_map/ppermute | solution.py:439
  21.5 7.5 %collective-permute-start.1 = (bf16[128,512]{1,0:T(8,128)(2,1)}, bf16[128,512]{1,0:T(8,128)(2,1)S(1)}, u32[]{:S(2)}, u32[]{:S(2)}) collective-permute-start(bf16[128,512]{1,0:T(8,128)(2,1)} %get-tuple-element.33.refs_0_), channel_id=1, source_target_pairs={{0,2},{1,3},{2,0},{3,1},{4,6},{5,7},{6,4},{7,5},{8,10},{9,11},{10,... | collective-permute-start | bytes 393224 | tf_op jit(solution)/shard_map/ppermute | solution.py:439
  22.0 12.9 %collective-permute-start = (bf16[128,512]{1,0:T(8,128)(2,1)}, bf16[128,512]{1,0:T(8,128)(2,1)S(1)}, u32[]{:S(2)}, u32[]{:S(2)}) collective-permute-start(bf16[128,512]{1,0:T(8,128)(2,1)} %get-tuple-element.33.refs_0_), channel_id=1, source_target_pairs={{0,1},{1,2},{2,3},{3,0},{4,5},{5,6},{6,7},{7,4},{8,9},{9,10},{10,1... | collective-permute-start | bytes 393224 | tf_op jit(solution)/shard_map/ppermute | solution.py:439
  44.2 21.1 %all-to-all-start.1 = ((bf16[32,7,8,128]{3,2,1,0:T(8,128)(2,1)}), bf16[32,7,8,128]{3,2,1,0:T(8,128)(2,1)S(1)}, u32[]{:S(2)}, u32[]{:S(2)}) async-start(bf16[32,7,8,128]{3,2,1,0:T(8,128)(2,1)} %shard_map.181), calls=%async_computation.1 | async-start | bytes 917504 | tf_op jit(solution)/shard_map/all_to_all | solution.py:431
  49.1 1.8 %collective-permute-start.3 = (bf16[128,512]{1,0:T(8,128)(2,1)S(1)}, bf16[128,512]{1,0:T(8,128)(2,1)S(1)}, u32[]{:S(2)}, u32[]{:S(2)}) collective-permute-start(bf16[128,512]{1,0:T(8,128)(2,1)S(1)} %copy-done.6), channel_id=1, source_target_pairs={{0,16},{16,0},{1,17},{17,1},{2,18},{18,2},{3,19},{19,3},{4,20},{20... | collective-permute-start | bytes 393224 | tf_op jit(solution)/shard_map/ppermute | solution.py:435
  49.9 1.3 %collective-permute-start.6 = (bf16[128,512]{1,0:T(8,128)(2,1)S(1)}, bf16[128,512]{1,0:T(8,128)(2,1)S(1)}, u32[]{:S(2)}, u32[]{:S(2)}) collective-permute-start(bf16[128,512]{1,0:T(8,128)(2,1)S(1)} %collective-permute-done.2.rest_2_.refs_3_), channel_id=1, source_target_pairs={{0,16},{16,0},{1,17},{17,1},{2,18},{18,2},{3,19},{19,3},{4,20},{20... | collective-permute-start | bytes 393224 | tf_op jit(solution)/shard_map/ppermute | solution.py:435
  50.0 1.4 %collective-permute-start.5 = (bf16[128,512]{1,0:T(8,128)(2,1)S(1)}, bf16[128,512]{1,0:T(8,128)(2,1)S(1)}, u32[]{:S(2)}, u32[]{:S(2)}) collective-permute-start(bf16[128,512]{1,0:T(8,128)(2,1)S(1)} %collective-permute-done.1.rest_1_.refs_2_), channel_id=1, source_target_pairs={{0,16},{16,0},{1,17},{17,1},{2,18},{18,2},{3,19},{19,3},{4,20},{20... | collective-permute-start | bytes 393224 | tf_op jit(solution)/shard_map/ppermute | solution.py:435
  50.4 1.3 %collective-permute-start.4 = (bf16[128,512]{1,0:T(8,128)(2,1)S(1)}, bf16[128,512]{1,0:T(8,128)(2,1)S(1)}, u32[]{:S(2)}, u32[]{:S(2)}) collective-permute-start(bf16[128,512]{1,0:T(8,128)(2,1)S(1)} %collective-permute-done.rest_0_.refs_1_), channel_id=1, source_target_pairs={{0,16},{16,0},{1,17},{17,1},{2,18},{18,2},{3,19},{19,3},{4,20},{20... | collective-permute-start | bytes 393224 | tf_op jit(solution)/shard_map/ppermute | solution.py:435
  65.8 4.1 %collective-permute-start.7 = (f32[32,256]{1,0:T(8,128)S(1)}, f32[32,256]{1,0:T(8,128)S(1)}, u32[]{:S(2)}, u32[]{:S(2)}) collective-permute-start(f32[32,256]{1,0:T(8,128)S(1)} %get-tuple-element.36), channel_id=1, source_target_pairs={{0,32},{32,64},{64,96},{96,0},{1,33},{33,65},{65,97},{97,1},{2,34}... | collective-permute-start | bytes 98312 | tf_op jit(solution)/shard_map/ppermute | solution.py:439
  65.9 4.3 %collective-permute-start.8 = (f32[32,256]{1,0:T(8,128)S(1)}, f32[32,256]{1,0:T(8,128)S(1)}, u32[]{:S(2)}, u32[]{:S(2)}) collective-permute-start(f32[32,256]{1,0:T(8,128)S(1)} %get-tuple-element.37), channel_id=1, source_target_pairs={{0,64},{32,96},{64,0},{96,32},{1,65},{33,97},{65,1},{97,33},{2,66}... | collective-permute-start | bytes 98312 | tf_op jit(solution)/shard_map/ppermute | solution.py:439
  67.7 3.1 %collective-permute-start.9 = (f32[32,256]{1,0:T(8,128)S(1)}, f32[32,256]{1,0:T(8,128)S(1)}, u32[]{:S(2)}, u32[]{:S(2)}) collective-permute-start(f32[32,256]{1,0:T(8,128)S(1)} %get-tuple-element.38), channel_id=1, source_target_pairs={{0,96},{32,0},{64,32},{96,64},{1,97},{33,1},{65,33},{97,65},{2,98}... | collective-permute-start | bytes 98312 | tf_op jit(solution)/shard_map/ppermute | solution.py:439
  71.5 11.4 %all-to-all-start.2 = ((bf16[8,64,128]{2,1,0:T(8,128)(2,1)}), bf16[8,64,128]{2,1,0:T(8,128)(2,1)S(1)}, u32[]{:S(2)}, u32[]{:S(2)}) async-start(bf16[8,64,128]{2,1,0:T(8,128)(2,1)} %get-tuple-element.43), calls=%async_computation.2 | async-start | bytes 262144 | tf_op jit(solution)/shard_map/all_to_all | solution.py:431
  75.0 4.9 %collective-permute-start.10 = (bf16[2,224,128]{2,1,0:T(8,128)(2,1)S(1)}, bf16[2,224,128]{2,1,0:T(8,128)(2,1)S(1)}, u32[]{:S(2)}, u32[]{:S(2)}) collective-permute-start(bf16[2,224,128]{2,1,0:T(8,128)(2,1)S(1)} %get-tuple-element.42), channel_id=1, source_target_pairs={{0,1},{1,2},{2,3},{3,0},{4,5},{5,6},{6,7},{7,4},{8,9},{9,10},{10,1... | collective-permute-start | bytes 344072 | tf_op jit(solution)/shard_map/ppermute | solution.py:439
  75.1 4.8 %collective-permute-start.11 = (bf16[2,224,128]{2,1,0:T(8,128)(2,1)S(1)}, bf16[2,224,128]{2,1,0:T(8,128)(2,1)S(1)}, u32[]{:S(2)}, u32[]{:S(2)}) collective-permute-start(bf16[2,224,128]{2,1,0:T(8,128)(2,1)S(1)} %get-tuple-element.44), channel_id=1, source_target_pairs={{0,3},{1,0},{2,1},{3,2},{4,7},{5,4},{6,5},{7,6},{8,11},{9,8},{10,9... | collective-permute-start | bytes 344072 | tf_op jit(solution)/shard_map/ppermute | solution.py:439
  83.6 18.4 %all-to-all-start.3 = ((bf16[16,64,128]{2,1,0:T(8,128)(2,1)}), bf16[16,64,128]{2,1,0:T(8,128)(2,1)S(1)}, u32[]{:S(2)}, u32[]{:S(2)}) async-start(bf16[16,64,128]{2,1,0:T(8,128)(2,1)} %get-tuple-element.49), calls=%async_computation.3 | async-start | bytes 524288 | tf_op jit(solution)/shard_map/all_to_all | solution.py:431
  88.0 8.6 %collective-permute-start.12 = (bf16[2,224,128]{2,1,0:T(8,128)(2,1)S(1)}, bf16[2,224,128]{2,1,0:T(8,128)(2,1)S(1)}, u32[]{:S(2)}, u32[]{:S(2)}) collective-permute-start(bf16[2,224,128]{2,1,0:T(8,128)(2,1)S(1)} %get-tuple-element.46), channel_id=1, source_target_pairs={{0,2},{1,3},{2,0},{3,1},{4,6},{5,7},{6,4},{7,5},{8,10},{9,11},{10,... | collective-permute-start | bytes 344072 | tf_op jit(solution)/shard_map/ppermute | solution.py:439
  90.9 8.8 %collective-permute-start.13 = (bf16[2,224,128]{2,1,0:T(8,128)(2,1)S(1)}, bf16[2,224,128]{2,1,0:T(8,128)(2,1)S(1)}, u32[]{:S(2)}, u32[]{:S(2)}) collective-permute-start(bf16[2,224,128]{2,1,0:T(8,128)(2,1)S(1)} %get-tuple-element.34.refs_0_), channel_id=1, source_target_pairs={{0,16},{16,0},{1,17},{17,1},{2,18},{18,2},{3,19},{19,3},{4,20},{20... | collective-permute-start | bytes 344072 | tf_op jit(solution)/shard_map/ppermute | solution.py:435
  96.1 3.6 %collective-permute-start.14 = (bf16[2,224,128]{2,1,0:T(8,128)(2,1)S(1)}, bf16[2,224,128]{2,1,0:T(8,128)(2,1)S(1)}, u32[]{:S(2)}, u32[]{:S(2)}) collective-permute-start(bf16[2,224,128]{2,1,0:T(8,128)(2,1)S(1)} %collective-permute-done.10.refs_0_.refs_1_), channel_id=1, source_target_pairs={{0,16},{16,0},{1,17},{17,1},{2,18},{18,2},{3,19},{19,3},{4,20},{20... | collective-permute-start | bytes 344072 | tf_op jit(solution)/shard_map/ppermute | solution.py:435
  96.1 3.6 %collective-permute-start.16 = (bf16[2,224,128]{2,1,0:T(8,128)(2,1)S(1)}, bf16[2,224,128]{2,1,0:T(8,128)(2,1)S(1)}, u32[]{:S(2)}, u32[]{:S(2)}) collective-permute-start(bf16[2,224,128]{2,1,0:T(8,128)(2,1)S(1)} %collective-permute-done.11.refs_1_.refs_3_), channel_id=1, source_target_pairs={{0,16},{16,0},{1,17},{17,1},{2,18},{18,2},{3,19},{19,3},{4,20},{20... | collective-permute-start | bytes 344072 | tf_op jit(solution)/shard_map/ppermute | solution.py:435
  96.6 4.0 %collective-permute-start.15 = (bf16[2,224,128]{2,1,0:T(8,128)(2,1)S(1)}, bf16[2,224,128]{2,1,0:T(8,128)(2,1)S(1)}, u32[]{:S(2)}, u32[]{:S(2)}) collective-permute-start(bf16[2,224,128]{2,1,0:T(8,128)(2,1)S(1)} %collective-permute-done.12.refs_2_), channel_id=1, source_target_pairs={{0,16},{16,0},{1,17},{17,1},{2,18},{18,2},{3,19},{19,3},{4,20},{20... | collective-permute-start | bytes 344072 | tf_op jit(solution)/shard_map/ppermute | solution.py:435
  102.0 1.5 %collective-permute-start.17 = (bf16[16,64,128]{2,1,0:T(8,128)(2,1)S(1)}, bf16[16,64,128]{2,1,0:T(8,128)(2,1)S(1)}, u32[]{:S(2)}, u32[]{:S(2)}) collective-permute-start(bf16[16,64,128]{2,1,0:T(8,128)(2,1)S(1)} %all-to-all-done.3.own_ref), channel_id=1, source_target_pairs={{0,16},{16,0},{1,17},{17,1},{2,18},{18,2},{3,19},{19,3},{4,20},{20... | collective-permute-start | bytes 786440 | tf_op jit(solution)/shard_map/ppermute | solution.py:435
  (8 other events, 225.1 us)

commit v7 on v6

--- a/solution.py
+++ b/solution.py
@@ -73,42 +73,36 @@
 
 def pack_kernel(seq_ref, in_weight_ref, one_ref, two_ref, out_weight_ref, grad_ref, out_ref, both_ref, rows_ref):
     width = out_weight_ref.shape[0]
-    slots = rows_ref.shape[0] // width
+    lanes = rows_ref.shape[2]
     contract_first = (((0,), (1,)), ((), ()))
     contract_last = (((1,), (1,)), ((), ()))
     seq = seq_ref[0]
 
     def put(index, x):
-        rows_ref[pl.ds(index, width, stride=slots), :] = x
-
-    def put_two(index, x):
-        high = x.astype(jnp.bfloat16).astype(jnp.float32)
-        put(index, high)
-        put(index + 1, x - high)
-
-    projected = [
-        lax.dot_general(
-            in_weight_ref[:, group * width : (group + 1) * width],
-            seq,
-            contract_first,
-            preferred_element_type=jnp.float32,
-        )
-        for group in range(3)
-    ]
-    put(0, projected[0])
-    put_two(1, projected[1])
-    put_two(3, projected[2])
+        rows_ref[index // 2, pl.ds(index % 2, width, stride=2), :] = x
+
+    for group in range(3):
+        weight = in_weight_ref[:, group * width : (group + 1) * width]
+        put(
+            group,
+            lax.dot_general(weight, seq, contract_first, preferred_element_type=jnp.float32),
+        )
     put(
-        5,
+        3,
         lax.dot_general(
             out_weight_ref[...], grad_ref[0], contract_last, preferred_element_type=jnp.float32
         ),
     )
-    chosen = jnp.where(lax.axis_index("zh") == 0, one_ref[...], two_ref[...])
-    put_two(6, chosen.T)
+    chosen = jnp.where(lax.axis_index("zh") == 0, one_ref[...], two_ref[...]).T
+    high = chosen.astype(jnp.bfloat16).astype(jnp.float32)
+    put(4, high)
+    put(5, chosen - high)
     both_ref[:, :width] = seq
     both_ref[:, width:] = grad_ref[0]
-    out_ref[...] = rows_ref[...].reshape(out_ref.shape).astype(jnp.bfloat16)
+    for pair in range(3):
+        out_ref[:, :, pair * lanes : (pair + 1) * lanes] = (
+            rows_ref[pair].reshape(width, 2, lanes).astype(jnp.bfloat16)
+        )
 
 
 def convolve_kernel(
@@ -123,7 +117,7 @@
     *rest,
 ):
     out_ref, rows_ref = rest[-2:]
-    sources, slots, rows = in_ref.shape
+    sources, rows = in_ref.shape[0], in_ref.shape[2] // 3
     blocks = sources // 2
     width = short_ref.shape[1] // 3
     scale = 1.0 / math.sqrt(sources * rows)
@@ -132,10 +126,15 @@
     lane = lax.broadcasted_iota(jnp.int32, (blocks, rows), 1)
     block = lax.broadcasted_iota(jnp.int32, (blocks, rows), 0)
 
-    rows_ref[...] = in_ref[...].astype(jnp.float32).reshape(sources * slots, rows)
+    for pair in range(3):
+        rows_ref[pair] = (
+            in_ref[:, :, pair * rows : (pair + 1) * rows]
+            .astype(jnp.float32)
+            .reshape(sources * 2, rows)
+        )
 
     def row(member, index):
-        return rows_ref[pl.ds(member * blocks * slots + index, blocks, stride=slots), :]
+        return rows_ref[index // 2, pl.ds(member * sources + index % 2, blocks, stride=2), :]
 
     def later(x, distance):
         moved = pltpu.roll(x, distance, 1)
@@ -200,11 +199,7 @@
 
     projected, lagged_one, lagged_two, mixed, pre = [], [], [], [], []
     for member in range(2):
-        now = [
-            row(member, 0),
-            row(member, 1) + row(member, 2),
-            row(member, 3) + row(member, 4),
-        ]
+        now = [row(member, group) for group in range(3)]
         one = [later(x, 1) for x in now]
         two = [later(x, 2) for x in now]
         projected.append(now)
@@ -216,11 +211,11 @@
                 for g in range(3)
             ]
         )
-        pre.append(row(member, 5))
+        pre.append(row(member, 3))
     members = range(2)
     grad_conv_two = [pre[m] * mixed[m][2] for m in members]
     spectra = forward(
-        [row(m, 6) + row(m, 7) for m in members] + [mixed[m][0] for m in members] + grad_conv_two
+        [row(m, 4) + row(m, 5) for m in members] + [mixed[m][0] for m in members] + grad_conv_two
     )
     one_spec, two_spec = spectra[0], spectra[1]
     value_spec, conv_two_spec = spectra[2:4], spectra[4:6]
@@ -381,7 +376,7 @@
 
 
 def add_z_kernel(scale, in_ref, *refs):
-    out_ref = refs[3]
+    out_ref = refs[-1]
     total = jnp.sum(in_ref[...].astype(jnp.float32), axis=0) * scale
     out_ref[...] = jnp.broadcast_to(total.astype(jnp.bfloat16)[None], out_ref.shape)
 
@@ -448,8 +443,8 @@
     f32, bf16 = jnp.float32, jnp.bfloat16
     packed, both = call(
         pack_kernel,
-        (shape((width, 8, rows), bf16), shape((rows, 2 * width), bf16)),
-        [pltpu.VMEM((width * 8, rows), f32)],
+        (shape((width, 2, 3 * rows), bf16), shape((rows, 2 * width), bf16)),
+        [pltpu.VMEM((3, 2 * width, rows), f32)],
         limit=56 * 1024 * 1024,
     )(inputs, in_weight, filter_one, filter_two, out_weight, out_grad)
     received = exchange(packed, everyone)
@@ -459,7 +454,7 @@
     back = call(
         convolve_kernel,
         shape((32, 7, 8, rows), bf16),
-        [pltpu.VMEM((devices * 8, rows), f32)],
+        [pltpu.VMEM((3, 2 * devices, rows), f32)],
         in_specs=specs(*[pltpu.VMEM] * (2 + len(tables)), *[pl.ANY] * 3),
     )(received, short_kernel, *tables, *gathered[1:4])
     halfway = exchange(back, ("zh", "x", "zl"))
@@ -477,16 +472,13 @@
         out_specs=specs(pltpu.VMEM, *[pl.ANY] * 3),
         input_output_aliases={4: 1, 5: 2, 6: 3},
     )(*part, *leaving)
-    near = [ring(leaving[0], "y", 1), ring(leaving[2], "y", 3)]
+    arrived = [found[4]] + [ring(x, "y", 1 + i) for i, x in enumerate(leaving)]
     part = exchange(part, ("zh", "zl"))
-    part, far = call(
+    part = call(
         functools.partial(add_z_kernel, scale),
-        (shape((16, 64, rows), bf16), shape(leaving[1].shape, bf16)),
+        shape((16, 64, rows), bf16),
         in_specs=specs(pltpu.VMEM, *[pl.ANY] * 3),
-        out_specs=specs(pltpu.VMEM, pl.ANY),
-        input_output_aliases={3: 1},
-    )(part, *near, leaving[1])
-    arrived = [found[4], near[0], ring(far, "y", 2), near[1]]
+    )(part, *arrived[1:])
     arrived += [swap_core(x) for x in arrived]
     part = exchange(part, ("x", "y"))
     outputs, grad_inputs, grad_short, grad_one, grad_two = call(

time: 105 us -> 104 us (level)
  waiting for transfers between devices: 40.6 us -> 37.9 us
    all_to_all x4, waiting for transfers between devices: 21.2 us -> 16.6 us  [exchange(): return lax.all_to_all(x, axes, split_axis=0, concat_axis=0, tiled=True)]
    ppermute x9, starting transfers between devices: 12.9 us -> 10 us  [ring(): return lax.ppermute(x, axis, [(i, (i + distance) % 4) for i in range(4)])]
    all_to_all x4, starting transfers between devices: 28.4 us -> 30.4 us  [exchange(): return lax.all_to_all(x, axes, split_axis=0, concat_axis=0, tiled=True)]
    ppermute x9, starting transfers between devices: 10.6 us -> 12.5 us  [swap_core(): return lax.ppermute(x, 'core', [(0, 1), (1, 0)])]
    ppermute x9, waiting for transfers between devices: 16 us -> 17.6 us  [ring(): return lax.ppermute(x, axis, [(i, (i + distance) % 4) for i in range(4)])]
  transfers between devices with their start and end apart: 22 -> 22, of which waited for: 16 -> 19; matrix products, arithmetic and copies ran while one was open for 0% -> 0% of each run, Pallas kernels for 1% -> 1%
where the time goes in v7:
time: 104 us; the launch traced here: 103 us
  starting transfers between devices  52.9 us (51%)
  waiting for transfers between devices  37.9 us (36%)
  Pallas kernels  11.8 us (11%)
    all_to_all x4, starting transfers between devices, exchange(): return lax.all_to_all(x, axes, split_axis=0, concat_axis=0, tiled=True)  30.4 us
    ppermute x9, waiting for transfers between devices, ring(): return lax.ppermute(x, axis, [(i, (i + distance) % 4) for i in range(4)])  17.6 us
    all_to_all x4, waiting for transfers between devices, exchange(): return lax.all_to_all(x, axes, split_axis=0, concat_axis=0, tiled=True)  16.6 us
    ppermute x9, starting transfers between devices, swap_core(): return lax.ppermute(x, 'core', [(0, 1), (1, 0)])  12.5 us
    ppermute x9, starting transfers between devices, ring(): return lax.ppermute(x, axis, [(i, (i + distance) % 4) for i in range(4)])  10 us
    pallas_call x1, Pallas kernels, per_device(): call(convolve_kernel, shape((32, 7, 8, rows), bf16), [pltpu.VMEM((3, 2 *...  4.61 us
    ppermute x9, waiting for transfers between devices, swap_core(): return lax.ppermute(x, 'core', [(0, 1), (1, 0)])  3.63 us
    pallas_call x1, Pallas kernels, per_device(): call(pack_kernel, (shape((width, 2, 3 * rows), bf16), shape((rows, 2 * wi...  2.53 us
  transfers between devices with their start and end apart: 22, of which 19 were waited for; matrix products, arithmetic and copies ran while one was open for 0% of the time, Pallas kernels for 1%

profile of v7, /device:TPU:1, one launch (start us, length us, event | category | flops | bytes accessed | tf_op | source)
XLA Modules:
  0.0 103.4 jit_solution(1149360845047761977)
XLA Ops:
  0.7 2.5 %shard_map.180 = (bf16[256,2,384]{2,1,0:T(2,128)(2,1)}, bf16[128,512]{1,0:T(8,128)(2,1)}) custom-call(bf16[1,128,256]{2,1,0:T(8,128)(2,1)} %seq_ref.1, bf16[256,768]{1,0:T(8,128)(2,1)} %refs_8_.1, f32[128,256]{1,0:T(8,128)} %one_ref.1, f32[128,256]{1,0:T(8,128)} %two_ref.1, bf16[256,256]{1,0:T(8,128)(2,1)} %refs_9_.1, bf16[1,128,256]{2,1,0:T(8,128)(2,1)} %grad_ref.1), custom_call_target="tpu_custom_call" | custom-call | tf_op jit(solution)/shard_map/pallas_call | solution.py:444
  3.2 15.7 %all-to-all-start = ((bf16[256,2,384]{2,1,0:T(2,128)(2,1)}), bf16[256,2,384]{2,1,0:T(2,128)(2,1)S(1)}, u32[]{:S(2)}, u32[]{:S(2)}) async-start(bf16[256,2,384]{2,1,0:T(2,128)(2,1)} %get-tuple-element.30), calls=%async_computation | async-start | bytes 786432 | tf_op jit(solution)/shard_map/all_to_all | solution.py:426
  18.9 2.7 %collective-permute-start.2 = (bf16[128,512]{1,0:T(8,128)(2,1)}, bf16[128,512]{1,0:T(8,128)(2,1)S(1)}, u32[]{:S(2)}, u32[]{:S(2)}) collective-permute-start(bf16[128,512]{1,0:T(8,128)(2,1)} %get-tuple-element.31.refs_0_), channel_id=1, source_target_pairs={{0,3},{1,0},{2,1},{3,2},{4,7},{5,4},{6,5},{7,6},{8,11},{9,8},{10,9... | collective-permute-start | bytes 393224 | tf_op jit(solution)/shard_map/ppermute | solution.py:434
  22.7 6.3 %collective-permute-done.2.rest_2_.refs_3_ = bf16[128,512]{1,0:T(8,128)(2,1)S(1)} collective-permute-done((bf16[128,512]{1,0:T(8,128)(2,1)}, bf16[128,512]{1,0:T(8,128)(2,1)S(1)}, u32[]{:S(2)}, u32[]{:S(2)}) %collective-permute-start.2) | collective-permute-done | bytes 131104 | tf_op jit(solution)/shard_map/ppermute | solution.py:434
  29.0 5.5 %collective-permute-done.rest_0_.refs_1_ = bf16[128,512]{1,0:T(8,128)(2,1)S(1)} collective-permute-done((bf16[128,512]{1,0:T(8,128)(2,1)}, bf16[128,512]{1,0:T(8,128)(2,1)S(1)}, u32[]{:S(2)}, u32[]{:S(2)}) %collective-permute-start) | collective-permute-done | bytes 131104 | tf_op jit(solution)/shard_map/ppermute | solution.py:434
  34.5 2.5 %all-to-all-done.in_ref = bf16[256,2,384]{2,1,0:T(2,128)(2,1)S(1)} async-done(((bf16[256,2,384]{2,1,0:T(2,128)(2,1)}), bf16[256,2,384]{2,1,0:T(2,128)(2,1)S(1)}, u32[]{:S(2)}, u32[]{:S(2)}) %all-to-all-start) | async-done | bytes 393248 | tf_op jit(solution)/shard_map/all_to_all | solution.py:426
  37.0 4.6 %shard_map.181 = bf16[32,7,8,128]{3,2,1,0:T(8,128)(2,1)} custom-call(bf16[256,2,384]{2,1,0:T(2,128)(2,1)S(1)} %all-to-all-done.in_ref, f32[3,768]{1,0:T(4,128)S(1)} %copy-done.9, bf16[256,384]{1,0:T(8,128)(2,1)S(1)} %copy-done.5, bf16[768,256]{1,0:T(8,128)(2,1)S(1)} %copy-done.3, bf16[768,256]{1,0:T(8,128)(2,1)S(1)} %copy-done.2, ...), custom_call_target="tpu_custom_call" | custom-call | tf_op jit(solution)/shard_map/pallas_call | solution.py:454
  41.6 6.4 %all-to-all-start.1 = ((bf16[32,7,8,128]{3,2,1,0:T(8,128)(2,1)}), bf16[32,7,8,128]{3,2,1,0:T(8,128)(2,1)S(1)}, u32[]{:S(2)}, u32[]{:S(2)}) async-start(bf16[32,7,8,128]{3,2,1,0:T(8,128)(2,1)} %shard_map.181), calls=%async_computation.1 | async-start | bytes 917504 | tf_op jit(solution)/shard_map/all_to_all | solution.py:426
  48.1 0.9 collective-permute-start.3
  50.8 13.4 %all-to-all-done.1.in_ref = bf16[32,7,8,128]{3,2,1,0:T(8,128)(2,1)S(1)} async-done(((bf16[32,7,8,128]{3,2,1,0:T(8,128)(2,1)}), bf16[32,7,8,128]{3,2,1,0:T(8,128)(2,1)S(1)}, u32[]{:S(2)}, u32[]{:S(2)}) %all-to-all-start.1) | async-done | bytes 458784 | tf_op jit(solution)/shard_map/all_to_all | solution.py:426
  64.9 1.7 %collective-permute-start.8 = (f32[32,256]{1,0:T(8,128)S(1)}, f32[32,256]{1,0:T(8,128)S(1)}, u32[]{:S(2)}, u32[]{:S(2)}) collective-permute-start(f32[32,256]{1,0:T(8,128)S(1)} %get-tuple-element.35), channel_id=1, source_target_pairs={{0,64},{32,96},{64,0},{96,32},{1,65},{33,97},{65,1},{97,33},{2,66}... | collective-permute-start | bytes 98312 | tf_op jit(solution)/shard_map/ppermute | solution.py:434
  66.6 1.6 %collective-permute-start.9 = (f32[32,256]{1,0:T(8,128)S(1)}, f32[32,256]{1,0:T(8,128)S(1)}, u32[]{:S(2)}, u32[]{:S(2)}) collective-permute-start(f32[32,256]{1,0:T(8,128)S(1)} %get-tuple-element.36), channel_id=1, source_target_pairs={{0,96},{32,0},{64,32},{96,64},{1,97},{33,1},{65,33},{97,65},{2,98}... | collective-permute-start | bytes 98312 | tf_op jit(solution)/shard_map/ppermute | solution.py:434
  70.4 3.4 %all-to-all-start.2 = ((bf16[8,64,128]{2,1,0:T(8,128)(2,1)}), bf16[8,64,128]{2,1,0:T(8,128)(2,1)S(1)}, u32[]{:S(2)}, u32[]{:S(2)}) async-start(bf16[8,64,128]{2,1,0:T(8,128)(2,1)} %get-tuple-element.45), calls=%async_computation.2 | async-start | bytes 262144 | tf_op jit(solution)/shard_map/all_to_all | solution.py:426
  74.6 2.0 %collective-permute-start.12 = (bf16[2,224,128]{2,1,0:T(8,128)(2,1)S(1)}, bf16[2,224,128]{2,1,0:T(8,128)(2,1)S(1)}, u32[]{:S(2)}, u32[]{:S(2)}) collective-permute-start(bf16[2,224,128]{2,1,0:T(8,128)(2,1)S(1)} %get-tuple-element.42), channel_id=1, source_target_pairs={{0,3},{1,0},{2,1},{3,2},{4,7},{5,4},{6,5},{7,6},{8,11},{9,8},{10,9... | collective-permute-start | bytes 344072 | tf_op jit(solution)/shard_map/ppermute | solution.py:434
  76.5 3.4 %collective-permute-done.10.refs_1_.refs_0_ = bf16[2,224,128]{2,1,0:T(8,128)(2,1)S(1)} collective-permute-done((bf16[2,224,128]{2,1,0:T(8,128)(2,1)S(1)}, bf16[2,224,128]{2,1,0:T(8,128)(2,1)S(1)}, u32[]{:S(2)}, u32[]{:S(2)}) %collective-permute-start.10) | collective-permute-done | bytes 114720 | tf_op jit(solution)/shard_map/ppermute | solution.py:434
  79.9 0.9 collective-permute-done.12.refs_3_.refs_2_
  80.8 0.8 all-to-all-done.2.in_ref
  81.6 0.7 shard_map.185
  82.4 5.0 %all-to-all-start.3 = ((bf16[16,64,128]{2,1,0:T(8,128)(2,1)}), bf16[16,64,128]{2,1,0:T(8,128)(2,1)S(1)}, u32[]{:S(2)}, u32[]{:S(2)}) async-start(bf16[16,64,128]{2,1,0:T(8,128)(2,1)} %shard_map.185), calls=%async_computation.3 | async-start | bytes 524288 | tf_op jit(solution)/shard_map/all_to_all | solution.py:426
  87.4 5.2 %collective-permute-start.13 = (bf16[2,224,128]{2,1,0:T(8,128)(2,1)S(1)}, bf16[2,224,128]{2,1,0:T(8,128)(2,1)S(1)}, u32[]{:S(2)}, u32[]{:S(2)}) collective-permute-start(bf16[2,224,128]{2,1,0:T(8,128)(2,1)S(1)} %get-tuple-element.32.refs_0_), channel_id=1, source_target_pairs={{0,16},{16,0},{1,17},{17,1},{2,18},{18,2},{3,19},{19,3},{4,20},{20... | collective-permute-start | bytes 344072 | tf_op jit(solution)/shard_map/ppermute | solution.py:430
  94.4 1.4 %shard_map.184 = (bf16[1,128,256]{2,1,0:T(8,128)(2,1)}, bf16[1,128,256]{2,1,0:T(8,128)(2,1)}, f32[3,768]{1,0:T(4,128)}, f32[128,256]{1,0:T(8,128)}, f32[128,256]{1,0:T(8,128)}) custom-call(bf16[2,224,128]{2,1,0:T(8,128)(2,1)S(1)} %get-tuple-element.32.refs_0_, bf16[2,224,128]{2,1,0:T(8,128)(2,1)S(1)} %collective-permute-done.10.refs_1_.refs_0_, ...), custom_call_target="tpu_custom_call" | custom-call | tf_op jit(solution)/shard_map/pallas_call | solution.py:484
  95.8 5.2 %collective-permute-start.17 = (bf16[16,64,128]{2,1,0:T(8,128)(2,1)S(1)}, bf16[16,64,128]{2,1,0:T(8,128)(2,1)S(1)}, u32[]{:S(2)}, u32[]{:S(2)}) collective-permute-start(bf16[16,64,128]{2,1,0:T(8,128)(2,1)S(1)} %all-to-all-done.3.own_ref), channel_id=1, source_target_pairs={{0,16},{16,0},{1,17},{17,1},{2,18},{18,2},{3,19},{19,3},{4,20},{20... | collective-permute-start | bytes 786440 | tf_op jit(solution)/shard_map/ppermute | solution.py:430
  101.0 1.2 %collective-permute-done.17.other_ref = bf16[16,64,128]{2,1,0:T(8,128)(2,1)S(1)} collective-permute-done((bf16[16,64,128]{2,1,0:T(8,128)(2,1)S(1)}, bf16[16,64,128]{2,1,0:T(8,128)(2,1)S(1)}, u32[]{:S(2)}, u32[]{:S(2)}) %collective-permute-start.17) | collective-permute-done | bytes 262176 | tf_op jit(solution)/shard_map/ppermute | solution.py:430
  102.1 1.3 %shard_map.186 = (f32[256,768]{1,0:T(8,128)}, f32[256,256]{1,0:T(8,128)}) custom-call(bf16[16,64,128]{2,1,0:T(8,128)(2,1)S(1)} %all-to-all-done.3.own_ref, bf16[16,64,128]{2,1,0:T(8,128)(2,1)S(1)} %collective-permute-done.17.other_ref), custom_call_target="tpu_custom_call" | custom-call | tf_op jit(solution)/shard_map/pallas_call | solution.py:495
  (47 shorter events, 8.5 us)
Async XLA Ops:
  0.6 36.4 %copy-start.4 = (bf16[128,768]{1,0:T(8,128)(2,1)S(1)}, bf16[128,768]{1,0:T(8,128)(2,1)}, u32[]{:S(2)}) copy-start(bf16[128,768]{1,0:T(8,128)(2,1)} %constant.15.clone.first_back_ref) | copy-start | bytes 589828
  0.6 36.3 %copy-start.5 = (bf16[256,384]{1,0:T(8,128)(2,1)S(1)}, bf16[256,384]{1,0:T(8,128)(2,1)}, u32[]{:S(2)}) copy-start(bf16[256,384]{1,0:T(8,128)(2,1)} %constant.12.clone.first_ref) | copy-start | bytes 589828
  3.2 33.8 %all-to-all-start = ((bf16[256,2,384]{2,1,0:T(2,128)(2,1)}), bf16[256,2,384]{2,1,0:T(2,128)(2,1)S(1)}, u32[]{:S(2)}, u32[]{:S(2)}) async-start(bf16[256,2,384]{2,1,0:T(2,128)(2,1)} %get-tuple-element.30), calls=%async_computation | async-start | bytes 786432 | tf_op jit(solution)/shard_map/all_to_all | solution.py:426
  18.9 10.2 %collective-permute-start.2 = (bf16[128,512]{1,0:T(8,128)(2,1)}, bf16[128,512]{1,0:T(8,128)(2,1)S(1)}, u32[]{:S(2)}, u32[]{:S(2)}) collective-permute-start(bf16[128,512]{1,0:T(8,128)(2,1)} %get-tuple-element.31.refs_0_), channel_id=1, source_target_pairs={{0,3},{1,0},{2,1},{3,2},{4,7},{5,4},{6,5},{7,6},{8,11},{9,8},{10,9... | collective-permute-start | bytes 393224 | tf_op jit(solution)/shard_map/ppermute | solution.py:434
  21.6 7.4 %collective-permute-start.1 = (bf16[128,512]{1,0:T(8,128)(2,1)}, bf16[128,512]{1,0:T(8,128)(2,1)S(1)}, u32[]{:S(2)}, u32[]{:S(2)}) collective-permute-start(bf16[128,512]{1,0:T(8,128)(2,1)} %get-tuple-element.31.refs_0_), channel_id=1, source_target_pairs={{0,2},{1,3},{2,0},{3,1},{4,6},{5,7},{6,4},{7,5},{8,10},{9,11},{10,... | collective-permute-start | bytes 393224 | tf_op jit(solution)/shard_map/ppermute | solution.py:434
  22.1 12.4 %collective-permute-start = (bf16[128,512]{1,0:T(8,128)(2,1)}, bf16[128,512]{1,0:T(8,128)(2,1)S(1)}, u32[]{:S(2)}, u32[]{:S(2)}) collective-permute-start(bf16[128,512]{1,0:T(8,128)(2,1)} %get-tuple-element.31.refs_0_), channel_id=1, source_target_pairs={{0,1},{1,2},{2,3},{3,0},{4,5},{5,6},{6,7},{7,4},{8,9},{9,10},{10,1... | collective-permute-start | bytes 393224 | tf_op jit(solution)/shard_map/ppermute | solution.py:434
  41.6 22.6 %all-to-all-start.1 = ((bf16[32,7,8,128]{3,2,1,0:T(8,128)(2,1)}), bf16[32,7,8,128]{3,2,1,0:T(8,128)(2,1)S(1)}, u32[]{:S(2)}, u32[]{:S(2)}) async-start(bf16[32,7,8,128]{3,2,1,0:T(8,128)(2,1)} %shard_map.181), calls=%async_computation.1 | async-start | bytes 917504 | tf_op jit(solution)/shard_map/all_to_all | solution.py:426
  48.1 1.9 %collective-permute-start.3 = (bf16[128,512]{1,0:T(8,128)(2,1)S(1)}, bf16[128,512]{1,0:T(8,128)(2,1)S(1)}, u32[]{:S(2)}, u32[]{:S(2)}) collective-permute-start(bf16[128,512]{1,0:T(8,128)(2,1)S(1)} %copy-done.6), channel_id=1, source_target_pairs={{0,16},{16,0},{1,17},{17,1},{2,18},{18,2},{3,19},{19,3},{4,20},{20... | collective-permute-start | bytes 393224 | tf_op jit(solution)/shard_map/ppermute | solution.py:430
  49.0 1.3 %collective-permute-start.6 = (bf16[128,512]{1,0:T(8,128)(2,1)S(1)}, bf16[128,512]{1,0:T(8,128)(2,1)S(1)}, u32[]{:S(2)}, u32[]{:S(2)}) collective-permute-start(bf16[128,512]{1,0:T(8,128)(2,1)S(1)} %collective-permute-done.2.rest_2_.refs_3_), channel_id=1, source_target_pairs={{0,16},{16,0},{1,17},{17,1},{2,18},{18,2},{3,19},{19,3},{4,20},{20... | collective-permute-start | bytes 393224 | tf_op jit(solution)/shard_map/ppermute | solution.py:430
  49.1 1.4 %collective-permute-start.5 = (bf16[128,512]{1,0:T(8,128)(2,1)S(1)}, bf16[128,512]{1,0:T(8,128)(2,1)S(1)}, u32[]{:S(2)}, u32[]{:S(2)}) collective-permute-start(bf16[128,512]{1,0:T(8,128)(2,1)S(1)} %collective-permute-done.1.rest_1_.refs_2_), channel_id=1, source_target_pairs={{0,16},{16,0},{1,17},{17,1},{2,18},{18,2},{3,19},{19,3},{4,20},{20... | collective-permute-start | bytes 393224 | tf_op jit(solution)/shard_map/ppermute | solution.py:430
  49.5 1.3 %collective-permute-start.4 = (bf16[128,512]{1,0:T(8,128)(2,1)S(1)}, bf16[128,512]{1,0:T(8,128)(2,1)S(1)}, u32[]{:S(2)}, u32[]{:S(2)}) collective-permute-start(bf16[128,512]{1,0:T(8,128)(2,1)S(1)} %collective-permute-done.rest_0_.refs_1_), channel_id=1, source_target_pairs={{0,16},{16,0},{1,17},{17,1},{2,18},{18,2},{3,19},{19,3},{4,20},{20... | collective-permute-start | bytes 393224 | tf_op jit(solution)/shard_map/ppermute | solution.py:430
  64.8 4.1 %collective-permute-start.7 = (f32[32,256]{1,0:T(8,128)S(1)}, f32[32,256]{1,0:T(8,128)S(1)}, u32[]{:S(2)}, u32[]{:S(2)}) collective-permute-start(f32[32,256]{1,0:T(8,128)S(1)} %get-tuple-element.34), channel_id=1, source_target_pairs={{0,32},{32,64},{64,96},{96,0},{1,33},{33,65},{65,97},{97,1},{2,34}... | collective-permute-start | bytes 98312 | tf_op jit(solution)/shard_map/ppermute | solution.py:434
  64.9 4.3 %collective-permute-start.8 = (f32[32,256]{1,0:T(8,128)S(1)}, f32[32,256]{1,0:T(8,128)S(1)}, u32[]{:S(2)}, u32[]{:S(2)}) collective-permute-start(f32[32,256]{1,0:T(8,128)S(1)} %get-tuple-element.35), channel_id=1, source_target_pairs={{0,64},{32,96},{64,0},{96,32},{1,65},{33,97},{65,1},{97,33},{2,66}... | collective-permute-start | bytes 98312 | tf_op jit(solution)/shard_map/ppermute | solution.py:434
  66.6 3.1 %collective-permute-start.9 = (f32[32,256]{1,0:T(8,128)S(1)}, f32[32,256]{1,0:T(8,128)S(1)}, u32[]{:S(2)}, u32[]{:S(2)}) collective-permute-start(f32[32,256]{1,0:T(8,128)S(1)} %get-tuple-element.36), channel_id=1, source_target_pairs={{0,96},{32,0},{64,32},{96,64},{1,97},{33,1},{65,33},{97,65},{2,98}... | collective-permute-start | bytes 98312 | tf_op jit(solution)/shard_map/ppermute | solution.py:434
  70.4 11.2 %all-to-all-start.2 = ((bf16[8,64,128]{2,1,0:T(8,128)(2,1)}), bf16[8,64,128]{2,1,0:T(8,128)(2,1)S(1)}, u32[]{:S(2)}, u32[]{:S(2)}) async-start(bf16[8,64,128]{2,1,0:T(8,128)(2,1)} %get-tuple-element.45), calls=%async_computation.2 | async-start | bytes 262144 | tf_op jit(solution)/shard_map/all_to_all | solution.py:426
  73.8 6.2 %collective-permute-start.10 = (bf16[2,224,128]{2,1,0:T(8,128)(2,1)S(1)}, bf16[2,224,128]{2,1,0:T(8,128)(2,1)S(1)}, u32[]{:S(2)}, u32[]{:S(2)}) collective-permute-start(bf16[2,224,128]{2,1,0:T(8,128)(2,1)S(1)} %get-tuple-element.40), channel_id=1, source_target_pairs={{0,1},{1,2},{2,3},{3,0},{4,5},{5,6},{6,7},{7,4},{8,9},{9,10},{10,1... | collective-permute-start | bytes 344072 | tf_op jit(solution)/shard_map/ppermute | solution.py:434
  73.9 6.1 %collective-permute-start.11 = (bf16[2,224,128]{2,1,0:T(8,128)(2,1)S(1)}, bf16[2,224,128]{2,1,0:T(8,128)(2,1)S(1)}, u32[]{:S(2)}, u32[]{:S(2)}) collective-permute-start(bf16[2,224,128]{2,1,0:T(8,128)(2,1)S(1)} %get-tuple-element.41), channel_id=1, source_target_pairs={{0,2},{1,3},{2,0},{3,1},{4,6},{5,7},{6,4},{7,5},{8,10},{9,11},{10,... | collective-permute-start | bytes 344072 | tf_op jit(solution)/shard_map/ppermute | solution.py:434
  74.6 6.3 %collective-permute-start.12 = (bf16[2,224,128]{2,1,0:T(8,128)(2,1)S(1)}, bf16[2,224,128]{2,1,0:T(8,128)(2,1)S(1)}, u32[]{:S(2)}, u32[]{:S(2)}) collective-permute-start(bf16[2,224,128]{2,1,0:T(8,128)(2,1)S(1)} %get-tuple-element.42), channel_id=1, source_target_pairs={{0,3},{1,0},{2,1},{3,2},{4,7},{5,4},{6,5},{7,6},{8,11},{9,8},{10,9... | collective-permute-start | bytes 344072 | tf_op jit(solution)/shard_map/ppermute | solution.py:434
  82.4 13.4 %all-to-all-start.3 = ((bf16[16,64,128]{2,1,0:T(8,128)(2,1)}), bf16[16,64,128]{2,1,0:T(8,128)(2,1)S(1)}, u32[]{:S(2)}, u32[]{:S(2)}) async-start(bf16[16,64,128]{2,1,0:T(8,128)(2,1)} %shard_map.185), calls=%async_computation.3 | async-start | bytes 524288 | tf_op jit(solution)/shard_map/all_to_all | solution.py:426
  87.4 6.2 %collective-permute-start.13 = (bf16[2,224,128]{2,1,0:T(8,128)(2,1)S(1)}, bf16[2,224,128]{2,1,0:T(8,128)(2,1)S(1)}, u32[]{:S(2)}, u32[]{:S(2)}) collective-permute-start(bf16[2,224,128]{2,1,0:T(8,128)(2,1)S(1)} %get-tuple-element.32.refs_0_), channel_id=1, source_target_pairs={{0,16},{16,0},{1,17},{17,1},{2,18},{18,2},{3,19},{19,3},{4,20},{20... | collective-permute-start | bytes 344072 | tf_op jit(solution)/shard_map/ppermute | solution.py:430
  92.6 1.3 %collective-permute-start.14 = (bf16[2,224,128]{2,1,0:T(8,128)(2,1)S(1)}, bf16[2,224,128]{2,1,0:T(8,128)(2,1)S(1)}, u32[]{:S(2)}, u32[]{:S(2)}) collective-permute-start(bf16[2,224,128]{2,1,0:T(8,128)(2,1)S(1)} %collective-permute-done.10.refs_1_.refs_0_), channel_id=1, source_target_pairs={{0,16},{16,0},{1,17},{17,1},{2,18},{18,2},{3,19},{19,3},{4,20},{20... | collective-permute-start | bytes 344072 | tf_op jit(solution)/shard_map/ppermute | solution.py:430
  92.7 1.4 %collective-permute-start.15 = (bf16[2,224,128]{2,1,0:T(8,128)(2,1)S(1)}, bf16[2,224,128]{2,1,0:T(8,128)(2,1)S(1)}, u32[]{:S(2)}, u32[]{:S(2)}) collective-permute-start(bf16[2,224,128]{2,1,0:T(8,128)(2,1)S(1)} %collective-permute-done.11.refs_2_.refs_1_), channel_id=1, source_target_pairs={{0,16},{16,0},{1,17},{17,1},{2,18},{18,2},{3,19},{19,3},{4,20},{20... | collective-permute-start | bytes 344072 | tf_op jit(solution)/shard_map/ppermute | solution.py:430
  93.1 1.3 %collective-permute-start.16 = (bf16[2,224,128]{2,1,0:T(8,128)(2,1)S(1)}, bf16[2,224,128]{2,1,0:T(8,128)(2,1)S(1)}, u32[]{:S(2)}, u32[]{:S(2)}) collective-permute-start(bf16[2,224,128]{2,1,0:T(8,128)(2,1)S(1)} %collective-permute-done.12.refs_3_.refs_2_), channel_id=1, source_target_pairs={{0,16},{16,0},{1,17},{17,1},{2,18},{18,2},{3,19},{19,3},{4,20},{20... | collective-permute-start | bytes 344072 | tf_op jit(solution)/shard_map/ppermute | solution.py:430
  95.8 6.3 %collective-permute-start.17 = (bf16[16,64,128]{2,1,0:T(8,128)(2,1)S(1)}, bf16[16,64,128]{2,1,0:T(8,128)(2,1)S(1)}, u32[]{:S(2)}, u32[]{:S(2)}) collective-permute-start(bf16[16,64,128]{2,1,0:T(8,128)(2,1)S(1)} %all-to-all-done.3.own_ref), channel_id=1, source_target_pairs={{0,16},{16,0},{1,17},{17,1},{2,18},{18,2},{3,19},{19,3},{4,20},{20... | collective-permute-start | bytes 786440 | tf_op jit(solution)/shard_map/ppermute | solution.py:430
  (8 other events, 207.1 us)

commit v8 on v7

--- a/solution.py
+++ b/solution.py
@@ -293,12 +293,13 @@
     sources, kinds, blocks, rows = in_ref.shape
     width = both_refs[0].shape[1] // 2
     x, core, y = lax.axis_index("x"), lax.axis_index("core"), lax.axis_index("y")
+    turn = 1 - 2 * core
     rows_ref[...] = in_ref[...].astype(jnp.float32).reshape(sources * kinds * blocks, rows)
     out_part = jnp.zeros((sources, width), jnp.float32)
     in_part = jnp.zeros((3 * sources, width), jnp.float32)
     for other in range(2):
         for ahead in range(4):
-            block = (core ^ other) * 4 + ((y + ahead) & 3)
+            block = (core ^ other) * 4 + ((y + turn * ahead) & 3)
             kept = jnp.concatenate(
                 [
                     rows_ref[pl.ds(kind * blocks + block, sources, stride=kinds * blocks), :]
@@ -307,14 +308,14 @@
                 0,
             ).astype(jnp.bfloat16)
             send_refs[ahead][other] = kept
-            both_ref = both_refs[other * 4 + (4 - ahead) % 4]
+            both_ref = both_refs[4 + ahead if other else (4 - ahead) % 4]
             out_part += bf16_dot(kept[:sources], both_ref[:, width:])
             in_part += bf16_dot(kept[sources : 4 * sources], both_ref[:, :width])
     sums_ref[0] = out_part
     for group in range(3):
         sums_ref[1 + group] = in_part[group * sources : (group + 1) * sources]
     for ahead in range(4):
-        part_refs[ahead][...] = sums_ref[(x + ahead) & 3]
+        part_refs[ahead][...] = sums_ref[(x + turn * ahead) & 3]
 
 
 def finish_kernel(*refs):
@@ -324,11 +325,14 @@
     width = out_weight_ref.shape[0]
     count = width // 8
     core, y = lax.axis_index("core"), lax.axis_index("y")
-    order = channel_order(
-        lambda zh, x, c, zl, v: (
-            (((c ^ core) * 4 + ((y - v) & 3)) * 32) + (zh * 16 + x * 4 + zl)
-        )
-    )
+    turn = 1 - 2 * core
+
+    def row_of(zh, x, c, zl, v):
+        other = c ^ core
+        step = (turn * (1 - 2 * other) * (y - v)) & 3
+        return (other * 4 + step) * 32 + (zh * 16 + x * 4 + zl)
+
+    order = channel_order(row_of)
     contract_first = (((0,), (1,)), ((), ()))
     contract_last = (((1,), (1,)), ((), ()))
 
@@ -431,7 +435,14 @@
 
 
 def ring(x, axis, distance):
-    return lax.ppermute(x, axis, [(i, (i + distance) % 4) for i in range(4)])
+    axes = ("x", "core") if axis == "x" else ("core", "y")
+    route = []
+    for core, turn in ((0, distance), (1, -distance)):
+        for i in range(4):
+            j = (i + turn) % 4
+            pair = (i * 2 + core, j * 2 + core) if axis == "x" else (core * 4 + i, core * 4 + j)
+            route.append(pair)
+    return lax.ppermute(x, axes, route)
 
 
 def per_device(inputs, in_weight, short_kernel, filter_one, filter_two, out_weight, out_grad):
@@ -455,8 +466,8 @@
         convolve_kernel,
         shape((32, 7, 8, rows), bf16),
         [pltpu.VMEM((3, 2 * devices, rows), f32)],
-        in_specs=specs(*[pltpu.VMEM] * (2 + len(tables)), *[pl.ANY] * 3),
-    )(received, short_kernel, *tables, *gathered[1:4])
+        in_specs=specs(*[pltpu.VMEM] * (2 + len(tables)), *[pl.ANY] * 2),
+    )(received, short_kernel, *tables, gathered[1], gathered[3])
     halfway = exchange(back, ("zh", "x", "zl"))
     found = call(
         part_kernel,

time: 104 us -> 102 us (0.981)
  starting transfers between devices: 52.9 us -> 45.8 us
  waiting for transfers between devices: 37.9 us -> 42.7 us
    ppermute x9, starting transfers between devices: 12.5 us -> 8.21 us  [swap_core(): return lax.ppermute(x, 'core', [(0, 1), (1, 0)])]
    all_to_all x4, starting transfers between devices: 30.4 us -> 26.7 us  [exchange(): return lax.all_to_all(x, axes, split_axis=0, concat_axis=0, tiled=True)]
    all_to_all x4, waiting for transfers between devices: 16.6 us -> 19.3 us  [exchange(): return lax.all_to_all(x, axes, split_axis=0, concat_axis=0, tiled=True)]
    ppermute x9, waiting for transfers between devices: 17.6 us -> 20 us  [ring(): return lax.ppermute(x, axes, route)]
  transfers between devices with their start and end apart: 22 -> 22, of which waited for: 19 -> 20; matrix products, arithmetic and copies ran while one was open for 0% -> 0% of each run, Pallas kernels for 1% -> 1%
where the time goes in v8:
time: 102 us; the launch traced here: 101 us
  starting transfers between devices  45.8 us (45%)
  waiting for transfers between devices  42.7 us (42%)
  Pallas kernels  11.8 us (12%)
    all_to_all x4, starting transfers between devices, exchange(): return lax.all_to_all(x, axes, split_axis=0, concat_axis=0, tiled=True)  26.7 us
    ppermute x9, waiting for transfers between devices, ring(): return lax.ppermute(x, axes, route)  20 us
    all_to_all x4, waiting for transfers between devices, exchange(): return lax.all_to_all(x, axes, split_axis=0, concat_axis=0, tiled=True)  19.3 us
    ppermute x9, starting transfers between devices, ring(): return lax.ppermute(x, axes, route)  10.9 us
    ppermute x9, starting transfers between devices, swap_core(): return lax.ppermute(x, 'core', [(0, 1), (1, 0)])  8.21 us
    pallas_call x1, Pallas kernels, per_device(): call(convolve_kernel, shape((32, 7, 8, rows), bf16), [pltpu.VMEM((3, 2 *...  4.61 us
    ppermute x9, waiting for transfers between devices, swap_core(): return lax.ppermute(x, 'core', [(0, 1), (1, 0)])  3.41 us
    pallas_call x1, Pallas kernels, per_device(): call(pack_kernel, (shape((width, 2, 3 * rows), bf16), shape((rows, 2 * wi...  2.53 us
  transfers between devices with their start and end apart: 22, of which 20 were waited for; matrix products, arithmetic and copies ran while one was open for 0% of the time, Pallas kernels for 1%

profile of v8, /device:TPU:1, one launch (start us, length us, event | category | flops | bytes accessed | tf_op | source)
XLA Modules:
  0.0 101.2 jit_solution(11570532148621934039)
XLA Ops:
  0.7 2.5 %shard_map.180 = (bf16[256,2,384]{2,1,0:T(2,128)(2,1)}, bf16[128,512]{1,0:T(8,128)(2,1)}) custom-call(bf16[1,128,256]{2,1,0:T(8,128)(2,1)} %seq_ref.1, bf16[256,768]{1,0:T(8,128)(2,1)} %refs_8_.1, f32[128,256]{1,0:T(8,128)} %one_ref.1, f32[128,256]{1,0:T(8,128)} %two_ref.1, bf16[256,256]{1,0:T(8,128)(2,1)} %refs_9_.1, bf16[1,128,256]{2,1,0:T(8,128)(2,1)} %grad_ref.1), custom_call_target="tpu_custom_call" | custom-call | tf_op jit(solution)/shard_map/pallas_call | solution.py:455
  3.2 15.7 %all-to-all-start = ((bf16[256,2,384]{2,1,0:T(2,128)(2,1)}), bf16[256,2,384]{2,1,0:T(2,128)(2,1)S(1)}, u32[]{:S(2)}, u32[]{:S(2)}) async-start(bf16[256,2,384]{2,1,0:T(2,128)(2,1)} %get-tuple-element.30), calls=%async_computation | async-start | bytes 786432 | tf_op jit(solution)/shard_map/all_to_all | solution.py:430
  18.9 1.5 %collective-permute-start.1 = (bf16[128,512]{1,0:T(8,128)(2,1)}, bf16[128,512]{1,0:T(8,128)(2,1)S(1)}, u32[]{:S(2)}, u32[]{:S(2)}) collective-permute-start(bf16[128,512]{1,0:T(8,128)(2,1)} %get-tuple-element.31.refs_0_), channel_id=1, source_target_pairs={{0,3},{1,0},{2,1},{3,2},{16,17},{17,18},{18,19},{19,16},{4,7},{5,4... | collective-permute-start | bytes 393224 | tf_op jit(solution)/shard_map/ppermute | solution.py:445
  20.4 1.4 %collective-permute-start = (bf16[128,512]{1,0:T(8,128)(2,1)}, bf16[128,512]{1,0:T(8,128)(2,1)S(1)}, u32[]{:S(2)}, u32[]{:S(2)}) collective-permute-start(bf16[128,512]{1,0:T(8,128)(2,1)} %get-tuple-element.31.refs_0_), channel_id=1, source_target_pairs={{0,1},{1,2},{2,3},{3,0},{16,19},{17,16},{18,17},{19,18},{4,5},{5,6... | collective-permute-start | bytes 393224 | tf_op jit(solution)/shard_map/ppermute | solution.py:445
  21.7 3.3 %collective-permute-done.1.rest_1_.refs_3_ = bf16[128,512]{1,0:T(8,128)(2,1)S(1)} collective-permute-done((bf16[128,512]{1,0:T(8,128)(2,1)}, bf16[128,512]{1,0:T(8,128)(2,1)S(1)}, u32[]{:S(2)}, u32[]{:S(2)}) %collective-permute-start.1) | collective-permute-done | bytes 131104 | tf_op jit(solution)/shard_map/ppermute | solution.py:445
  25.0 1.3 %collective-permute-done.rest_0_.refs_1_ = bf16[128,512]{1,0:T(8,128)(2,1)S(1)} collective-permute-done((bf16[128,512]{1,0:T(8,128)(2,1)}, bf16[128,512]{1,0:T(8,128)(2,1)S(1)}, u32[]{:S(2)}, u32[]{:S(2)}) %collective-permute-start) | collective-permute-done | bytes 131104 | tf_op jit(solution)/shard_map/ppermute | solution.py:445
  26.3 10.7 %all-to-all-done.in_ref = bf16[256,2,384]{2,1,0:T(2,128)(2,1)S(1)} async-done(((bf16[256,2,384]{2,1,0:T(2,128)(2,1)}), bf16[256,2,384]{2,1,0:T(2,128)(2,1)S(1)}, u32[]{:S(2)}, u32[]{:S(2)}) %all-to-all-start) | async-done | bytes 393248 | tf_op jit(solution)/shard_map/all_to_all | solution.py:430
  37.0 4.6 %shard_map.181 = bf16[32,7,8,128]{3,2,1,0:T(8,128)(2,1)} custom-call(bf16[256,2,384]{2,1,0:T(2,128)(2,1)S(1)} %all-to-all-done.in_ref, f32[3,768]{1,0:T(4,128)S(1)} %copy-done.9, bf16[256,384]{1,0:T(8,128)(2,1)S(1)} %copy-done.5, bf16[768,256]{1,0:T(8,128)(2,1)S(1)} %copy-done.3, bf16[768,256]{1,0:T(8,128)(2,1)S(1)} %copy-done.2, ...), custom_call_target="tpu_custom_call" | custom-call | tf_op jit(solution)/shard_map/pallas_call | solution.py:465
  41.6 4.0 %all-to-all-start.1 = ((bf16[32,7,8,128]{3,2,1,0:T(8,128)(2,1)}), bf16[32,7,8,128]{3,2,1,0:T(8,128)(2,1)S(1)}, u32[]{:S(2)}, u32[]{:S(2)}) async-start(bf16[32,7,8,128]{3,2,1,0:T(8,128)(2,1)} %shard_map.181), calls=%async_computation.1 | async-start | bytes 917504 | tf_op jit(solution)/shard_map/all_to_all | solution.py:430
  45.7 1.6 %collective-permute-start.2 = (bf16[128,512]{1,0:T(8,128)(2,1)S(1)}, bf16[128,512]{1,0:T(8,128)(2,1)S(1)}, u32[]{:S(2)}, u32[]{:S(2)}) collective-permute-start(bf16[128,512]{1,0:T(8,128)(2,1)S(1)} %copy-done.6), channel_id=1, source_target_pairs={{0,2},{1,3},{2,0},{3,1},{16,18},{17,19},{18,16},{19,17},{4,6},{5,7... | collective-permute-start | bytes 393224 | tf_op jit(solution)/shard_map/ppermute | solution.py:445
  47.3 4.0 %collective-permute-done.2.refs_2_ = bf16[128,512]{1,0:T(8,128)(2,1)S(1)} collective-permute-done((bf16[128,512]{1,0:T(8,128)(2,1)S(1)}, bf16[128,512]{1,0:T(8,128)(2,1)S(1)}, u32[]{:S(2)}, u32[]{:S(2)}) %collective-permute-start.2) | collective-permute-done | bytes 131104 | tf_op jit(solution)/shard_map/ppermute | solution.py:445
  51.3 1.9 %collective-permute-start.5 = (bf16[128,512]{1,0:T(8,128)(2,1)S(1)}, bf16[128,512]{1,0:T(8,128)(2,1)S(1)}, u32[]{:S(2)}, u32[]{:S(2)}) collective-permute-start(bf16[128,512]{1,0:T(8,128)(2,1)S(1)} %collective-permute-done.2.refs_2_), channel_id=1, source_target_pairs={{0,16},{16,0},{1,17},{17,1},{2,18},{18,2},{3,19},{19,3},{4,20},{20... | collective-permute-start | bytes 393224 | tf_op jit(solution)/shard_map/ppermute | solution.py:434
  54.8 6.6 %all-to-all-done.1.in_ref = bf16[32,7,8,128]{3,2,1,0:T(8,128)(2,1)S(1)} async-done(((bf16[32,7,8,128]{3,2,1,0:T(8,128)(2,1)}), bf16[32,7,8,128]{3,2,1,0:T(8,128)(2,1)S(1)}, u32[]{:S(2)}, u32[]{:S(2)}) %all-to-all-start.1) | async-done | bytes 458784 | tf_op jit(solution)/shard_map/all_to_all | solution.py:430
  64.8 2.3 %collective-permute-done.8.refs_2_ = f32[32,256]{1,0:T(8,128)S(1)} collective-permute-done((f32[32,256]{1,0:T(8,128)S(1)}, f32[32,256]{1,0:T(8,128)S(1)}, u32[]{:S(2)}, u32[]{:S(2)}) %collective-permute-start.8) | collective-permute-done | bytes 32800 | tf_op jit(solution)/shard_map/ppermute | solution.py:445
  68.6 3.4 %all-to-all-start.2 = ((bf16[8,64,128]{2,1,0:T(8,128)(2,1)}), bf16[8,64,128]{2,1,0:T(8,128)(2,1)S(1)}, u32[]{:S(2)}, u32[]{:S(2)}) async-start(bf16[8,64,128]{2,1,0:T(8,128)(2,1)} %get-tuple-element.45), calls=%async_computation.2 | async-start | bytes 262144 | tf_op jit(solution)/shard_map/all_to_all | solution.py:430
  71.9 3.0 %collective-permute-start.10 = (bf16[2,224,128]{2,1,0:T(8,128)(2,1)S(1)}, bf16[2,224,128]{2,1,0:T(8,128)(2,1)S(1)}, u32[]{:S(2)}, u32[]{:S(2)}) collective-permute-start(bf16[2,224,128]{2,1,0:T(8,128)(2,1)S(1)} %get-tuple-element.40), channel_id=1, source_target_pairs={{0,1},{1,2},{2,3},{3,0},{16,19},{17,16},{18,17},{19,18},{4,5},{5,6... | collective-permute-start | bytes 344072 | tf_op jit(solution)/shard_map/ppermute | solution.py:445
  76.0 2.0 %collective-permute-done.10.refs_1_.refs_0_ = bf16[2,224,128]{2,1,0:T(8,128)(2,1)S(1)} collective-permute-done((bf16[2,224,128]{2,1,0:T(8,128)(2,1)S(1)}, bf16[2,224,128]{2,1,0:T(8,128)(2,1)S(1)}, u32[]{:S(2)}, u32[]{:S(2)}) %collective-permute-start.10) | collective-permute-done | bytes 114720 | tf_op jit(solution)/shard_map/ppermute | solution.py:445
  77.9 3.7 %collective-permute-done.11.refs_2_.refs_1_ = bf16[2,224,128]{2,1,0:T(8,128)(2,1)S(1)} collective-permute-done((bf16[2,224,128]{2,1,0:T(8,128)(2,1)S(1)}, bf16[2,224,128]{2,1,0:T(8,128)(2,1)S(1)}, u32[]{:S(2)}, u32[]{:S(2)}) %collective-permute-start.11) | collective-permute-done | bytes 114720 | tf_op jit(solution)/shard_map/ppermute | solution.py:445
  81.6 2.2 %collective-permute-done.12.refs_3_.refs_2_ = bf16[2,224,128]{2,1,0:T(8,128)(2,1)S(1)} collective-permute-done((bf16[2,224,128]{2,1,0:T(8,128)(2,1)S(1)}, bf16[2,224,128]{2,1,0:T(8,128)(2,1)S(1)}, u32[]{:S(2)}, u32[]{:S(2)}) %collective-permute-start.12) | collective-permute-done | bytes 114720 | tf_op jit(solution)/shard_map/ppermute | solution.py:445
  84.6 3.7 %all-to-all-start.3 = ((bf16[16,64,128]{2,1,0:T(8,128)(2,1)}), bf16[16,64,128]{2,1,0:T(8,128)(2,1)S(1)}, u32[]{:S(2)}, u32[]{:S(2)}) async-start(bf16[16,64,128]{2,1,0:T(8,128)(2,1)} %shard_map.185), calls=%async_computation.3 | async-start | bytes 524288 | tf_op jit(solution)/shard_map/all_to_all | solution.py:430
  88.3 2.0 %collective-permute-start.13 = (bf16[2,224,128]{2,1,0:T(8,128)(2,1)S(1)}, bf16[2,224,128]{2,1,0:T(8,128)(2,1)S(1)}, u32[]{:S(2)}, u32[]{:S(2)}) collective-permute-start(bf16[2,224,128]{2,1,0:T(8,128)(2,1)S(1)} %get-tuple-element.32.refs_0_), channel_id=1, source_target_pairs={{0,16},{16,0},{1,17},{17,1},{2,18},{18,2},{3,19},{19,3},{4,20},{20... | collective-permute-start | bytes 344072 | tf_op jit(solution)/shard_map/ppermute | solution.py:434
  92.1 1.4 %shard_map.184 = (bf16[1,128,256]{2,1,0:T(8,128)(2,1)}, bf16[1,128,256]{2,1,0:T(8,128)(2,1)}, f32[3,768]{1,0:T(4,128)}, f32[128,256]{1,0:T(8,128)}, f32[128,256]{1,0:T(8,128)}) custom-call(bf16[2,224,128]{2,1,0:T(8,128)(2,1)S(1)} %get-tuple-element.32.refs_0_, bf16[2,224,128]{2,1,0:T(8,128)(2,1)S(1)} %collective-permute-done.10.refs_1_.refs_0_, ...), custom_call_target="tpu_custom_call" | custom-call | tf_op jit(solution)/shard_map/pallas_call | solution.py:495
  93.5 2.1 %all-to-all-done.3.own_ref = bf16[16,64,128]{2,1,0:T(8,128)(2,1)S(1)} async-done(((bf16[16,64,128]{2,1,0:T(8,128)(2,1)}), bf16[16,64,128]{2,1,0:T(8,128)(2,1)S(1)}, u32[]{:S(2)}, u32[]{:S(2)}) %all-to-all-start.3) | async-done | bytes 262176 | tf_op jit(solution)/shard_map/all_to_all | solution.py:430
  95.6 3.1 %collective-permute-start.17 = (bf16[16,64,128]{2,1,0:T(8,128)(2,1)S(1)}, bf16[16,64,128]{2,1,0:T(8,128)(2,1)S(1)}, u32[]{:S(2)}, u32[]{:S(2)}) collective-permute-start(bf16[16,64,128]{2,1,0:T(8,128)(2,1)S(1)} %all-to-all-done.3.own_ref), channel_id=1, source_target_pairs={{0,16},{16,0},{1,17},{17,1},{2,18},{18,2},{3,19},{19,3},{4,20},{20... | collective-permute-start | bytes 786440 | tf_op jit(solution)/shard_map/ppermute | solution.py:434
  (47 shorter events, 12.5 us)
Async XLA Ops:
  0.6 36.4 %copy-start.4 = (bf16[128,768]{1,0:T(8,128)(2,1)S(1)}, bf16[128,768]{1,0:T(8,128)(2,1)}, u32[]{:S(2)}) copy-start(bf16[128,768]{1,0:T(8,128)(2,1)} %constant.15.clone.first_back_ref) | copy-start | bytes 589828
  0.6 36.3 %copy-start.5 = (bf16[256,384]{1,0:T(8,128)(2,1)S(1)}, bf16[256,384]{1,0:T(8,128)(2,1)}, u32[]{:S(2)}) copy-start(bf16[256,384]{1,0:T(8,128)(2,1)} %constant.12.clone.first_ref) | copy-start | bytes 589828
  3.2 33.8 %all-to-all-start = ((bf16[256,2,384]{2,1,0:T(2,128)(2,1)}), bf16[256,2,384]{2,1,0:T(2,128)(2,1)S(1)}, u32[]{:S(2)}, u32[]{:S(2)}) async-start(bf16[256,2,384]{2,1,0:T(2,128)(2,1)} %get-tuple-element.30), calls=%async_computation | async-start | bytes 786432 | tf_op jit(solution)/shard_map/all_to_all | solution.py:430
  18.9 6.1 %collective-permute-start.1 = (bf16[128,512]{1,0:T(8,128)(2,1)}, bf16[128,512]{1,0:T(8,128)(2,1)S(1)}, u32[]{:S(2)}, u32[]{:S(2)}) collective-permute-start(bf16[128,512]{1,0:T(8,128)(2,1)} %get-tuple-element.31.refs_0_), channel_id=1, source_target_pairs={{0,3},{1,0},{2,1},{3,2},{16,17},{17,18},{18,19},{19,16},{4,7},{5,4... | collective-permute-start | bytes 393224 | tf_op jit(solution)/shard_map/ppermute | solution.py:445
  20.4 6.0 %collective-permute-start = (bf16[128,512]{1,0:T(8,128)(2,1)}, bf16[128,512]{1,0:T(8,128)(2,1)S(1)}, u32[]{:S(2)}, u32[]{:S(2)}) collective-permute-start(bf16[128,512]{1,0:T(8,128)(2,1)} %get-tuple-element.31.refs_0_), channel_id=1, source_target_pairs={{0,1},{1,2},{2,3},{3,0},{16,19},{17,16},{18,17},{19,18},{4,5},{5,6... | collective-permute-start | bytes 393224 | tf_op jit(solution)/shard_map/ppermute | solution.py:445
  41.6 19.7 %all-to-all-start.1 = ((bf16[32,7,8,128]{3,2,1,0:T(8,128)(2,1)}), bf16[32,7,8,128]{3,2,1,0:T(8,128)(2,1)S(1)}, u32[]{:S(2)}, u32[]{:S(2)}) async-start(bf16[32,7,8,128]{3,2,1,0:T(8,128)(2,1)} %shard_map.181), calls=%async_computation.1 | async-start | bytes 917504 | tf_op jit(solution)/shard_map/all_to_all | solution.py:430
  45.7 5.6 %collective-permute-start.2 = (bf16[128,512]{1,0:T(8,128)(2,1)S(1)}, bf16[128,512]{1,0:T(8,128)(2,1)S(1)}, u32[]{:S(2)}, u32[]{:S(2)}) collective-permute-start(bf16[128,512]{1,0:T(8,128)(2,1)S(1)} %copy-done.6), channel_id=1, source_target_pairs={{0,2},{1,3},{2,0},{3,1},{16,18},{17,19},{18,16},{19,17},{4,6},{5,7... | collective-permute-start | bytes 393224 | tf_op jit(solution)/shard_map/ppermute | solution.py:445
  47.3 6.5 %collective-permute-start.3 = (bf16[128,512]{1,0:T(8,128)(2,1)S(1)}, bf16[128,512]{1,0:T(8,128)(2,1)S(1)}, u32[]{:S(2)}, u32[]{:S(2)}) collective-permute-start(bf16[128,512]{1,0:T(8,128)(2,1)S(1)} %copy-done.6), channel_id=1, source_target_pairs={{0,16},{16,0},{1,17},{17,1},{2,18},{18,2},{3,19},{19,3},{4,20},{20... | collective-permute-start | bytes 393224 | tf_op jit(solution)/shard_map/ppermute | solution.py:434
  51.3 2.9 %collective-permute-start.5 = (bf16[128,512]{1,0:T(8,128)(2,1)S(1)}, bf16[128,512]{1,0:T(8,128)(2,1)S(1)}, u32[]{:S(2)}, u32[]{:S(2)}) collective-permute-start(bf16[128,512]{1,0:T(8,128)(2,1)S(1)} %collective-permute-done.2.refs_2_), channel_id=1, source_target_pairs={{0,16},{16,0},{1,17},{17,1},{2,18},{18,2},{3,19},{19,3},{4,20},{20... | collective-permute-start | bytes 393224 | tf_op jit(solution)/shard_map/ppermute | solution.py:434
  53.3 1.3 %collective-permute-start.6 = (bf16[128,512]{1,0:T(8,128)(2,1)S(1)}, bf16[128,512]{1,0:T(8,128)(2,1)S(1)}, u32[]{:S(2)}, u32[]{:S(2)}) collective-permute-start(bf16[128,512]{1,0:T(8,128)(2,1)S(1)} %collective-permute-done.1.rest_1_.refs_3_), channel_id=1, source_target_pairs={{0,16},{16,0},{1,17},{17,1},{2,18},{18,2},{3,19},{19,3},{4,20},{20... | collective-permute-start | bytes 393224 | tf_op jit(solution)/shard_map/ppermute | solution.py:434
  53.3 1.5 %collective-permute-start.4 = (bf16[128,512]{1,0:T(8,128)(2,1)S(1)}, bf16[128,512]{1,0:T(8,128)(2,1)S(1)}, u32[]{:S(2)}, u32[]{:S(2)}) collective-permute-start(bf16[128,512]{1,0:T(8,128)(2,1)S(1)} %collective-permute-done.rest_0_.refs_1_), channel_id=1, source_target_pairs={{0,16},{16,0},{1,17},{17,1},{2,18},{18,2},{3,19},{19,3},{4,20},{20... | collective-permute-start | bytes 393224 | tf_op jit(solution)/shard_map/ppermute | solution.py:434
  61.9 2.8 %collective-permute-start.7 = (f32[32,256]{1,0:T(8,128)S(1)}, f32[32,256]{1,0:T(8,128)S(1)}, u32[]{:S(2)}, u32[]{:S(2)}) collective-permute-start(f32[32,256]{1,0:T(8,128)S(1)} %get-tuple-element.34), channel_id=1, source_target_pairs={{0,32},{32,64},{64,96},{96,0},{16,112},{48,16},{80,48},{112,80},{1... | collective-permute-start | bytes 98312 | tf_op jit(solution)/shard_map/ppermute | solution.py:445
  62.8 4.3 %collective-permute-start.8 = (f32[32,256]{1,0:T(8,128)S(1)}, f32[32,256]{1,0:T(8,128)S(1)}, u32[]{:S(2)}, u32[]{:S(2)}) collective-permute-start(f32[32,256]{1,0:T(8,128)S(1)} %get-tuple-element.35), channel_id=1, source_target_pairs={{0,64},{32,96},{64,0},{96,32},{16,80},{48,112},{80,16},{112,48},{1... | collective-permute-start | bytes 98312 | tf_op jit(solution)/shard_map/ppermute | solution.py:445
  63.9 4.0 %collective-permute-start.9 = (f32[32,256]{1,0:T(8,128)S(1)}, f32[32,256]{1,0:T(8,128)S(1)}, u32[]{:S(2)}, u32[]{:S(2)}) collective-permute-start(f32[32,256]{1,0:T(8,128)S(1)} %get-tuple-element.36), channel_id=1, source_target_pairs={{0,96},{32,0},{64,32},{96,64},{16,48},{48,80},{80,112},{112,16},{1... | collective-permute-start | bytes 98312 | tf_op jit(solution)/shard_map/ppermute | solution.py:445
  68.6 15.3 %all-to-all-start.2 = ((bf16[8,64,128]{2,1,0:T(8,128)(2,1)}), bf16[8,64,128]{2,1,0:T(8,128)(2,1)S(1)}, u32[]{:S(2)}, u32[]{:S(2)}) async-start(bf16[8,64,128]{2,1,0:T(8,128)(2,1)} %get-tuple-element.45), calls=%async_computation.2 | async-start | bytes 262144 | tf_op jit(solution)/shard_map/all_to_all | solution.py:430
  71.9 6.0 %collective-permute-start.10 = (bf16[2,224,128]{2,1,0:T(8,128)(2,1)S(1)}, bf16[2,224,128]{2,1,0:T(8,128)(2,1)S(1)}, u32[]{:S(2)}, u32[]{:S(2)}) collective-permute-start(bf16[2,224,128]{2,1,0:T(8,128)(2,1)S(1)} %get-tuple-element.40), channel_id=1, source_target_pairs={{0,1},{1,2},{2,3},{3,0},{16,19},{17,16},{18,17},{19,18},{4,5},{5,6... | collective-permute-start | bytes 344072 | tf_op jit(solution)/shard_map/ppermute | solution.py:445
  74.9 6.7 %collective-permute-start.11 = (bf16[2,224,128]{2,1,0:T(8,128)(2,1)S(1)}, bf16[2,224,128]{2,1,0:T(8,128)(2,1)S(1)}, u32[]{:S(2)}, u32[]{:S(2)}) collective-permute-start(bf16[2,224,128]{2,1,0:T(8,128)(2,1)S(1)} %get-tuple-element.41), channel_id=1, source_target_pairs={{0,2},{1,3},{2,0},{3,1},{16,18},{17,19},{18,16},{19,17},{4,6},{5,7... | collective-permute-start | bytes 344072 | tf_op jit(solution)/shard_map/ppermute | solution.py:445
  75.2 8.6 %collective-permute-start.12 = (bf16[2,224,128]{2,1,0:T(8,128)(2,1)S(1)}, bf16[2,224,128]{2,1,0:T(8,128)(2,1)S(1)}, u32[]{:S(2)}, u32[]{:S(2)}) collective-permute-start(bf16[2,224,128]{2,1,0:T(8,128)(2,1)S(1)} %get-tuple-element.42), channel_id=1, source_target_pairs={{0,3},{1,0},{2,1},{3,2},{16,17},{17,18},{18,19},{19,16},{4,7},{5,4... | collective-permute-start | bytes 344072 | tf_op jit(solution)/shard_map/ppermute | solution.py:445
  84.6 11.0 %all-to-all-start.3 = ((bf16[16,64,128]{2,1,0:T(8,128)(2,1)}), bf16[16,64,128]{2,1,0:T(8,128)(2,1)S(1)}, u32[]{:S(2)}, u32[]{:S(2)}) async-start(bf16[16,64,128]{2,1,0:T(8,128)(2,1)} %shard_map.185), calls=%async_computation.3 | async-start | bytes 524288 | tf_op jit(solution)/shard_map/all_to_all | solution.py:430
  88.3 3.0 %collective-permute-start.13 = (bf16[2,224,128]{2,1,0:T(8,128)(2,1)S(1)}, bf16[2,224,128]{2,1,0:T(8,128)(2,1)S(1)}, u32[]{:S(2)}, u32[]{:S(2)}) collective-permute-start(bf16[2,224,128]{2,1,0:T(8,128)(2,1)S(1)} %get-tuple-element.32.refs_0_), channel_id=1, source_target_pairs={{0,16},{16,0},{1,17},{17,1},{2,18},{18,2},{3,19},{19,3},{4,20},{20... | collective-permute-start | bytes 344072 | tf_op jit(solution)/shard_map/ppermute | solution.py:434
  90.3 1.3 %collective-permute-start.14 = (bf16[2,224,128]{2,1,0:T(8,128)(2,1)S(1)}, bf16[2,224,128]{2,1,0:T(8,128)(2,1)S(1)}, u32[]{:S(2)}, u32[]{:S(2)}) collective-permute-start(bf16[2,224,128]{2,1,0:T(8,128)(2,1)S(1)} %collective-permute-done.10.refs_1_.refs_0_), channel_id=1, source_target_pairs={{0,16},{16,0},{1,17},{17,1},{2,18},{18,2},{3,19},{19,3},{4,20},{20... | collective-permute-start | bytes 344072 | tf_op jit(solution)/shard_map/ppermute | solution.py:434
  90.4 1.4 %collective-permute-start.15 = (bf16[2,224,128]{2,1,0:T(8,128)(2,1)S(1)}, bf16[2,224,128]{2,1,0:T(8,128)(2,1)S(1)}, u32[]{:S(2)}, u32[]{:S(2)}) collective-permute-start(bf16[2,224,128]{2,1,0:T(8,128)(2,1)S(1)} %collective-permute-done.11.refs_2_.refs_1_), channel_id=1, source_target_pairs={{0,16},{16,0},{1,17},{17,1},{2,18},{18,2},{3,19},{19,3},{4,20},{20... | collective-permute-start | bytes 344072 | tf_op jit(solution)/shard_map/ppermute | solution.py:434
  90.8 1.3 %collective-permute-start.16 = (bf16[2,224,128]{2,1,0:T(8,128)(2,1)S(1)}, bf16[2,224,128]{2,1,0:T(8,128)(2,1)S(1)}, u32[]{:S(2)}, u32[]{:S(2)}) collective-permute-start(bf16[2,224,128]{2,1,0:T(8,128)(2,1)S(1)} %collective-permute-done.12.refs_3_.refs_2_), channel_id=1, source_target_pairs={{0,16},{16,0},{1,17},{17,1},{2,18},{18,2},{3,19},{19,3},{4,20},{20... | collective-permute-start | bytes 344072 | tf_op jit(solution)/shard_map/ppermute | solution.py:434
  95.6 4.3 %collective-permute-start.17 = (bf16[16,64,128]{2,1,0:T(8,128)(2,1)S(1)}, bf16[16,64,128]{2,1,0:T(8,128)(2,1)S(1)}, u32[]{:S(2)}, u32[]{:S(2)}) collective-permute-start(bf16[16,64,128]{2,1,0:T(8,128)(2,1)S(1)} %all-to-all-done.3.own_ref), channel_id=1, source_target_pairs={{0,16},{16,0},{1,17},{17,1},{2,18},{18,2},{3,19},{19,3},{4,20},{20... | collective-permute-start | bytes 786440 | tf_op jit(solution)/shard_map/ppermute | solution.py:434
  (8 other events, 195.7 us)

commit v9 on v8

--- a/solution.py
+++ b/solution.py
@@ -475,21 +475,21 @@
         [pltpu.VMEM((32 * 7 * 8, rows), f32), pltpu.VMEM((4, 32, width), f32)],
     )(halfway, *gathered)
     part = [found[0]] + [ring(found[distance], "x", distance) for distance in (1, 2, 3)]
-    leaving = found[5:]
+    far = ring(found[6], "y", 2)
     part, *leaving = call(
         add_x_kernel,
-        (shape((8, 64, rows), bf16),) + (shape(leaving[0].shape, bf16),) * 3,
+        (shape((8, 64, rows), bf16),) + (shape(found[5].shape, bf16),) * 2,
         in_specs=specs(*[pltpu.VMEM] * 4, *[pl.ANY] * 3),
-        out_specs=specs(pltpu.VMEM, *[pl.ANY] * 3),
-        input_output_aliases={4: 1, 5: 2, 6: 3},
-    )(*part, *leaving)
-    arrived = [found[4]] + [ring(x, "y", 1 + i) for i, x in enumerate(leaving)]
+        out_specs=specs(pltpu.VMEM, *[pl.ANY] * 2),
+        input_output_aliases={5: 1, 6: 2},
+    )(*part, far, found[5], found[7])
+    arrived = [found[4], ring(leaving[0], "y", 1), far, ring(leaving[1], "y", 3)]
     part = exchange(part, ("zh", "zl"))
     part = call(
         functools.partial(add_z_kernel, scale),
         shape((16, 64, rows), bf16),
-        in_specs=specs(pltpu.VMEM, *[pl.ANY] * 3),
-    )(part, *arrived[1:])
+        in_specs=specs(pltpu.VMEM, *[pl.ANY] * 2),
+    )(part, arrived[1], arrived[3])
     arrived += [swap_core(x) for x in arrived]
     part = exchange(part, ("x", "y"))
     outputs, grad_inputs, grad_short, grad_one, grad_two = call(

time: 102 us -> 103 us (level)
  starting transfers between devices: 45.8 us -> 50.8 us
  waiting for transfers between devices: 42.7 us -> 39.4 us
    ppermute x9, starting transfers between devices: 8.21 us -> 13 us  [swap_core(): return lax.ppermute(x, 'core', [(0, 1), (1, 0)])]
    ppermute x9, waiting for transfers between devices: 20 us -> 16.1 us  [ring(): return lax.ppermute(x, axes, route)]
  transfers between devices with their start and end apart: 22 -> 22, of which waited for: 20 -> 19; matrix products, arithmetic and copies ran while one was open for 0% -> 0% of each run, Pallas kernels for 1% -> 1%
where the time goes in v9:
time: 103 us
  starting transfers between devices  50.8 us (49%)
  waiting for transfers between devices  39.4 us (38%)
  Pallas kernels  11.8 us (11%)
    all_to_all x4, starting transfers between devices, exchange(): return lax.all_to_all(x, axes, split_axis=0, concat_axis=0, tiled=True)  26.7 us
    all_to_all x4, waiting for transfers between devices, exchange(): return lax.all_to_all(x, axes, split_axis=0, concat_axis=0, tiled=True)  19.9 us
    ppermute x9, waiting for transfers between devices, ring(): return lax.ppermute(x, axes, route)  16.1 us
    ppermute x9, starting transfers between devices, swap_core(): return lax.ppermute(x, 'core', [(0, 1), (1, 0)])  13 us
    ppermute x9, starting transfers between devices, ring(): return lax.ppermute(x, axes, route)  11.2 us
    pallas_call x1, Pallas kernels, per_device(): call(convolve_kernel, shape((32, 7, 8, rows), bf16), [pltpu.VMEM((3, 2 *...  4.64 us
    ppermute x9, waiting for transfers between devices, swap_core(): return lax.ppermute(x, 'core', [(0, 1), (1, 0)])  3.41 us
    pallas_call x1, Pallas kernels, per_device(): call(pack_kernel, (shape((width, 2, 3 * rows), bf16), shape((rows, 2 * wi...  2.53 us
  transfers between devices with their start and end apart: 22, of which 19 were waited for; matrix products, arithmetic and copies ran while one was open for 0% of the time, Pallas kernels for 1%

profile of v9, /device:TPU:1, one launch (start us, length us, event | category | flops | bytes accessed | tf_op | source)
XLA Modules:
  0.0 102.9 jit_solution(15681601991449359410)
XLA Ops:
  0.7 2.5 %shard_map.180 = (bf16[256,2,384]{2,1,0:T(2,128)(2,1)}, bf16[128,512]{1,0:T(8,128)(2,1)}) custom-call(bf16[1,128,256]{2,1,0:T(8,128)(2,1)} %seq_ref.1, bf16[256,768]{1,0:T(8,128)(2,1)} %refs_8_.1, f32[128,256]{1,0:T(8,128)} %one_ref.1, f32[128,256]{1,0:T(8,128)} %two_ref.1, bf16[256,256]{1,0:T(8,128)(2,1)} %refs_9_.1, bf16[1,128,256]{2,1,0:T(8,128)(2,1)} %grad_ref.1), custom_call_target="tpu_custom_call" | custom-call | tf_op jit(solution)/shard_map/pallas_call | solution.py:455
  3.2 15.7 %all-to-all-start = ((bf16[256,2,384]{2,1,0:T(2,128)(2,1)}), bf16[256,2,384]{2,1,0:T(2,128)(2,1)S(1)}, u32[]{:S(2)}, u32[]{:S(2)}) async-start(bf16[256,2,384]{2,1,0:T(2,128)(2,1)} %get-tuple-element.29), calls=%async_computation | async-start | bytes 786432 | tf_op jit(solution)/shard_map/all_to_all | solution.py:430
  18.9 1.5 %collective-permute-start.1 = (bf16[128,512]{1,0:T(8,128)(2,1)}, bf16[128,512]{1,0:T(8,128)(2,1)S(1)}, u32[]{:S(2)}, u32[]{:S(2)}) collective-permute-start(bf16[128,512]{1,0:T(8,128)(2,1)} %get-tuple-element.30.refs_0_), channel_id=1, source_target_pairs={{0,3},{1,0},{2,1},{3,2},{16,17},{17,18},{18,19},{19,16},{4,7},{5,4... | collective-permute-start | bytes 393224 | tf_op jit(solution)/shard_map/ppermute | solution.py:445
  20.4 1.4 %collective-permute-start = (bf16[128,512]{1,0:T(8,128)(2,1)}, bf16[128,512]{1,0:T(8,128)(2,1)S(1)}, u32[]{:S(2)}, u32[]{:S(2)}) collective-permute-start(bf16[128,512]{1,0:T(8,128)(2,1)} %get-tuple-element.30.refs_0_), channel_id=1, source_target_pairs={{0,1},{1,2},{2,3},{3,0},{16,19},{17,16},{18,17},{19,18},{4,5},{5,6... | collective-permute-start | bytes 393224 | tf_op jit(solution)/shard_map/ppermute | solution.py:445
  21.7 3.3 %collective-permute-done.1.rest_1_.refs_3_ = bf16[128,512]{1,0:T(8,128)(2,1)S(1)} collective-permute-done((bf16[128,512]{1,0:T(8,128)(2,1)}, bf16[128,512]{1,0:T(8,128)(2,1)S(1)}, u32[]{:S(2)}, u32[]{:S(2)}) %collective-permute-start.1) | collective-permute-done | bytes 131104 | tf_op jit(solution)/shard_map/ppermute | solution.py:445
  25.0 1.3 %collective-permute-done.rest_0_.refs_1_ = bf16[128,512]{1,0:T(8,128)(2,1)S(1)} collective-permute-done((bf16[128,512]{1,0:T(8,128)(2,1)}, bf16[128,512]{1,0:T(8,128)(2,1)S(1)}, u32[]{:S(2)}, u32[]{:S(2)}) %collective-permute-start) | collective-permute-done | bytes 131104 | tf_op jit(solution)/shard_map/ppermute | solution.py:445
  26.3 10.7 %all-to-all-done.in_ref = bf16[256,2,384]{2,1,0:T(2,128)(2,1)S(1)} async-done(((bf16[256,2,384]{2,1,0:T(2,128)(2,1)}), bf16[256,2,384]{2,1,0:T(2,128)(2,1)S(1)}, u32[]{:S(2)}, u32[]{:S(2)}) %all-to-all-start) | async-done | bytes 393248 | tf_op jit(solution)/shard_map/all_to_all | solution.py:430
  37.0 4.6 %shard_map.181 = bf16[32,7,8,128]{3,2,1,0:T(8,128)(2,1)} custom-call(bf16[256,2,384]{2,1,0:T(2,128)(2,1)S(1)} %all-to-all-done.in_ref, f32[3,768]{1,0:T(4,128)S(1)} %copy-done.9, bf16[256,384]{1,0:T(8,128)(2,1)S(1)} %copy-done.5, bf16[768,256]{1,0:T(8,128)(2,1)S(1)} %copy-done.3, bf16[768,256]{1,0:T(8,128)(2,1)S(1)} %copy-done.2, ...), custom_call_target="tpu_custom_call" | custom-call | tf_op jit(solution)/shard_map/pallas_call | solution.py:465
  41.7 4.0 %all-to-all-start.1 = ((bf16[32,7,8,128]{3,2,1,0:T(8,128)(2,1)}), bf16[32,7,8,128]{3,2,1,0:T(8,128)(2,1)S(1)}, u32[]{:S(2)}, u32[]{:S(2)}) async-start(bf16[32,7,8,128]{3,2,1,0:T(8,128)(2,1)} %shard_map.181), calls=%async_computation.1 | async-start | bytes 917504 | tf_op jit(solution)/shard_map/all_to_all | solution.py:430
  45.7 1.6 %collective-permute-start.2 = (bf16[128,512]{1,0:T(8,128)(2,1)S(1)}, bf16[128,512]{1,0:T(8,128)(2,1)S(1)}, u32[]{:S(2)}, u32[]{:S(2)}) collective-permute-start(bf16[128,512]{1,0:T(8,128)(2,1)S(1)} %copy-done.6), channel_id=1, source_target_pairs={{0,2},{1,3},{2,0},{3,1},{16,18},{17,19},{18,16},{19,17},{4,6},{5,7... | collective-permute-start | bytes 393224 | tf_op jit(solution)/shard_map/ppermute | solution.py:445
  47.3 4.0 %collective-permute-done.2.refs_2_ = bf16[128,512]{1,0:T(8,128)(2,1)S(1)} collective-permute-done((bf16[128,512]{1,0:T(8,128)(2,1)S(1)}, bf16[128,512]{1,0:T(8,128)(2,1)S(1)}, u32[]{:S(2)}, u32[]{:S(2)}) %collective-permute-start.2) | collective-permute-done | bytes 131104 | tf_op jit(solution)/shard_map/ppermute | solution.py:445
  51.3 1.9 %collective-permute-start.5 = (bf16[128,512]{1,0:T(8,128)(2,1)S(1)}, bf16[128,512]{1,0:T(8,128)(2,1)S(1)}, u32[]{:S(2)}, u32[]{:S(2)}) collective-permute-start(bf16[128,512]{1,0:T(8,128)(2,1)S(1)} %collective-permute-done.2.refs_2_), channel_id=1, source_target_pairs={{0,16},{16,0},{1,17},{17,1},{2,18},{18,2},{3,19},{19,3},{4,20},{20... | collective-permute-start | bytes 393224 | tf_op jit(solution)/shard_map/ppermute | solution.py:434
  54.8 6.6 %all-to-all-done.1.in_ref = bf16[32,7,8,128]{3,2,1,0:T(8,128)(2,1)S(1)} async-done(((bf16[32,7,8,128]{3,2,1,0:T(8,128)(2,1)}), bf16[32,7,8,128]{3,2,1,0:T(8,128)(2,1)S(1)}, u32[]{:S(2)}, u32[]{:S(2)}) %all-to-all-start.1) | async-done | bytes 458784 | tf_op jit(solution)/shard_map/all_to_all | solution.py:430
  61.9 3.2 %collective-permute-start.10 = (bf16[2,224,128]{2,1,0:T(8,128)(2,1)S(1)}, bf16[2,224,128]{2,1,0:T(8,128)(2,1)S(1)}, u32[]{:S(2)}, u32[]{:S(2)}) collective-permute-start(bf16[2,224,128]{2,1,0:T(8,128)(2,1)S(1)} %get-tuple-element.36), channel_id=1, source_target_pairs={{0,2},{1,3},{2,0},{3,1},{16,18},{17,19},{18,16},{19,17},{4,6},{5,7... | collective-permute-start | bytes 344072 | tf_op jit(solution)/shard_map/ppermute | solution.py:445
  67.9 2.3 %collective-permute-done.8.refs_2_ = f32[32,256]{1,0:T(8,128)S(1)} collective-permute-done((f32[32,256]{1,0:T(8,128)S(1)}, f32[32,256]{1,0:T(8,128)S(1)}, u32[]{:S(2)}, u32[]{:S(2)}) %collective-permute-start.8) | collective-permute-done | bytes 32800 | tf_op jit(solution)/shard_map/ppermute | solution.py:445
  71.8 3.4 %all-to-all-start.2 = ((bf16[8,64,128]{2,1,0:T(8,128)(2,1)}), bf16[8,64,128]{2,1,0:T(8,128)(2,1)S(1)}, u32[]{:S(2)}, u32[]{:S(2)}) async-start(bf16[8,64,128]{2,1,0:T(8,128)(2,1)} %get-tuple-element.43), calls=%async_computation.2 | async-start | bytes 262144 | tf_op jit(solution)/shard_map/all_to_all | solution.py:430
  75.3 1.5 %collective-permute-start.12 = (bf16[2,224,128]{2,1,0:T(8,128)(2,1)S(1)}, bf16[2,224,128]{2,1,0:T(8,128)(2,1)S(1)}, u32[]{:S(2)}, u32[]{:S(2)}) collective-permute-start(bf16[2,224,128]{2,1,0:T(8,128)(2,1)S(1)} %get-tuple-element.40), channel_id=1, source_target_pairs={{0,3},{1,0},{2,1},{3,2},{16,17},{17,18},{18,19},{19,16},{4,7},{5,4... | collective-permute-start | bytes 344072 | tf_op jit(solution)/shard_map/ppermute | solution.py:445
  76.7 2.2 %collective-permute-done.11.refs_1_.refs_0_ = bf16[2,224,128]{2,1,0:T(8,128)(2,1)S(1)} collective-permute-done((bf16[2,224,128]{2,1,0:T(8,128)(2,1)S(1)}, bf16[2,224,128]{2,1,0:T(8,128)(2,1)S(1)}, u32[]{:S(2)}, u32[]{:S(2)}) %collective-permute-start.11) | collective-permute-done | bytes 114720 | tf_op jit(solution)/shard_map/ppermute | solution.py:445
  80.2 2.6 %all-to-all-done.2.in_ref = bf16[8,64,128]{2,1,0:T(8,128)(2,1)S(1)} async-done(((bf16[8,64,128]{2,1,0:T(8,128)(2,1)}), bf16[8,64,128]{2,1,0:T(8,128)(2,1)S(1)}, u32[]{:S(2)}, u32[]{:S(2)}) %all-to-all-start.2) | async-done | bytes 131104 | tf_op jit(solution)/shard_map/all_to_all | solution.py:430
  83.6 3.7 %all-to-all-start.3 = ((bf16[16,64,128]{2,1,0:T(8,128)(2,1)}), bf16[16,64,128]{2,1,0:T(8,128)(2,1)S(1)}, u32[]{:S(2)}, u32[]{:S(2)}) async-start(bf16[16,64,128]{2,1,0:T(8,128)(2,1)} %shard_map.185), calls=%async_computation.3 | async-start | bytes 524288 | tf_op jit(solution)/shard_map/all_to_all | solution.py:430
  87.3 4.7 %collective-permute-start.13 = (bf16[2,224,128]{2,1,0:T(8,128)(2,1)S(1)}, bf16[2,224,128]{2,1,0:T(8,128)(2,1)S(1)}, u32[]{:S(2)}, u32[]{:S(2)}) collective-permute-start(bf16[2,224,128]{2,1,0:T(8,128)(2,1)S(1)} %get-tuple-element.31.refs_0_), channel_id=1, source_target_pairs={{0,16},{16,0},{1,17},{17,1},{2,18},{18,2},{3,19},{19,3},{4,20},{20... | collective-permute-start | bytes 344072 | tf_op jit(solution)/shard_map/ppermute | solution.py:434
  93.9 1.4 %shard_map.184 = (bf16[1,128,256]{2,1,0:T(8,128)(2,1)}, bf16[1,128,256]{2,1,0:T(8,128)(2,1)}, f32[3,768]{1,0:T(4,128)}, f32[128,256]{1,0:T(8,128)}, f32[128,256]{1,0:T(8,128)}) custom-call(bf16[2,224,128]{2,1,0:T(8,128)(2,1)S(1)} %get-tuple-element.31.refs_0_, bf16[2,224,128]{2,1,0:T(8,128)(2,1)S(1)} %collective-permute-done.11.refs_1_.refs_0_, ...), custom_call_target="tpu_custom_call" | custom-call | tf_op jit(solution)/shard_map/pallas_call | solution.py:495
  95.2 5.2 %collective-permute-start.17 = (bf16[16,64,128]{2,1,0:T(8,128)(2,1)S(1)}, bf16[16,64,128]{2,1,0:T(8,128)(2,1)S(1)}, u32[]{:S(2)}, u32[]{:S(2)}) collective-permute-start(bf16[16,64,128]{2,1,0:T(8,128)(2,1)S(1)} %all-to-all-done.3.own_ref), channel_id=1, source_target_pairs={{0,16},{16,0},{1,17},{17,1},{2,18},{18,2},{3,19},{19,3},{4,20},{20... | collective-permute-start | bytes 786440 | tf_op jit(solution)/shard_map/ppermute | solution.py:434
  101.6 1.3 %shard_map.186 = (f32[256,768]{1,0:T(8,128)}, f32[256,256]{1,0:T(8,128)}) custom-call(bf16[16,64,128]{2,1,0:T(8,128)(2,1)S(1)} %all-to-all-done.3.own_ref, bf16[16,64,128]{2,1,0:T(8,128)(2,1)S(1)} %collective-permute-done.17.other_ref), custom_call_target="tpu_custom_call" | custom-call | tf_op jit(solution)/shard_map/pallas_call | solution.py:506
  (47 shorter events, 11.6 us)
Async XLA Ops:
  0.6 36.4 %copy-start.4 = (bf16[128,768]{1,0:T(8,128)(2,1)S(1)}, bf16[128,768]{1,0:T(8,128)(2,1)}, u32[]{:S(2)}) copy-start(bf16[128,768]{1,0:T(8,128)(2,1)} %constant.15.clone.first_back_ref) | copy-start | bytes 589828
  0.6 36.3 %copy-start.5 = (bf16[256,384]{1,0:T(8,128)(2,1)S(1)}, bf16[256,384]{1,0:T(8,128)(2,1)}, u32[]{:S(2)}) copy-start(bf16[256,384]{1,0:T(8,128)(2,1)} %constant.12.clone.first_ref) | copy-start | bytes 589828
  3.2 33.8 %all-to-all-start = ((bf16[256,2,384]{2,1,0:T(2,128)(2,1)}), bf16[256,2,384]{2,1,0:T(2,128)(2,1)S(1)}, u32[]{:S(2)}, u32[]{:S(2)}) async-start(bf16[256,2,384]{2,1,0:T(2,128)(2,1)} %get-tuple-element.29), calls=%async_computation | async-start | bytes 786432 | tf_op jit(solution)/shard_map/all_to_all | solution.py:430
  18.9 6.1 %collective-permute-start.1 = (bf16[128,512]{1,0:T(8,128)(2,1)}, bf16[128,512]{1,0:T(8,128)(2,1)S(1)}, u32[]{:S(2)}, u32[]{:S(2)}) collective-permute-start(bf16[128,512]{1,0:T(8,128)(2,1)} %get-tuple-element.30.refs_0_), channel_id=1, source_target_pairs={{0,3},{1,0},{2,1},{3,2},{16,17},{17,18},{18,19},{19,16},{4,7},{5,4... | collective-permute-start | bytes 393224 | tf_op jit(solution)/shard_map/ppermute | solution.py:445
  20.4 6.0 %collective-permute-start = (bf16[128,512]{1,0:T(8,128)(2,1)}, bf16[128,512]{1,0:T(8,128)(2,1)S(1)}, u32[]{:S(2)}, u32[]{:S(2)}) collective-permute-start(bf16[128,512]{1,0:T(8,128)(2,1)} %get-tuple-element.30.refs_0_), channel_id=1, source_target_pairs={{0,1},{1,2},{2,3},{3,0},{16,19},{17,16},{18,17},{19,18},{4,5},{5,6... | collective-permute-start | bytes 393224 | tf_op jit(solution)/shard_map/ppermute | solution.py:445
  41.7 19.7 %all-to-all-start.1 = ((bf16[32,7,8,128]{3,2,1,0:T(8,128)(2,1)}), bf16[32,7,8,128]{3,2,1,0:T(8,128)(2,1)S(1)}, u32[]{:S(2)}, u32[]{:S(2)}) async-start(bf16[32,7,8,128]{3,2,1,0:T(8,128)(2,1)} %shard_map.181), calls=%async_computation.1 | async-start | bytes 917504 | tf_op jit(solution)/shard_map/all_to_all | solution.py:430
  45.7 5.6 %collective-permute-start.2 = (bf16[128,512]{1,0:T(8,128)(2,1)S(1)}, bf16[128,512]{1,0:T(8,128)(2,1)S(1)}, u32[]{:S(2)}, u32[]{:S(2)}) collective-permute-start(bf16[128,512]{1,0:T(8,128)(2,1)S(1)} %copy-done.6), channel_id=1, source_target_pairs={{0,2},{1,3},{2,0},{3,1},{16,18},{17,19},{18,16},{19,17},{4,6},{5,7... | collective-permute-start | bytes 393224 | tf_op jit(solution)/shard_map/ppermute | solution.py:445
  47.3 6.5 %collective-permute-start.3 = (bf16[128,512]{1,0:T(8,128)(2,1)S(1)}, bf16[128,512]{1,0:T(8,128)(2,1)S(1)}, u32[]{:S(2)}, u32[]{:S(2)}) collective-permute-start(bf16[128,512]{1,0:T(8,128)(2,1)S(1)} %copy-done.6), channel_id=1, source_target_pairs={{0,16},{16,0},{1,17},{17,1},{2,18},{18,2},{3,19},{19,3},{4,20},{20... | collective-permute-start | bytes 393224 | tf_op jit(solution)/shard_map/ppermute | solution.py:434
  51.3 2.9 %collective-permute-start.5 = (bf16[128,512]{1,0:T(8,128)(2,1)S(1)}, bf16[128,512]{1,0:T(8,128)(2,1)S(1)}, u32[]{:S(2)}, u32[]{:S(2)}) collective-permute-start(bf16[128,512]{1,0:T(8,128)(2,1)S(1)} %collective-permute-done.2.refs_2_), channel_id=1, source_target_pairs={{0,16},{16,0},{1,17},{17,1},{2,18},{18,2},{3,19},{19,3},{4,20},{20... | collective-permute-start | bytes 393224 | tf_op jit(solution)/shard_map/ppermute | solution.py:434
  53.3 1.3 %collective-permute-start.6 = (bf16[128,512]{1,0:T(8,128)(2,1)S(1)}, bf16[128,512]{1,0:T(8,128)(2,1)S(1)}, u32[]{:S(2)}, u32[]{:S(2)}) collective-permute-start(bf16[128,512]{1,0:T(8,128)(2,1)S(1)} %collective-permute-done.1.rest_1_.refs_3_), channel_id=1, source_target_pairs={{0,16},{16,0},{1,17},{17,1},{2,18},{18,2},{3,19},{19,3},{4,20},{20... | collective-permute-start | bytes 393224 | tf_op jit(solution)/shard_map/ppermute | solution.py:434
  53.3 1.5 %collective-permute-start.4 = (bf16[128,512]{1,0:T(8,128)(2,1)S(1)}, bf16[128,512]{1,0:T(8,128)(2,1)S(1)}, u32[]{:S(2)}, u32[]{:S(2)}) collective-permute-start(bf16[128,512]{1,0:T(8,128)(2,1)S(1)} %collective-permute-done.rest_0_.refs_1_), channel_id=1, source_target_pairs={{0,16},{16,0},{1,17},{17,1},{2,18},{18,2},{3,19},{19,3},{4,20},{20... | collective-permute-start | bytes 393224 | tf_op jit(solution)/shard_map/ppermute | solution.py:434
  61.9 9.2 %collective-permute-start.10 = (bf16[2,224,128]{2,1,0:T(8,128)(2,1)S(1)}, bf16[2,224,128]{2,1,0:T(8,128)(2,1)S(1)}, u32[]{:S(2)}, u32[]{:S(2)}) collective-permute-start(bf16[2,224,128]{2,1,0:T(8,128)(2,1)S(1)} %get-tuple-element.36), channel_id=1, source_target_pairs={{0,2},{1,3},{2,0},{3,1},{16,18},{17,19},{18,16},{19,17},{4,6},{5,7... | collective-permute-start | bytes 344072 | tf_op jit(solution)/shard_map/ppermute | solution.py:445
  65.1 2.8 %collective-permute-start.7 = (f32[32,256]{1,0:T(8,128)S(1)}, f32[32,256]{1,0:T(8,128)S(1)}, u32[]{:S(2)}, u32[]{:S(2)}) collective-permute-start(f32[32,256]{1,0:T(8,128)S(1)} %get-tuple-element.33), channel_id=1, source_target_pairs={{0,32},{32,64},{64,96},{96,0},{16,112},{48,16},{80,48},{112,80},{1... | collective-permute-start | bytes 98312 | tf_op jit(solution)/shard_map/ppermute | solution.py:445
  65.7 4.6 %collective-permute-start.8 = (f32[32,256]{1,0:T(8,128)S(1)}, f32[32,256]{1,0:T(8,128)S(1)}, u32[]{:S(2)}, u32[]{:S(2)}) collective-permute-start(f32[32,256]{1,0:T(8,128)S(1)} %get-tuple-element.34), channel_id=1, source_target_pairs={{0,64},{32,96},{64,0},{96,32},{16,80},{48,112},{80,16},{112,48},{1... | collective-permute-start | bytes 98312 | tf_op jit(solution)/shard_map/ppermute | solution.py:445
  66.9 4.3 %collective-permute-start.9 = (f32[32,256]{1,0:T(8,128)S(1)}, f32[32,256]{1,0:T(8,128)S(1)}, u32[]{:S(2)}, u32[]{:S(2)}) collective-permute-start(f32[32,256]{1,0:T(8,128)S(1)} %get-tuple-element.35), channel_id=1, source_target_pairs={{0,96},{32,0},{64,32},{96,64},{16,48},{48,80},{80,112},{112,16},{1... | collective-permute-start | bytes 98312 | tf_op jit(solution)/shard_map/ppermute | solution.py:445
  71.8 11.0 %all-to-all-start.2 = ((bf16[8,64,128]{2,1,0:T(8,128)(2,1)}), bf16[8,64,128]{2,1,0:T(8,128)(2,1)S(1)}, u32[]{:S(2)}, u32[]{:S(2)}) async-start(bf16[8,64,128]{2,1,0:T(8,128)(2,1)} %get-tuple-element.43), calls=%async_computation.2 | async-start | bytes 262144 | tf_op jit(solution)/shard_map/all_to_all | solution.py:430
  75.2 3.7 %collective-permute-start.11 = (bf16[2,224,128]{2,1,0:T(8,128)(2,1)S(1)}, bf16[2,224,128]{2,1,0:T(8,128)(2,1)S(1)}, u32[]{:S(2)}, u32[]{:S(2)}) collective-permute-start(bf16[2,224,128]{2,1,0:T(8,128)(2,1)S(1)} %get-tuple-element.39), channel_id=1, source_target_pairs={{0,1},{1,2},{2,3},{3,0},{16,19},{17,16},{18,17},{19,18},{4,5},{5,6... | collective-permute-start | bytes 344072 | tf_op jit(solution)/shard_map/ppermute | solution.py:445
  75.3 4.9 %collective-permute-start.12 = (bf16[2,224,128]{2,1,0:T(8,128)(2,1)S(1)}, bf16[2,224,128]{2,1,0:T(8,128)(2,1)S(1)}, u32[]{:S(2)}, u32[]{:S(2)}) collective-permute-start(bf16[2,224,128]{2,1,0:T(8,128)(2,1)S(1)} %get-tuple-element.40), channel_id=1, source_target_pairs={{0,3},{1,0},{2,1},{3,2},{16,17},{17,18},{18,19},{19,16},{4,7},{5,4... | collective-permute-start | bytes 344072 | tf_op jit(solution)/shard_map/ppermute | solution.py:445
  83.6 11.6 %all-to-all-start.3 = ((bf16[16,64,128]{2,1,0:T(8,128)(2,1)}), bf16[16,64,128]{2,1,0:T(8,128)(2,1)S(1)}, u32[]{:S(2)}, u32[]{:S(2)}) async-start(bf16[16,64,128]{2,1,0:T(8,128)(2,1)} %shard_map.185), calls=%async_computation.3 | async-start | bytes 524288 | tf_op jit(solution)/shard_map/all_to_all | solution.py:430
  87.3 5.7 %collective-permute-start.13 = (bf16[2,224,128]{2,1,0:T(8,128)(2,1)S(1)}, bf16[2,224,128]{2,1,0:T(8,128)(2,1)S(1)}, u32[]{:S(2)}, u32[]{:S(2)}) collective-permute-start(bf16[2,224,128]{2,1,0:T(8,128)(2,1)S(1)} %get-tuple-element.31.refs_0_), channel_id=1, source_target_pairs={{0,16},{16,0},{1,17},{17,1},{2,18},{18,2},{3,19},{19,3},{4,20},{20... | collective-permute-start | bytes 344072 | tf_op jit(solution)/shard_map/ppermute | solution.py:434
  92.0 1.3 %collective-permute-start.15 = (bf16[2,224,128]{2,1,0:T(8,128)(2,1)S(1)}, bf16[2,224,128]{2,1,0:T(8,128)(2,1)S(1)}, u32[]{:S(2)}, u32[]{:S(2)}) collective-permute-start(bf16[2,224,128]{2,1,0:T(8,128)(2,1)S(1)} %collective-permute-done.10.refs_4_.refs_2_), channel_id=1, source_target_pairs={{0,16},{16,0},{1,17},{17,1},{2,18},{18,2},{3,19},{19,3},{4,20},{20... | collective-permute-start | bytes 344072 | tf_op jit(solution)/shard_map/ppermute | solution.py:434
  92.1 1.4 %collective-permute-start.14 = (bf16[2,224,128]{2,1,0:T(8,128)(2,1)S(1)}, bf16[2,224,128]{2,1,0:T(8,128)(2,1)S(1)}, u32[]{:S(2)}, u32[]{:S(2)}) collective-permute-start(bf16[2,224,128]{2,1,0:T(8,128)(2,1)S(1)} %collective-permute-done.11.refs_1_.refs_0_), channel_id=1, source_target_pairs={{0,16},{16,0},{1,17},{17,1},{2,18},{18,2},{3,19},{19,3},{4,20},{20... | collective-permute-start | bytes 344072 | tf_op jit(solution)/shard_map/ppermute | solution.py:434
  92.5 1.3 %collective-permute-start.16 = (bf16[2,224,128]{2,1,0:T(8,128)(2,1)S(1)}, bf16[2,224,128]{2,1,0:T(8,128)(2,1)S(1)}, u32[]{:S(2)}, u32[]{:S(2)}) collective-permute-start(bf16[2,224,128]{2,1,0:T(8,128)(2,1)S(1)} %collective-permute-done.12.refs_3_.refs_1_), channel_id=1, source_target_pairs={{0,16},{16,0},{1,17},{17,1},{2,18},{18,2},{3,19},{19,3},{4,20},{20... | collective-permute-start | bytes 344072 | tf_op jit(solution)/shard_map/ppermute | solution.py:434
  95.2 6.3 %collective-permute-start.17 = (bf16[16,64,128]{2,1,0:T(8,128)(2,1)S(1)}, bf16[16,64,128]{2,1,0:T(8,128)(2,1)S(1)}, u32[]{:S(2)}, u32[]{:S(2)}) collective-permute-start(bf16[16,64,128]{2,1,0:T(8,128)(2,1)S(1)} %all-to-all-done.3.own_ref), channel_id=1, source_target_pairs={{0,16},{16,0},{1,17},{17,1},{2,18},{18,2},{3,19},{19,3},{4,20},{20... | collective-permute-start | bytes 786440 | tf_op jit(solution)/shard_map/ppermute | solution.py:434
  (8 other events, 201.1 us)

commit v10 on v8

--- a/solution.py
+++ b/solution.py
@@ -288,11 +288,11 @@
 
 
 def part_kernel(in_ref, *refs):
-    both_refs, part_refs, send_refs = refs[:8], refs[8:12], refs[12:16]
-    rows_ref, sums_ref = refs[16:]
+    both_refs, part_ref, send_refs = refs[:8], refs[8], refs[9:13]
+    rows_ref, sums_ref = refs[13:]
     sources, kinds, blocks, rows = in_ref.shape
     width = both_refs[0].shape[1] // 2
-    x, core, y = lax.axis_index("x"), lax.axis_index("core"), lax.axis_index("y")
+    core, y = lax.axis_index("core"), lax.axis_index("y")
     turn = 1 - 2 * core
     rows_ref[...] = in_ref[...].astype(jnp.float32).reshape(sources * kinds * blocks, rows)
     out_part = jnp.zeros((sources, width), jnp.float32)
@@ -311,11 +311,14 @@
             both_ref = both_refs[4 + ahead if other else (4 - ahead) % 4]
             out_part += bf16_dot(kept[:sources], both_ref[:, width:])
             in_part += bf16_dot(kept[sources : 4 * sources], both_ref[:, :width])
-    sums_ref[0] = out_part
-    for group in range(3):
-        sums_ref[1 + group] = in_part[group * sources : (group + 1) * sources]
-    for ahead in range(4):
-        part_refs[ahead][...] = sums_ref[(x + turn * ahead) & 3]
+    lanes = sums_ref.shape[1]
+    for kind in range(4):
+        part = out_part if kind == 0 else in_part[(kind - 1) * sources : kind * sources]
+        for half in range(2):
+            sums_ref[pl.ds(kind * 2 + half, sources, stride=8), :] = part[
+                :, half * lanes : (half + 1) * lanes
+            ]
+    part_ref[...] = sums_ref[...].reshape(part_ref.shape).astype(jnp.bfloat16)
 
 
 def finish_kernel(*refs):
@@ -371,37 +374,31 @@
         )
 
 
-def add_x_kernel(*refs):
-    out_ref = refs[7]
-    total = refs[0][...] + refs[1][...] + refs[2][...] + refs[3][...]
-    lanes = out_ref.shape[2]
-    rows = jnp.concatenate([total[:, :lanes], total[:, lanes:]], 0)
-    out_ref[...] = jnp.broadcast_to(rows.astype(jnp.bfloat16)[None], out_ref.shape)
-
-
-def add_z_kernel(scale, in_ref, *refs):
-    out_ref = refs[-1]
+def add_kernel(scale, in_ref, *refs):
+    out_ref = refs[3]
     total = jnp.sum(in_ref[...].astype(jnp.float32), axis=0) * scale
     out_ref[...] = jnp.broadcast_to(total.astype(jnp.bfloat16)[None], out_ref.shape)
 
 
-def place_kernel(own_ref, other_ref, in_weight_ref, out_weight_ref):
+def place_kernel(own_ref, other_ref, in_weight_ref, out_weight_ref, rows_ref):
     width, lanes = out_weight_ref.shape[0], own_ref.shape[2]
+    chips, slots = own_ref.shape[0], own_ref.shape[1]
     core = lax.axis_index("core")
     order = channel_order(
-        lambda zh, x, c, zl, y: ((c ^ core) * 4 + y) * 32 + (zh * 16 + x * 4 + zl)
+        lambda zh, x, c, zl, y: (c ^ core) * 128 + (zh * 4 + x) * 16 + zl * 4 + y
     )
     contract_first = (((0,), (1,)), ((), ()))
+    for other, ref in enumerate((own_ref, other_ref)):
+        rows_ref[other] = ref[...].astype(jnp.float32).reshape(chips * slots, lanes)
     for kind in range(4):
         for half in range(2):
             stacked = jnp.concatenate(
                 [
-                    ref[kind * 4 + y, half * 32 : (half + 1) * 32, :]
-                    for ref in (own_ref, other_ref)
-                    for y in range(4)
+                    rows_ref[other, pl.ds(kind * 2 + half, chips, stride=slots), :]
+                    for other in range(2)
                 ],
                 0,
-            )
+            ).astype(jnp.bfloat16)
             if kind == 0:
                 out_weight_ref[:, half * lanes : (half + 1) * lanes] = bf16_dot(order, stacked)
             else:
@@ -434,15 +431,10 @@
     return lax.ppermute(x, "core", [(0, 1), (1, 0)])
 
 
-def ring(x, axis, distance):
-    axes = ("x", "core") if axis == "x" else ("core", "y")
-    route = []
-    for core, turn in ((0, distance), (1, -distance)):
-        for i in range(4):
-            j = (i + turn) % 4
-            pair = (i * 2 + core, j * 2 + core) if axis == "x" else (core * 4 + i, core * 4 + j)
-            route.append(pair)
-    return lax.ppermute(x, axes, route)
+def ring(x, distance):
+    route = [(i, (i + distance) % 4) for i in range(4)]
+    route += [(4 + i, 4 + (i - distance) % 4) for i in range(4)]
+    return lax.ppermute(x, ("core", "y"), route)
 
 
 def per_device(inputs, in_weight, short_kernel, filter_one, filter_two, out_weight, out_grad):
@@ -459,7 +451,7 @@
         limit=56 * 1024 * 1024,
     )(inputs, in_weight, filter_one, filter_two, out_weight, out_grad)
     received = exchange(packed, everyone)
-    gathered = [both] + [ring(both, "y", distance) for distance in (1, 2, 3)]
+    gathered = [both] + [ring(both, distance) for distance in (1, 2, 3)]
     gathered += [swap_core(x) for x in gathered]
     tables = [jnp.asarray(t) for t in transform_tables(devices // 2, rows)]
     back = call(
@@ -469,29 +461,22 @@
         in_specs=specs(*[pltpu.VMEM] * (2 + len(tables)), *[pl.ANY] * 2),
     )(received, short_kernel, *tables, gathered[1], gathered[3])
     halfway = exchange(back, ("zh", "x", "zl"))
-    found = call(
+    part, *leaving = call(
         part_kernel,
-        (shape((32, width), f32),) * 4 + (shape((2, 7 * 32, rows), bf16),) * 4,
-        [pltpu.VMEM((32 * 7 * 8, rows), f32), pltpu.VMEM((4, 32, width), f32)],
+        (shape((32, 8, rows), bf16),) + (shape((2, 7 * 32, rows), bf16),) * 4,
+        [pltpu.VMEM((32 * 7 * 8, rows), f32), pltpu.VMEM((32 * 8, rows), f32)],
     )(halfway, *gathered)
-    part = [found[0]] + [ring(found[distance], "x", distance) for distance in (1, 2, 3)]
-    leaving = found[5:]
-    part, *leaving = call(
-        add_x_kernel,
-        (shape((8, 64, rows), bf16),) + (shape(leaving[0].shape, bf16),) * 3,
-        in_specs=specs(*[pltpu.VMEM] * 4, *[pl.ANY] * 3),
+    part = exchange(part, ("zh", "x", "zl"))
+    part, *leaving[1:] = call(
+        functools.partial(add_kernel, scale),
+        (shape((devices // 2, 8, rows), bf16),) + (shape(leaving[0].shape, bf16),) * 3,
+        in_specs=specs(pltpu.VMEM, *[pl.ANY] * 3),
         out_specs=specs(pltpu.VMEM, *[pl.ANY] * 3),
-        input_output_aliases={4: 1, 5: 2, 6: 3},
-    )(*part, *leaving)
-    arrived = [found[4]] + [ring(x, "y", 1 + i) for i, x in enumerate(leaving)]
-    part = exchange(part, ("zh", "zl"))
-    part = call(
-        functools.partial(add_z_kernel, scale),
-        shape((16, 64, rows), bf16),
-        in_specs=specs(pltpu.VMEM, *[pl.ANY] * 3),
-    )(part, *arrived[1:])
+        input_output_aliases={1: 1, 2: 2, 3: 3},
+    )(part, *leaving[1:])
+    arrived = [leaving[0]] + [ring(leaving[i], i) for i in (1, 2, 3)]
     arrived += [swap_core(x) for x in arrived]
-    part = exchange(part, ("x", "y"))
+    part = exchange(part, ("zh", "x", "zl", "y"))
     outputs, grad_inputs, grad_short, grad_one, grad_two = call(
         finish_kernel,
         (
@@ -504,7 +489,9 @@
     )(*arrived, in_weight, out_weight)
     part, grad_short = lax.optimization_barrier((part, grad_short))
     grad_in_weight, grad_out_weight = call(
-        place_kernel, (shape((width, 3 * width), f32), shape((width, width), f32))
+        place_kernel,
+        (shape((width, 3 * width), f32), shape((width, width), f32)),
+        [pltpu.VMEM((2, devices * 4, rows), f32)],
     )(part, swap_core(part))
     return (
         outputs,

time: 102 us -> 103 us (level)
  waiting for transfers between devices: 42.7 us -> 29.6 us
  blocking collectives: 0 us -> 13 us
  starting transfers between devices: 45.8 us -> 47.5 us
    all_to_all x0 -> x1, blocking collectives: none -> 13 us  [exchange(): return lax.all_to_all(x, axes, split_axis=0, concat_axis=0, tiled=True)]
    ppermute x9 -> x6, waiting for transfers between devices: 20 us -> 8.67 us  [ring(): return lax.ppermute(x, ('core', 'y'), route)]
    ppermute x9, starting transfers between devices: 8.21 us -> 13.3 us  [swap_core(): return lax.ppermute(x, 'core', [(0, 1), (1, 0)])]
    ppermute x9 -> x6, starting transfers between devices: 10.9 us -> 7.4 us  [ring(): return lax.ppermute(x, ('core', 'y'), route)]
    all_to_all x4 -> x3, waiting for transfers between devices: 19.3 us -> 17.2 us  [exchange(): return lax.all_to_all(x, axes, split_axis=0, concat_axis=0, tiled=True)]
    all_to_all x4 -> x3, starting transfers between devices: 26.7 us -> 26.8 us  [exchange(): return lax.all_to_all(x, axes, split_axis=0, concat_axis=0, tiled=True)]
  transfers between devices with their start and end apart: 22 -> 18, of which waited for: 20 -> 11; matrix products, arithmetic and copies ran while one was open for 0% -> 0% of each run, Pallas kernels for 1% -> 1%
where the time goes in v10:
time: 103 us; the launch traced here: 102 us
  starting transfers between devices  47.5 us (46%)
  waiting for transfers between devices  29.6 us (29%)
  blocking collectives  13 us (13%)
  Pallas kernels  11.2 us (11%)
    all_to_all x3, starting transfers between devices, exchange(): return lax.all_to_all(x, axes, split_axis=0, concat_axis=0, tiled=True)  26.8 us
    all_to_all x3, waiting for transfers between devices, exchange(): return lax.all_to_all(x, axes, split_axis=0, concat_axis=0, tiled=True)  17.2 us
    ppermute x9, starting transfers between devices, swap_core(): return lax.ppermute(x, 'core', [(0, 1), (1, 0)])  13.3 us
    all_to_all x1, blocking collectives, exchange(): return lax.all_to_all(x, axes, split_axis=0, concat_axis=0, tiled=True)  13 us
    ppermute x6, waiting for transfers between devices, ring(): return lax.ppermute(x, ('core', 'y'), route)  8.67 us
    ppermute x6, starting transfers between devices, ring(): return lax.ppermute(x, ('core', 'y'), route)  7.4 us
    pallas_call x1, Pallas kernels, per_device(): call(convolve_kernel, shape((32, 7, 8, rows), bf16), [pltpu.VMEM((3, 2 *...  4.61 us
    ppermute x9, waiting for transfers between devices, swap_core(): return lax.ppermute(x, 'core', [(0, 1), (1, 0)])  3.71 us
  transfers between devices with their start and end apart: 18, of which 11 were waited for; matrix products, arithmetic and copies ran while one was open for 0% of the time, Pallas kernels for 1%

profile of v10, /device:TPU:1, one launch (start us, length us, event | category | flops | bytes accessed | tf_op | source)
XLA Modules:
  0.0 102.2 jit_solution(13187161856249699490)
XLA Ops:
  0.7 2.5 %shard_map.180 = (bf16[256,2,384]{2,1,0:T(2,128)(2,1)}, bf16[128,512]{1,0:T(8,128)(2,1)}) custom-call(bf16[1,128,256]{2,1,0:T(8,128)(2,1)} %seq_ref.1, bf16[256,768]{1,0:T(8,128)(2,1)} %refs_8_.1, f32[128,256]{1,0:T(8,128)} %one_ref.1, f32[128,256]{1,0:T(8,128)} %two_ref.1, bf16[256,256]{1,0:T(8,128)(2,1)} %refs_9_.1, bf16[1,128,256]{2,1,0:T(8,128)(2,1)} %grad_ref.1), custom_call_target="tpu_custom_call" | custom-call | tf_op jit(solution)/shard_map/pallas_call | solution.py:447
  3.2 15.7 %all-to-all-start = ((bf16[256,2,384]{2,1,0:T(2,128)(2,1)}), bf16[256,2,384]{2,1,0:T(2,128)(2,1)S(1)}, u32[]{:S(2)}, u32[]{:S(2)}) async-start(bf16[256,2,384]{2,1,0:T(2,128)(2,1)} %get-tuple-element.27), calls=%async_computation | async-start | bytes 786432 | tf_op jit(solution)/shard_map/all_to_all | solution.py:427
  18.9 1.5 %collective-permute-start.1 = (bf16[128,512]{1,0:T(8,128)(2,1)}, bf16[128,512]{1,0:T(8,128)(2,1)S(1)}, u32[]{:S(2)}, u32[]{:S(2)}) collective-permute-start(bf16[128,512]{1,0:T(8,128)(2,1)} %get-tuple-element.28.refs_0_), channel_id=1, source_target_pairs={{0,3},{1,0},{2,1},{3,2},{16,17},{17,18},{18,19},{19,16},{4,7},{5,4... | collective-permute-start | bytes 393224 | tf_op jit(solution)/shard_map/ppermute | solution.py:437
  20.4 1.4 %collective-permute-start = (bf16[128,512]{1,0:T(8,128)(2,1)}, bf16[128,512]{1,0:T(8,128)(2,1)S(1)}, u32[]{:S(2)}, u32[]{:S(2)}) collective-permute-start(bf16[128,512]{1,0:T(8,128)(2,1)} %get-tuple-element.28.refs_0_), channel_id=1, source_target_pairs={{0,1},{1,2},{2,3},{3,0},{16,19},{17,16},{18,17},{19,18},{4,5},{5,6... | collective-permute-start | bytes 393224 | tf_op jit(solution)/shard_map/ppermute | solution.py:437
  21.7 3.3 %collective-permute-done.1.rest_1_.refs_3_ = bf16[128,512]{1,0:T(8,128)(2,1)S(1)} collective-permute-done((bf16[128,512]{1,0:T(8,128)(2,1)}, bf16[128,512]{1,0:T(8,128)(2,1)S(1)}, u32[]{:S(2)}, u32[]{:S(2)}) %collective-permute-start.1) | collective-permute-done | bytes 131104 | tf_op jit(solution)/shard_map/ppermute | solution.py:437
  25.0 1.3 %collective-permute-done.rest_0_.refs_1_ = bf16[128,512]{1,0:T(8,128)(2,1)S(1)} collective-permute-done((bf16[128,512]{1,0:T(8,128)(2,1)}, bf16[128,512]{1,0:T(8,128)(2,1)S(1)}, u32[]{:S(2)}, u32[]{:S(2)}) %collective-permute-start) | collective-permute-done | bytes 131104 | tf_op jit(solution)/shard_map/ppermute | solution.py:437
  26.3 10.7 %all-to-all-done.in_ref = bf16[256,2,384]{2,1,0:T(2,128)(2,1)S(1)} async-done(((bf16[256,2,384]{2,1,0:T(2,128)(2,1)}), bf16[256,2,384]{2,1,0:T(2,128)(2,1)S(1)}, u32[]{:S(2)}, u32[]{:S(2)}) %all-to-all-start) | async-done | bytes 393248 | tf_op jit(solution)/shard_map/all_to_all | solution.py:427
  37.0 4.6 %shard_map.181 = bf16[32,7,8,128]{3,2,1,0:T(8,128)(2,1)} custom-call(bf16[256,2,384]{2,1,0:T(2,128)(2,1)S(1)} %all-to-all-done.in_ref, f32[3,768]{1,0:T(4,128)S(1)} %copy-done.9, bf16[256,384]{1,0:T(8,128)(2,1)S(1)} %copy-done.5, bf16[768,256]{1,0:T(8,128)(2,1)S(1)} %copy-done.3, bf16[768,256]{1,0:T(8,128)(2,1)S(1)} %copy-done.2, ...), custom_call_target="tpu_custom_call" | custom-call | tf_op jit(solution)/shard_map/pallas_call | solution.py:457
  41.6 4.0 %all-to-all-start.1 = ((bf16[32,7,8,128]{3,2,1,0:T(8,128)(2,1)}), bf16[32,7,8,128]{3,2,1,0:T(8,128)(2,1)S(1)}, u32[]{:S(2)}, u32[]{:S(2)}) async-start(bf16[32,7,8,128]{3,2,1,0:T(8,128)(2,1)} %shard_map.181), calls=%async_computation.1 | async-start | bytes 917504 | tf_op jit(solution)/shard_map/all_to_all | solution.py:427
  45.7 1.6 %collective-permute-start.2 = (bf16[128,512]{1,0:T(8,128)(2,1)S(1)}, bf16[128,512]{1,0:T(8,128)(2,1)S(1)}, u32[]{:S(2)}, u32[]{:S(2)}) collective-permute-start(bf16[128,512]{1,0:T(8,128)(2,1)S(1)} %copy-done.6), channel_id=1, source_target_pairs={{0,2},{1,3},{2,0},{3,1},{16,18},{17,19},{18,16},{19,17},{4,6},{5,7... | collective-permute-start | bytes 393224 | tf_op jit(solution)/shard_map/ppermute | solution.py:437
  47.3 4.0 %collective-permute-done.2.refs_2_ = bf16[128,512]{1,0:T(8,128)(2,1)S(1)} collective-permute-done((bf16[128,512]{1,0:T(8,128)(2,1)S(1)}, bf16[128,512]{1,0:T(8,128)(2,1)S(1)}, u32[]{:S(2)}, u32[]{:S(2)}) %collective-permute-start.2) | collective-permute-done | bytes 131104 | tf_op jit(solution)/shard_map/ppermute | solution.py:437
  51.3 1.9 %collective-permute-start.5 = (bf16[128,512]{1,0:T(8,128)(2,1)S(1)}, bf16[128,512]{1,0:T(8,128)(2,1)S(1)}, u32[]{:S(2)}, u32[]{:S(2)}) collective-permute-start(bf16[128,512]{1,0:T(8,128)(2,1)S(1)} %collective-permute-done.2.refs_2_), channel_id=1, source_target_pairs={{0,16},{16,0},{1,17},{17,1},{2,18},{18,2},{3,19},{19,3},{4,20},{20... | collective-permute-start | bytes 393224 | tf_op jit(solution)/shard_map/ppermute | solution.py:431
  54.8 6.6 %all-to-all-done.1.in_ref = bf16[32,7,8,128]{3,2,1,0:T(8,128)(2,1)S(1)} async-done(((bf16[32,7,8,128]{3,2,1,0:T(8,128)(2,1)}), bf16[32,7,8,128]{3,2,1,0:T(8,128)(2,1)S(1)}, u32[]{:S(2)}, u32[]{:S(2)}) %all-to-all-start.1) | async-done | bytes 458784 | tf_op jit(solution)/shard_map/all_to_all | solution.py:427
  61.9 13.0 %all_to_all.20.in_ref = bf16[32,8,128]{2,1,0:T(8,128)(2,1)S(1)} all-to-all(bf16[32,8,128]{2,1,0:T(8,128)(2,1)S(1)} %get-tuple-element.30), channel_id=1, replica_groups=mesh['zh'=2,'x'=4,'core'=2,'zl'=4,'y'=4] {'zh','x','zl'}, dimensions={0} | all-to-all | bytes 131072 | tf_op jit(solution)/shard_map/all_to_all | solution.py:427
  74.9 0.8 shard_map.183
  75.7 7.1 %all-to-all-start.3 = ((bf16[128,8,128]{2,1,0:T(8,128)(2,1)}), bf16[128,8,128]{2,1,0:T(8,128)(2,1)S(1)}, u32[]{:S(2)}, u32[]{:S(2)}) async-start(bf16[128,8,128]{2,1,0:T(8,128)(2,1)} %get-tuple-element.39), calls=%async_computation.3 | async-start | bytes 524288 | tf_op jit(solution)/shard_map/all_to_all | solution.py:427
  82.8 1.9 %collective-permute-start.7 = (bf16[2,224,128]{2,1,0:T(8,128)(2,1)S(1)}, bf16[2,224,128]{2,1,0:T(8,128)(2,1)S(1)}, u32[]{:S(2)}, u32[]{:S(2)}) collective-permute-start(bf16[2,224,128]{2,1,0:T(8,128)(2,1)S(1)} %get-tuple-element.34), channel_id=1, source_target_pairs={{0,1},{1,2},{2,3},{3,0},{16,19},{17,16},{18,17},{19,18},{4,5},{5,6... | collective-permute-start | bytes 344072 | tf_op jit(solution)/shard_map/ppermute | solution.py:437
  85.8 4.9 %collective-permute-start.10 = (bf16[2,224,128]{2,1,0:T(8,128)(2,1)S(1)}, bf16[2,224,128]{2,1,0:T(8,128)(2,1)S(1)}, u32[]{:S(2)}, u32[]{:S(2)}) collective-permute-start(bf16[2,224,128]{2,1,0:T(8,128)(2,1)S(1)} %get-tuple-element.29.refs_0_), channel_id=1, source_target_pairs={{0,16},{16,0},{1,17},{17,1},{2,18},{18,2},{3,19},{19,3},{4,20},{20... | collective-permute-start | bytes 344072 | tf_op jit(solution)/shard_map/ppermute | solution.py:431
  90.7 4.3 %collective-permute-start.11 = (bf16[2,224,128]{2,1,0:T(8,128)(2,1)S(1)}, bf16[2,224,128]{2,1,0:T(8,128)(2,1)S(1)}, u32[]{:S(2)}, u32[]{:S(2)}) collective-permute-start(bf16[2,224,128]{2,1,0:T(8,128)(2,1)S(1)} %collective-permute-done.7.refs_1_), channel_id=1, source_target_pairs={{0,16},{16,0},{1,17},{17,1},{2,18},{18,2},{3,19},{19,3},{4,20},{20... | collective-permute-start | bytes 344072 | tf_op jit(solution)/shard_map/ppermute | solution.py:431
  95.0 1.5 %collective-permute-start.12 = (bf16[2,224,128]{2,1,0:T(8,128)(2,1)S(1)}, bf16[2,224,128]{2,1,0:T(8,128)(2,1)S(1)}, u32[]{:S(2)}, u32[]{:S(2)}) collective-permute-start(bf16[2,224,128]{2,1,0:T(8,128)(2,1)S(1)} %collective-permute-done.8.refs_2_), channel_id=1, source_target_pairs={{0,16},{16,0},{1,17},{17,1},{2,18},{18,2},{3,19},{19,3},{4,20},{20... | collective-permute-start | bytes 344072 | tf_op jit(solution)/shard_map/ppermute | solution.py:431
  96.6 0.9 collective-permute-done.12.refs_6_
  97.9 1.4 %shard_map.184 = (bf16[1,128,256]{2,1,0:T(8,128)(2,1)}, bf16[1,128,256]{2,1,0:T(8,128)(2,1)}, f32[3,768]{1,0:T(4,128)}, f32[128,256]{1,0:T(8,128)}, f32[128,256]{1,0:T(8,128)}) custom-call(bf16[2,224,128]{2,1,0:T(8,128)(2,1)S(1)} %get-tuple-element.29.refs_0_, bf16[2,224,128]{2,1,0:T(8,128)(2,1)S(1)} %collective-permute-done.7.refs_1_, ...), custom_call_target="tpu_custom_call" | custom-call | tf_op jit(solution)/shard_map/pallas_call | solution.py:480
  99.4 1.4 %collective-permute-done.14.other_ref = bf16[128,8,128]{2,1,0:T(8,128)(2,1)S(1)} collective-permute-done((bf16[128,8,128]{2,1,0:T(8,128)(2,1)S(1)}, bf16[128,8,128]{2,1,0:T(8,128)(2,1)S(1)}, u32[]{:S(2)}, u32[]{:S(2)}) %collective-permute-start.14) | collective-permute-done | bytes 262176 | tf_op jit(solution)/shard_map/ppermute | solution.py:431
  100.8 1.4 %shard_map.185 = (f32[256,768]{1,0:T(8,128)}, f32[256,256]{1,0:T(8,128)}) custom-call(bf16[128,8,128]{2,1,0:T(8,128)(2,1)S(1)} %all-to-all-done.3.own_ref, bf16[128,8,128]{2,1,0:T(8,128)(2,1)S(1)} %collective-permute-done.14.other_ref), custom_call_target="tpu_custom_call" | custom-call | tf_op jit(solution)/shard_map/pallas_call | solution.py:491
  (39 shorter events, 3.8 us)
Async XLA Ops:
  0.6 36.4 %copy-start.4 = (bf16[128,768]{1,0:T(8,128)(2,1)S(1)}, bf16[128,768]{1,0:T(8,128)(2,1)}, u32[]{:S(2)}) copy-start(bf16[128,768]{1,0:T(8,128)(2,1)} %constant.15.clone.first_back_ref) | copy-start | bytes 589828
  0.6 36.3 %copy-start.5 = (bf16[256,384]{1,0:T(8,128)(2,1)S(1)}, bf16[256,384]{1,0:T(8,128)(2,1)}, u32[]{:S(2)}) copy-start(bf16[256,384]{1,0:T(8,128)(2,1)} %constant.12.clone.first_ref) | copy-start | bytes 589828
  0.7 36.3 %copy-start.7 = (f32[128,128]{1,0:T(8,128)S(1)}, f32[128,128]{1,0:T(8,128)}, u32[]{:S(2)}) copy-start(f32[128,128]{1,0:T(8,128)} %constant.17.clone.turn_sin_ref) | copy-start | bytes 196612
  0.7 36.3 %copy-start.8 = (f32[128,128]{1,0:T(8,128)S(1)}, f32[128,128]{1,0:T(8,128)}, u32[]{:S(2)}) copy-start(f32[128,128]{1,0:T(8,128)} %constant.16.clone.turn_cos_ref) | copy-start | bytes 196612
  0.7 36.3 %copy-start.9 = (f32[3,768]{1,0:T(4,128)S(1)}, f32[3,768]{1,0:T(4,128)}, u32[]{:S(2)}) copy-start(f32[3,768]{1,0:T(4,128)} %short_ref.1) | copy-start | bytes 27652
  3.2 33.8 %copy-start.3 = (bf16[768,256]{1,0:T(8,128)(2,1)S(1)}, bf16[768,256]{1,0:T(8,128)(2,1)}, u32[]{:S(2)}) copy-start(bf16[768,256]{1,0:T(8,128)(2,1)} %constant.13.clone.second_ref) | copy-start | bytes 1179652
  3.2 33.8 %all-to-all-start = ((bf16[256,2,384]{2,1,0:T(2,128)(2,1)}), bf16[256,2,384]{2,1,0:T(2,128)(2,1)S(1)}, u32[]{:S(2)}, u32[]{:S(2)}) async-start(bf16[256,2,384]{2,1,0:T(2,128)(2,1)} %get-tuple-element.27), calls=%async_computation | async-start | bytes 786432 | tf_op jit(solution)/shard_map/all_to_all | solution.py:427
  18.9 6.1 %collective-permute-start.1 = (bf16[128,512]{1,0:T(8,128)(2,1)}, bf16[128,512]{1,0:T(8,128)(2,1)S(1)}, u32[]{:S(2)}, u32[]{:S(2)}) collective-permute-start(bf16[128,512]{1,0:T(8,128)(2,1)} %get-tuple-element.28.refs_0_), channel_id=1, source_target_pairs={{0,3},{1,0},{2,1},{3,2},{16,17},{17,18},{18,19},{19,16},{4,7},{5,4... | collective-permute-start | bytes 393224 | tf_op jit(solution)/shard_map/ppermute | solution.py:437
  20.4 6.0 %collective-permute-start = (bf16[128,512]{1,0:T(8,128)(2,1)}, bf16[128,512]{1,0:T(8,128)(2,1)S(1)}, u32[]{:S(2)}, u32[]{:S(2)}) collective-permute-start(bf16[128,512]{1,0:T(8,128)(2,1)} %get-tuple-element.28.refs_0_), channel_id=1, source_target_pairs={{0,1},{1,2},{2,3},{3,0},{16,19},{17,16},{18,17},{19,18},{4,5},{5,6... | collective-permute-start | bytes 393224 | tf_op jit(solution)/shard_map/ppermute | solution.py:437
  41.6 19.7 %all-to-all-start.1 = ((bf16[32,7,8,128]{3,2,1,0:T(8,128)(2,1)}), bf16[32,7,8,128]{3,2,1,0:T(8,128)(2,1)S(1)}, u32[]{:S(2)}, u32[]{:S(2)}) async-start(bf16[32,7,8,128]{3,2,1,0:T(8,128)(2,1)} %shard_map.181), calls=%async_computation.1 | async-start | bytes 917504 | tf_op jit(solution)/shard_map/all_to_all | solution.py:427
  45.7 5.6 %collective-permute-start.2 = (bf16[128,512]{1,0:T(8,128)(2,1)S(1)}, bf16[128,512]{1,0:T(8,128)(2,1)S(1)}, u32[]{:S(2)}, u32[]{:S(2)}) collective-permute-start(bf16[128,512]{1,0:T(8,128)(2,1)S(1)} %copy-done.6), channel_id=1, source_target_pairs={{0,2},{1,3},{2,0},{3,1},{16,18},{17,19},{18,16},{19,17},{4,6},{5,7... | collective-permute-start | bytes 393224 | tf_op jit(solution)/shard_map/ppermute | solution.py:437
  47.3 6.5 %collective-permute-start.3 = (bf16[128,512]{1,0:T(8,128)(2,1)S(1)}, bf16[128,512]{1,0:T(8,128)(2,1)S(1)}, u32[]{:S(2)}, u32[]{:S(2)}) collective-permute-start(bf16[128,512]{1,0:T(8,128)(2,1)S(1)} %copy-done.6), channel_id=1, source_target_pairs={{0,16},{16,0},{1,17},{17,1},{2,18},{18,2},{3,19},{19,3},{4,20},{20... | collective-permute-start | bytes 393224 | tf_op jit(solution)/shard_map/ppermute | solution.py:431
  51.3 2.9 %collective-permute-start.5 = (bf16[128,512]{1,0:T(8,128)(2,1)S(1)}, bf16[128,512]{1,0:T(8,128)(2,1)S(1)}, u32[]{:S(2)}, u32[]{:S(2)}) collective-permute-start(bf16[128,512]{1,0:T(8,128)(2,1)S(1)} %collective-permute-done.2.refs_2_), channel_id=1, source_target_pairs={{0,16},{16,0},{1,17},{17,1},{2,18},{18,2},{3,19},{19,3},{4,20},{20... | collective-permute-start | bytes 393224 | tf_op jit(solution)/shard_map/ppermute | solution.py:431
  53.3 1.3 %collective-permute-start.6 = (bf16[128,512]{1,0:T(8,128)(2,1)S(1)}, bf16[128,512]{1,0:T(8,128)(2,1)S(1)}, u32[]{:S(2)}, u32[]{:S(2)}) collective-permute-start(bf16[128,512]{1,0:T(8,128)(2,1)S(1)} %collective-permute-done.1.rest_1_.refs_3_), channel_id=1, source_target_pairs={{0,16},{16,0},{1,17},{17,1},{2,18},{18,2},{3,19},{19,3},{4,20},{20... | collective-permute-start | bytes 393224 | tf_op jit(solution)/shard_map/ppermute | solution.py:431
  53.3 1.5 %collective-permute-start.4 = (bf16[128,512]{1,0:T(8,128)(2,1)S(1)}, bf16[128,512]{1,0:T(8,128)(2,1)S(1)}, u32[]{:S(2)}, u32[]{:S(2)}) collective-permute-start(bf16[128,512]{1,0:T(8,128)(2,1)S(1)} %collective-permute-done.rest_0_.refs_1_), channel_id=1, source_target_pairs={{0,16},{16,0},{1,17},{17,1},{2,18},{18,2},{3,19},{19,3},{4,20},{20... | collective-permute-start | bytes 393224 | tf_op jit(solution)/shard_map/ppermute | solution.py:431
  75.7 23.6 %all-to-all-start.3 = ((bf16[128,8,128]{2,1,0:T(8,128)(2,1)}), bf16[128,8,128]{2,1,0:T(8,128)(2,1)S(1)}, u32[]{:S(2)}, u32[]{:S(2)}) async-start(bf16[128,8,128]{2,1,0:T(8,128)(2,1)} %get-tuple-element.39), calls=%async_computation.3 | async-start | bytes 524288 | tf_op jit(solution)/shard_map/all_to_all | solution.py:427
  82.8 7.9 %collective-permute-start.7 = (bf16[2,224,128]{2,1,0:T(8,128)(2,1)S(1)}, bf16[2,224,128]{2,1,0:T(8,128)(2,1)S(1)}, u32[]{:S(2)}, u32[]{:S(2)}) collective-permute-start(bf16[2,224,128]{2,1,0:T(8,128)(2,1)S(1)} %get-tuple-element.34), channel_id=1, source_target_pairs={{0,1},{1,2},{2,3},{3,0},{16,19},{17,16},{18,17},{19,18},{4,5},{5,6... | collective-permute-start | bytes 344072 | tf_op jit(solution)/shard_map/ppermute | solution.py:437
  84.7 10.4 %collective-permute-start.8 = (bf16[2,224,128]{2,1,0:T(8,128)(2,1)S(1)}, bf16[2,224,128]{2,1,0:T(8,128)(2,1)S(1)}, u32[]{:S(2)}, u32[]{:S(2)}) collective-permute-start(bf16[2,224,128]{2,1,0:T(8,128)(2,1)S(1)} %get-tuple-element.35), channel_id=1, source_target_pairs={{0,2},{1,3},{2,0},{3,1},{16,18},{17,19},{18,16},{19,17},{4,6},{5,7... | collective-permute-start | bytes 344072 | tf_op jit(solution)/shard_map/ppermute | solution.py:437
  85.3 11.3 %collective-permute-start.9 = (bf16[2,224,128]{2,1,0:T(8,128)(2,1)S(1)}, bf16[2,224,128]{2,1,0:T(8,128)(2,1)S(1)}, u32[]{:S(2)}, u32[]{:S(2)}) collective-permute-start(bf16[2,224,128]{2,1,0:T(8,128)(2,1)S(1)} %get-tuple-element.36), channel_id=1, source_target_pairs={{0,3},{1,0},{2,1},{3,2},{16,17},{17,18},{18,19},{19,16},{4,7},{5,4... | collective-permute-start | bytes 344072 | tf_op jit(solution)/shard_map/ppermute | solution.py:437
  85.8 10.7 %collective-permute-start.10 = (bf16[2,224,128]{2,1,0:T(8,128)(2,1)S(1)}, bf16[2,224,128]{2,1,0:T(8,128)(2,1)S(1)}, u32[]{:S(2)}, u32[]{:S(2)}) collective-permute-start(bf16[2,224,128]{2,1,0:T(8,128)(2,1)S(1)} %get-tuple-element.29.refs_0_), channel_id=1, source_target_pairs={{0,16},{16,0},{1,17},{17,1},{2,18},{18,2},{3,19},{19,3},{4,20},{20... | collective-permute-start | bytes 344072 | tf_op jit(solution)/shard_map/ppermute | solution.py:431
  90.7 5.8 %collective-permute-start.11 = (bf16[2,224,128]{2,1,0:T(8,128)(2,1)S(1)}, bf16[2,224,128]{2,1,0:T(8,128)(2,1)S(1)}, u32[]{:S(2)}, u32[]{:S(2)}) collective-permute-start(bf16[2,224,128]{2,1,0:T(8,128)(2,1)S(1)} %collective-permute-done.7.refs_1_), channel_id=1, source_target_pairs={{0,16},{16,0},{1,17},{17,1},{2,18},{18,2},{3,19},{19,3},{4,20},{20... | collective-permute-start | bytes 344072 | tf_op jit(solution)/shard_map/ppermute | solution.py:431
  95.0 2.5 %collective-permute-start.12 = (bf16[2,224,128]{2,1,0:T(8,128)(2,1)S(1)}, bf16[2,224,128]{2,1,0:T(8,128)(2,1)S(1)}, u32[]{:S(2)}, u32[]{:S(2)}) collective-permute-start(bf16[2,224,128]{2,1,0:T(8,128)(2,1)S(1)} %collective-permute-done.8.refs_2_), channel_id=1, source_target_pairs={{0,16},{16,0},{1,17},{17,1},{2,18},{18,2},{3,19},{19,3},{4,20},{20... | collective-permute-start | bytes 344072 | tf_op jit(solution)/shard_map/ppermute | solution.py:431
  96.5 1.3 %collective-permute-start.13 = (bf16[2,224,128]{2,1,0:T(8,128)(2,1)S(1)}, bf16[2,224,128]{2,1,0:T(8,128)(2,1)S(1)}, u32[]{:S(2)}, u32[]{:S(2)}) collective-permute-start(bf16[2,224,128]{2,1,0:T(8,128)(2,1)S(1)} %collective-permute-done.9.refs_3_), channel_id=1, source_target_pairs={{0,16},{16,0},{1,17},{17,1},{2,18},{18,2},{3,19},{19,3},{4,20},{20... | collective-permute-start | bytes 344072 | tf_op jit(solution)/shard_map/ppermute | solution.py:431
  99.3 1.5 %collective-permute-start.14 = (bf16[128,8,128]{2,1,0:T(8,128)(2,1)S(1)}, bf16[128,8,128]{2,1,0:T(8,128)(2,1)S(1)}, u32[]{:S(2)}, u32[]{:S(2)}) collective-permute-start(bf16[128,8,128]{2,1,0:T(8,128)(2,1)S(1)} %all-to-all-done.3.own_ref), channel_id=1, source_target_pairs={{0,16},{16,0},{1,17},{17,1},{2,18},{18,2},{3,19},{19,3},{4,20},{20... | collective-permute-start | bytes 786440 | tf_op jit(solution)/shard_map/ppermute | solution.py:431
  (4 other events, 83.0 us)

commit v11 on v10

--- a/solution.py
+++ b/solution.py
@@ -467,14 +467,15 @@
         [pltpu.VMEM((32 * 7 * 8, rows), f32), pltpu.VMEM((32 * 8, rows), f32)],
     )(halfway, *gathered)
     part = exchange(part, ("zh", "x", "zl"))
-    part, *leaving[1:] = call(
+    near = [ring(leaving[1], 1), ring(leaving[3], 3)]
+    part, far = call(
         functools.partial(add_kernel, scale),
-        (shape((devices // 2, 8, rows), bf16),) + (shape(leaving[0].shape, bf16),) * 3,
+        (shape((devices // 2, 8, rows), bf16), shape(leaving[2].shape, bf16)),
         in_specs=specs(pltpu.VMEM, *[pl.ANY] * 3),
-        out_specs=specs(pltpu.VMEM, *[pl.ANY] * 3),
-        input_output_aliases={1: 1, 2: 2, 3: 3},
-    )(part, *leaving[1:])
-    arrived = [leaving[0]] + [ring(leaving[i], i) for i in (1, 2, 3)]
+        out_specs=specs(pltpu.VMEM, pl.ANY),
+        input_output_aliases={3: 1},
+    )(part, *near, leaving[2])
+    arrived = [leaving[0], near[0], ring(far, 2), near[1]]
     arrived += [swap_core(x) for x in arrived]
     part = exchange(part, ("zh", "x", "zl", "y"))
     outputs, grad_inputs, grad_short, grad_one, grad_two = call(

time: 103 us -> 107 us (1.039)
  blocking collectives: 13 us -> 0 us
  starting transfers between devices: 47.5 us -> 58 us
  waiting for transfers between devices: 29.6 us -> 36 us
    all_to_all x1 -> x0, blocking collectives: 13 us -> none  [exchange(): return lax.all_to_all(x, axes, split_axis=0, concat_axis=0, tiled=True)]
    all_to_all x3 -> x4, starting transfers between devices: 26.8 us -> 33.5 us  [exchange(): return lax.all_to_all(x, axes, split_axis=0, concat_axis=0, tiled=True)]
    ppermute x6, waiting for transfers between devices: 8.67 us -> 14.3 us  [ring(): return lax.ppermute(x, ('core', 'y'), route)]
    ppermute x9, starting transfers between devices: 13.3 us -> 15.7 us  [swap_core(): return lax.ppermute(x, 'core', [(0, 1), (1, 0)])]
    ppermute x6, starting transfers between devices: 7.4 us -> 8.82 us  [ring(): return lax.ppermute(x, ('core', 'y'), route)]
    all_to_all x3 -> x4, waiting for transfers between devices: 17.2 us -> 18.5 us  [exchange(): return lax.all_to_all(x, axes, split_axis=0, concat_axis=0, tiled=True)]
  transfers between devices with their start and end apart: 18 -> 19, of which waited for: 11 -> 13; matrix products, arithmetic and copies ran while one was open for 0% -> 0% of each run, Pallas kernels for 1% -> 1%
where the time goes in v11:
time: 107 us
  starting transfers between devices  58 us (54%)
  waiting for transfers between devices  36 us (34%)
  Pallas kernels  11.9 us (11%)
    all_to_all x4, starting transfers between devices, exchange(): return lax.all_to_all(x, axes, split_axis=0, concat_axis=0, tiled=True)  33.5 us
    all_to_all x4, waiting for transfers between devices, exchange(): return lax.all_to_all(x, axes, split_axis=0, concat_axis=0, tiled=True)  18.5 us
    ppermute x9, starting transfers between devices, swap_core(): return lax.ppermute(x, 'core', [(0, 1), (1, 0)])  15.7 us
    ppermute x6, waiting for transfers between devices, ring(): return lax.ppermute(x, ('core', 'y'), route)  14.3 us
    ppermute x6, starting transfers between devices, ring(): return lax.ppermute(x, ('core', 'y'), route)  8.82 us
    pallas_call x1, Pallas kernels, per_device(): call(convolve_kernel, shape((32, 7, 8, rows), bf16), [pltpu.VMEM((3, 2 *...  4.61 us
    ppermute x9, waiting for transfers between devices, swap_core(): return lax.ppermute(x, 'core', [(0, 1), (1, 0)])  3.15 us
    pallas_call x1, Pallas kernels, per_device(): call(pack_kernel, (shape((width, 2, 3 * rows), bf16), shape((rows, 2 * wi...  2.53 us
  transfers between devices with their start and end apart: 19, of which 13 were waited for; matrix products, arithmetic and copies ran while one was open for 0% of the time, Pallas kernels for 1%

profile of v11, /device:TPU:1, one launch (start us, length us, event | category | flops | bytes accessed | tf_op | source)
XLA Modules:
  0.0 106.7 jit_solution(15947612147797888875)
XLA Ops:
  0.7 2.5 %shard_map.180 = (bf16[256,2,384]{2,1,0:T(2,128)(2,1)}, bf16[128,512]{1,0:T(8,128)(2,1)}) custom-call(bf16[1,128,256]{2,1,0:T(8,128)(2,1)} %seq_ref.1, bf16[256,768]{1,0:T(8,128)(2,1)} %refs_8_.1, f32[128,256]{1,0:T(8,128)} %one_ref.1, f32[128,256]{1,0:T(8,128)} %two_ref.1, bf16[256,256]{1,0:T(8,128)(2,1)} %refs_9_.1, bf16[1,128,256]{2,1,0:T(8,128)(2,1)} %grad_ref.1), custom_call_target="tpu_custom_call" | custom-call | tf_op jit(solution)/shard_map/pallas_call | solution.py:447
  3.2 15.7 %all-to-all-start = ((bf16[256,2,384]{2,1,0:T(2,128)(2,1)}), bf16[256,2,384]{2,1,0:T(2,128)(2,1)S(1)}, u32[]{:S(2)}, u32[]{:S(2)}) async-start(bf16[256,2,384]{2,1,0:T(2,128)(2,1)} %get-tuple-element.25), calls=%async_computation | async-start | bytes 786432 | tf_op jit(solution)/shard_map/all_to_all | solution.py:427
  18.9 1.5 %collective-permute-start.1 = (bf16[128,512]{1,0:T(8,128)(2,1)}, bf16[128,512]{1,0:T(8,128)(2,1)S(1)}, u32[]{:S(2)}, u32[]{:S(2)}) collective-permute-start(bf16[128,512]{1,0:T(8,128)(2,1)} %get-tuple-element.26.refs_0_), channel_id=1, source_target_pairs={{0,3},{1,0},{2,1},{3,2},{16,17},{17,18},{18,19},{19,16},{4,7},{5,4... | collective-permute-start | bytes 393224 | tf_op jit(solution)/shard_map/ppermute | solution.py:437
  20.4 1.4 %collective-permute-start = (bf16[128,512]{1,0:T(8,128)(2,1)}, bf16[128,512]{1,0:T(8,128)(2,1)S(1)}, u32[]{:S(2)}, u32[]{:S(2)}) collective-permute-start(bf16[128,512]{1,0:T(8,128)(2,1)} %get-tuple-element.26.refs_0_), channel_id=1, source_target_pairs={{0,1},{1,2},{2,3},{3,0},{16,19},{17,16},{18,17},{19,18},{4,5},{5,6... | collective-permute-start | bytes 393224 | tf_op jit(solution)/shard_map/ppermute | solution.py:437
  21.7 3.3 %collective-permute-done.1.rest_1_.refs_3_ = bf16[128,512]{1,0:T(8,128)(2,1)S(1)} collective-permute-done((bf16[128,512]{1,0:T(8,128)(2,1)}, bf16[128,512]{1,0:T(8,128)(2,1)S(1)}, u32[]{:S(2)}, u32[]{:S(2)}) %collective-permute-start.1) | collective-permute-done | bytes 131104 | tf_op jit(solution)/shard_map/ppermute | solution.py:437
  25.0 1.3 %collective-permute-done.rest_0_.refs_1_ = bf16[128,512]{1,0:T(8,128)(2,1)S(1)} collective-permute-done((bf16[128,512]{1,0:T(8,128)(2,1)}, bf16[128,512]{1,0:T(8,128)(2,1)S(1)}, u32[]{:S(2)}, u32[]{:S(2)}) %collective-permute-start) | collective-permute-done | bytes 131104 | tf_op jit(solution)/shard_map/ppermute | solution.py:437
  26.3 10.7 %all-to-all-done.in_ref = bf16[256,2,384]{2,1,0:T(2,128)(2,1)S(1)} async-done(((bf16[256,2,384]{2,1,0:T(2,128)(2,1)}), bf16[256,2,384]{2,1,0:T(2,128)(2,1)S(1)}, u32[]{:S(2)}, u32[]{:S(2)}) %all-to-all-start) | async-done | bytes 393248 | tf_op jit(solution)/shard_map/all_to_all | solution.py:427
  37.0 4.6 %shard_map.181 = bf16[32,7,8,128]{3,2,1,0:T(8,128)(2,1)} custom-call(bf16[256,2,384]{2,1,0:T(2,128)(2,1)S(1)} %all-to-all-done.in_ref, f32[3,768]{1,0:T(4,128)S(1)} %copy-done.9, bf16[256,384]{1,0:T(8,128)(2,1)S(1)} %copy-done.5, bf16[768,256]{1,0:T(8,128)(2,1)S(1)} %copy-done.3, bf16[768,256]{1,0:T(8,128)(2,1)S(1)} %copy-done.2, ...), custom_call_target="tpu_custom_call" | custom-call | tf_op jit(solution)/shard_map/pallas_call | solution.py:457
  41.6 4.0 %all-to-all-start.1 = ((bf16[32,7,8,128]{3,2,1,0:T(8,128)(2,1)}), bf16[32,7,8,128]{3,2,1,0:T(8,128)(2,1)S(1)}, u32[]{:S(2)}, u32[]{:S(2)}) async-start(bf16[32,7,8,128]{3,2,1,0:T(8,128)(2,1)} %shard_map.181), calls=%async_computation.1 | async-start | bytes 917504 | tf_op jit(solution)/shard_map/all_to_all | solution.py:427
  45.7 1.6 %collective-permute-start.2 = (bf16[128,512]{1,0:T(8,128)(2,1)S(1)}, bf16[128,512]{1,0:T(8,128)(2,1)S(1)}, u32[]{:S(2)}, u32[]{:S(2)}) collective-permute-start(bf16[128,512]{1,0:T(8,128)(2,1)S(1)} %copy-done.6), channel_id=1, source_target_pairs={{0,2},{1,3},{2,0},{3,1},{16,18},{17,19},{18,16},{19,17},{4,6},{5,7... | collective-permute-start | bytes 393224 | tf_op jit(solution)/shard_map/ppermute | solution.py:437
  47.3 4.0 %collective-permute-done.2.refs_2_ = bf16[128,512]{1,0:T(8,128)(2,1)S(1)} collective-permute-done((bf16[128,512]{1,0:T(8,128)(2,1)S(1)}, bf16[128,512]{1,0:T(8,128)(2,1)S(1)}, u32[]{:S(2)}, u32[]{:S(2)}) %collective-permute-start.2) | collective-permute-done | bytes 131104 | tf_op jit(solution)/shard_map/ppermute | solution.py:437
  51.3 1.9 %collective-permute-start.5 = (bf16[128,512]{1,0:T(8,128)(2,1)S(1)}, bf16[128,512]{1,0:T(8,128)(2,1)S(1)}, u32[]{:S(2)}, u32[]{:S(2)}) collective-permute-start(bf16[128,512]{1,0:T(8,128)(2,1)S(1)} %collective-permute-done.2.refs_2_), channel_id=1, source_target_pairs={{0,16},{16,0},{1,17},{17,1},{2,18},{18,2},{3,19},{19,3},{4,20},{20... | collective-permute-start | bytes 393224 | tf_op jit(solution)/shard_map/ppermute | solution.py:431
  54.8 6.6 %all-to-all-done.1.in_ref = bf16[32,7,8,128]{3,2,1,0:T(8,128)(2,1)S(1)} async-done(((bf16[32,7,8,128]{3,2,1,0:T(8,128)(2,1)}), bf16[32,7,8,128]{3,2,1,0:T(8,128)(2,1)S(1)}, u32[]{:S(2)}, u32[]{:S(2)}) %all-to-all-start.1) | async-done | bytes 458784 | tf_op jit(solution)/shard_map/all_to_all | solution.py:427
  62.5 4.0 %all-to-all-start.2 = ((bf16[32,8,128]{2,1,0:T(8,128)(2,1)}), bf16[32,8,128]{2,1,0:T(8,128)(2,1)S(1)}, u32[]{:S(2)}, u32[]{:S(2)}) async-start(bf16[32,8,128]{2,1,0:T(8,128)(2,1)} %get-tuple-element.29), calls=%async_computation.2 | async-start | bytes 131072 | tf_op jit(solution)/shard_map/all_to_all | solution.py:427
  66.6 2.3 %collective-permute-start.7 = (bf16[2,224,128]{2,1,0:T(8,128)(2,1)S(1)}, bf16[2,224,128]{2,1,0:T(8,128)(2,1)S(1)}, u32[]{:S(2)}, u32[]{:S(2)}) collective-permute-start(bf16[2,224,128]{2,1,0:T(8,128)(2,1)S(1)} %get-tuple-element.28), channel_id=1, source_target_pairs={{0,1},{1,2},{2,3},{3,0},{16,19},{17,16},{18,17},{19,18},{4,5},{5,6... | collective-permute-start | bytes 344072 | tf_op jit(solution)/shard_map/ppermute | solution.py:437
  68.8 1.8 %collective-permute-done.7.refs_0_.refs_1_ = bf16[2,224,128]{2,1,0:T(8,128)(2,1)S(1)} collective-permute-done((bf16[2,224,128]{2,1,0:T(8,128)(2,1)S(1)}, bf16[2,224,128]{2,1,0:T(8,128)(2,1)S(1)}, u32[]{:S(2)}, u32[]{:S(2)}) %collective-permute-start.7) | collective-permute-done | bytes 114720 | tf_op jit(solution)/shard_map/ppermute | solution.py:437
  70.6 3.9 %collective-permute-done.8.refs_1_.refs_3_ = bf16[2,224,128]{2,1,0:T(8,128)(2,1)S(1)} collective-permute-done((bf16[2,224,128]{2,1,0:T(8,128)(2,1)S(1)}, bf16[2,224,128]{2,1,0:T(8,128)(2,1)S(1)}, u32[]{:S(2)}, u32[]{:S(2)}) %collective-permute-start.8) | collective-permute-done | bytes 114720 | tf_op jit(solution)/shard_map/ppermute | solution.py:437
  76.5 9.8 %all-to-all-start.3 = ((bf16[128,8,128]{2,1,0:T(8,128)(2,1)}), bf16[128,8,128]{2,1,0:T(8,128)(2,1)S(1)}, u32[]{:S(2)}, u32[]{:S(2)}) async-start(bf16[128,8,128]{2,1,0:T(8,128)(2,1)} %get-tuple-element.35), calls=%async_computation.3 | async-start | bytes 524288 | tf_op jit(solution)/shard_map/all_to_all | solution.py:427
  86.4 2.2 %collective-permute-start.9 = (bf16[2,224,128]{2,1,0:T(8,128)(2,1)S(1)}, bf16[2,224,128]{2,1,0:T(8,128)(2,1)S(1)}, u32[]{:S(2)}, u32[]{:S(2)}) collective-permute-start(bf16[2,224,128]{2,1,0:T(8,128)(2,1)S(1)} %get-tuple-element.32), channel_id=1, source_target_pairs={{0,2},{1,3},{2,0},{3,1},{16,18},{17,19},{18,16},{19,17},{4,6},{5,7... | collective-permute-start | bytes 344072 | tf_op jit(solution)/shard_map/ppermute | solution.py:437
  88.5 4.7 %collective-permute-start.10 = (bf16[2,224,128]{2,1,0:T(8,128)(2,1)S(1)}, bf16[2,224,128]{2,1,0:T(8,128)(2,1)S(1)}, u32[]{:S(2)}, u32[]{:S(2)}) collective-permute-start(bf16[2,224,128]{2,1,0:T(8,128)(2,1)S(1)} %get-tuple-element.27.refs_0_), channel_id=1, source_target_pairs={{0,16},{16,0},{1,17},{17,1},{2,18},{18,2},{3,19},{19,3},{4,20},{20... | collective-permute-start | bytes 344072 | tf_op jit(solution)/shard_map/ppermute | solution.py:431
  93.7 3.7 %collective-permute-start.12 = (bf16[2,224,128]{2,1,0:T(8,128)(2,1)S(1)}, bf16[2,224,128]{2,1,0:T(8,128)(2,1)S(1)}, u32[]{:S(2)}, u32[]{:S(2)}) collective-permute-start(bf16[2,224,128]{2,1,0:T(8,128)(2,1)S(1)} %collective-permute-done.9.refs_2_), channel_id=1, source_target_pairs={{0,16},{16,0},{1,17},{17,1},{2,18},{18,2},{3,19},{19,3},{4,20},{20... | collective-permute-start | bytes 344072 | tf_op jit(solution)/shard_map/ppermute | solution.py:431
  98.4 1.4 %shard_map.184 = (bf16[1,128,256]{2,1,0:T(8,128)(2,1)}, bf16[1,128,256]{2,1,0:T(8,128)(2,1)}, f32[3,768]{1,0:T(4,128)}, f32[128,256]{1,0:T(8,128)}, f32[128,256]{1,0:T(8,128)}) custom-call(bf16[2,224,128]{2,1,0:T(8,128)(2,1)S(1)} %get-tuple-element.27.refs_0_, bf16[2,224,128]{2,1,0:T(8,128)(2,1)S(1)} %collective-permute-done.7.refs_0_.refs_1_, ...), custom_call_target="tpu_custom_call" | custom-call | tf_op jit(solution)/shard_map/pallas_call | solution.py:481
  99.8 4.3 %collective-permute-start.14 = (bf16[128,8,128]{2,1,0:T(8,128)(2,1)S(1)}, bf16[128,8,128]{2,1,0:T(8,128)(2,1)S(1)}, u32[]{:S(2)}, u32[]{:S(2)}) collective-permute-start(bf16[128,8,128]{2,1,0:T(8,128)(2,1)S(1)} %all-to-all-done.3.own_ref), channel_id=1, source_target_pairs={{0,16},{16,0},{1,17},{17,1},{2,18},{18,2},{3,19},{19,3},{4,20},{20... | collective-permute-start | bytes 786440 | tf_op jit(solution)/shard_map/ppermute | solution.py:431
  105.2 1.4 %shard_map.185 = (f32[256,768]{1,0:T(8,128)}, f32[256,256]{1,0:T(8,128)}) custom-call(bf16[128,8,128]{2,1,0:T(8,128)(2,1)S(1)} %all-to-all-done.3.own_ref, bf16[128,8,128]{2,1,0:T(8,128)(2,1)S(1)} %collective-permute-done.14.other_ref), custom_call_target="tpu_custom_call" | custom-call | tf_op jit(solution)/shard_map/pallas_call | solution.py:492
  (40 shorter events, 7.4 us)
Async XLA Ops:
  0.6 36.4 %copy-start.4 = (bf16[128,768]{1,0:T(8,128)(2,1)S(1)}, bf16[128,768]{1,0:T(8,128)(2,1)}, u32[]{:S(2)}) copy-start(bf16[128,768]{1,0:T(8,128)(2,1)} %constant.15.clone.first_back_ref) | copy-start | bytes 589828
  0.6 36.3 %copy-start.5 = (bf16[256,384]{1,0:T(8,128)(2,1)S(1)}, bf16[256,384]{1,0:T(8,128)(2,1)}, u32[]{:S(2)}) copy-start(bf16[256,384]{1,0:T(8,128)(2,1)} %constant.12.clone.first_ref) | copy-start | bytes 589828
  0.7 36.3 %copy-start.7 = (f32[128,128]{1,0:T(8,128)S(1)}, f32[128,128]{1,0:T(8,128)}, u32[]{:S(2)}) copy-start(f32[128,128]{1,0:T(8,128)} %constant.17.clone.turn_sin_ref) | copy-start | bytes 196612
  0.7 36.3 %copy-start.8 = (f32[128,128]{1,0:T(8,128)S(1)}, f32[128,128]{1,0:T(8,128)}, u32[]{:S(2)}) copy-start(f32[128,128]{1,0:T(8,128)} %constant.16.clone.turn_cos_ref) | copy-start | bytes 196612
  0.7 36.3 %copy-start.9 = (f32[3,768]{1,0:T(4,128)S(1)}, f32[3,768]{1,0:T(4,128)}, u32[]{:S(2)}) copy-start(f32[3,768]{1,0:T(4,128)} %short_ref.1) | copy-start | bytes 27652
  3.2 33.8 %all-to-all-start = ((bf16[256,2,384]{2,1,0:T(2,128)(2,1)}), bf16[256,2,384]{2,1,0:T(2,128)(2,1)S(1)}, u32[]{:S(2)}, u32[]{:S(2)}) async-start(bf16[256,2,384]{2,1,0:T(2,128)(2,1)} %get-tuple-element.25), calls=%async_computation | async-start | bytes 786432 | tf_op jit(solution)/shard_map/all_to_all | solution.py:427
  18.9 6.1 %collective-permute-start.1 = (bf16[128,512]{1,0:T(8,128)(2,1)}, bf16[128,512]{1,0:T(8,128)(2,1)S(1)}, u32[]{:S(2)}, u32[]{:S(2)}) collective-permute-start(bf16[128,512]{1,0:T(8,128)(2,1)} %get-tuple-element.26.refs_0_), channel_id=1, source_target_pairs={{0,3},{1,0},{2,1},{3,2},{16,17},{17,18},{18,19},{19,16},{4,7},{5,4... | collective-permute-start | bytes 393224 | tf_op jit(solution)/shard_map/ppermute | solution.py:437
  20.4 6.0 %collective-permute-start = (bf16[128,512]{1,0:T(8,128)(2,1)}, bf16[128,512]{1,0:T(8,128)(2,1)S(1)}, u32[]{:S(2)}, u32[]{:S(2)}) collective-permute-start(bf16[128,512]{1,0:T(8,128)(2,1)} %get-tuple-element.26.refs_0_), channel_id=1, source_target_pairs={{0,1},{1,2},{2,3},{3,0},{16,19},{17,16},{18,17},{19,18},{4,5},{5,6... | collective-permute-start | bytes 393224 | tf_op jit(solution)/shard_map/ppermute | solution.py:437
  41.6 19.7 %all-to-all-start.1 = ((bf16[32,7,8,128]{3,2,1,0:T(8,128)(2,1)}), bf16[32,7,8,128]{3,2,1,0:T(8,128)(2,1)S(1)}, u32[]{:S(2)}, u32[]{:S(2)}) async-start(bf16[32,7,8,128]{3,2,1,0:T(8,128)(2,1)} %shard_map.181), calls=%async_computation.1 | async-start | bytes 917504 | tf_op jit(solution)/shard_map/all_to_all | solution.py:427
  45.7 5.6 %collective-permute-start.2 = (bf16[128,512]{1,0:T(8,128)(2,1)S(1)}, bf16[128,512]{1,0:T(8,128)(2,1)S(1)}, u32[]{:S(2)}, u32[]{:S(2)}) collective-permute-start(bf16[128,512]{1,0:T(8,128)(2,1)S(1)} %copy-done.6), channel_id=1, source_target_pairs={{0,2},{1,3},{2,0},{3,1},{16,18},{17,19},{18,16},{19,17},{4,6},{5,7... | collective-permute-start | bytes 393224 | tf_op jit(solution)/shard_map/ppermute | solution.py:437
  47.3 6.5 %collective-permute-start.3 = (bf16[128,512]{1,0:T(8,128)(2,1)S(1)}, bf16[128,512]{1,0:T(8,128)(2,1)S(1)}, u32[]{:S(2)}, u32[]{:S(2)}) collective-permute-start(bf16[128,512]{1,0:T(8,128)(2,1)S(1)} %copy-done.6), channel_id=1, source_target_pairs={{0,16},{16,0},{1,17},{17,1},{2,18},{18,2},{3,19},{19,3},{4,20},{20... | collective-permute-start | bytes 393224 | tf_op jit(solution)/shard_map/ppermute | solution.py:431
  51.3 2.9 %collective-permute-start.5 = (bf16[128,512]{1,0:T(8,128)(2,1)S(1)}, bf16[128,512]{1,0:T(8,128)(2,1)S(1)}, u32[]{:S(2)}, u32[]{:S(2)}) collective-permute-start(bf16[128,512]{1,0:T(8,128)(2,1)S(1)} %collective-permute-done.2.refs_2_), channel_id=1, source_target_pairs={{0,16},{16,0},{1,17},{17,1},{2,18},{18,2},{3,19},{19,3},{4,20},{20... | collective-permute-start | bytes 393224 | tf_op jit(solution)/shard_map/ppermute | solution.py:431
  53.3 1.3 %collective-permute-start.6 = (bf16[128,512]{1,0:T(8,128)(2,1)S(1)}, bf16[128,512]{1,0:T(8,128)(2,1)S(1)}, u32[]{:S(2)}, u32[]{:S(2)}) collective-permute-start(bf16[128,512]{1,0:T(8,128)(2,1)S(1)} %collective-permute-done.1.rest_1_.refs_3_), channel_id=1, source_target_pairs={{0,16},{16,0},{1,17},{17,1},{2,18},{18,2},{3,19},{19,3},{4,20},{20... | collective-permute-start | bytes 393224 | tf_op jit(solution)/shard_map/ppermute | solution.py:431
  53.3 1.5 %collective-permute-start.4 = (bf16[128,512]{1,0:T(8,128)(2,1)S(1)}, bf16[128,512]{1,0:T(8,128)(2,1)S(1)}, u32[]{:S(2)}, u32[]{:S(2)}) collective-permute-start(bf16[128,512]{1,0:T(8,128)(2,1)S(1)} %collective-permute-done.rest_0_.refs_1_), channel_id=1, source_target_pairs={{0,16},{16,0},{1,17},{17,1},{2,18},{18,2},{3,19},{19,3},{4,20},{20... | collective-permute-start | bytes 393224 | tf_op jit(solution)/shard_map/ppermute | solution.py:431
  62.5 13.2 %all-to-all-start.2 = ((bf16[32,8,128]{2,1,0:T(8,128)(2,1)}), bf16[32,8,128]{2,1,0:T(8,128)(2,1)S(1)}, u32[]{:S(2)}, u32[]{:S(2)}) async-start(bf16[32,8,128]{2,1,0:T(8,128)(2,1)} %get-tuple-element.29), calls=%async_computation.2 | async-start | bytes 131072 | tf_op jit(solution)/shard_map/all_to_all | solution.py:427
  66.6 4.1 %collective-permute-start.7 = (bf16[2,224,128]{2,1,0:T(8,128)(2,1)S(1)}, bf16[2,224,128]{2,1,0:T(8,128)(2,1)S(1)}, u32[]{:S(2)}, u32[]{:S(2)}) collective-permute-start(bf16[2,224,128]{2,1,0:T(8,128)(2,1)S(1)} %get-tuple-element.28), channel_id=1, source_target_pairs={{0,1},{1,2},{2,3},{3,0},{16,19},{17,16},{18,17},{19,18},{4,5},{5,6... | collective-permute-start | bytes 344072 | tf_op jit(solution)/shard_map/ppermute | solution.py:437
  68.8 5.7 %collective-permute-start.8 = (bf16[2,224,128]{2,1,0:T(8,128)(2,1)S(1)}, bf16[2,224,128]{2,1,0:T(8,128)(2,1)S(1)}, u32[]{:S(2)}, u32[]{:S(2)}) collective-permute-start(bf16[2,224,128]{2,1,0:T(8,128)(2,1)S(1)} %get-tuple-element.30), channel_id=1, source_target_pairs={{0,3},{1,0},{2,1},{3,2},{16,17},{17,18},{18,19},{19,16},{4,7},{5,4... | collective-permute-start | bytes 344072 | tf_op jit(solution)/shard_map/ppermute | solution.py:437
  76.5 23.3 %all-to-all-start.3 = ((bf16[128,8,128]{2,1,0:T(8,128)(2,1)}), bf16[128,8,128]{2,1,0:T(8,128)(2,1)S(1)}, u32[]{:S(2)}, u32[]{:S(2)}) async-start(bf16[128,8,128]{2,1,0:T(8,128)(2,1)} %get-tuple-element.35), calls=%async_computation.3 | async-start | bytes 524288 | tf_op jit(solution)/shard_map/all_to_all | solution.py:427
  86.4 7.4 %collective-permute-start.9 = (bf16[2,224,128]{2,1,0:T(8,128)(2,1)S(1)}, bf16[2,224,128]{2,1,0:T(8,128)(2,1)S(1)}, u32[]{:S(2)}, u32[]{:S(2)}) collective-permute-start(bf16[2,224,128]{2,1,0:T(8,128)(2,1)S(1)} %get-tuple-element.32), channel_id=1, source_target_pairs={{0,2},{1,3},{2,0},{3,1},{16,18},{17,19},{18,16},{19,17},{4,6},{5,7... | collective-permute-start | bytes 344072 | tf_op jit(solution)/shard_map/ppermute | solution.py:437
  88.5 8.9 %collective-permute-start.10 = (bf16[2,224,128]{2,1,0:T(8,128)(2,1)S(1)}, bf16[2,224,128]{2,1,0:T(8,128)(2,1)S(1)}, u32[]{:S(2)}, u32[]{:S(2)}) collective-permute-start(bf16[2,224,128]{2,1,0:T(8,128)(2,1)S(1)} %get-tuple-element.27.refs_0_), channel_id=1, source_target_pairs={{0,16},{16,0},{1,17},{17,1},{2,18},{18,2},{3,19},{19,3},{4,20},{20... | collective-permute-start | bytes 344072 | tf_op jit(solution)/shard_map/ppermute | solution.py:431
  93.2 4.2 %collective-permute-start.11 = (bf16[2,224,128]{2,1,0:T(8,128)(2,1)S(1)}, bf16[2,224,128]{2,1,0:T(8,128)(2,1)S(1)}, u32[]{:S(2)}, u32[]{:S(2)}) collective-permute-start(bf16[2,224,128]{2,1,0:T(8,128)(2,1)S(1)} %collective-permute-done.7.refs_0_.refs_1_), channel_id=1, source_target_pairs={{0,16},{16,0},{1,17},{17,1},{2,18},{18,2},{3,19},{19,3},{4,20},{20... | collective-permute-start | bytes 344072 | tf_op jit(solution)/shard_map/ppermute | solution.py:431
  93.2 4.2 %collective-permute-start.13 = (bf16[2,224,128]{2,1,0:T(8,128)(2,1)S(1)}, bf16[2,224,128]{2,1,0:T(8,128)(2,1)S(1)}, u32[]{:S(2)}, u32[]{:S(2)}) collective-permute-start(bf16[2,224,128]{2,1,0:T(8,128)(2,1)S(1)} %collective-permute-done.8.refs_1_.refs_3_), channel_id=1, source_target_pairs={{0,16},{16,0},{1,17},{17,1},{2,18},{18,2},{3,19},{19,3},{4,20},{20... | collective-permute-start | bytes 344072 | tf_op jit(solution)/shard_map/ppermute | solution.py:431
  93.7 4.7 %collective-permute-start.12 = (bf16[2,224,128]{2,1,0:T(8,128)(2,1)S(1)}, bf16[2,224,128]{2,1,0:T(8,128)(2,1)S(1)}, u32[]{:S(2)}, u32[]{:S(2)}) collective-permute-start(bf16[2,224,128]{2,1,0:T(8,128)(2,1)S(1)} %collective-permute-done.9.refs_2_), channel_id=1, source_target_pairs={{0,16},{16,0},{1,17},{17,1},{2,18},{18,2},{3,19},{19,3},{4,20},{20... | collective-permute-start | bytes 344072 | tf_op jit(solution)/shard_map/ppermute | solution.py:431
  99.8 5.5 %collective-permute-start.14 = (bf16[128,8,128]{2,1,0:T(8,128)(2,1)S(1)}, bf16[128,8,128]{2,1,0:T(8,128)(2,1)S(1)}, u32[]{:S(2)}, u32[]{:S(2)}) collective-permute-start(bf16[128,8,128]{2,1,0:T(8,128)(2,1)S(1)} %all-to-all-done.3.own_ref), channel_id=1, source_target_pairs={{0,16},{16,0},{1,17},{17,1},{2,18},{18,2},{3,19},{19,3},{4,20},{20... | collective-permute-start | bytes 786440 | tf_op jit(solution)/shard_map/ppermute | solution.py:431
  (5 other events, 116.1 us)

commit v12 on v9

--- a/solution.py
+++ b/solution.py
@@ -372,7 +372,7 @@
 
 
 def add_x_kernel(*refs):
-    out_ref = refs[7]
+    out_ref = refs[4]
     total = refs[0][...] + refs[1][...] + refs[2][...] + refs[3][...]
     lanes = out_ref.shape[2]
     rows = jnp.concatenate([total[:, :lanes], total[:, lanes:]], 0)
@@ -475,22 +475,15 @@
         [pltpu.VMEM((32 * 7 * 8, rows), f32), pltpu.VMEM((4, 32, width), f32)],
     )(halfway, *gathered)
     part = [found[0]] + [ring(found[distance], "x", distance) for distance in (1, 2, 3)]
-    far = ring(found[6], "y", 2)
-    part, *leaving = call(
-        add_x_kernel,
-        (shape((8, 64, rows), bf16),) + (shape(found[5].shape, bf16),) * 2,
-        in_specs=specs(*[pltpu.VMEM] * 4, *[pl.ANY] * 3),
-        out_specs=specs(pltpu.VMEM, *[pl.ANY] * 2),
-        input_output_aliases={5: 1, 6: 2},
-    )(*part, far, found[5], found[7])
-    arrived = [found[4], ring(leaving[0], "y", 1), far, ring(leaving[1], "y", 3)]
+    arrived = [found[4]] + [ring(found[4 + i], "y", i) for i in (1, 2, 3)]
+    arrived += [swap_core(x) for x in arrived]
+    part = call(add_x_kernel, shape((8, 64, rows), bf16))(*part)
     part = exchange(part, ("zh", "zl"))
     part = call(
         functools.partial(add_z_kernel, scale),
         shape((16, 64, rows), bf16),
-        in_specs=specs(pltpu.VMEM, *[pl.ANY] * 2),
-    )(part, arrived[1], arrived[3])
-    arrived += [swap_core(x) for x in arrived]
+        in_specs=specs(pltpu.VMEM, *[pl.ANY] * 4),
+    )(part, *arrived[4:])
     part = exchange(part, ("x", "y"))
     outputs, grad_inputs, grad_short, grad_one, grad_two = call(
         finish_kernel,

time: 103 us -> 103 us (level)
  waiting for transfers between devices: 39.4 us -> 36.6 us
  starting transfers between devices: 50.8 us -> 53.4 us
    ppermute x9, waiting for transfers between devices: 16.1 us -> 8.67 us  [ring(): return lax.ppermute(x, axes, route)]
    all_to_all x4, waiting for transfers between devices: 19.9 us -> 24.5 us  [exchange(): return lax.all_to_all(x, axes, split_axis=0, concat_axis=0, tiled=True)]
    all_to_all x4, starting transfers between devices: 26.7 us -> 29.2 us  [exchange(): return lax.all_to_all(x, axes, split_axis=0, concat_axis=0, tiled=True)]
  transfers between devices with their start and end apart: 22 -> 22, of which waited for: 19 -> 15; matrix products, arithmetic and copies ran while one was open for 0% -> 0% of each run, Pallas kernels for 1% -> 2%
where the time goes in v12:
time: 103 us
  starting transfers between devices  53.4 us (52%)
  waiting for transfers between devices  36.6 us (36%)
  Pallas kernels  11.8 us (11%)
    all_to_all x4, starting transfers between devices, exchange(): return lax.all_to_all(x, axes, split_axis=0, concat_axis=0, tiled=True)  29.2 us
    all_to_all x4, waiting for transfers between devices, exchange(): return lax.all_to_all(x, axes, split_axis=0, concat_axis=0, tiled=True)  24.5 us
    ppermute x9, starting transfers between devices, swap_core(): return lax.ppermute(x, 'core', [(0, 1), (1, 0)])  13.7 us
    ppermute x9, starting transfers between devices, ring(): return lax.ppermute(x, axes, route)  10.5 us
    ppermute x9, waiting for transfers between devices, ring(): return lax.ppermute(x, axes, route)  8.67 us
    pallas_call x1, Pallas kernels, per_device(): call(convolve_kernel, shape((32, 7, 8, rows), bf16), [pltpu.VMEM((3, 2 *...  4.61 us
    ppermute x9, waiting for transfers between devices, swap_core(): return lax.ppermute(x, 'core', [(0, 1), (1, 0)])  3.4 us
    pallas_call x1, Pallas kernels, per_device(): call(pack_kernel, (shape((width, 2, 3 * rows), bf16), shape((rows, 2 * wi...  2.53 us
  transfers between devices with their start and end apart: 22, of which 15 were waited for; matrix products, arithmetic and copies ran while one was open for 0% of the time, Pallas kernels for 2%

profile of v12, /device:TPU:1, one launch (start us, length us, event | category | flops | bytes accessed | tf_op | source)
XLA Modules:
  0.0 102.6 jit_solution(8270473127773510150)
XLA Ops:
  0.7 2.5 %shard_map.180 = (bf16[256,2,384]{2,1,0:T(2,128)(2,1)}, bf16[128,512]{1,0:T(8,128)(2,1)}) custom-call(bf16[1,128,256]{2,1,0:T(8,128)(2,1)} %seq_ref.1, bf16[256,768]{1,0:T(8,128)(2,1)} %refs_8_.1, f32[128,256]{1,0:T(8,128)} %one_ref.1, f32[128,256]{1,0:T(8,128)} %two_ref.1, bf16[256,256]{1,0:T(8,128)(2,1)} %refs_9_.1, bf16[1,128,256]{2,1,0:T(8,128)(2,1)} %grad_ref.1), custom_call_target="tpu_custom_call" | custom-call | tf_op jit(solution)/shard_map/pallas_call | solution.py:455
  3.2 15.7 %all-to-all-start = ((bf16[256,2,384]{2,1,0:T(2,128)(2,1)}), bf16[256,2,384]{2,1,0:T(2,128)(2,1)S(1)}, u32[]{:S(2)}, u32[]{:S(2)}) async-start(bf16[256,2,384]{2,1,0:T(2,128)(2,1)} %get-tuple-element.26), calls=%async_computation | async-start | bytes 786432 | tf_op jit(solution)/shard_map/all_to_all | solution.py:430
  18.9 1.5 %collective-permute-start.1 = (bf16[128,512]{1,0:T(8,128)(2,1)}, bf16[128,512]{1,0:T(8,128)(2,1)S(1)}, u32[]{:S(2)}, u32[]{:S(2)}) collective-permute-start(bf16[128,512]{1,0:T(8,128)(2,1)} %get-tuple-element.27.refs_0_), channel_id=1, source_target_pairs={{0,3},{1,0},{2,1},{3,2},{16,17},{17,18},{18,19},{19,16},{4,7},{5,4... | collective-permute-start | bytes 393224 | tf_op jit(solution)/shard_map/ppermute | solution.py:445
  20.4 1.4 %collective-permute-start = (bf16[128,512]{1,0:T(8,128)(2,1)}, bf16[128,512]{1,0:T(8,128)(2,1)S(1)}, u32[]{:S(2)}, u32[]{:S(2)}) collective-permute-start(bf16[128,512]{1,0:T(8,128)(2,1)} %get-tuple-element.27.refs_0_), channel_id=1, source_target_pairs={{0,1},{1,2},{2,3},{3,0},{16,19},{17,16},{18,17},{19,18},{4,5},{5,6... | collective-permute-start | bytes 393224 | tf_op jit(solution)/shard_map/ppermute | solution.py:445
  21.7 3.3 %collective-permute-done.1.rest_1_.refs_3_ = bf16[128,512]{1,0:T(8,128)(2,1)S(1)} collective-permute-done((bf16[128,512]{1,0:T(8,128)(2,1)}, bf16[128,512]{1,0:T(8,128)(2,1)S(1)}, u32[]{:S(2)}, u32[]{:S(2)}) %collective-permute-start.1) | collective-permute-done | bytes 131104 | tf_op jit(solution)/shard_map/ppermute | solution.py:445
  25.0 1.3 %collective-permute-done.rest_0_.refs_1_ = bf16[128,512]{1,0:T(8,128)(2,1)S(1)} collective-permute-done((bf16[128,512]{1,0:T(8,128)(2,1)}, bf16[128,512]{1,0:T(8,128)(2,1)S(1)}, u32[]{:S(2)}, u32[]{:S(2)}) %collective-permute-start) | collective-permute-done | bytes 131104 | tf_op jit(solution)/shard_map/ppermute | solution.py:445
  26.3 10.7 %all-to-all-done.in_ref = bf16[256,2,384]{2,1,0:T(2,128)(2,1)S(1)} async-done(((bf16[256,2,384]{2,1,0:T(2,128)(2,1)}), bf16[256,2,384]{2,1,0:T(2,128)(2,1)S(1)}, u32[]{:S(2)}, u32[]{:S(2)}) %all-to-all-start) | async-done | bytes 393248 | tf_op jit(solution)/shard_map/all_to_all | solution.py:430
  37.0 4.6 %shard_map.181 = bf16[32,7,8,128]{3,2,1,0:T(8,128)(2,1)} custom-call(bf16[256,2,384]{2,1,0:T(2,128)(2,1)S(1)} %all-to-all-done.in_ref, f32[3,768]{1,0:T(4,128)S(1)} %copy-done.9, bf16[256,384]{1,0:T(8,128)(2,1)S(1)} %copy-done.5, bf16[768,256]{1,0:T(8,128)(2,1)S(1)} %copy-done.3, bf16[768,256]{1,0:T(8,128)(2,1)S(1)} %copy-done.2, ...), custom_call_target="tpu_custom_call" | custom-call | tf_op jit(solution)/shard_map/pallas_call | solution.py:465
  41.6 4.0 %all-to-all-start.1 = ((bf16[32,7,8,128]{3,2,1,0:T(8,128)(2,1)}), bf16[32,7,8,128]{3,2,1,0:T(8,128)(2,1)S(1)}, u32[]{:S(2)}, u32[]{:S(2)}) async-start(bf16[32,7,8,128]{3,2,1,0:T(8,128)(2,1)} %shard_map.181), calls=%async_computation.1 | async-start | bytes 917504 | tf_op jit(solution)/shard_map/all_to_all | solution.py:430
  45.7 1.6 %collective-permute-start.2 = (bf16[128,512]{1,0:T(8,128)(2,1)S(1)}, bf16[128,512]{1,0:T(8,128)(2,1)S(1)}, u32[]{:S(2)}, u32[]{:S(2)}) collective-permute-start(bf16[128,512]{1,0:T(8,128)(2,1)S(1)} %copy-done.6), channel_id=1, source_target_pairs={{0,2},{1,3},{2,0},{3,1},{16,18},{17,19},{18,16},{19,17},{4,6},{5,7... | collective-permute-start | bytes 393224 | tf_op jit(solution)/shard_map/ppermute | solution.py:445
  47.3 4.0 %collective-permute-done.2.refs_2_ = bf16[128,512]{1,0:T(8,128)(2,1)S(1)} collective-permute-done((bf16[128,512]{1,0:T(8,128)(2,1)S(1)}, bf16[128,512]{1,0:T(8,128)(2,1)S(1)}, u32[]{:S(2)}, u32[]{:S(2)}) %collective-permute-start.2) | collective-permute-done | bytes 131104 | tf_op jit(solution)/shard_map/ppermute | solution.py:445
  51.3 1.9 %collective-permute-start.5 = (bf16[128,512]{1,0:T(8,128)(2,1)S(1)}, bf16[128,512]{1,0:T(8,128)(2,1)S(1)}, u32[]{:S(2)}, u32[]{:S(2)}) collective-permute-start(bf16[128,512]{1,0:T(8,128)(2,1)S(1)} %collective-permute-done.2.refs_2_), channel_id=1, source_target_pairs={{0,16},{16,0},{1,17},{17,1},{2,18},{18,2},{3,19},{19,3},{4,20},{20... | collective-permute-start | bytes 393224 | tf_op jit(solution)/shard_map/ppermute | solution.py:434
  54.8 6.6 %all-to-all-done.1.in_ref = bf16[32,7,8,128]{3,2,1,0:T(8,128)(2,1)S(1)} async-done(((bf16[32,7,8,128]{3,2,1,0:T(8,128)(2,1)}), bf16[32,7,8,128]{3,2,1,0:T(8,128)(2,1)S(1)}, u32[]{:S(2)}, u32[]{:S(2)}) %all-to-all-start.1) | async-done | bytes 458784 | tf_op jit(solution)/shard_map/all_to_all | solution.py:430
  62.8 1.1 %collective-permute-start.15 = (f32[32,256]{1,0:T(8,128)S(1)}, f32[32,256]{1,0:T(8,128)S(1)}, u32[]{:S(2)}, u32[]{:S(2)}) collective-permute-start(f32[32,256]{1,0:T(8,128)S(1)} %get-tuple-element.36), channel_id=1, source_target_pairs={{0,64},{32,96},{64,0},{96,32},{16,80},{48,112},{80,16},{112,48},{1... | collective-permute-start | bytes 98312 | tf_op jit(solution)/shard_map/ppermute | solution.py:445
  64.4 1.8 %collective-permute-start.7 = (bf16[2,224,128]{2,1,0:T(8,128)(2,1)S(1)}, bf16[2,224,128]{2,1,0:T(8,128)(2,1)S(1)}, u32[]{:S(2)}, u32[]{:S(2)}) collective-permute-start(bf16[2,224,128]{2,1,0:T(8,128)(2,1)S(1)} %get-tuple-element.29), channel_id=1, source_target_pairs={{0,1},{1,2},{2,3},{3,0},{16,19},{17,16},{18,17},{19,18},{4,5},{5,6... | collective-permute-start | bytes 344072 | tf_op jit(solution)/shard_map/ppermute | solution.py:445
  68.7 3.4 %all-to-all-start.2 = ((bf16[8,64,128]{2,1,0:T(8,128)(2,1)}), bf16[8,64,128]{2,1,0:T(8,128)(2,1)S(1)}, u32[]{:S(2)}, u32[]{:S(2)}) async-start(bf16[8,64,128]{2,1,0:T(8,128)(2,1)} %shard_map.184), calls=%async_computation.2 | async-start | bytes 262144 | tf_op jit(solution)/shard_map/all_to_all | solution.py:430
  72.0 4.6 %collective-permute-start.10 = (bf16[2,224,128]{2,1,0:T(8,128)(2,1)S(1)}, bf16[2,224,128]{2,1,0:T(8,128)(2,1)S(1)}, u32[]{:S(2)}, u32[]{:S(2)}) collective-permute-start(bf16[2,224,128]{2,1,0:T(8,128)(2,1)S(1)} %get-tuple-element.28.refs_0_), channel_id=1, source_target_pairs={{0,16},{16,0},{1,17},{17,1},{2,18},{18,2},{3,19},{19,3},{4,20},{20... | collective-permute-start | bytes 344072 | tf_op jit(solution)/shard_map/ppermute | solution.py:434
  78.5 1.4 %all-to-all-done.2.in_ref = bf16[8,64,128]{2,1,0:T(8,128)(2,1)S(1)} async-done(((bf16[8,64,128]{2,1,0:T(8,128)(2,1)}), bf16[8,64,128]{2,1,0:T(8,128)(2,1)S(1)}, u32[]{:S(2)}, u32[]{:S(2)}) %all-to-all-start.2) | async-done | bytes 131104 | tf_op jit(solution)/shard_map/all_to_all | solution.py:430
  80.6 6.2 %all-to-all-start.3 = ((bf16[16,64,128]{2,1,0:T(8,128)(2,1)}), bf16[16,64,128]{2,1,0:T(8,128)(2,1)S(1)}, u32[]{:S(2)}, u32[]{:S(2)}) async-start(bf16[16,64,128]{2,1,0:T(8,128)(2,1)} %shard_map.185), calls=%async_computation.3 | async-start | bytes 524288 | tf_op jit(solution)/shard_map/all_to_all | solution.py:430
  86.8 1.4 %shard_map.183 = (bf16[1,128,256]{2,1,0:T(8,128)(2,1)}, bf16[1,128,256]{2,1,0:T(8,128)(2,1)}, f32[3,768]{1,0:T(4,128)}, f32[128,256]{1,0:T(8,128)}, f32[128,256]{1,0:T(8,128)}) custom-call(bf16[2,224,128]{2,1,0:T(8,128)(2,1)S(1)} %get-tuple-element.28.refs_0_, bf16[2,224,128]{2,1,0:T(8,128)(2,1)S(1)} %collective-permute-done.7.refs_1_, ...), custom_call_target="tpu_custom_call" | custom-call | tf_op jit(solution)/shard_map/pallas_call | solution.py:488
  88.2 5.9 %all-to-all-done.3.own_ref = bf16[16,64,128]{2,1,0:T(8,128)(2,1)S(1)} async-done(((bf16[16,64,128]{2,1,0:T(8,128)(2,1)}), bf16[16,64,128]{2,1,0:T(8,128)(2,1)S(1)}, u32[]{:S(2)}, u32[]{:S(2)}) %all-to-all-start.3) | async-done | bytes 262176 | tf_op jit(solution)/shard_map/all_to_all | solution.py:430
  94.1 6.0 %collective-permute-start.17 = (bf16[16,64,128]{2,1,0:T(8,128)(2,1)S(1)}, bf16[16,64,128]{2,1,0:T(8,128)(2,1)S(1)}, u32[]{:S(2)}, u32[]{:S(2)}) collective-permute-start(bf16[16,64,128]{2,1,0:T(8,128)(2,1)S(1)} %all-to-all-done.3.own_ref), channel_id=1, source_target_pairs={{0,16},{16,0},{1,17},{17,1},{2,18},{18,2},{3,19},{19,3},{4,20},{20... | collective-permute-start | bytes 786440 | tf_op jit(solution)/shard_map/ppermute | solution.py:434
  100.2 1.2 %collective-permute-done.17.other_ref = bf16[16,64,128]{2,1,0:T(8,128)(2,1)S(1)} collective-permute-done((bf16[16,64,128]{2,1,0:T(8,128)(2,1)S(1)}, bf16[16,64,128]{2,1,0:T(8,128)(2,1)S(1)}, u32[]{:S(2)}, u32[]{:S(2)}) %collective-permute-start.17) | collective-permute-done | bytes 262176 | tf_op jit(solution)/shard_map/ppermute | solution.py:434
  101.3 1.3 %shard_map.186 = (f32[256,768]{1,0:T(8,128)}, f32[256,256]{1,0:T(8,128)}) custom-call(bf16[16,64,128]{2,1,0:T(8,128)(2,1)S(1)} %all-to-all-done.3.own_ref, bf16[16,64,128]{2,1,0:T(8,128)(2,1)S(1)} %collective-permute-done.17.other_ref), custom_call_target="tpu_custom_call" | custom-call | tf_op jit(solution)/shard_map/pallas_call | solution.py:499
  (47 shorter events, 8.5 us)
Async XLA Ops:
  0.6 36.4 %copy-start.4 = (bf16[128,768]{1,0:T(8,128)(2,1)S(1)}, bf16[128,768]{1,0:T(8,128)(2,1)}, u32[]{:S(2)}) copy-start(bf16[128,768]{1,0:T(8,128)(2,1)} %constant.15.clone.first_back_ref) | copy-start | bytes 589828
  0.6 36.3 %copy-start.5 = (bf16[256,384]{1,0:T(8,128)(2,1)S(1)}, bf16[256,384]{1,0:T(8,128)(2,1)}, u32[]{:S(2)}) copy-start(bf16[256,384]{1,0:T(8,128)(2,1)} %constant.12.clone.first_ref) | copy-start | bytes 589828
  3.2 33.8 %all-to-all-start = ((bf16[256,2,384]{2,1,0:T(2,128)(2,1)}), bf16[256,2,384]{2,1,0:T(2,128)(2,1)S(1)}, u32[]{:S(2)}, u32[]{:S(2)}) async-start(bf16[256,2,384]{2,1,0:T(2,128)(2,1)} %get-tuple-element.26), calls=%async_computation | async-start | bytes 786432 | tf_op jit(solution)/shard_map/all_to_all | solution.py:430
  18.9 6.1 %collective-permute-start.1 = (bf16[128,512]{1,0:T(8,128)(2,1)}, bf16[128,512]{1,0:T(8,128)(2,1)S(1)}, u32[]{:S(2)}, u32[]{:S(2)}) collective-permute-start(bf16[128,512]{1,0:T(8,128)(2,1)} %get-tuple-element.27.refs_0_), channel_id=1, source_target_pairs={{0,3},{1,0},{2,1},{3,2},{16,17},{17,18},{18,19},{19,16},{4,7},{5,4... | collective-permute-start | bytes 393224 | tf_op jit(solution)/shard_map/ppermute | solution.py:445
  20.4 6.0 %collective-permute-start = (bf16[128,512]{1,0:T(8,128)(2,1)}, bf16[128,512]{1,0:T(8,128)(2,1)S(1)}, u32[]{:S(2)}, u32[]{:S(2)}) collective-permute-start(bf16[128,512]{1,0:T(8,128)(2,1)} %get-tuple-element.27.refs_0_), channel_id=1, source_target_pairs={{0,1},{1,2},{2,3},{3,0},{16,19},{17,16},{18,17},{19,18},{4,5},{5,6... | collective-permute-start | bytes 393224 | tf_op jit(solution)/shard_map/ppermute | solution.py:445
  41.6 19.7 %all-to-all-start.1 = ((bf16[32,7,8,128]{3,2,1,0:T(8,128)(2,1)}), bf16[32,7,8,128]{3,2,1,0:T(8,128)(2,1)S(1)}, u32[]{:S(2)}, u32[]{:S(2)}) async-start(bf16[32,7,8,128]{3,2,1,0:T(8,128)(2,1)} %shard_map.181), calls=%async_computation.1 | async-start | bytes 917504 | tf_op jit(solution)/shard_map/all_to_all | solution.py:430
  45.7 5.6 %collective-permute-start.2 = (bf16[128,512]{1,0:T(8,128)(2,1)S(1)}, bf16[128,512]{1,0:T(8,128)(2,1)S(1)}, u32[]{:S(2)}, u32[]{:S(2)}) collective-permute-start(bf16[128,512]{1,0:T(8,128)(2,1)S(1)} %copy-done.6), channel_id=1, source_target_pairs={{0,2},{1,3},{2,0},{3,1},{16,18},{17,19},{18,16},{19,17},{4,6},{5,7... | collective-permute-start | bytes 393224 | tf_op jit(solution)/shard_map/ppermute | solution.py:445
  47.3 6.5 %collective-permute-start.3 = (bf16[128,512]{1,0:T(8,128)(2,1)S(1)}, bf16[128,512]{1,0:T(8,128)(2,1)S(1)}, u32[]{:S(2)}, u32[]{:S(2)}) collective-permute-start(bf16[128,512]{1,0:T(8,128)(2,1)S(1)} %copy-done.6), channel_id=1, source_target_pairs={{0,16},{16,0},{1,17},{17,1},{2,18},{18,2},{3,19},{19,3},{4,20},{20... | collective-permute-start | bytes 393224 | tf_op jit(solution)/shard_map/ppermute | solution.py:434
  51.3 2.9 %collective-permute-start.5 = (bf16[128,512]{1,0:T(8,128)(2,1)S(1)}, bf16[128,512]{1,0:T(8,128)(2,1)S(1)}, u32[]{:S(2)}, u32[]{:S(2)}) collective-permute-start(bf16[128,512]{1,0:T(8,128)(2,1)S(1)} %collective-permute-done.2.refs_2_), channel_id=1, source_target_pairs={{0,16},{16,0},{1,17},{17,1},{2,18},{18,2},{3,19},{19,3},{4,20},{20... | collective-permute-start | bytes 393224 | tf_op jit(solution)/shard_map/ppermute | solution.py:434
  53.3 1.3 %collective-permute-start.6 = (bf16[128,512]{1,0:T(8,128)(2,1)S(1)}, bf16[128,512]{1,0:T(8,128)(2,1)S(1)}, u32[]{:S(2)}, u32[]{:S(2)}) collective-permute-start(bf16[128,512]{1,0:T(8,128)(2,1)S(1)} %collective-permute-done.1.rest_1_.refs_3_), channel_id=1, source_target_pairs={{0,16},{16,0},{1,17},{17,1},{2,18},{18,2},{3,19},{19,3},{4,20},{20... | collective-permute-start | bytes 393224 | tf_op jit(solution)/shard_map/ppermute | solution.py:434
  53.3 1.5 %collective-permute-start.4 = (bf16[128,512]{1,0:T(8,128)(2,1)S(1)}, bf16[128,512]{1,0:T(8,128)(2,1)S(1)}, u32[]{:S(2)}, u32[]{:S(2)}) collective-permute-start(bf16[128,512]{1,0:T(8,128)(2,1)S(1)} %collective-permute-done.rest_0_.refs_1_), channel_id=1, source_target_pairs={{0,16},{16,0},{1,17},{17,1},{2,18},{18,2},{3,19},{19,3},{4,20},{20... | collective-permute-start | bytes 393224 | tf_op jit(solution)/shard_map/ppermute | solution.py:434
  61.9 5.2 %collective-permute-start.14 = (f32[32,256]{1,0:T(8,128)S(1)}, f32[32,256]{1,0:T(8,128)S(1)}, u32[]{:S(2)}, u32[]{:S(2)}) collective-permute-start(f32[32,256]{1,0:T(8,128)S(1)} %get-tuple-element.35), channel_id=1, source_target_pairs={{0,32},{32,64},{64,96},{96,0},{16,112},{48,16},{80,48},{112,80},{1... | collective-permute-start | bytes 98312 | tf_op jit(solution)/shard_map/ppermute | solution.py:445
  62.8 5.2 %collective-permute-start.15 = (f32[32,256]{1,0:T(8,128)S(1)}, f32[32,256]{1,0:T(8,128)S(1)}, u32[]{:S(2)}, u32[]{:S(2)}) collective-permute-start(f32[32,256]{1,0:T(8,128)S(1)} %get-tuple-element.36), channel_id=1, source_target_pairs={{0,64},{32,96},{64,0},{96,32},{16,80},{48,112},{80,16},{112,48},{1... | collective-permute-start | bytes 98312 | tf_op jit(solution)/shard_map/ppermute | solution.py:445
  63.9 4.1 %collective-permute-start.16 = (f32[32,256]{1,0:T(8,128)S(1)}, f32[32,256]{1,0:T(8,128)S(1)}, u32[]{:S(2)}, u32[]{:S(2)}) collective-permute-start(f32[32,256]{1,0:T(8,128)S(1)} %get-tuple-element.37), channel_id=1, source_target_pairs={{0,96},{32,0},{64,32},{96,64},{16,48},{48,80},{80,112},{112,16},{1... | collective-permute-start | bytes 98312 | tf_op jit(solution)/shard_map/ppermute | solution.py:445
  64.4 12.3 %collective-permute-start.7 = (bf16[2,224,128]{2,1,0:T(8,128)(2,1)S(1)}, bf16[2,224,128]{2,1,0:T(8,128)(2,1)S(1)}, u32[]{:S(2)}, u32[]{:S(2)}) collective-permute-start(bf16[2,224,128]{2,1,0:T(8,128)(2,1)S(1)} %get-tuple-element.29), channel_id=1, source_target_pairs={{0,1},{1,2},{2,3},{3,0},{16,19},{17,16},{18,17},{19,18},{4,5},{5,6... | collective-permute-start | bytes 344072 | tf_op jit(solution)/shard_map/ppermute | solution.py:445
  66.2 10.6 %collective-permute-start.8 = (bf16[2,224,128]{2,1,0:T(8,128)(2,1)S(1)}, bf16[2,224,128]{2,1,0:T(8,128)(2,1)S(1)}, u32[]{:S(2)}, u32[]{:S(2)}) collective-permute-start(bf16[2,224,128]{2,1,0:T(8,128)(2,1)S(1)} %get-tuple-element.30), channel_id=1, source_target_pairs={{0,2},{1,3},{2,0},{3,1},{16,18},{17,19},{18,16},{19,17},{4,6},{5,7... | collective-permute-start | bytes 344072 | tf_op jit(solution)/shard_map/ppermute | solution.py:445
  67.1 10.1 %collective-permute-start.9 = (bf16[2,224,128]{2,1,0:T(8,128)(2,1)S(1)}, bf16[2,224,128]{2,1,0:T(8,128)(2,1)S(1)}, u32[]{:S(2)}, u32[]{:S(2)}) collective-permute-start(bf16[2,224,128]{2,1,0:T(8,128)(2,1)S(1)} %get-tuple-element.31), channel_id=1, source_target_pairs={{0,3},{1,0},{2,1},{3,2},{16,17},{17,18},{18,19},{19,16},{4,7},{5,4... | collective-permute-start | bytes 344072 | tf_op jit(solution)/shard_map/ppermute | solution.py:445
  68.7 11.2 %all-to-all-start.2 = ((bf16[8,64,128]{2,1,0:T(8,128)(2,1)}), bf16[8,64,128]{2,1,0:T(8,128)(2,1)S(1)}, u32[]{:S(2)}, u32[]{:S(2)}) async-start(bf16[8,64,128]{2,1,0:T(8,128)(2,1)} %shard_map.184), calls=%async_computation.2 | async-start | bytes 262144 | tf_op jit(solution)/shard_map/all_to_all | solution.py:430
  72.0 5.6 %collective-permute-start.10 = (bf16[2,224,128]{2,1,0:T(8,128)(2,1)S(1)}, bf16[2,224,128]{2,1,0:T(8,128)(2,1)S(1)}, u32[]{:S(2)}, u32[]{:S(2)}) collective-permute-start(bf16[2,224,128]{2,1,0:T(8,128)(2,1)S(1)} %get-tuple-element.28.refs_0_), channel_id=1, source_target_pairs={{0,16},{16,0},{1,17},{17,1},{2,18},{18,2},{3,19},{19,3},{4,20},{20... | collective-permute-start | bytes 344072 | tf_op jit(solution)/shard_map/ppermute | solution.py:434
  76.7 1.3 %collective-permute-start.11 = (bf16[2,224,128]{2,1,0:T(8,128)(2,1)S(1)}, bf16[2,224,128]{2,1,0:T(8,128)(2,1)S(1)}, u32[]{:S(2)}, u32[]{:S(2)}) collective-permute-start(bf16[2,224,128]{2,1,0:T(8,128)(2,1)S(1)} %collective-permute-done.7.refs_1_), channel_id=1, source_target_pairs={{0,16},{16,0},{1,17},{17,1},{2,18},{18,2},{3,19},{19,3},{4,20},{20... | collective-permute-start | bytes 344072 | tf_op jit(solution)/shard_map/ppermute | solution.py:434
  76.8 1.4 %collective-permute-start.12 = (bf16[2,224,128]{2,1,0:T(8,128)(2,1)S(1)}, bf16[2,224,128]{2,1,0:T(8,128)(2,1)S(1)}, u32[]{:S(2)}, u32[]{:S(2)}) collective-permute-start(bf16[2,224,128]{2,1,0:T(8,128)(2,1)S(1)} %collective-permute-done.8.refs_2_), channel_id=1, source_target_pairs={{0,16},{16,0},{1,17},{17,1},{2,18},{18,2},{3,19},{19,3},{4,20},{20... | collective-permute-start | bytes 344072 | tf_op jit(solution)/shard_map/ppermute | solution.py:434
  77.2 1.3 %collective-permute-start.13 = (bf16[2,224,128]{2,1,0:T(8,128)(2,1)S(1)}, bf16[2,224,128]{2,1,0:T(8,128)(2,1)S(1)}, u32[]{:S(2)}, u32[]{:S(2)}) collective-permute-start(bf16[2,224,128]{2,1,0:T(8,128)(2,1)S(1)} %collective-permute-done.9.refs_3_), channel_id=1, source_target_pairs={{0,16},{16,0},{1,17},{17,1},{2,18},{18,2},{3,19},{19,3},{4,20},{20... | collective-permute-start | bytes 344072 | tf_op jit(solution)/shard_map/ppermute | solution.py:434
  80.6 13.5 %all-to-all-start.3 = ((bf16[16,64,128]{2,1,0:T(8,128)(2,1)}), bf16[16,64,128]{2,1,0:T(8,128)(2,1)S(1)}, u32[]{:S(2)}, u32[]{:S(2)}) async-start(bf16[16,64,128]{2,1,0:T(8,128)(2,1)} %shard_map.185), calls=%async_computation.3 | async-start | bytes 524288 | tf_op jit(solution)/shard_map/all_to_all | solution.py:430
  94.1 7.2 %collective-permute-start.17 = (bf16[16,64,128]{2,1,0:T(8,128)(2,1)S(1)}, bf16[16,64,128]{2,1,0:T(8,128)(2,1)S(1)}, u32[]{:S(2)}, u32[]{:S(2)}) collective-permute-start(bf16[16,64,128]{2,1,0:T(8,128)(2,1)S(1)} %all-to-all-done.3.own_ref), channel_id=1, source_target_pairs={{0,16},{16,0},{1,17},{17,1},{2,18},{18,2},{3,19},{19,3},{4,20},{20... | collective-permute-start | bytes 786440 | tf_op jit(solution)/shard_map/ppermute | solution.py:434
  (8 other events, 193.0 us)

commit v13 on v12

--- a/solution.py
+++ b/solution.py
@@ -242,7 +242,8 @@
 
     new = lax.broadcasted_iota(jnp.int32, (blocks, blocks), 0)
     old = lax.broadcasted_iota(jnp.int32, (blocks, blocks), 1)
-    wanted = (new & 99) | (((new >> 2) & 1) << 4) | (((new >> 3) & 3) << 2)
+    wanted = (((new >> 3) & 3) << 5) | (((new >> 6) & 1) << 4) | (((new >> 1) & 3) << 2)
+    wanted = wanted | (((new >> 5) & 1) << 1) | (new & 1)
     reorder = jnp.where(old == wanted, 1.0, 0.0).astype(jnp.bfloat16)
     sums = [[0.0] * 3 for _ in range(3)]
     for m in members:
@@ -261,13 +262,16 @@
         sent.extend(grad_filters)
         turned = bf16_dot(reorder, jnp.concatenate(sent, 1).astype(jnp.bfloat16))
         half = out_ref.shape[0] // 2
+        count = 2 * half
         for index in range(len(sent)):
-            out_ref[m * half : (m + 1) * half, index] = (
-                turned[:, index * rows : (index + 1) * rows]
-                .reshape(half, blocks // half, rows)
-                .astype(jnp.bfloat16)
-            )
-    shape = (blocks // half, rows)
+            for pair in range(4):
+                place = (index * 4 + pair) * rows
+                out_ref[m * half : (m + 1) * half, :, place : place + rows] = (
+                    turned[pair * count : (pair + 1) * count, index * rows : (index + 1) * rows]
+                    .reshape(half, 2, rows)
+                    .astype(jnp.bfloat16)
+                )
+    shape = (2, rows)
     sum_lane = lax.broadcasted_iota(jnp.int32, shape, 1)
     line = jnp.zeros(shape, jnp.float32)
     for g in range(3):
@@ -276,7 +280,9 @@
             high = total.astype(jnp.bfloat16).astype(jnp.float32)
             line = jnp.where(sum_lane == g * 3 + tap, high, line)
             line = jnp.where(sum_lane == 16 + g * 3 + tap, total - high, line)
-    out_ref[:, 6] = jnp.broadcast_to(line[None], (2 * half,) + shape).astype(jnp.bfloat16)
+    out_ref[:, :, 24 * rows :] = jnp.broadcast_to(line[None], (2 * half,) + shape).astype(
+        jnp.bfloat16
+    )
 
 
 def channel_order(place_of):
@@ -290,23 +296,28 @@
 def part_kernel(in_ref, *refs):
     both_refs, part_refs, send_refs = refs[:8], refs[8:12], refs[12:16]
     rows_ref, sums_ref = refs[16:]
-    sources, kinds, blocks, rows = in_ref.shape
+    tiles, rows = rows_ref.shape[0], rows_ref.shape[2]
+    sources = in_ref.shape[0]
     width = both_refs[0].shape[1] // 2
     x, core, y = lax.axis_index("x"), lax.axis_index("core"), lax.axis_index("y")
     turn = 1 - 2 * core
-    rows_ref[...] = in_ref[...].astype(jnp.float32).reshape(sources * kinds * blocks, rows)
+    for tile in range(tiles):
+        rows_ref[tile] = (
+            in_ref[:, :, tile * rows : (tile + 1) * rows]
+            .astype(jnp.float32)
+            .reshape(sources * 2, rows)
+        )
+    sums = rows_ref[tiles - 1, pl.ds(0, sources, stride=2), :]
     out_part = jnp.zeros((sources, width), jnp.float32)
     in_part = jnp.zeros((3 * sources, width), jnp.float32)
     for other in range(2):
         for ahead in range(4):
             block = (core ^ other) * 4 + ((y + turn * ahead) & 3)
-            kept = jnp.concatenate(
-                [
-                    rows_ref[pl.ds(kind * blocks + block, sources, stride=kinds * blocks), :]
-                    for kind in range(kinds)
-                ],
-                0,
-            ).astype(jnp.bfloat16)
+            kept = [
+                rows_ref[kind * 4 + (block >> 1), pl.ds(block & 1, sources, stride=2), :]
+                for kind in range(6)
+            ]
+            kept = jnp.concatenate(kept + [sums], 0).astype(jnp.bfloat16)
             send_refs[ahead][other] = kept
             both_ref = both_refs[4 + ahead if other else (4 - ahead) % 4]
             out_part += bf16_dot(kept[:sources], both_ref[:, width:])
@@ -464,7 +475,7 @@
     tables = [jnp.asarray(t) for t in transform_tables(devices // 2, rows)]
     back = call(
         convolve_kernel,
-        shape((32, 7, 8, rows), bf16),
+        shape((32, 2, 25 * rows), bf16),
         [pltpu.VMEM((3, 2 * devices, rows), f32)],
         in_specs=specs(*[pltpu.VMEM] * (2 + len(tables)), *[pl.ANY] * 2),
     )(received, short_kernel, *tables, gathered[1], gathered[3])
@@ -472,7 +483,7 @@
     found = call(
         part_kernel,
         (shape((32, width), f32),) * 4 + (shape((2, 7 * 32, rows), bf16),) * 4,
-        [pltpu.VMEM((32 * 7 * 8, rows), f32), pltpu.VMEM((4, 32, width), f32)],
+        [pltpu.VMEM((25, 64, rows), f32), pltpu.VMEM((4, 32, width), f32)],
     )(halfway, *gathered)
     part = [found[0]] + [ring(found[distance], "x", distance) for distance in (1, 2, 3)]
     arrived = [found[4]] + [ring(found[4 + i], "y", i) for i in (1, 2, 3)]

time: 103 us -> 102 us (level)
  waiting for transfers between devices: 36.6 us -> 35.5 us
    all_to_all x4, waiting for transfers between devices: 24.5 us -> 23.5 us  [exchange(): return lax.all_to_all(x, axes, split_axis=0, concat_axis=0, tiled=True)]
where the time goes in v13:
time: 102 us
  starting transfers between devices  53.6 us (53%)
  waiting for transfers between devices  35.5 us (35%)
  Pallas kernels  11.9 us (12%)
    all_to_all x4, starting transfers between devices, exchange(): return lax.all_to_all(x, axes, split_axis=0, concat_axis=0, tiled=True)  29.3 us
    all_to_all x4, waiting for transfers between devices, exchange(): return lax.all_to_all(x, axes, split_axis=0, concat_axis=0, tiled=True)  23.5 us
    ppermute x9, starting transfers between devices, swap_core(): return lax.ppermute(x, 'core', [(0, 1), (1, 0)])  13.8 us
    ppermute x9, starting transfers between devices, ring(): return lax.ppermute(x, axes, route)  10.5 us
    ppermute x9, waiting for transfers between devices, ring(): return lax.ppermute(x, axes, route)  8.66 us
    pallas_call x1, Pallas kernels, per_device(): call(convolve_kernel, shape((32, 2, 25 * rows), bf16), [pltpu.VMEM((3, 2...  4.73 us
    ppermute x9, waiting for transfers between devices, swap_core(): return lax.ppermute(x, 'core', [(0, 1), (1, 0)])  3.4 us
    pallas_call x1, Pallas kernels, per_device(): call(pack_kernel, (shape((width, 2, 3 * rows), bf16), shape((rows, 2 * wi...  2.53 us
  transfers between devices with their start and end apart: 22, of which 15 were waited for; matrix products, arithmetic and copies ran while one was open for 0% of the time, Pallas kernels for 2%

profile of v13, /device:TPU:1, one launch (start us, length us, event | category | flops | bytes accessed | tf_op | source)
XLA Modules:
  0.0 101.9 jit_solution(17026212045132507606)
XLA Ops:
  0.7 2.5 %shard_map.180 = (bf16[256,2,384]{2,1,0:T(2,128)(2,1)}, bf16[128,512]{1,0:T(8,128)(2,1)}) custom-call(bf16[1,128,256]{2,1,0:T(8,128)(2,1)} %seq_ref.1, bf16[256,768]{1,0:T(8,128)(2,1)} %refs_8_.1, f32[128,256]{1,0:T(8,128)} %one_ref.1, f32[128,256]{1,0:T(8,128)} %two_ref.1, bf16[256,256]{1,0:T(8,128)(2,1)} %refs_9_.1, bf16[1,128,256]{2,1,0:T(8,128)(2,1)} %grad_ref.1), custom_call_target="tpu_custom_call" | custom-call | tf_op jit(solution)/shard_map/pallas_call | solution.py:466
  3.2 15.7 %all-to-all-start = ((bf16[256,2,384]{2,1,0:T(2,128)(2,1)}), bf16[256,2,384]{2,1,0:T(2,128)(2,1)S(1)}, u32[]{:S(2)}, u32[]{:S(2)}) async-start(bf16[256,2,384]{2,1,0:T(2,128)(2,1)} %get-tuple-element.26), calls=%async_computation | async-start | bytes 786432 | tf_op jit(solution)/shard_map/all_to_all | solution.py:441
  18.9 1.5 %collective-permute-start.1 = (bf16[128,512]{1,0:T(8,128)(2,1)}, bf16[128,512]{1,0:T(8,128)(2,1)S(1)}, u32[]{:S(2)}, u32[]{:S(2)}) collective-permute-start(bf16[128,512]{1,0:T(8,128)(2,1)} %get-tuple-element.27.refs_0_), channel_id=1, source_target_pairs={{0,3},{1,0},{2,1},{3,2},{16,17},{17,18},{18,19},{19,16},{4,7},{5,4... | collective-permute-start | bytes 393224 | tf_op jit(solution)/shard_map/ppermute | solution.py:456
  20.4 1.4 %collective-permute-start = (bf16[128,512]{1,0:T(8,128)(2,1)}, bf16[128,512]{1,0:T(8,128)(2,1)S(1)}, u32[]{:S(2)}, u32[]{:S(2)}) collective-permute-start(bf16[128,512]{1,0:T(8,128)(2,1)} %get-tuple-element.27.refs_0_), channel_id=1, source_target_pairs={{0,1},{1,2},{2,3},{3,0},{16,19},{17,16},{18,17},{19,18},{4,5},{5,6... | collective-permute-start | bytes 393224 | tf_op jit(solution)/shard_map/ppermute | solution.py:456
  21.7 3.3 %collective-permute-done.1.rest_1_.refs_3_ = bf16[128,512]{1,0:T(8,128)(2,1)S(1)} collective-permute-done((bf16[128,512]{1,0:T(8,128)(2,1)}, bf16[128,512]{1,0:T(8,128)(2,1)S(1)}, u32[]{:S(2)}, u32[]{:S(2)}) %collective-permute-start.1) | collective-permute-done | bytes 131104 | tf_op jit(solution)/shard_map/ppermute | solution.py:456
  25.0 1.3 %collective-permute-done.rest_0_.refs_1_ = bf16[128,512]{1,0:T(8,128)(2,1)S(1)} collective-permute-done((bf16[128,512]{1,0:T(8,128)(2,1)}, bf16[128,512]{1,0:T(8,128)(2,1)S(1)}, u32[]{:S(2)}, u32[]{:S(2)}) %collective-permute-start) | collective-permute-done | bytes 131104 | tf_op jit(solution)/shard_map/ppermute | solution.py:456
  26.3 10.7 %all-to-all-done.in_ref = bf16[256,2,384]{2,1,0:T(2,128)(2,1)S(1)} async-done(((bf16[256,2,384]{2,1,0:T(2,128)(2,1)}), bf16[256,2,384]{2,1,0:T(2,128)(2,1)S(1)}, u32[]{:S(2)}, u32[]{:S(2)}) %all-to-all-start) | async-done | bytes 393248 | tf_op jit(solution)/shard_map/all_to_all | solution.py:441
  37.0 4.7 %shard_map.181 = bf16[32,2,3200]{2,1,0:T(2,128)(2,1)} custom-call(bf16[256,2,384]{2,1,0:T(2,128)(2,1)S(1)} %all-to-all-done.in_ref, f32[3,768]{1,0:T(4,128)S(1)} %copy-done.9, bf16[256,384]{1,0:T(8,128)(2,1)S(1)} %copy-done.5, bf16[768,256]{1,0:T(8,128)(2,1)S(1)} %copy-done.3, bf16[768,256]{1,0:T(8,128)(2,1)S(1)} %copy-done.2, ...), custom_call_target="tpu_custom_call" | custom-call | tf_op jit(solution)/shard_map/pallas_call | solution.py:476
  41.8 4.0 %all-to-all-start.1 = ((bf16[32,2,3200]{2,1,0:T(2,128)(2,1)}), bf16[32,2,3200]{2,1,0:T(2,128)(2,1)S(1)}, u32[]{:S(2)}, u32[]{:S(2)}) async-start(bf16[32,2,3200]{2,1,0:T(2,128)(2,1)} %shard_map.181), calls=%async_computation.1 | async-start | bytes 819200 | tf_op jit(solution)/shard_map/all_to_all | solution.py:441
  45.8 1.6 %collective-permute-start.2 = (bf16[128,512]{1,0:T(8,128)(2,1)S(1)}, bf16[128,512]{1,0:T(8,128)(2,1)S(1)}, u32[]{:S(2)}, u32[]{:S(2)}) collective-permute-start(bf16[128,512]{1,0:T(8,128)(2,1)S(1)} %copy-done.6), channel_id=1, source_target_pairs={{0,2},{1,3},{2,0},{3,1},{16,18},{17,19},{18,16},{19,17},{4,6},{5,7... | collective-permute-start | bytes 393224 | tf_op jit(solution)/shard_map/ppermute | solution.py:456
  47.4 4.0 %collective-permute-done.2.refs_2_ = bf16[128,512]{1,0:T(8,128)(2,1)S(1)} collective-permute-done((bf16[128,512]{1,0:T(8,128)(2,1)S(1)}, bf16[128,512]{1,0:T(8,128)(2,1)S(1)}, u32[]{:S(2)}, u32[]{:S(2)}) %collective-permute-start.2) | collective-permute-done | bytes 131104 | tf_op jit(solution)/shard_map/ppermute | solution.py:456
  51.4 2.0 %collective-permute-start.5 = (bf16[128,512]{1,0:T(8,128)(2,1)S(1)}, bf16[128,512]{1,0:T(8,128)(2,1)S(1)}, u32[]{:S(2)}, u32[]{:S(2)}) collective-permute-start(bf16[128,512]{1,0:T(8,128)(2,1)S(1)} %collective-permute-done.2.refs_2_), channel_id=1, source_target_pairs={{0,16},{16,0},{1,17},{17,1},{2,18},{18,2},{3,19},{19,3},{4,20},{20... | collective-permute-start | bytes 393224 | tf_op jit(solution)/shard_map/ppermute | solution.py:445
  54.9 5.5 %all-to-all-done.1.in_ref = bf16[32,2,3200]{2,1,0:T(2,128)(2,1)S(1)} async-done(((bf16[32,2,3200]{2,1,0:T(2,128)(2,1)}), bf16[32,2,3200]{2,1,0:T(2,128)(2,1)S(1)}, u32[]{:S(2)}, u32[]{:S(2)}) %all-to-all-start.1) | async-done | bytes 409632 | tf_op jit(solution)/shard_map/all_to_all | solution.py:441
  62.0 1.1 %collective-permute-start.15 = (f32[32,256]{1,0:T(8,128)S(1)}, f32[32,256]{1,0:T(8,128)S(1)}, u32[]{:S(2)}, u32[]{:S(2)}) collective-permute-start(f32[32,256]{1,0:T(8,128)S(1)} %get-tuple-element.36), channel_id=1, source_target_pairs={{0,64},{32,96},{64,0},{96,32},{16,80},{48,112},{80,16},{112,48},{1... | collective-permute-start | bytes 98312 | tf_op jit(solution)/shard_map/ppermute | solution.py:456
  63.5 1.9 %collective-permute-start.7 = (bf16[2,224,128]{2,1,0:T(8,128)(2,1)S(1)}, bf16[2,224,128]{2,1,0:T(8,128)(2,1)S(1)}, u32[]{:S(2)}, u32[]{:S(2)}) collective-permute-start(bf16[2,224,128]{2,1,0:T(8,128)(2,1)S(1)} %get-tuple-element.29), channel_id=1, source_target_pairs={{0,1},{1,2},{2,3},{3,0},{16,19},{17,16},{18,17},{19,18},{4,5},{5,6... | collective-permute-start | bytes 344072 | tf_op jit(solution)/shard_map/ppermute | solution.py:456
  67.8 3.4 %all-to-all-start.2 = ((bf16[8,64,128]{2,1,0:T(8,128)(2,1)}), bf16[8,64,128]{2,1,0:T(8,128)(2,1)S(1)}, u32[]{:S(2)}, u32[]{:S(2)}) async-start(bf16[8,64,128]{2,1,0:T(8,128)(2,1)} %shard_map.184), calls=%async_computation.2 | async-start | bytes 262144 | tf_op jit(solution)/shard_map/all_to_all | solution.py:441
  71.2 4.6 %collective-permute-start.10 = (bf16[2,224,128]{2,1,0:T(8,128)(2,1)S(1)}, bf16[2,224,128]{2,1,0:T(8,128)(2,1)S(1)}, u32[]{:S(2)}, u32[]{:S(2)}) collective-permute-start(bf16[2,224,128]{2,1,0:T(8,128)(2,1)S(1)} %get-tuple-element.28.refs_0_), channel_id=1, source_target_pairs={{0,16},{16,0},{1,17},{17,1},{2,18},{18,2},{3,19},{19,3},{4,20},{20... | collective-permute-start | bytes 344072 | tf_op jit(solution)/shard_map/ppermute | solution.py:445
  77.7 1.4 %all-to-all-done.2.in_ref = bf16[8,64,128]{2,1,0:T(8,128)(2,1)S(1)} async-done(((bf16[8,64,128]{2,1,0:T(8,128)(2,1)}), bf16[8,64,128]{2,1,0:T(8,128)(2,1)S(1)}, u32[]{:S(2)}, u32[]{:S(2)}) %all-to-all-start.2) | async-done | bytes 131104 | tf_op jit(solution)/shard_map/all_to_all | solution.py:441
  79.8 6.2 %all-to-all-start.3 = ((bf16[16,64,128]{2,1,0:T(8,128)(2,1)}), bf16[16,64,128]{2,1,0:T(8,128)(2,1)S(1)}, u32[]{:S(2)}, u32[]{:S(2)}) async-start(bf16[16,64,128]{2,1,0:T(8,128)(2,1)} %shard_map.185), calls=%async_computation.3 | async-start | bytes 524288 | tf_op jit(solution)/shard_map/all_to_all | solution.py:441
  86.0 1.4 %shard_map.183 = (bf16[1,128,256]{2,1,0:T(8,128)(2,1)}, bf16[1,128,256]{2,1,0:T(8,128)(2,1)}, f32[3,768]{1,0:T(4,128)}, f32[128,256]{1,0:T(8,128)}, f32[128,256]{1,0:T(8,128)}) custom-call(bf16[2,224,128]{2,1,0:T(8,128)(2,1)S(1)} %get-tuple-element.28.refs_0_, bf16[2,224,128]{2,1,0:T(8,128)(2,1)S(1)} %collective-permute-done.7.refs_1_, ...), custom_call_target="tpu_custom_call" | custom-call | tf_op jit(solution)/shard_map/pallas_call | solution.py:499
  87.4 5.9 %all-to-all-done.3.own_ref = bf16[16,64,128]{2,1,0:T(8,128)(2,1)S(1)} async-done(((bf16[16,64,128]{2,1,0:T(8,128)(2,1)}), bf16[16,64,128]{2,1,0:T(8,128)(2,1)S(1)}, u32[]{:S(2)}, u32[]{:S(2)}) %all-to-all-start.3) | async-done | bytes 262176 | tf_op jit(solution)/shard_map/all_to_all | solution.py:441
  93.3 6.1 %collective-permute-start.17 = (bf16[16,64,128]{2,1,0:T(8,128)(2,1)S(1)}, bf16[16,64,128]{2,1,0:T(8,128)(2,1)S(1)}, u32[]{:S(2)}, u32[]{:S(2)}) collective-permute-start(bf16[16,64,128]{2,1,0:T(8,128)(2,1)S(1)} %all-to-all-done.3.own_ref), channel_id=1, source_target_pairs={{0,16},{16,0},{1,17},{17,1},{2,18},{18,2},{3,19},{19,3},{4,20},{20... | collective-permute-start | bytes 786440 | tf_op jit(solution)/shard_map/ppermute | solution.py:445
  99.5 1.2 %collective-permute-done.17.other_ref = bf16[16,64,128]{2,1,0:T(8,128)(2,1)S(1)} collective-permute-done((bf16[16,64,128]{2,1,0:T(8,128)(2,1)S(1)}, bf16[16,64,128]{2,1,0:T(8,128)(2,1)S(1)}, u32[]{:S(2)}, u32[]{:S(2)}) %collective-permute-start.17) | collective-permute-done | bytes 262176 | tf_op jit(solution)/shard_map/ppermute | solution.py:445
  100.6 1.3 %shard_map.186 = (f32[256,768]{1,0:T(8,128)}, f32[256,256]{1,0:T(8,128)}) custom-call(bf16[16,64,128]{2,1,0:T(8,128)(2,1)S(1)} %all-to-all-done.3.own_ref, bf16[16,64,128]{2,1,0:T(8,128)(2,1)S(1)} %collective-permute-done.17.other_ref), custom_call_target="tpu_custom_call" | custom-call | tf_op jit(solution)/shard_map/pallas_call | solution.py:510
  (47 shorter events, 8.6 us)
Async XLA Ops:
  0.6 36.4 %copy-start.4 = (bf16[128,768]{1,0:T(8,128)(2,1)S(1)}, bf16[128,768]{1,0:T(8,128)(2,1)}, u32[]{:S(2)}) copy-start(bf16[128,768]{1,0:T(8,128)(2,1)} %constant.15.clone.first_back_ref) | copy-start | bytes 589828
  0.6 36.3 %copy-start.5 = (bf16[256,384]{1,0:T(8,128)(2,1)S(1)}, bf16[256,384]{1,0:T(8,128)(2,1)}, u32[]{:S(2)}) copy-start(bf16[256,384]{1,0:T(8,128)(2,1)} %constant.12.clone.first_ref) | copy-start | bytes 589828
  3.2 33.8 %all-to-all-start = ((bf16[256,2,384]{2,1,0:T(2,128)(2,1)}), bf16[256,2,384]{2,1,0:T(2,128)(2,1)S(1)}, u32[]{:S(2)}, u32[]{:S(2)}) async-start(bf16[256,2,384]{2,1,0:T(2,128)(2,1)} %get-tuple-element.26), calls=%async_computation | async-start | bytes 786432 | tf_op jit(solution)/shard_map/all_to_all | solution.py:441
  18.9 6.1 %collective-permute-start.1 = (bf16[128,512]{1,0:T(8,128)(2,1)}, bf16[128,512]{1,0:T(8,128)(2,1)S(1)}, u32[]{:S(2)}, u32[]{:S(2)}) collective-permute-start(bf16[128,512]{1,0:T(8,128)(2,1)} %get-tuple-element.27.refs_0_), channel_id=1, source_target_pairs={{0,3},{1,0},{2,1},{3,2},{16,17},{17,18},{18,19},{19,16},{4,7},{5,4... | collective-permute-start | bytes 393224 | tf_op jit(solution)/shard_map/ppermute | solution.py:456
  20.4 6.0 %collective-permute-start = (bf16[128,512]{1,0:T(8,128)(2,1)}, bf16[128,512]{1,0:T(8,128)(2,1)S(1)}, u32[]{:S(2)}, u32[]{:S(2)}) collective-permute-start(bf16[128,512]{1,0:T(8,128)(2,1)} %get-tuple-element.27.refs_0_), channel_id=1, source_target_pairs={{0,1},{1,2},{2,3},{3,0},{16,19},{17,16},{18,17},{19,18},{4,5},{5,6... | collective-permute-start | bytes 393224 | tf_op jit(solution)/shard_map/ppermute | solution.py:456
  41.8 18.7 %all-to-all-start.1 = ((bf16[32,2,3200]{2,1,0:T(2,128)(2,1)}), bf16[32,2,3200]{2,1,0:T(2,128)(2,1)S(1)}, u32[]{:S(2)}, u32[]{:S(2)}) async-start(bf16[32,2,3200]{2,1,0:T(2,128)(2,1)} %shard_map.181), calls=%async_computation.1 | async-start | bytes 819200 | tf_op jit(solution)/shard_map/all_to_all | solution.py:441
  45.8 5.6 %collective-permute-start.2 = (bf16[128,512]{1,0:T(8,128)(2,1)S(1)}, bf16[128,512]{1,0:T(8,128)(2,1)S(1)}, u32[]{:S(2)}, u32[]{:S(2)}) collective-permute-start(bf16[128,512]{1,0:T(8,128)(2,1)S(1)} %copy-done.6), channel_id=1, source_target_pairs={{0,2},{1,3},{2,0},{3,1},{16,18},{17,19},{18,16},{19,17},{4,6},{5,7... | collective-permute-start | bytes 393224 | tf_op jit(solution)/shard_map/ppermute | solution.py:456
  47.4 6.5 %collective-permute-start.3 = (bf16[128,512]{1,0:T(8,128)(2,1)S(1)}, bf16[128,512]{1,0:T(8,128)(2,1)S(1)}, u32[]{:S(2)}, u32[]{:S(2)}) collective-permute-start(bf16[128,512]{1,0:T(8,128)(2,1)S(1)} %copy-done.6), channel_id=1, source_target_pairs={{0,16},{16,0},{1,17},{17,1},{2,18},{18,2},{3,19},{19,3},{4,20},{20... | collective-permute-start | bytes 393224 | tf_op jit(solution)/shard_map/ppermute | solution.py:445
  51.4 2.9 %collective-permute-start.5 = (bf16[128,512]{1,0:T(8,128)(2,1)S(1)}, bf16[128,512]{1,0:T(8,128)(2,1)S(1)}, u32[]{:S(2)}, u32[]{:S(2)}) collective-permute-start(bf16[128,512]{1,0:T(8,128)(2,1)S(1)} %collective-permute-done.2.refs_2_), channel_id=1, source_target_pairs={{0,16},{16,0},{1,17},{17,1},{2,18},{18,2},{3,19},{19,3},{4,20},{20... | collective-permute-start | bytes 393224 | tf_op jit(solution)/shard_map/ppermute | solution.py:445
  53.4 1.3 %collective-permute-start.6 = (bf16[128,512]{1,0:T(8,128)(2,1)S(1)}, bf16[128,512]{1,0:T(8,128)(2,1)S(1)}, u32[]{:S(2)}, u32[]{:S(2)}) collective-permute-start(bf16[128,512]{1,0:T(8,128)(2,1)S(1)} %collective-permute-done.1.rest_1_.refs_3_), channel_id=1, source_target_pairs={{0,16},{16,0},{1,17},{17,1},{2,18},{18,2},{3,19},{19,3},{4,20},{20... | collective-permute-start | bytes 393224 | tf_op jit(solution)/shard_map/ppermute | solution.py:445
  53.4 1.5 %collective-permute-start.4 = (bf16[128,512]{1,0:T(8,128)(2,1)S(1)}, bf16[128,512]{1,0:T(8,128)(2,1)S(1)}, u32[]{:S(2)}, u32[]{:S(2)}) collective-permute-start(bf16[128,512]{1,0:T(8,128)(2,1)S(1)} %collective-permute-done.rest_0_.refs_1_), channel_id=1, source_target_pairs={{0,16},{16,0},{1,17},{17,1},{2,18},{18,2},{3,19},{19,3},{4,20},{20... | collective-permute-start | bytes 393224 | tf_op jit(solution)/shard_map/ppermute | solution.py:445
  61.0 5.3 %collective-permute-start.14 = (f32[32,256]{1,0:T(8,128)S(1)}, f32[32,256]{1,0:T(8,128)S(1)}, u32[]{:S(2)}, u32[]{:S(2)}) collective-permute-start(f32[32,256]{1,0:T(8,128)S(1)} %get-tuple-element.35), channel_id=1, source_target_pairs={{0,32},{32,64},{64,96},{96,0},{16,112},{48,16},{80,48},{112,80},{1... | collective-permute-start | bytes 98312 | tf_op jit(solution)/shard_map/ppermute | solution.py:456
  62.0 5.1 %collective-permute-start.15 = (f32[32,256]{1,0:T(8,128)S(1)}, f32[32,256]{1,0:T(8,128)S(1)}, u32[]{:S(2)}, u32[]{:S(2)}) collective-permute-start(f32[32,256]{1,0:T(8,128)S(1)} %get-tuple-element.36), channel_id=1, source_target_pairs={{0,64},{32,96},{64,0},{96,32},{16,80},{48,112},{80,16},{112,48},{1... | collective-permute-start | bytes 98312 | tf_op jit(solution)/shard_map/ppermute | solution.py:456
  63.1 4.1 %collective-permute-start.16 = (f32[32,256]{1,0:T(8,128)S(1)}, f32[32,256]{1,0:T(8,128)S(1)}, u32[]{:S(2)}, u32[]{:S(2)}) collective-permute-start(f32[32,256]{1,0:T(8,128)S(1)} %get-tuple-element.37), channel_id=1, source_target_pairs={{0,96},{32,0},{64,32},{96,64},{16,48},{48,80},{80,112},{112,16},{1... | collective-permute-start | bytes 98312 | tf_op jit(solution)/shard_map/ppermute | solution.py:456
  63.5 12.3 %collective-permute-start.7 = (bf16[2,224,128]{2,1,0:T(8,128)(2,1)S(1)}, bf16[2,224,128]{2,1,0:T(8,128)(2,1)S(1)}, u32[]{:S(2)}, u32[]{:S(2)}) collective-permute-start(bf16[2,224,128]{2,1,0:T(8,128)(2,1)S(1)} %get-tuple-element.29), channel_id=1, source_target_pairs={{0,1},{1,2},{2,3},{3,0},{16,19},{17,16},{18,17},{19,18},{4,5},{5,6... | collective-permute-start | bytes 344072 | tf_op jit(solution)/shard_map/ppermute | solution.py:456
  65.3 10.6 %collective-permute-start.8 = (bf16[2,224,128]{2,1,0:T(8,128)(2,1)S(1)}, bf16[2,224,128]{2,1,0:T(8,128)(2,1)S(1)}, u32[]{:S(2)}, u32[]{:S(2)}) collective-permute-start(bf16[2,224,128]{2,1,0:T(8,128)(2,1)S(1)} %get-tuple-element.30), channel_id=1, source_target_pairs={{0,2},{1,3},{2,0},{3,1},{16,18},{17,19},{18,16},{19,17},{4,6},{5,7... | collective-permute-start | bytes 344072 | tf_op jit(solution)/shard_map/ppermute | solution.py:456
  66.3 10.1 %collective-permute-start.9 = (bf16[2,224,128]{2,1,0:T(8,128)(2,1)S(1)}, bf16[2,224,128]{2,1,0:T(8,128)(2,1)S(1)}, u32[]{:S(2)}, u32[]{:S(2)}) collective-permute-start(bf16[2,224,128]{2,1,0:T(8,128)(2,1)S(1)} %get-tuple-element.31), channel_id=1, source_target_pairs={{0,3},{1,0},{2,1},{3,2},{16,17},{17,18},{18,19},{19,16},{4,7},{5,4... | collective-permute-start | bytes 344072 | tf_op jit(solution)/shard_map/ppermute | solution.py:456
  67.8 11.2 %all-to-all-start.2 = ((bf16[8,64,128]{2,1,0:T(8,128)(2,1)}), bf16[8,64,128]{2,1,0:T(8,128)(2,1)S(1)}, u32[]{:S(2)}, u32[]{:S(2)}) async-start(bf16[8,64,128]{2,1,0:T(8,128)(2,1)} %shard_map.184), calls=%async_computation.2 | async-start | bytes 262144 | tf_op jit(solution)/shard_map/all_to_all | solution.py:441
  71.2 5.6 %collective-permute-start.10 = (bf16[2,224,128]{2,1,0:T(8,128)(2,1)S(1)}, bf16[2,224,128]{2,1,0:T(8,128)(2,1)S(1)}, u32[]{:S(2)}, u32[]{:S(2)}) collective-permute-start(bf16[2,224,128]{2,1,0:T(8,128)(2,1)S(1)} %get-tuple-element.28.refs_0_), channel_id=1, source_target_pairs={{0,16},{16,0},{1,17},{17,1},{2,18},{18,2},{3,19},{19,3},{4,20},{20... | collective-permute-start | bytes 344072 | tf_op jit(solution)/shard_map/ppermute | solution.py:445
  75.8 1.3 %collective-permute-start.11 = (bf16[2,224,128]{2,1,0:T(8,128)(2,1)S(1)}, bf16[2,224,128]{2,1,0:T(8,128)(2,1)S(1)}, u32[]{:S(2)}, u32[]{:S(2)}) collective-permute-start(bf16[2,224,128]{2,1,0:T(8,128)(2,1)S(1)} %collective-permute-done.7.refs_1_), channel_id=1, source_target_pairs={{0,16},{16,0},{1,17},{17,1},{2,18},{18,2},{3,19},{19,3},{4,20},{20... | collective-permute-start | bytes 344072 | tf_op jit(solution)/shard_map/ppermute | solution.py:445
  75.9 1.4 %collective-permute-start.12 = (bf16[2,224,128]{2,1,0:T(8,128)(2,1)S(1)}, bf16[2,224,128]{2,1,0:T(8,128)(2,1)S(1)}, u32[]{:S(2)}, u32[]{:S(2)}) collective-permute-start(bf16[2,224,128]{2,1,0:T(8,128)(2,1)S(1)} %collective-permute-done.8.refs_2_), channel_id=1, source_target_pairs={{0,16},{16,0},{1,17},{17,1},{2,18},{18,2},{3,19},{19,3},{4,20},{20... | collective-permute-start | bytes 344072 | tf_op jit(solution)/shard_map/ppermute | solution.py:445
  76.3 1.3 %collective-permute-start.13 = (bf16[2,224,128]{2,1,0:T(8,128)(2,1)S(1)}, bf16[2,224,128]{2,1,0:T(8,128)(2,1)S(1)}, u32[]{:S(2)}, u32[]{:S(2)}) collective-permute-start(bf16[2,224,128]{2,1,0:T(8,128)(2,1)S(1)} %collective-permute-done.9.refs_3_), channel_id=1, source_target_pairs={{0,16},{16,0},{1,17},{17,1},{2,18},{18,2},{3,19},{19,3},{4,20},{20... | collective-permute-start | bytes 344072 | tf_op jit(solution)/shard_map/ppermute | solution.py:445
  79.8 13.5 %all-to-all-start.3 = ((bf16[16,64,128]{2,1,0:T(8,128)(2,1)}), bf16[16,64,128]{2,1,0:T(8,128)(2,1)S(1)}, u32[]{:S(2)}, u32[]{:S(2)}) async-start(bf16[16,64,128]{2,1,0:T(8,128)(2,1)} %shard_map.185), calls=%async_computation.3 | async-start | bytes 524288 | tf_op jit(solution)/shard_map/all_to_all | solution.py:441
  93.3 7.3 %collective-permute-start.17 = (bf16[16,64,128]{2,1,0:T(8,128)(2,1)S(1)}, bf16[16,64,128]{2,1,0:T(8,128)(2,1)S(1)}, u32[]{:S(2)}, u32[]{:S(2)}) collective-permute-start(bf16[16,64,128]{2,1,0:T(8,128)(2,1)S(1)} %all-to-all-done.3.own_ref), channel_id=1, source_target_pairs={{0,16},{16,0},{1,17},{17,1},{2,18},{18,2},{3,19},{19,3},{4,20},{20... | collective-permute-start | bytes 786440 | tf_op jit(solution)/shard_map/ppermute | solution.py:445
  (8 other events, 193.1 us)

commit v14 on v13

--- a/solution.py
+++ b/solution.py
@@ -383,7 +383,7 @@
 
 
 def add_x_kernel(*refs):
-    out_ref = refs[4]
+    out_ref = refs[7]
     total = refs[0][...] + refs[1][...] + refs[2][...] + refs[3][...]
     lanes = out_ref.shape[2]
     rows = jnp.concatenate([total[:, :lanes], total[:, lanes:]], 0)
@@ -486,15 +486,22 @@
         [pltpu.VMEM((25, 64, rows), f32), pltpu.VMEM((4, 32, width), f32)],
     )(halfway, *gathered)
     part = [found[0]] + [ring(found[distance], "x", distance) for distance in (1, 2, 3)]
-    arrived = [found[4]] + [ring(found[4 + i], "y", i) for i in (1, 2, 3)]
-    arrived += [swap_core(x) for x in arrived]
-    part = call(add_x_kernel, shape((8, 64, rows), bf16))(*part)
+    leaving = found[5:]
+    part, *leaving = call(
+        add_x_kernel,
+        (shape((8, 64, rows), bf16),) + (shape(leaving[0].shape, bf16),) * 3,
+        in_specs=specs(*[pltpu.VMEM] * 4, *[pl.ANY] * 3),
+        out_specs=specs(pltpu.VMEM, *[pl.ANY] * 3),
+        input_output_aliases={4: 1, 5: 2, 6: 3},
+    )(*part, *leaving)
+    arrived = [found[4]] + [ring(x, "y", 1 + i) for i, x in enumerate(leaving)]
     part = exchange(part, ("zh", "zl"))
     part = call(
         functools.partial(add_z_kernel, scale),
         shape((16, 64, rows), bf16),
-        in_specs=specs(pltpu.VMEM, *[pl.ANY] * 4),
-    )(part, *arrived[4:])
+        in_specs=specs(pltpu.VMEM, *[pl.ANY] * 3),
+    )(part, *arrived[1:])
+    arrived += [swap_core(x) for x in arrived]
     part = exchange(part, ("x", "y"))
     outputs, grad_inputs, grad_short, grad_one, grad_two = call(
         finish_kernel,

time: 102 us -> 101 us (level)
  starting transfers between devices: 53.6 us -> 46 us
  waiting for transfers between devices: 35.5 us -> 41.6 us
    ppermute x9, waiting for transfers between devices: 8.66 us -> 20 us  [ring(): return lax.ppermute(x, axes, route)]
    ppermute x9, starting transfers between devices: 13.8 us -> 8.33 us  [swap_core(): return lax.ppermute(x, 'core', [(0, 1), (1, 0)])]
    all_to_all x4, waiting for transfers between devices: 23.5 us -> 18.2 us  [exchange(): return lax.all_to_all(x, axes, split_axis=0, concat_axis=0, tiled=True)]
    all_to_all x4, starting transfers between devices: 29.3 us -> 26.7 us  [exchange(): return lax.all_to_all(x, axes, split_axis=0, concat_axis=0, tiled=True)]
  transfers between devices with their start and end apart: 22 -> 22, of which waited for: 15 -> 20; matrix products, arithmetic and copies ran while one was open for 0% -> 0% of each run, Pallas kernels for 2% -> 1%
where the time goes in v14:
time: 101 us; the launch traced here: 100 us
  starting transfers between devices  46 us (46%)
  waiting for transfers between devices  41.6 us (41%)
  Pallas kernels  11.9 us (12%)
    all_to_all x4, starting transfers between devices, exchange(): return lax.all_to_all(x, axes, split_axis=0, concat_axis=0, tiled=True)  26.7 us
    ppermute x9, waiting for transfers between devices, ring(): return lax.ppermute(x, axes, route)  20 us
    all_to_all x4, waiting for transfers between devices, exchange(): return lax.all_to_all(x, axes, split_axis=0, concat_axis=0, tiled=True)  18.2 us
    ppermute x9, starting transfers between devices, ring(): return lax.ppermute(x, axes, route)  11 us
    ppermute x9, starting transfers between devices, swap_core(): return lax.ppermute(x, 'core', [(0, 1), (1, 0)])  8.33 us
    pallas_call x1, Pallas kernels, per_device(): call(convolve_kernel, shape((32, 2, 25 * rows), bf16), [pltpu.VMEM((3, 2...  4.73 us
    ppermute x9, waiting for transfers between devices, swap_core(): return lax.ppermute(x, 'core', [(0, 1), (1, 0)])  3.41 us
    pallas_call x1, Pallas kernels, per_device(): call(pack_kernel, (shape((width, 2, 3 * rows), bf16), shape((rows, 2 * wi...  2.53 us
  transfers between devices with their start and end apart: 22, of which 20 were waited for; matrix products, arithmetic and copies ran while one was open for 0% of the time, Pallas kernels for 1%

profile of v14, /device:TPU:1, one launch (start us, length us, event | category | flops | bytes accessed | tf_op | source)
XLA Modules:
  0.0 100.4 jit_solution(1553320871756681856)
XLA Ops:
  0.7 2.5 %shard_map.180 = (bf16[256,2,384]{2,1,0:T(2,128)(2,1)}, bf16[128,512]{1,0:T(8,128)(2,1)}) custom-call(bf16[1,128,256]{2,1,0:T(8,128)(2,1)} %seq_ref.1, bf16[256,768]{1,0:T(8,128)(2,1)} %refs_8_.1, f32[128,256]{1,0:T(8,128)} %one_ref.1, f32[128,256]{1,0:T(8,128)} %two_ref.1, bf16[256,256]{1,0:T(8,128)(2,1)} %refs_9_.1, bf16[1,128,256]{2,1,0:T(8,128)(2,1)} %grad_ref.1), custom_call_target="tpu_custom_call" | custom-call | tf_op jit(solution)/shard_map/pallas_call | solution.py:466
  3.2 15.7 %all-to-all-start = ((bf16[256,2,384]{2,1,0:T(2,128)(2,1)}), bf16[256,2,384]{2,1,0:T(2,128)(2,1)S(1)}, u32[]{:S(2)}, u32[]{:S(2)}) async-start(bf16[256,2,384]{2,1,0:T(2,128)(2,1)} %get-tuple-element.30), calls=%async_computation | async-start | bytes 786432 | tf_op jit(solution)/shard_map/all_to_all | solution.py:441
  18.9 1.5 %collective-permute-start.1 = (bf16[128,512]{1,0:T(8,128)(2,1)}, bf16[128,512]{1,0:T(8,128)(2,1)S(1)}, u32[]{:S(2)}, u32[]{:S(2)}) collective-permute-start(bf16[128,512]{1,0:T(8,128)(2,1)} %get-tuple-element.31.refs_0_), channel_id=1, source_target_pairs={{0,3},{1,0},{2,1},{3,2},{16,17},{17,18},{18,19},{19,16},{4,7},{5,4... | collective-permute-start | bytes 393224 | tf_op jit(solution)/shard_map/ppermute | solution.py:456
  20.4 1.4 %collective-permute-start = (bf16[128,512]{1,0:T(8,128)(2,1)}, bf16[128,512]{1,0:T(8,128)(2,1)S(1)}, u32[]{:S(2)}, u32[]{:S(2)}) collective-permute-start(bf16[128,512]{1,0:T(8,128)(2,1)} %get-tuple-element.31.refs_0_), channel_id=1, source_target_pairs={{0,1},{1,2},{2,3},{3,0},{16,19},{17,16},{18,17},{19,18},{4,5},{5,6... | collective-permute-start | bytes 393224 | tf_op jit(solution)/shard_map/ppermute | solution.py:456
  21.7 3.3 %collective-permute-done.1.rest_1_.refs_3_ = bf16[128,512]{1,0:T(8,128)(2,1)S(1)} collective-permute-done((bf16[128,512]{1,0:T(8,128)(2,1)}, bf16[128,512]{1,0:T(8,128)(2,1)S(1)}, u32[]{:S(2)}, u32[]{:S(2)}) %collective-permute-start.1) | collective-permute-done | bytes 131104 | tf_op jit(solution)/shard_map/ppermute | solution.py:456
  25.0 1.3 %collective-permute-done.rest_0_.refs_1_ = bf16[128,512]{1,0:T(8,128)(2,1)S(1)} collective-permute-done((bf16[128,512]{1,0:T(8,128)(2,1)}, bf16[128,512]{1,0:T(8,128)(2,1)S(1)}, u32[]{:S(2)}, u32[]{:S(2)}) %collective-permute-start) | collective-permute-done | bytes 131104 | tf_op jit(solution)/shard_map/ppermute | solution.py:456
  26.3 10.7 %all-to-all-done.in_ref = bf16[256,2,384]{2,1,0:T(2,128)(2,1)S(1)} async-done(((bf16[256,2,384]{2,1,0:T(2,128)(2,1)}), bf16[256,2,384]{2,1,0:T(2,128)(2,1)S(1)}, u32[]{:S(2)}, u32[]{:S(2)}) %all-to-all-start) | async-done | bytes 393248 | tf_op jit(solution)/shard_map/all_to_all | solution.py:441
  37.0 4.7 %shard_map.181 = bf16[32,2,3200]{2,1,0:T(2,128)(2,1)} custom-call(bf16[256,2,384]{2,1,0:T(2,128)(2,1)S(1)} %all-to-all-done.in_ref, f32[3,768]{1,0:T(4,128)S(1)} %copy-done.9, bf16[256,384]{1,0:T(8,128)(2,1)S(1)} %copy-done.5, bf16[768,256]{1,0:T(8,128)(2,1)S(1)} %copy-done.3, bf16[768,256]{1,0:T(8,128)(2,1)S(1)} %copy-done.2, ...), custom_call_target="tpu_custom_call" | custom-call | tf_op jit(solution)/shard_map/pallas_call | solution.py:476
  41.8 4.0 %all-to-all-start.1 = ((bf16[32,2,3200]{2,1,0:T(2,128)(2,1)}), bf16[32,2,3200]{2,1,0:T(2,128)(2,1)S(1)}, u32[]{:S(2)}, u32[]{:S(2)}) async-start(bf16[32,2,3200]{2,1,0:T(2,128)(2,1)} %shard_map.181), calls=%async_computation.1 | async-start | bytes 819200 | tf_op jit(solution)/shard_map/all_to_all | solution.py:441
  45.8 1.6 %collective-permute-start.2 = (bf16[128,512]{1,0:T(8,128)(2,1)S(1)}, bf16[128,512]{1,0:T(8,128)(2,1)S(1)}, u32[]{:S(2)}, u32[]{:S(2)}) collective-permute-start(bf16[128,512]{1,0:T(8,128)(2,1)S(1)} %copy-done.6), channel_id=1, source_target_pairs={{0,2},{1,3},{2,0},{3,1},{16,18},{17,19},{18,16},{19,17},{4,6},{5,7... | collective-permute-start | bytes 393224 | tf_op jit(solution)/shard_map/ppermute | solution.py:456
  47.4 4.0 %collective-permute-done.2.refs_2_ = bf16[128,512]{1,0:T(8,128)(2,1)S(1)} collective-permute-done((bf16[128,512]{1,0:T(8,128)(2,1)S(1)}, bf16[128,512]{1,0:T(8,128)(2,1)S(1)}, u32[]{:S(2)}, u32[]{:S(2)}) %collective-permute-start.2) | collective-permute-done | bytes 131104 | tf_op jit(solution)/shard_map/ppermute | solution.py:456
  51.4 2.0 %collective-permute-start.5 = (bf16[128,512]{1,0:T(8,128)(2,1)S(1)}, bf16[128,512]{1,0:T(8,128)(2,1)S(1)}, u32[]{:S(2)}, u32[]{:S(2)}) collective-permute-start(bf16[128,512]{1,0:T(8,128)(2,1)S(1)} %collective-permute-done.2.refs_2_), channel_id=1, source_target_pairs={{0,16},{16,0},{1,17},{17,1},{2,18},{18,2},{3,19},{19,3},{4,20},{20... | collective-permute-start | bytes 393224 | tf_op jit(solution)/shard_map/ppermute | solution.py:445
  54.9 5.5 %all-to-all-done.1.in_ref = bf16[32,2,3200]{2,1,0:T(2,128)(2,1)S(1)} async-done(((bf16[32,2,3200]{2,1,0:T(2,128)(2,1)}), bf16[32,2,3200]{2,1,0:T(2,128)(2,1)S(1)}, u32[]{:S(2)}, u32[]{:S(2)}) %all-to-all-start.1) | async-done | bytes 409632 | tf_op jit(solution)/shard_map/all_to_all | solution.py:441
  63.8 2.4 %collective-permute-done.8.refs_2_ = f32[32,256]{1,0:T(8,128)S(1)} collective-permute-done((f32[32,256]{1,0:T(8,128)S(1)}, f32[32,256]{1,0:T(8,128)S(1)}, u32[]{:S(2)}, u32[]{:S(2)}) %collective-permute-start.8) | collective-permute-done | bytes 32800 | tf_op jit(solution)/shard_map/ppermute | solution.py:456
  67.7 3.4 %all-to-all-start.2 = ((bf16[8,64,128]{2,1,0:T(8,128)(2,1)}), bf16[8,64,128]{2,1,0:T(8,128)(2,1)S(1)}, u32[]{:S(2)}, u32[]{:S(2)}) async-start(bf16[8,64,128]{2,1,0:T(8,128)(2,1)} %get-tuple-element.45), calls=%async_computation.2 | async-start | bytes 262144 | tf_op jit(solution)/shard_map/all_to_all | solution.py:441
  71.1 3.3 %collective-permute-start.10 = (bf16[2,224,128]{2,1,0:T(8,128)(2,1)S(1)}, bf16[2,224,128]{2,1,0:T(8,128)(2,1)S(1)}, u32[]{:S(2)}, u32[]{:S(2)}) collective-permute-start(bf16[2,224,128]{2,1,0:T(8,128)(2,1)S(1)} %get-tuple-element.40), channel_id=1, source_target_pairs={{0,1},{1,2},{2,3},{3,0},{16,19},{17,16},{18,17},{19,18},{4,5},{5,6... | collective-permute-start | bytes 344072 | tf_op jit(solution)/shard_map/ppermute | solution.py:456
  75.2 2.2 %collective-permute-done.10.refs_1_.refs_0_ = bf16[2,224,128]{2,1,0:T(8,128)(2,1)S(1)} collective-permute-done((bf16[2,224,128]{2,1,0:T(8,128)(2,1)S(1)}, bf16[2,224,128]{2,1,0:T(8,128)(2,1)S(1)}, u32[]{:S(2)}, u32[]{:S(2)}) %collective-permute-start.10) | collective-permute-done | bytes 114720 | tf_op jit(solution)/shard_map/ppermute | solution.py:456
  77.4 3.6 %collective-permute-done.11.refs_2_.refs_1_ = bf16[2,224,128]{2,1,0:T(8,128)(2,1)S(1)} collective-permute-done((bf16[2,224,128]{2,1,0:T(8,128)(2,1)S(1)}, bf16[2,224,128]{2,1,0:T(8,128)(2,1)S(1)}, u32[]{:S(2)}, u32[]{:S(2)}) %collective-permute-start.11) | collective-permute-done | bytes 114720 | tf_op jit(solution)/shard_map/ppermute | solution.py:456
  81.0 2.0 %collective-permute-done.12.refs_3_.refs_2_ = bf16[2,224,128]{2,1,0:T(8,128)(2,1)S(1)} collective-permute-done((bf16[2,224,128]{2,1,0:T(8,128)(2,1)S(1)}, bf16[2,224,128]{2,1,0:T(8,128)(2,1)S(1)}, u32[]{:S(2)}, u32[]{:S(2)}) %collective-permute-start.12) | collective-permute-done | bytes 114720 | tf_op jit(solution)/shard_map/ppermute | solution.py:456
  83.8 3.7 %all-to-all-start.3 = ((bf16[16,64,128]{2,1,0:T(8,128)(2,1)}), bf16[16,64,128]{2,1,0:T(8,128)(2,1)S(1)}, u32[]{:S(2)}, u32[]{:S(2)}) async-start(bf16[16,64,128]{2,1,0:T(8,128)(2,1)} %shard_map.185), calls=%async_computation.3 | async-start | bytes 524288 | tf_op jit(solution)/shard_map/all_to_all | solution.py:441
  87.4 2.1 %collective-permute-start.13 = (bf16[2,224,128]{2,1,0:T(8,128)(2,1)S(1)}, bf16[2,224,128]{2,1,0:T(8,128)(2,1)S(1)}, u32[]{:S(2)}, u32[]{:S(2)}) collective-permute-start(bf16[2,224,128]{2,1,0:T(8,128)(2,1)S(1)} %get-tuple-element.32.refs_0_), channel_id=1, source_target_pairs={{0,16},{16,0},{1,17},{17,1},{2,18},{18,2},{3,19},{19,3},{4,20},{20... | collective-permute-start | bytes 344072 | tf_op jit(solution)/shard_map/ppermute | solution.py:445
  91.4 1.4 %shard_map.184 = (bf16[1,128,256]{2,1,0:T(8,128)(2,1)}, bf16[1,128,256]{2,1,0:T(8,128)(2,1)}, f32[3,768]{1,0:T(4,128)}, f32[128,256]{1,0:T(8,128)}, f32[128,256]{1,0:T(8,128)}) custom-call(bf16[2,224,128]{2,1,0:T(8,128)(2,1)S(1)} %get-tuple-element.32.refs_0_, bf16[2,224,128]{2,1,0:T(8,128)(2,1)S(1)} %collective-permute-done.10.refs_1_.refs_0_, ...), custom_call_target="tpu_custom_call" | custom-call | tf_op jit(solution)/shard_map/pallas_call | solution.py:506
  92.7 2.0 %all-to-all-done.3.own_ref = bf16[16,64,128]{2,1,0:T(8,128)(2,1)S(1)} async-done(((bf16[16,64,128]{2,1,0:T(8,128)(2,1)}), bf16[16,64,128]{2,1,0:T(8,128)(2,1)S(1)}, u32[]{:S(2)}, u32[]{:S(2)}) %all-to-all-start.3) | async-done | bytes 262176 | tf_op jit(solution)/shard_map/all_to_all | solution.py:441
  94.8 3.1 %collective-permute-start.17 = (bf16[16,64,128]{2,1,0:T(8,128)(2,1)S(1)}, bf16[16,64,128]{2,1,0:T(8,128)(2,1)S(1)}, u32[]{:S(2)}, u32[]{:S(2)}) collective-permute-start(bf16[16,64,128]{2,1,0:T(8,128)(2,1)S(1)} %all-to-all-done.3.own_ref), channel_id=1, source_target_pairs={{0,16},{16,0},{1,17},{17,1},{2,18},{18,2},{3,19},{19,3},{4,20},{20... | collective-permute-start | bytes 786440 | tf_op jit(solution)/shard_map/ppermute | solution.py:445
  (47 shorter events, 12.3 us)
Async XLA Ops:
  0.6 36.4 %copy-start.4 = (bf16[128,768]{1,0:T(8,128)(2,1)S(1)}, bf16[128,768]{1,0:T(8,128)(2,1)}, u32[]{:S(2)}) copy-start(bf16[128,768]{1,0:T(8,128)(2,1)} %constant.15.clone.first_back_ref) | copy-start | bytes 589828
  0.6 36.3 %copy-start.5 = (bf16[256,384]{1,0:T(8,128)(2,1)S(1)}, bf16[256,384]{1,0:T(8,128)(2,1)}, u32[]{:S(2)}) copy-start(bf16[256,384]{1,0:T(8,128)(2,1)} %constant.12.clone.first_ref) | copy-start | bytes 589828
  3.2 33.8 %all-to-all-start = ((bf16[256,2,384]{2,1,0:T(2,128)(2,1)}), bf16[256,2,384]{2,1,0:T(2,128)(2,1)S(1)}, u32[]{:S(2)}, u32[]{:S(2)}) async-start(bf16[256,2,384]{2,1,0:T(2,128)(2,1)} %get-tuple-element.30), calls=%async_computation | async-start | bytes 786432 | tf_op jit(solution)/shard_map/all_to_all | solution.py:441
  18.9 6.1 %collective-permute-start.1 = (bf16[128,512]{1,0:T(8,128)(2,1)}, bf16[128,512]{1,0:T(8,128)(2,1)S(1)}, u32[]{:S(2)}, u32[]{:S(2)}) collective-permute-start(bf16[128,512]{1,0:T(8,128)(2,1)} %get-tuple-element.31.refs_0_), channel_id=1, source_target_pairs={{0,3},{1,0},{2,1},{3,2},{16,17},{17,18},{18,19},{19,16},{4,7},{5,4... | collective-permute-start | bytes 393224 | tf_op jit(solution)/shard_map/ppermute | solution.py:456
  20.4 6.0 %collective-permute-start = (bf16[128,512]{1,0:T(8,128)(2,1)}, bf16[128,512]{1,0:T(8,128)(2,1)S(1)}, u32[]{:S(2)}, u32[]{:S(2)}) collective-permute-start(bf16[128,512]{1,0:T(8,128)(2,1)} %get-tuple-element.31.refs_0_), channel_id=1, source_target_pairs={{0,1},{1,2},{2,3},{3,0},{16,19},{17,16},{18,17},{19,18},{4,5},{5,6... | collective-permute-start | bytes 393224 | tf_op jit(solution)/shard_map/ppermute | solution.py:456
  41.8 18.7 %all-to-all-start.1 = ((bf16[32,2,3200]{2,1,0:T(2,128)(2,1)}), bf16[32,2,3200]{2,1,0:T(2,128)(2,1)S(1)}, u32[]{:S(2)}, u32[]{:S(2)}) async-start(bf16[32,2,3200]{2,1,0:T(2,128)(2,1)} %shard_map.181), calls=%async_computation.1 | async-start | bytes 819200 | tf_op jit(solution)/shard_map/all_to_all | solution.py:441
  45.8 5.6 %collective-permute-start.2 = (bf16[128,512]{1,0:T(8,128)(2,1)S(1)}, bf16[128,512]{1,0:T(8,128)(2,1)S(1)}, u32[]{:S(2)}, u32[]{:S(2)}) collective-permute-start(bf16[128,512]{1,0:T(8,128)(2,1)S(1)} %copy-done.6), channel_id=1, source_target_pairs={{0,2},{1,3},{2,0},{3,1},{16,18},{17,19},{18,16},{19,17},{4,6},{5,7... | collective-permute-start | bytes 393224 | tf_op jit(solution)/shard_map/ppermute | solution.py:456
  47.4 6.5 %collective-permute-start.3 = (bf16[128,512]{1,0:T(8,128)(2,1)S(1)}, bf16[128,512]{1,0:T(8,128)(2,1)S(1)}, u32[]{:S(2)}, u32[]{:S(2)}) collective-permute-start(bf16[128,512]{1,0:T(8,128)(2,1)S(1)} %copy-done.6), channel_id=1, source_target_pairs={{0,16},{16,0},{1,17},{17,1},{2,18},{18,2},{3,19},{19,3},{4,20},{20... | collective-permute-start | bytes 393224 | tf_op jit(solution)/shard_map/ppermute | solution.py:445
  51.4 2.9 %collective-permute-start.5 = (bf16[128,512]{1,0:T(8,128)(2,1)S(1)}, bf16[128,512]{1,0:T(8,128)(2,1)S(1)}, u32[]{:S(2)}, u32[]{:S(2)}) collective-permute-start(bf16[128,512]{1,0:T(8,128)(2,1)S(1)} %collective-permute-done.2.refs_2_), channel_id=1, source_target_pairs={{0,16},{16,0},{1,17},{17,1},{2,18},{18,2},{3,19},{19,3},{4,20},{20... | collective-permute-start | bytes 393224 | tf_op jit(solution)/shard_map/ppermute | solution.py:445
  53.4 1.3 %collective-permute-start.6 = (bf16[128,512]{1,0:T(8,128)(2,1)S(1)}, bf16[128,512]{1,0:T(8,128)(2,1)S(1)}, u32[]{:S(2)}, u32[]{:S(2)}) collective-permute-start(bf16[128,512]{1,0:T(8,128)(2,1)S(1)} %collective-permute-done.1.rest_1_.refs_3_), channel_id=1, source_target_pairs={{0,16},{16,0},{1,17},{17,1},{2,18},{18,2},{3,19},{19,3},{4,20},{20... | collective-permute-start | bytes 393224 | tf_op jit(solution)/shard_map/ppermute | solution.py:445
  53.4 1.5 %collective-permute-start.4 = (bf16[128,512]{1,0:T(8,128)(2,1)S(1)}, bf16[128,512]{1,0:T(8,128)(2,1)S(1)}, u32[]{:S(2)}, u32[]{:S(2)}) collective-permute-start(bf16[128,512]{1,0:T(8,128)(2,1)S(1)} %collective-permute-done.rest_0_.refs_1_), channel_id=1, source_target_pairs={{0,16},{16,0},{1,17},{17,1},{2,18},{18,2},{3,19},{19,3},{4,20},{20... | collective-permute-start | bytes 393224 | tf_op jit(solution)/shard_map/ppermute | solution.py:445
  61.0 2.8 %collective-permute-start.7 = (f32[32,256]{1,0:T(8,128)S(1)}, f32[32,256]{1,0:T(8,128)S(1)}, u32[]{:S(2)}, u32[]{:S(2)}) collective-permute-start(f32[32,256]{1,0:T(8,128)S(1)} %get-tuple-element.34), channel_id=1, source_target_pairs={{0,32},{32,64},{64,96},{96,0},{16,112},{48,16},{80,48},{112,80},{1... | collective-permute-start | bytes 98312 | tf_op jit(solution)/shard_map/ppermute | solution.py:456
  62.0 4.3 %collective-permute-start.8 = (f32[32,256]{1,0:T(8,128)S(1)}, f32[32,256]{1,0:T(8,128)S(1)}, u32[]{:S(2)}, u32[]{:S(2)}) collective-permute-start(f32[32,256]{1,0:T(8,128)S(1)} %get-tuple-element.35), channel_id=1, source_target_pairs={{0,64},{32,96},{64,0},{96,32},{16,80},{48,112},{80,16},{112,48},{1... | collective-permute-start | bytes 98312 | tf_op jit(solution)/shard_map/ppermute | solution.py:456
  63.1 4.0 %collective-permute-start.9 = (f32[32,256]{1,0:T(8,128)S(1)}, f32[32,256]{1,0:T(8,128)S(1)}, u32[]{:S(2)}, u32[]{:S(2)}) collective-permute-start(f32[32,256]{1,0:T(8,128)S(1)} %get-tuple-element.36), channel_id=1, source_target_pairs={{0,96},{32,0},{64,32},{96,64},{16,48},{48,80},{80,112},{112,16},{1... | collective-permute-start | bytes 98312 | tf_op jit(solution)/shard_map/ppermute | solution.py:456
  67.7 15.3 %all-to-all-start.2 = ((bf16[8,64,128]{2,1,0:T(8,128)(2,1)}), bf16[8,64,128]{2,1,0:T(8,128)(2,1)S(1)}, u32[]{:S(2)}, u32[]{:S(2)}) async-start(bf16[8,64,128]{2,1,0:T(8,128)(2,1)} %get-tuple-element.45), calls=%async_computation.2 | async-start | bytes 262144 | tf_op jit(solution)/shard_map/all_to_all | solution.py:441
  71.1 6.3 %collective-permute-start.10 = (bf16[2,224,128]{2,1,0:T(8,128)(2,1)S(1)}, bf16[2,224,128]{2,1,0:T(8,128)(2,1)S(1)}, u32[]{:S(2)}, u32[]{:S(2)}) collective-permute-start(bf16[2,224,128]{2,1,0:T(8,128)(2,1)S(1)} %get-tuple-element.40), channel_id=1, source_target_pairs={{0,1},{1,2},{2,3},{3,0},{16,19},{17,16},{18,17},{19,18},{4,5},{5,6... | collective-permute-start | bytes 344072 | tf_op jit(solution)/shard_map/ppermute | solution.py:456
  74.4 6.6 %collective-permute-start.11 = (bf16[2,224,128]{2,1,0:T(8,128)(2,1)S(1)}, bf16[2,224,128]{2,1,0:T(8,128)(2,1)S(1)}, u32[]{:S(2)}, u32[]{:S(2)}) collective-permute-start(bf16[2,224,128]{2,1,0:T(8,128)(2,1)S(1)} %get-tuple-element.41), channel_id=1, source_target_pairs={{0,2},{1,3},{2,0},{3,1},{16,18},{17,19},{18,16},{19,17},{4,6},{5,7... | collective-permute-start | bytes 344072 | tf_op jit(solution)/shard_map/ppermute | solution.py:456
  74.5 8.6 %collective-permute-start.12 = (bf16[2,224,128]{2,1,0:T(8,128)(2,1)S(1)}, bf16[2,224,128]{2,1,0:T(8,128)(2,1)S(1)}, u32[]{:S(2)}, u32[]{:S(2)}) collective-permute-start(bf16[2,224,128]{2,1,0:T(8,128)(2,1)S(1)} %get-tuple-element.42), channel_id=1, source_target_pairs={{0,3},{1,0},{2,1},{3,2},{16,17},{17,18},{18,19},{19,16},{4,7},{5,4... | collective-permute-start | bytes 344072 | tf_op jit(solution)/shard_map/ppermute | solution.py:456
  83.8 11.0 %all-to-all-start.3 = ((bf16[16,64,128]{2,1,0:T(8,128)(2,1)}), bf16[16,64,128]{2,1,0:T(8,128)(2,1)S(1)}, u32[]{:S(2)}, u32[]{:S(2)}) async-start(bf16[16,64,128]{2,1,0:T(8,128)(2,1)} %shard_map.185), calls=%async_computation.3 | async-start | bytes 524288 | tf_op jit(solution)/shard_map/all_to_all | solution.py:441
  87.4 3.1 %collective-permute-start.13 = (bf16[2,224,128]{2,1,0:T(8,128)(2,1)S(1)}, bf16[2,224,128]{2,1,0:T(8,128)(2,1)S(1)}, u32[]{:S(2)}, u32[]{:S(2)}) collective-permute-start(bf16[2,224,128]{2,1,0:T(8,128)(2,1)S(1)} %get-tuple-element.32.refs_0_), channel_id=1, source_target_pairs={{0,16},{16,0},{1,17},{17,1},{2,18},{18,2},{3,19},{19,3},{4,20},{20... | collective-permute-start | bytes 344072 | tf_op jit(solution)/shard_map/ppermute | solution.py:445
  89.5 1.3 %collective-permute-start.14 = (bf16[2,224,128]{2,1,0:T(8,128)(2,1)S(1)}, bf16[2,224,128]{2,1,0:T(8,128)(2,1)S(1)}, u32[]{:S(2)}, u32[]{:S(2)}) collective-permute-start(bf16[2,224,128]{2,1,0:T(8,128)(2,1)S(1)} %collective-permute-done.10.refs_1_.refs_0_), channel_id=1, source_target_pairs={{0,16},{16,0},{1,17},{17,1},{2,18},{18,2},{3,19},{19,3},{4,20},{20... | collective-permute-start | bytes 344072 | tf_op jit(solution)/shard_map/ppermute | solution.py:445
  89.6 1.4 %collective-permute-start.15 = (bf16[2,224,128]{2,1,0:T(8,128)(2,1)S(1)}, bf16[2,224,128]{2,1,0:T(8,128)(2,1)S(1)}, u32[]{:S(2)}, u32[]{:S(2)}) collective-permute-start(bf16[2,224,128]{2,1,0:T(8,128)(2,1)S(1)} %collective-permute-done.11.refs_2_.refs_1_), channel_id=1, source_target_pairs={{0,16},{16,0},{1,17},{17,1},{2,18},{18,2},{3,19},{19,3},{4,20},{20... | collective-permute-start | bytes 344072 | tf_op jit(solution)/shard_map/ppermute | solution.py:445
  90.0 1.3 %collective-permute-start.16 = (bf16[2,224,128]{2,1,0:T(8,128)(2,1)S(1)}, bf16[2,224,128]{2,1,0:T(8,128)(2,1)S(1)}, u32[]{:S(2)}, u32[]{:S(2)}) collective-permute-start(bf16[2,224,128]{2,1,0:T(8,128)(2,1)S(1)} %collective-permute-done.12.refs_3_.refs_2_), channel_id=1, source_target_pairs={{0,16},{16,0},{1,17},{17,1},{2,18},{18,2},{3,19},{19,3},{4,20},{20... | collective-permute-start | bytes 344072 | tf_op jit(solution)/shard_map/ppermute | solution.py:445
  94.8 4.3 %collective-permute-start.17 = (bf16[16,64,128]{2,1,0:T(8,128)(2,1)S(1)}, bf16[16,64,128]{2,1,0:T(8,128)(2,1)S(1)}, u32[]{:S(2)}, u32[]{:S(2)}) collective-permute-start(bf16[16,64,128]{2,1,0:T(8,128)(2,1)S(1)} %all-to-all-done.3.own_ref), channel_id=1, source_target_pairs={{0,16},{16,0},{1,17},{17,1},{2,18},{18,2},{3,19},{19,3},{4,20},{20... | collective-permute-start | bytes 786440 | tf_op jit(solution)/shard_map/ppermute | solution.py:445
  (8 other events, 195.8 us)

commit v15 on v13

--- a/solution.py
+++ b/solution.py
@@ -383,7 +383,7 @@
 
 
 def add_x_kernel(*refs):
-    out_ref = refs[4]
+    out_ref = refs[6]
     total = refs[0][...] + refs[1][...] + refs[2][...] + refs[3][...]
     lanes = out_ref.shape[2]
     rows = jnp.concatenate([total[:, :lanes], total[:, lanes:]], 0)
@@ -486,15 +486,22 @@
         [pltpu.VMEM((25, 64, rows), f32), pltpu.VMEM((4, 32, width), f32)],
     )(halfway, *gathered)
     part = [found[0]] + [ring(found[distance], "x", distance) for distance in (1, 2, 3)]
-    arrived = [found[4]] + [ring(found[4 + i], "y", i) for i in (1, 2, 3)]
+    far = ring(found[6], "y", 2)
+    part, *leaving = call(
+        add_x_kernel,
+        (shape((8, 64, rows), bf16),) + (shape(found[5].shape, bf16),) * 2,
+        in_specs=specs(*[pltpu.VMEM] * 4, *[pl.ANY] * 2),
+        out_specs=specs(pltpu.VMEM, *[pl.ANY] * 2),
+        input_output_aliases={4: 1, 5: 2},
+    )(*part, found[5], found[7])
+    arrived = [found[4], ring(leaving[0], "y", 1), far, ring(leaving[1], "y", 3)]
     arrived += [swap_core(x) for x in arrived]
-    part = call(add_x_kernel, shape((8, 64, rows), bf16))(*part)
     part = exchange(part, ("zh", "zl"))
     part = call(
         functools.partial(add_z_kernel, scale),
         shape((16, 64, rows), bf16),
-        in_specs=specs(pltpu.VMEM, *[pl.ANY] * 4),
-    )(part, *arrived[4:])
+        in_specs=specs(pltpu.VMEM, *[pl.ANY] * 3),
+    )(part, arrived[1], arrived[3], arrived[6])
     part = exchange(part, ("x", "y"))
     outputs, grad_inputs, grad_short, grad_one, grad_two = call(
         finish_kernel,

time: 102 us -> 100 us (0.980)
  waiting for transfers between devices: 35.5 us -> 32 us
  starting transfers between devices: 53.6 us -> 55.1 us
    all_to_all x4, waiting for transfers between devices: 23.5 us -> 16.5 us  [exchange(): return lax.all_to_all(x, axes, split_axis=0, concat_axis=0, tiled=True)]
    ppermute x9, waiting for transfers between devices: 8.66 us -> 12.3 us  [ring(): return lax.ppermute(x, axes, route)]
    all_to_all x4, starting transfers between devices: 29.3 us -> 26.7 us  [exchange(): return lax.all_to_all(x, axes, split_axis=0, concat_axis=0, tiled=True)]
    ppermute x9, starting transfers between devices: 10.5 us -> 13 us  [ring(): return lax.ppermute(x, axes, route)]
    ppermute x9, starting transfers between devices: 13.8 us -> 15.4 us  [swap_core(): return lax.ppermute(x, 'core', [(0, 1), (1, 0)])]
where the time goes in v15:
time: 100 us; the launch traced here: 99.9 us
  starting transfers between devices  55.1 us (55%)
  waiting for transfers between devices  32 us (32%)
  Pallas kernels  11.9 us (12%)
    all_to_all x4, starting transfers between devices, exchange(): return lax.all_to_all(x, axes, split_axis=0, concat_axis=0, tiled=True)  26.7 us
    all_to_all x4, waiting for transfers between devices, exchange(): return lax.all_to_all(x, axes, split_axis=0, concat_axis=0, tiled=True)  16.5 us
    ppermute x9, starting transfers between devices, swap_core(): return lax.ppermute(x, 'core', [(0, 1), (1, 0)])  15.4 us
    ppermute x9, starting transfers between devices, ring(): return lax.ppermute(x, axes, route)  13 us
    ppermute x9, waiting for transfers between devices, ring(): return lax.ppermute(x, axes, route)  12.3 us
    pallas_call x1, Pallas kernels, per_device(): call(convolve_kernel, shape((32, 2, 25 * rows), bf16), [pltpu.VMEM((3, 2...  4.73 us
    ppermute x9, waiting for transfers between devices, swap_core(): return lax.ppermute(x, 'core', [(0, 1), (1, 0)])  3.16 us
    pallas_call x1, Pallas kernels, per_device(): call(pack_kernel, (shape((width, 2, 3 * rows), bf16), shape((rows, 2 * wi...  2.53 us
  transfers between devices with their start and end apart: 22, of which 15 were waited for; matrix products, arithmetic and copies ran while one was open for 0% of the time, Pallas kernels for 2%

profile of v15, /device:TPU:1, one launch (start us, length us, event | category | flops | bytes accessed | tf_op | source)
XLA Modules:
  0.0 99.9 jit_solution(10749109201781493228)
XLA Ops:
  0.7 2.5 %shard_map.180 = (bf16[256,2,384]{2,1,0:T(2,128)(2,1)}, bf16[128,512]{1,0:T(8,128)(2,1)}) custom-call(bf16[1,128,256]{2,1,0:T(8,128)(2,1)} %seq_ref.1, bf16[256,768]{1,0:T(8,128)(2,1)} %refs_8_.1, f32[128,256]{1,0:T(8,128)} %one_ref.1, f32[128,256]{1,0:T(8,128)} %two_ref.1, bf16[256,256]{1,0:T(8,128)(2,1)} %refs_9_.1, bf16[1,128,256]{2,1,0:T(8,128)(2,1)} %grad_ref.1), custom_call_target="tpu_custom_call" | custom-call | tf_op jit(solution)/shard_map/pallas_call | solution.py:466
  3.2 15.7 %all-to-all-start = ((bf16[256,2,384]{2,1,0:T(2,128)(2,1)}), bf16[256,2,384]{2,1,0:T(2,128)(2,1)S(1)}, u32[]{:S(2)}, u32[]{:S(2)}) async-start(bf16[256,2,384]{2,1,0:T(2,128)(2,1)} %get-tuple-element.29), calls=%async_computation | async-start | bytes 786432 | tf_op jit(solution)/shard_map/all_to_all | solution.py:441
  18.9 1.5 %collective-permute-start.1 = (bf16[128,512]{1,0:T(8,128)(2,1)}, bf16[128,512]{1,0:T(8,128)(2,1)S(1)}, u32[]{:S(2)}, u32[]{:S(2)}) collective-permute-start(bf16[128,512]{1,0:T(8,128)(2,1)} %get-tuple-element.30.refs_0_), channel_id=1, source_target_pairs={{0,3},{1,0},{2,1},{3,2},{16,17},{17,18},{18,19},{19,16},{4,7},{5,4... | collective-permute-start | bytes 393224 | tf_op jit(solution)/shard_map/ppermute | solution.py:456
  20.4 1.4 %collective-permute-start = (bf16[128,512]{1,0:T(8,128)(2,1)}, bf16[128,512]{1,0:T(8,128)(2,1)S(1)}, u32[]{:S(2)}, u32[]{:S(2)}) collective-permute-start(bf16[128,512]{1,0:T(8,128)(2,1)} %get-tuple-element.30.refs_0_), channel_id=1, source_target_pairs={{0,1},{1,2},{2,3},{3,0},{16,19},{17,16},{18,17},{19,18},{4,5},{5,6... | collective-permute-start | bytes 393224 | tf_op jit(solution)/shard_map/ppermute | solution.py:456
  21.7 3.3 %collective-permute-done.1.rest_1_.refs_3_ = bf16[128,512]{1,0:T(8,128)(2,1)S(1)} collective-permute-done((bf16[128,512]{1,0:T(8,128)(2,1)}, bf16[128,512]{1,0:T(8,128)(2,1)S(1)}, u32[]{:S(2)}, u32[]{:S(2)}) %collective-permute-start.1) | collective-permute-done | bytes 131104 | tf_op jit(solution)/shard_map/ppermute | solution.py:456
  25.0 1.3 %collective-permute-done.rest_0_.refs_1_ = bf16[128,512]{1,0:T(8,128)(2,1)S(1)} collective-permute-done((bf16[128,512]{1,0:T(8,128)(2,1)}, bf16[128,512]{1,0:T(8,128)(2,1)S(1)}, u32[]{:S(2)}, u32[]{:S(2)}) %collective-permute-start) | collective-permute-done | bytes 131104 | tf_op jit(solution)/shard_map/ppermute | solution.py:456
  26.3 10.7 %all-to-all-done.in_ref = bf16[256,2,384]{2,1,0:T(2,128)(2,1)S(1)} async-done(((bf16[256,2,384]{2,1,0:T(2,128)(2,1)}), bf16[256,2,384]{2,1,0:T(2,128)(2,1)S(1)}, u32[]{:S(2)}, u32[]{:S(2)}) %all-to-all-start) | async-done | bytes 393248 | tf_op jit(solution)/shard_map/all_to_all | solution.py:441
  37.0 4.7 %shard_map.181 = bf16[32,2,3200]{2,1,0:T(2,128)(2,1)} custom-call(bf16[256,2,384]{2,1,0:T(2,128)(2,1)S(1)} %all-to-all-done.in_ref, f32[3,768]{1,0:T(4,128)S(1)} %copy-done.9, bf16[256,384]{1,0:T(8,128)(2,1)S(1)} %copy-done.5, bf16[768,256]{1,0:T(8,128)(2,1)S(1)} %copy-done.3, bf16[768,256]{1,0:T(8,128)(2,1)S(1)} %copy-done.2, ...), custom_call_target="tpu_custom_call" | custom-call | tf_op jit(solution)/shard_map/pallas_call | solution.py:476
  41.8 4.0 %all-to-all-start.1 = ((bf16[32,2,3200]{2,1,0:T(2,128)(2,1)}), bf16[32,2,3200]{2,1,0:T(2,128)(2,1)S(1)}, u32[]{:S(2)}, u32[]{:S(2)}) async-start(bf16[32,2,3200]{2,1,0:T(2,128)(2,1)} %shard_map.181), calls=%async_computation.1 | async-start | bytes 819200 | tf_op jit(solution)/shard_map/all_to_all | solution.py:441
  45.8 1.6 %collective-permute-start.2 = (bf16[128,512]{1,0:T(8,128)(2,1)S(1)}, bf16[128,512]{1,0:T(8,128)(2,1)S(1)}, u32[]{:S(2)}, u32[]{:S(2)}) collective-permute-start(bf16[128,512]{1,0:T(8,128)(2,1)S(1)} %copy-done.6), channel_id=1, source_target_pairs={{0,2},{1,3},{2,0},{3,1},{16,18},{17,19},{18,16},{19,17},{4,6},{5,7... | collective-permute-start | bytes 393224 | tf_op jit(solution)/shard_map/ppermute | solution.py:456
  47.4 4.0 %collective-permute-done.2.refs_2_ = bf16[128,512]{1,0:T(8,128)(2,1)S(1)} collective-permute-done((bf16[128,512]{1,0:T(8,128)(2,1)S(1)}, bf16[128,512]{1,0:T(8,128)(2,1)S(1)}, u32[]{:S(2)}, u32[]{:S(2)}) %collective-permute-start.2) | collective-permute-done | bytes 131104 | tf_op jit(solution)/shard_map/ppermute | solution.py:456
  51.4 2.0 %collective-permute-start.5 = (bf16[128,512]{1,0:T(8,128)(2,1)S(1)}, bf16[128,512]{1,0:T(8,128)(2,1)S(1)}, u32[]{:S(2)}, u32[]{:S(2)}) collective-permute-start(bf16[128,512]{1,0:T(8,128)(2,1)S(1)} %collective-permute-done.2.refs_2_), channel_id=1, source_target_pairs={{0,16},{16,0},{1,17},{17,1},{2,18},{18,2},{3,19},{19,3},{4,20},{20... | collective-permute-start | bytes 393224 | tf_op jit(solution)/shard_map/ppermute | solution.py:445
  54.9 5.5 %all-to-all-done.1.in_ref = bf16[32,2,3200]{2,1,0:T(2,128)(2,1)S(1)} async-done(((bf16[32,2,3200]{2,1,0:T(2,128)(2,1)}), bf16[32,2,3200]{2,1,0:T(2,128)(2,1)S(1)}, u32[]{:S(2)}, u32[]{:S(2)}) %all-to-all-start.1) | async-done | bytes 409632 | tf_op jit(solution)/shard_map/all_to_all | solution.py:441
  63.5 2.8 %collective-permute-start.11 = (bf16[2,224,128]{2,1,0:T(8,128)(2,1)S(1)}, bf16[2,224,128]{2,1,0:T(8,128)(2,1)S(1)}, u32[]{:S(2)}, u32[]{:S(2)}) collective-permute-start(bf16[2,224,128]{2,1,0:T(8,128)(2,1)S(1)} %get-tuple-element.39), channel_id=1, source_target_pairs={{0,2},{1,3},{2,0},{3,1},{16,18},{17,19},{18,16},{19,17},{4,6},{5,7... | collective-permute-start | bytes 344072 | tf_op jit(solution)/shard_map/ppermute | solution.py:456
  67.7 3.4 %all-to-all-start.2 = ((bf16[8,64,128]{2,1,0:T(8,128)(2,1)}), bf16[8,64,128]{2,1,0:T(8,128)(2,1)S(1)}, u32[]{:S(2)}, u32[]{:S(2)}) async-start(bf16[8,64,128]{2,1,0:T(8,128)(2,1)} %get-tuple-element.43), calls=%async_computation.2 | async-start | bytes 262144 | tf_op jit(solution)/shard_map/all_to_all | solution.py:441
  71.1 3.3 %collective-permute-start.10 = (bf16[2,224,128]{2,1,0:T(8,128)(2,1)S(1)}, bf16[2,224,128]{2,1,0:T(8,128)(2,1)S(1)}, u32[]{:S(2)}, u32[]{:S(2)}) collective-permute-start(bf16[2,224,128]{2,1,0:T(8,128)(2,1)S(1)} %get-tuple-element.38), channel_id=1, source_target_pairs={{0,1},{1,2},{2,3},{3,0},{16,19},{17,16},{18,17},{19,18},{4,5},{5,6... | collective-permute-start | bytes 344072 | tf_op jit(solution)/shard_map/ppermute | solution.py:456
  74.4 3.2 %collective-permute-start.15 = (bf16[2,224,128]{2,1,0:T(8,128)(2,1)S(1)}, bf16[2,224,128]{2,1,0:T(8,128)(2,1)S(1)}, u32[]{:S(2)}, u32[]{:S(2)}) collective-permute-start(bf16[2,224,128]{2,1,0:T(8,128)(2,1)S(1)} %collective-permute-done.11.refs_2_), channel_id=1, source_target_pairs={{0,16},{16,0},{1,17},{17,1},{2,18},{18,2},{3,19},{19,3},{4,20},{20... | collective-permute-start | bytes 344072 | tf_op jit(solution)/shard_map/ppermute | solution.py:445
  77.6 2.9 %collective-permute-done.12.refs_3_.refs_1_ = bf16[2,224,128]{2,1,0:T(8,128)(2,1)S(1)} collective-permute-done((bf16[2,224,128]{2,1,0:T(8,128)(2,1)S(1)}, bf16[2,224,128]{2,1,0:T(8,128)(2,1)S(1)}, u32[]{:S(2)}, u32[]{:S(2)}) %collective-permute-start.12) | collective-permute-done | bytes 114720 | tf_op jit(solution)/shard_map/ppermute | solution.py:456
  81.3 3.7 %all-to-all-start.3 = ((bf16[16,64,128]{2,1,0:T(8,128)(2,1)}), bf16[16,64,128]{2,1,0:T(8,128)(2,1)S(1)}, u32[]{:S(2)}, u32[]{:S(2)}) async-start(bf16[16,64,128]{2,1,0:T(8,128)(2,1)} %shard_map.185), calls=%async_computation.3 | async-start | bytes 524288 | tf_op jit(solution)/shard_map/all_to_all | solution.py:441
  84.9 4.1 %collective-permute-start.13 = (bf16[2,224,128]{2,1,0:T(8,128)(2,1)S(1)}, bf16[2,224,128]{2,1,0:T(8,128)(2,1)S(1)}, u32[]{:S(2)}, u32[]{:S(2)}) collective-permute-start(bf16[2,224,128]{2,1,0:T(8,128)(2,1)S(1)} %get-tuple-element.31.refs_0_), channel_id=1, source_target_pairs={{0,16},{16,0},{1,17},{17,1},{2,18},{18,2},{3,19},{19,3},{4,20},{20... | collective-permute-start | bytes 344072 | tf_op jit(solution)/shard_map/ppermute | solution.py:445
  90.5 1.4 %shard_map.184 = (bf16[1,128,256]{2,1,0:T(8,128)(2,1)}, bf16[1,128,256]{2,1,0:T(8,128)(2,1)}, f32[3,768]{1,0:T(4,128)}, f32[128,256]{1,0:T(8,128)}, f32[128,256]{1,0:T(8,128)}) custom-call(bf16[2,224,128]{2,1,0:T(8,128)(2,1)S(1)} %get-tuple-element.31.refs_0_, bf16[2,224,128]{2,1,0:T(8,128)(2,1)S(1)} %collective-permute-done.10.refs_1_.refs_0_, ...), custom_call_target="tpu_custom_call" | custom-call | tf_op jit(solution)/shard_map/pallas_call | solution.py:506
  92.2 5.2 %collective-permute-start.17 = (bf16[16,64,128]{2,1,0:T(8,128)(2,1)S(1)}, bf16[16,64,128]{2,1,0:T(8,128)(2,1)S(1)}, u32[]{:S(2)}, u32[]{:S(2)}) collective-permute-start(bf16[16,64,128]{2,1,0:T(8,128)(2,1)S(1)} %all-to-all-done.3.own_ref), channel_id=1, source_target_pairs={{0,16},{16,0},{1,17},{17,1},{2,18},{18,2},{3,19},{19,3},{4,20},{20... | collective-permute-start | bytes 786440 | tf_op jit(solution)/shard_map/ppermute | solution.py:445
  97.4 1.2 %collective-permute-done.17.other_ref = bf16[16,64,128]{2,1,0:T(8,128)(2,1)S(1)} collective-permute-done((bf16[16,64,128]{2,1,0:T(8,128)(2,1)S(1)}, bf16[16,64,128]{2,1,0:T(8,128)(2,1)S(1)}, u32[]{:S(2)}, u32[]{:S(2)}) %collective-permute-start.17) | collective-permute-done | bytes 262176 | tf_op jit(solution)/shard_map/ppermute | solution.py:445
  98.5 1.3 %shard_map.186 = (f32[256,768]{1,0:T(8,128)}, f32[256,256]{1,0:T(8,128)}) custom-call(bf16[16,64,128]{2,1,0:T(8,128)(2,1)S(1)} %all-to-all-done.3.own_ref, bf16[16,64,128]{2,1,0:T(8,128)(2,1)S(1)} %collective-permute-done.17.other_ref), custom_call_target="tpu_custom_call" | custom-call | tf_op jit(solution)/shard_map/pallas_call | solution.py:517
  (47 shorter events, 8.7 us)
Async XLA Ops:
  0.6 36.4 %copy-start.4 = (bf16[128,768]{1,0:T(8,128)(2,1)S(1)}, bf16[128,768]{1,0:T(8,128)(2,1)}, u32[]{:S(2)}) copy-start(bf16[128,768]{1,0:T(8,128)(2,1)} %constant.15.clone.first_back_ref) | copy-start | bytes 589828
  0.6 36.3 %copy-start.5 = (bf16[256,384]{1,0:T(8,128)(2,1)S(1)}, bf16[256,384]{1,0:T(8,128)(2,1)}, u32[]{:S(2)}) copy-start(bf16[256,384]{1,0:T(8,128)(2,1)} %constant.12.clone.first_ref) | copy-start | bytes 589828
  3.2 33.8 %all-to-all-start = ((bf16[256,2,384]{2,1,0:T(2,128)(2,1)}), bf16[256,2,384]{2,1,0:T(2,128)(2,1)S(1)}, u32[]{:S(2)}, u32[]{:S(2)}) async-start(bf16[256,2,384]{2,1,0:T(2,128)(2,1)} %get-tuple-element.29), calls=%async_computation | async-start | bytes 786432 | tf_op jit(solution)/shard_map/all_to_all | solution.py:441
  18.9 6.1 %collective-permute-start.1 = (bf16[128,512]{1,0:T(8,128)(2,1)}, bf16[128,512]{1,0:T(8,128)(2,1)S(1)}, u32[]{:S(2)}, u32[]{:S(2)}) collective-permute-start(bf16[128,512]{1,0:T(8,128)(2,1)} %get-tuple-element.30.refs_0_), channel_id=1, source_target_pairs={{0,3},{1,0},{2,1},{3,2},{16,17},{17,18},{18,19},{19,16},{4,7},{5,4... | collective-permute-start | bytes 393224 | tf_op jit(solution)/shard_map/ppermute | solution.py:456
  20.4 6.0 %collective-permute-start = (bf16[128,512]{1,0:T(8,128)(2,1)}, bf16[128,512]{1,0:T(8,128)(2,1)S(1)}, u32[]{:S(2)}, u32[]{:S(2)}) collective-permute-start(bf16[128,512]{1,0:T(8,128)(2,1)} %get-tuple-element.30.refs_0_), channel_id=1, source_target_pairs={{0,1},{1,2},{2,3},{3,0},{16,19},{17,16},{18,17},{19,18},{4,5},{5,6... | collective-permute-start | bytes 393224 | tf_op jit(solution)/shard_map/ppermute | solution.py:456
  41.8 18.7 %all-to-all-start.1 = ((bf16[32,2,3200]{2,1,0:T(2,128)(2,1)}), bf16[32,2,3200]{2,1,0:T(2,128)(2,1)S(1)}, u32[]{:S(2)}, u32[]{:S(2)}) async-start(bf16[32,2,3200]{2,1,0:T(2,128)(2,1)} %shard_map.181), calls=%async_computation.1 | async-start | bytes 819200 | tf_op jit(solution)/shard_map/all_to_all | solution.py:441
  45.8 5.6 %collective-permute-start.2 = (bf16[128,512]{1,0:T(8,128)(2,1)S(1)}, bf16[128,512]{1,0:T(8,128)(2,1)S(1)}, u32[]{:S(2)}, u32[]{:S(2)}) collective-permute-start(bf16[128,512]{1,0:T(8,128)(2,1)S(1)} %copy-done.6), channel_id=1, source_target_pairs={{0,2},{1,3},{2,0},{3,1},{16,18},{17,19},{18,16},{19,17},{4,6},{5,7... | collective-permute-start | bytes 393224 | tf_op jit(solution)/shard_map/ppermute | solution.py:456
  47.4 6.5 %collective-permute-start.3 = (bf16[128,512]{1,0:T(8,128)(2,1)S(1)}, bf16[128,512]{1,0:T(8,128)(2,1)S(1)}, u32[]{:S(2)}, u32[]{:S(2)}) collective-permute-start(bf16[128,512]{1,0:T(8,128)(2,1)S(1)} %copy-done.6), channel_id=1, source_target_pairs={{0,16},{16,0},{1,17},{17,1},{2,18},{18,2},{3,19},{19,3},{4,20},{20... | collective-permute-start | bytes 393224 | tf_op jit(solution)/shard_map/ppermute | solution.py:445
  51.4 2.9 %collective-permute-start.5 = (bf16[128,512]{1,0:T(8,128)(2,1)S(1)}, bf16[128,512]{1,0:T(8,128)(2,1)S(1)}, u32[]{:S(2)}, u32[]{:S(2)}) collective-permute-start(bf16[128,512]{1,0:T(8,128)(2,1)S(1)} %collective-permute-done.2.refs_2_), channel_id=1, source_target_pairs={{0,16},{16,0},{1,17},{17,1},{2,18},{18,2},{3,19},{19,3},{4,20},{20... | collective-permute-start | bytes 393224 | tf_op jit(solution)/shard_map/ppermute | solution.py:445
  53.4 1.3 %collective-permute-start.6 = (bf16[128,512]{1,0:T(8,128)(2,1)S(1)}, bf16[128,512]{1,0:T(8,128)(2,1)S(1)}, u32[]{:S(2)}, u32[]{:S(2)}) collective-permute-start(bf16[128,512]{1,0:T(8,128)(2,1)S(1)} %collective-permute-done.1.rest_1_.refs_3_), channel_id=1, source_target_pairs={{0,16},{16,0},{1,17},{17,1},{2,18},{18,2},{3,19},{19,3},{4,20},{20... | collective-permute-start | bytes 393224 | tf_op jit(solution)/shard_map/ppermute | solution.py:445
  53.4 1.5 %collective-permute-start.4 = (bf16[128,512]{1,0:T(8,128)(2,1)S(1)}, bf16[128,512]{1,0:T(8,128)(2,1)S(1)}, u32[]{:S(2)}, u32[]{:S(2)}) collective-permute-start(bf16[128,512]{1,0:T(8,128)(2,1)S(1)} %collective-permute-done.rest_0_.refs_1_), channel_id=1, source_target_pairs={{0,16},{16,0},{1,17},{17,1},{2,18},{18,2},{3,19},{19,3},{4,20},{20... | collective-permute-start | bytes 393224 | tf_op jit(solution)/shard_map/ppermute | solution.py:445
  61.0 5.3 %collective-permute-start.7 = (f32[32,256]{1,0:T(8,128)S(1)}, f32[32,256]{1,0:T(8,128)S(1)}, u32[]{:S(2)}, u32[]{:S(2)}) collective-permute-start(f32[32,256]{1,0:T(8,128)S(1)} %get-tuple-element.33), channel_id=1, source_target_pairs={{0,32},{32,64},{64,96},{96,0},{16,112},{48,16},{80,48},{112,80},{1... | collective-permute-start | bytes 98312 | tf_op jit(solution)/shard_map/ppermute | solution.py:456
  62.0 4.3 %collective-permute-start.8 = (f32[32,256]{1,0:T(8,128)S(1)}, f32[32,256]{1,0:T(8,128)S(1)}, u32[]{:S(2)}, u32[]{:S(2)}) collective-permute-start(f32[32,256]{1,0:T(8,128)S(1)} %get-tuple-element.34), channel_id=1, source_target_pairs={{0,64},{32,96},{64,0},{96,32},{16,80},{48,112},{80,16},{112,48},{1... | collective-permute-start | bytes 98312 | tf_op jit(solution)/shard_map/ppermute | solution.py:456
  63.1 4.0 %collective-permute-start.9 = (f32[32,256]{1,0:T(8,128)S(1)}, f32[32,256]{1,0:T(8,128)S(1)}, u32[]{:S(2)}, u32[]{:S(2)}) collective-permute-start(f32[32,256]{1,0:T(8,128)S(1)} %get-tuple-element.35), channel_id=1, source_target_pairs={{0,96},{32,0},{64,32},{96,64},{16,48},{48,80},{80,112},{112,16},{1... | collective-permute-start | bytes 98312 | tf_op jit(solution)/shard_map/ppermute | solution.py:456
  63.5 11.0 %collective-permute-start.11 = (bf16[2,224,128]{2,1,0:T(8,128)(2,1)S(1)}, bf16[2,224,128]{2,1,0:T(8,128)(2,1)S(1)}, u32[]{:S(2)}, u32[]{:S(2)}) collective-permute-start(bf16[2,224,128]{2,1,0:T(8,128)(2,1)S(1)} %get-tuple-element.39), channel_id=1, source_target_pairs={{0,2},{1,3},{2,0},{3,1},{16,18},{17,19},{18,16},{19,17},{4,6},{5,7... | collective-permute-start | bytes 344072 | tf_op jit(solution)/shard_map/ppermute | solution.py:456
  67.7 12.8 %all-to-all-start.2 = ((bf16[8,64,128]{2,1,0:T(8,128)(2,1)}), bf16[8,64,128]{2,1,0:T(8,128)(2,1)S(1)}, u32[]{:S(2)}, u32[]{:S(2)}) async-start(bf16[8,64,128]{2,1,0:T(8,128)(2,1)} %get-tuple-element.43), calls=%async_computation.2 | async-start | bytes 262144 | tf_op jit(solution)/shard_map/all_to_all | solution.py:441
  71.1 6.5 %collective-permute-start.10 = (bf16[2,224,128]{2,1,0:T(8,128)(2,1)S(1)}, bf16[2,224,128]{2,1,0:T(8,128)(2,1)S(1)}, u32[]{:S(2)}, u32[]{:S(2)}) collective-permute-start(bf16[2,224,128]{2,1,0:T(8,128)(2,1)S(1)} %get-tuple-element.38), channel_id=1, source_target_pairs={{0,1},{1,2},{2,3},{3,0},{16,19},{17,16},{18,17},{19,18},{4,5},{5,6... | collective-permute-start | bytes 344072 | tf_op jit(solution)/shard_map/ppermute | solution.py:456
  74.4 6.1 %collective-permute-start.12 = (bf16[2,224,128]{2,1,0:T(8,128)(2,1)S(1)}, bf16[2,224,128]{2,1,0:T(8,128)(2,1)S(1)}, u32[]{:S(2)}, u32[]{:S(2)}) collective-permute-start(bf16[2,224,128]{2,1,0:T(8,128)(2,1)S(1)} %get-tuple-element.40), channel_id=1, source_target_pairs={{0,3},{1,0},{2,1},{3,2},{16,17},{17,18},{18,19},{19,16},{4,7},{5,4... | collective-permute-start | bytes 344072 | tf_op jit(solution)/shard_map/ppermute | solution.py:456
  74.4 6.1 %collective-permute-start.15 = (bf16[2,224,128]{2,1,0:T(8,128)(2,1)S(1)}, bf16[2,224,128]{2,1,0:T(8,128)(2,1)S(1)}, u32[]{:S(2)}, u32[]{:S(2)}) collective-permute-start(bf16[2,224,128]{2,1,0:T(8,128)(2,1)S(1)} %collective-permute-done.11.refs_2_), channel_id=1, source_target_pairs={{0,16},{16,0},{1,17},{17,1},{2,18},{18,2},{3,19},{19,3},{4,20},{20... | collective-permute-start | bytes 344072 | tf_op jit(solution)/shard_map/ppermute | solution.py:445
  81.3 11.0 %all-to-all-start.3 = ((bf16[16,64,128]{2,1,0:T(8,128)(2,1)}), bf16[16,64,128]{2,1,0:T(8,128)(2,1)S(1)}, u32[]{:S(2)}, u32[]{:S(2)}) async-start(bf16[16,64,128]{2,1,0:T(8,128)(2,1)} %shard_map.185), calls=%async_computation.3 | async-start | bytes 524288 | tf_op jit(solution)/shard_map/all_to_all | solution.py:441
  84.9 5.0 %collective-permute-start.13 = (bf16[2,224,128]{2,1,0:T(8,128)(2,1)S(1)}, bf16[2,224,128]{2,1,0:T(8,128)(2,1)S(1)}, u32[]{:S(2)}, u32[]{:S(2)}) collective-permute-start(bf16[2,224,128]{2,1,0:T(8,128)(2,1)S(1)} %get-tuple-element.31.refs_0_), channel_id=1, source_target_pairs={{0,16},{16,0},{1,17},{17,1},{2,18},{18,2},{3,19},{19,3},{4,20},{20... | collective-permute-start | bytes 344072 | tf_op jit(solution)/shard_map/ppermute | solution.py:445
  89.0 1.3 %collective-permute-start.14 = (bf16[2,224,128]{2,1,0:T(8,128)(2,1)S(1)}, bf16[2,224,128]{2,1,0:T(8,128)(2,1)S(1)}, u32[]{:S(2)}, u32[]{:S(2)}) collective-permute-start(bf16[2,224,128]{2,1,0:T(8,128)(2,1)S(1)} %collective-permute-done.10.refs_1_.refs_0_), channel_id=1, source_target_pairs={{0,16},{16,0},{1,17},{17,1},{2,18},{18,2},{3,19},{19,3},{4,20},{20... | collective-permute-start | bytes 344072 | tf_op jit(solution)/shard_map/ppermute | solution.py:445
  89.1 1.4 %collective-permute-start.16 = (bf16[2,224,128]{2,1,0:T(8,128)(2,1)S(1)}, bf16[2,224,128]{2,1,0:T(8,128)(2,1)S(1)}, u32[]{:S(2)}, u32[]{:S(2)}) collective-permute-start(bf16[2,224,128]{2,1,0:T(8,128)(2,1)S(1)} %collective-permute-done.12.refs_3_.refs_1_), channel_id=1, source_target_pairs={{0,16},{16,0},{1,17},{17,1},{2,18},{18,2},{3,19},{19,3},{4,20},{20... | collective-permute-start | bytes 344072 | tf_op jit(solution)/shard_map/ppermute | solution.py:445
  92.2 6.3 %collective-permute-start.17 = (bf16[16,64,128]{2,1,0:T(8,128)(2,1)S(1)}, bf16[16,64,128]{2,1,0:T(8,128)(2,1)S(1)}, u32[]{:S(2)}, u32[]{:S(2)}) collective-permute-start(bf16[16,64,128]{2,1,0:T(8,128)(2,1)S(1)} %all-to-all-done.3.own_ref), channel_id=1, source_target_pairs={{0,16},{16,0},{1,17},{17,1},{2,18},{18,2},{3,19},{19,3},{4,20},{20... | collective-permute-start | bytes 786440 | tf_op jit(solution)/shard_map/ppermute | solution.py:445
  (8 other events, 199.1 us)

commit v16 on v15

--- a/solution.py
+++ b/solution.py
@@ -300,7 +300,7 @@
     sources = in_ref.shape[0]
     width = both_refs[0].shape[1] // 2
     x, core, y = lax.axis_index("x"), lax.axis_index("core"), lax.axis_index("y")
-    turn = 1 - 2 * core
+    turn = 2 * core - 1
     for tile in range(tiles):
         rows_ref[tile] = (
             in_ref[:, :, tile * rows : (tile + 1) * rows]
@@ -336,7 +336,7 @@
     width = out_weight_ref.shape[0]
     count = width // 8
     core, y = lax.axis_index("core"), lax.axis_index("y")
-    turn = 1 - 2 * core
+    turn = 2 * core - 1
 
     def row_of(zh, x, c, zl, v):
         other = c ^ core
@@ -448,7 +448,7 @@
 def ring(x, axis, distance):
     axes = ("x", "core") if axis == "x" else ("core", "y")
     route = []
-    for core, turn in ((0, distance), (1, -distance)):
+    for core, turn in ((0, -distance), (1, distance)):
         for i in range(4):
             j = (i + turn) % 4
             pair = (i * 2 + core, j * 2 + core) if axis == "x" else (core * 4 + i, core * 4 + j)

time: 100 us -> 100 us (level)
    ppermute x9, starting transfers between devices: 15.4 us -> 12.5 us  [swap_core(): return lax.ppermute(x, 'core', [(0, 1), (1, 0)])]
    all_to_all x4, starting transfers between devices: 26.7 us -> 28.6 us  [exchange(): return lax.all_to_all(x, axes, split_axis=0, concat_axis=0, tiled=True)]
    all_to_all x4, waiting for transfers between devices: 16.5 us -> 15.4 us  [exchange(): return lax.all_to_all(x, axes, split_axis=0, concat_axis=0, tiled=True)]
where the time goes in v16:
time: 100 us; the launch traced here: 99.5 us
  starting transfers between devices  54.7 us (55%)
  waiting for transfers between devices  32 us (32%)
  Pallas kernels  11.9 us (12%)
    all_to_all x4, starting transfers between devices, exchange(): return lax.all_to_all(x, axes, split_axis=0, concat_axis=0, tiled=True)  28.6 us
    all_to_all x4, waiting for transfers between devices, exchange(): return lax.all_to_all(x, axes, split_axis=0, concat_axis=0, tiled=True)  15.4 us
    ppermute x9, starting transfers between devices, ring(): return lax.ppermute(x, axes, route)  13.5 us
    ppermute x9, waiting for transfers between devices, ring(): return lax.ppermute(x, axes, route)  12.5 us
    ppermute x9, starting transfers between devices, swap_core(): return lax.ppermute(x, 'core', [(0, 1), (1, 0)])  12.5 us
    pallas_call x1, Pallas kernels, per_device(): call(convolve_kernel, shape((32, 2, 25 * rows), bf16), [pltpu.VMEM((3, 2...  4.73 us
    ppermute x9, waiting for transfers between devices, swap_core(): return lax.ppermute(x, 'core', [(0, 1), (1, 0)])  4.12 us
    pallas_call x1, Pallas kernels, per_device(): call(pack_kernel, (shape((width, 2, 3 * rows), bf16), shape((rows, 2 * wi...  2.53 us
  transfers between devices with their start and end apart: 22, of which 15 were waited for; matrix products, arithmetic and copies ran while one was open for 0% of the time, Pallas kernels for 2%

profile of v16, /device:TPU:1, one launch (start us, length us, event | category | flops | bytes accessed | tf_op | source)
XLA Modules:
  0.0 99.5 jit_solution(13817163312521070648)
XLA Ops:
  0.7 2.5 %shard_map.180 = (bf16[256,2,384]{2,1,0:T(2,128)(2,1)}, bf16[128,512]{1,0:T(8,128)(2,1)}) custom-call(bf16[1,128,256]{2,1,0:T(8,128)(2,1)} %seq_ref.1, bf16[256,768]{1,0:T(8,128)(2,1)} %refs_8_.1, f32[128,256]{1,0:T(8,128)} %one_ref.1, f32[128,256]{1,0:T(8,128)} %two_ref.1, bf16[256,256]{1,0:T(8,128)(2,1)} %refs_9_.1, bf16[1,128,256]{2,1,0:T(8,128)(2,1)} %grad_ref.1), custom_call_target="tpu_custom_call" | custom-call | tf_op jit(solution)/shard_map/pallas_call | solution.py:466
  3.2 15.7 %all-to-all-start = ((bf16[256,2,384]{2,1,0:T(2,128)(2,1)}), bf16[256,2,384]{2,1,0:T(2,128)(2,1)S(1)}, u32[]{:S(2)}, u32[]{:S(2)}) async-start(bf16[256,2,384]{2,1,0:T(2,128)(2,1)} %get-tuple-element.29), calls=%async_computation | async-start | bytes 786432 | tf_op jit(solution)/shard_map/all_to_all | solution.py:441
  18.9 2.7 %collective-permute-start.1 = (bf16[128,512]{1,0:T(8,128)(2,1)}, bf16[128,512]{1,0:T(8,128)(2,1)S(1)}, u32[]{:S(2)}, u32[]{:S(2)}) collective-permute-start(bf16[128,512]{1,0:T(8,128)(2,1)} %get-tuple-element.30.refs_0_), channel_id=1, source_target_pairs={{0,1},{1,2},{2,3},{3,0},{16,19},{17,16},{18,17},{19,18},{4,5},{5,6... | collective-permute-start | bytes 393224 | tf_op jit(solution)/shard_map/ppermute | solution.py:456
  21.6 2.9 %collective-permute-done.1.rest_1_.refs_3_ = bf16[128,512]{1,0:T(8,128)(2,1)S(1)} collective-permute-done((bf16[128,512]{1,0:T(8,128)(2,1)}, bf16[128,512]{1,0:T(8,128)(2,1)S(1)}, u32[]{:S(2)}, u32[]{:S(2)}) %collective-permute-start.1) | collective-permute-done | bytes 131104 | tf_op jit(solution)/shard_map/ppermute | solution.py:456
  24.6 5.6 %collective-permute-done.rest_0_.refs_1_ = bf16[128,512]{1,0:T(8,128)(2,1)S(1)} collective-permute-done((bf16[128,512]{1,0:T(8,128)(2,1)}, bf16[128,512]{1,0:T(8,128)(2,1)S(1)}, u32[]{:S(2)}, u32[]{:S(2)}) %collective-permute-start) | collective-permute-done | bytes 131104 | tf_op jit(solution)/shard_map/ppermute | solution.py:456
  30.1 6.9 %all-to-all-done.in_ref = bf16[256,2,384]{2,1,0:T(2,128)(2,1)S(1)} async-done(((bf16[256,2,384]{2,1,0:T(2,128)(2,1)}), bf16[256,2,384]{2,1,0:T(2,128)(2,1)S(1)}, u32[]{:S(2)}, u32[]{:S(2)}) %all-to-all-start) | async-done | bytes 393248 | tf_op jit(solution)/shard_map/all_to_all | solution.py:441
  37.0 4.7 %shard_map.181 = bf16[32,2,3200]{2,1,0:T(2,128)(2,1)} custom-call(bf16[256,2,384]{2,1,0:T(2,128)(2,1)S(1)} %all-to-all-done.in_ref, f32[3,768]{1,0:T(4,128)S(1)} %copy-done.9, bf16[256,384]{1,0:T(8,128)(2,1)S(1)} %copy-done.5, bf16[768,256]{1,0:T(8,128)(2,1)S(1)} %copy-done.3, bf16[768,256]{1,0:T(8,128)(2,1)S(1)} %copy-done.2, ...), custom_call_target="tpu_custom_call" | custom-call | tf_op jit(solution)/shard_map/pallas_call | solution.py:476
  41.8 4.0 %all-to-all-start.1 = ((bf16[32,2,3200]{2,1,0:T(2,128)(2,1)}), bf16[32,2,3200]{2,1,0:T(2,128)(2,1)S(1)}, u32[]{:S(2)}, u32[]{:S(2)}) async-start(bf16[32,2,3200]{2,1,0:T(2,128)(2,1)} %shard_map.181), calls=%async_computation.1 | async-start | bytes 819200 | tf_op jit(solution)/shard_map/all_to_all | solution.py:441
  45.8 1.6 %collective-permute-start.2 = (bf16[128,512]{1,0:T(8,128)(2,1)S(1)}, bf16[128,512]{1,0:T(8,128)(2,1)S(1)}, u32[]{:S(2)}, u32[]{:S(2)}) collective-permute-start(bf16[128,512]{1,0:T(8,128)(2,1)S(1)} %copy-done.6), channel_id=1, source_target_pairs={{0,2},{1,3},{2,0},{3,1},{16,18},{17,19},{18,16},{19,17},{4,6},{5,7... | collective-permute-start | bytes 393224 | tf_op jit(solution)/shard_map/ppermute | solution.py:456
  47.4 4.0 %collective-permute-done.2.refs_2_ = bf16[128,512]{1,0:T(8,128)(2,1)S(1)} collective-permute-done((bf16[128,512]{1,0:T(8,128)(2,1)S(1)}, bf16[128,512]{1,0:T(8,128)(2,1)S(1)}, u32[]{:S(2)}, u32[]{:S(2)}) %collective-permute-start.2) | collective-permute-done | bytes 131104 | tf_op jit(solution)/shard_map/ppermute | solution.py:456
  51.4 2.0 %collective-permute-start.5 = (bf16[128,512]{1,0:T(8,128)(2,1)S(1)}, bf16[128,512]{1,0:T(8,128)(2,1)S(1)}, u32[]{:S(2)}, u32[]{:S(2)}) collective-permute-start(bf16[128,512]{1,0:T(8,128)(2,1)S(1)} %collective-permute-done.2.refs_2_), channel_id=1, source_target_pairs={{0,16},{16,0},{1,17},{17,1},{2,18},{18,2},{3,19},{19,3},{4,20},{20... | collective-permute-start | bytes 393224 | tf_op jit(solution)/shard_map/ppermute | solution.py:445
  54.9 5.5 %all-to-all-done.1.in_ref = bf16[32,2,3200]{2,1,0:T(2,128)(2,1)S(1)} async-done(((bf16[32,2,3200]{2,1,0:T(2,128)(2,1)}), bf16[32,2,3200]{2,1,0:T(2,128)(2,1)S(1)}, u32[]{:S(2)}, u32[]{:S(2)}) %all-to-all-start.1) | async-done | bytes 409632 | tf_op jit(solution)/shard_map/all_to_all | solution.py:441
  61.3 1.9 %collective-permute-start.8 = (f32[32,256]{1,0:T(8,128)S(1)}, f32[32,256]{1,0:T(8,128)S(1)}, u32[]{:S(2)}, u32[]{:S(2)}) collective-permute-start(f32[32,256]{1,0:T(8,128)S(1)} %get-tuple-element.34), channel_id=1, source_target_pairs={{0,64},{32,96},{64,0},{96,32},{16,80},{48,112},{80,16},{112,48},{1... | collective-permute-start | bytes 98312 | tf_op jit(solution)/shard_map/ppermute | solution.py:456
  63.2 1.5 %collective-permute-start.9 = (f32[32,256]{1,0:T(8,128)S(1)}, f32[32,256]{1,0:T(8,128)S(1)}, u32[]{:S(2)}, u32[]{:S(2)}) collective-permute-start(f32[32,256]{1,0:T(8,128)S(1)} %get-tuple-element.35), channel_id=1, source_target_pairs={{0,32},{32,64},{64,96},{96,0},{16,112},{48,16},{80,48},{112,80},{1... | collective-permute-start | bytes 98312 | tf_op jit(solution)/shard_map/ppermute | solution.py:456
  64.7 2.8 %collective-permute-start.11 = (bf16[2,224,128]{2,1,0:T(8,128)(2,1)S(1)}, bf16[2,224,128]{2,1,0:T(8,128)(2,1)S(1)}, u32[]{:S(2)}, u32[]{:S(2)}) collective-permute-start(bf16[2,224,128]{2,1,0:T(8,128)(2,1)S(1)} %get-tuple-element.39), channel_id=1, source_target_pairs={{0,2},{1,3},{2,0},{3,1},{16,18},{17,19},{18,16},{19,17},{4,6},{5,7... | collective-permute-start | bytes 344072 | tf_op jit(solution)/shard_map/ppermute | solution.py:456
  68.2 3.4 %all-to-all-start.2 = ((bf16[8,64,128]{2,1,0:T(8,128)(2,1)}), bf16[8,64,128]{2,1,0:T(8,128)(2,1)S(1)}, u32[]{:S(2)}, u32[]{:S(2)}) async-start(bf16[8,64,128]{2,1,0:T(8,128)(2,1)} %get-tuple-element.43), calls=%async_computation.2 | async-start | bytes 262144 | tf_op jit(solution)/shard_map/all_to_all | solution.py:441
  71.6 2.7 %collective-permute-start.12 = (bf16[2,224,128]{2,1,0:T(8,128)(2,1)S(1)}, bf16[2,224,128]{2,1,0:T(8,128)(2,1)S(1)}, u32[]{:S(2)}, u32[]{:S(2)}) collective-permute-start(bf16[2,224,128]{2,1,0:T(8,128)(2,1)S(1)} %get-tuple-element.40), channel_id=1, source_target_pairs={{0,1},{1,2},{2,3},{3,0},{16,19},{17,16},{18,17},{19,18},{4,5},{5,6... | collective-permute-start | bytes 344072 | tf_op jit(solution)/shard_map/ppermute | solution.py:456
  74.3 2.8 %collective-permute-start.15 = (bf16[2,224,128]{2,1,0:T(8,128)(2,1)S(1)}, bf16[2,224,128]{2,1,0:T(8,128)(2,1)S(1)}, u32[]{:S(2)}, u32[]{:S(2)}) collective-permute-start(bf16[2,224,128]{2,1,0:T(8,128)(2,1)S(1)} %collective-permute-done.11.refs_2_), channel_id=1, source_target_pairs={{0,16},{16,0},{1,17},{17,1},{2,18},{18,2},{3,19},{19,3},{4,20},{20... | collective-permute-start | bytes 344072 | tf_op jit(solution)/shard_map/ppermute | solution.py:445
  80.1 5.6 %all-to-all-start.3 = ((bf16[16,64,128]{2,1,0:T(8,128)(2,1)}), bf16[16,64,128]{2,1,0:T(8,128)(2,1)S(1)}, u32[]{:S(2)}, u32[]{:S(2)}) async-start(bf16[16,64,128]{2,1,0:T(8,128)(2,1)} %shard_map.185), calls=%async_computation.3 | async-start | bytes 524288 | tf_op jit(solution)/shard_map/all_to_all | solution.py:441
  85.8 2.9 %collective-permute-start.13 = (bf16[2,224,128]{2,1,0:T(8,128)(2,1)S(1)}, bf16[2,224,128]{2,1,0:T(8,128)(2,1)S(1)}, u32[]{:S(2)}, u32[]{:S(2)}) collective-permute-start(bf16[2,224,128]{2,1,0:T(8,128)(2,1)S(1)} %get-tuple-element.31.refs_0_), channel_id=1, source_target_pairs={{0,16},{16,0},{1,17},{17,1},{2,18},{18,2},{3,19},{19,3},{4,20},{20... | collective-permute-start | bytes 344072 | tf_op jit(solution)/shard_map/ppermute | solution.py:445
  90.1 1.4 %shard_map.184 = (bf16[1,128,256]{2,1,0:T(8,128)(2,1)}, bf16[1,128,256]{2,1,0:T(8,128)(2,1)}, f32[3,768]{1,0:T(4,128)}, f32[128,256]{1,0:T(8,128)}, f32[128,256]{1,0:T(8,128)}) custom-call(bf16[2,224,128]{2,1,0:T(8,128)(2,1)S(1)} %get-tuple-element.31.refs_0_, bf16[2,224,128]{2,1,0:T(8,128)(2,1)S(1)} %collective-permute-done.10.refs_1_.refs_0_, ...), custom_call_target="tpu_custom_call" | custom-call | tf_op jit(solution)/shard_map/pallas_call | solution.py:506
  91.5 1.7 %all-to-all-done.3.own_ref = bf16[16,64,128]{2,1,0:T(8,128)(2,1)S(1)} async-done(((bf16[16,64,128]{2,1,0:T(8,128)(2,1)}), bf16[16,64,128]{2,1,0:T(8,128)(2,1)S(1)}, u32[]{:S(2)}, u32[]{:S(2)}) %all-to-all-start.3) | async-done | bytes 262176 | tf_op jit(solution)/shard_map/all_to_all | solution.py:441
  93.2 3.8 %collective-permute-start.17 = (bf16[16,64,128]{2,1,0:T(8,128)(2,1)S(1)}, bf16[16,64,128]{2,1,0:T(8,128)(2,1)S(1)}, u32[]{:S(2)}, u32[]{:S(2)}) collective-permute-start(bf16[16,64,128]{2,1,0:T(8,128)(2,1)S(1)} %all-to-all-done.3.own_ref), channel_id=1, source_target_pairs={{0,16},{16,0},{1,17},{17,1},{2,18},{18,2},{3,19},{19,3},{4,20},{20... | collective-permute-start | bytes 786440 | tf_op jit(solution)/shard_map/ppermute | solution.py:445
  98.2 1.3 %shard_map.186 = (f32[256,768]{1,0:T(8,128)}, f32[256,256]{1,0:T(8,128)}) custom-call(bf16[16,64,128]{2,1,0:T(8,128)(2,1)S(1)} %all-to-all-done.3.own_ref, bf16[16,64,128]{2,1,0:T(8,128)(2,1)S(1)} %collective-permute-done.17.other_ref), custom_call_target="tpu_custom_call" | custom-call | tf_op jit(solution)/shard_map/pallas_call | solution.py:517
  (47 shorter events, 8.9 us)
Async XLA Ops:
  0.6 36.4 %copy-start.4 = (bf16[128,768]{1,0:T(8,128)(2,1)S(1)}, bf16[128,768]{1,0:T(8,128)(2,1)}, u32[]{:S(2)}) copy-start(bf16[128,768]{1,0:T(8,128)(2,1)} %constant.15.clone.first_back_ref) | copy-start | bytes 589828
  0.6 36.3 %copy-start.5 = (bf16[256,384]{1,0:T(8,128)(2,1)S(1)}, bf16[256,384]{1,0:T(8,128)(2,1)}, u32[]{:S(2)}) copy-start(bf16[256,384]{1,0:T(8,128)(2,1)} %constant.12.clone.first_ref) | copy-start | bytes 589828
  3.2 33.8 %all-to-all-start = ((bf16[256,2,384]{2,1,0:T(2,128)(2,1)}), bf16[256,2,384]{2,1,0:T(2,128)(2,1)S(1)}, u32[]{:S(2)}, u32[]{:S(2)}) async-start(bf16[256,2,384]{2,1,0:T(2,128)(2,1)} %get-tuple-element.29), calls=%async_computation | async-start | bytes 786432 | tf_op jit(solution)/shard_map/all_to_all | solution.py:441
  18.9 5.7 %collective-permute-start.1 = (bf16[128,512]{1,0:T(8,128)(2,1)}, bf16[128,512]{1,0:T(8,128)(2,1)S(1)}, u32[]{:S(2)}, u32[]{:S(2)}) collective-permute-start(bf16[128,512]{1,0:T(8,128)(2,1)} %get-tuple-element.30.refs_0_), channel_id=1, source_target_pairs={{0,1},{1,2},{2,3},{3,0},{16,19},{17,16},{18,17},{19,18},{4,5},{5,6... | collective-permute-start | bytes 393224 | tf_op jit(solution)/shard_map/ppermute | solution.py:456
  21.6 8.5 %collective-permute-start = (bf16[128,512]{1,0:T(8,128)(2,1)}, bf16[128,512]{1,0:T(8,128)(2,1)S(1)}, u32[]{:S(2)}, u32[]{:S(2)}) collective-permute-start(bf16[128,512]{1,0:T(8,128)(2,1)} %get-tuple-element.30.refs_0_), channel_id=1, source_target_pairs={{0,3},{1,0},{2,1},{3,2},{16,17},{17,18},{18,19},{19,16},{4,7},{5,4... | collective-permute-start | bytes 393224 | tf_op jit(solution)/shard_map/ppermute | solution.py:456
  41.8 18.7 %all-to-all-start.1 = ((bf16[32,2,3200]{2,1,0:T(2,128)(2,1)}), bf16[32,2,3200]{2,1,0:T(2,128)(2,1)S(1)}, u32[]{:S(2)}, u32[]{:S(2)}) async-start(bf16[32,2,3200]{2,1,0:T(2,128)(2,1)} %shard_map.181), calls=%async_computation.1 | async-start | bytes 819200 | tf_op jit(solution)/shard_map/all_to_all | solution.py:441
  45.8 5.6 %collective-permute-start.2 = (bf16[128,512]{1,0:T(8,128)(2,1)S(1)}, bf16[128,512]{1,0:T(8,128)(2,1)S(1)}, u32[]{:S(2)}, u32[]{:S(2)}) collective-permute-start(bf16[128,512]{1,0:T(8,128)(2,1)S(1)} %copy-done.6), channel_id=1, source_target_pairs={{0,2},{1,3},{2,0},{3,1},{16,18},{17,19},{18,16},{19,17},{4,6},{5,7... | collective-permute-start | bytes 393224 | tf_op jit(solution)/shard_map/ppermute | solution.py:456
  47.4 6.5 %collective-permute-start.3 = (bf16[128,512]{1,0:T(8,128)(2,1)S(1)}, bf16[128,512]{1,0:T(8,128)(2,1)S(1)}, u32[]{:S(2)}, u32[]{:S(2)}) collective-permute-start(bf16[128,512]{1,0:T(8,128)(2,1)S(1)} %copy-done.6), channel_id=1, source_target_pairs={{0,16},{16,0},{1,17},{17,1},{2,18},{18,2},{3,19},{19,3},{4,20},{20... | collective-permute-start | bytes 393224 | tf_op jit(solution)/shard_map/ppermute | solution.py:445
  51.4 2.9 %collective-permute-start.5 = (bf16[128,512]{1,0:T(8,128)(2,1)S(1)}, bf16[128,512]{1,0:T(8,128)(2,1)S(1)}, u32[]{:S(2)}, u32[]{:S(2)}) collective-permute-start(bf16[128,512]{1,0:T(8,128)(2,1)S(1)} %collective-permute-done.2.refs_2_), channel_id=1, source_target_pairs={{0,16},{16,0},{1,17},{17,1},{2,18},{18,2},{3,19},{19,3},{4,20},{20... | collective-permute-start | bytes 393224 | tf_op jit(solution)/shard_map/ppermute | solution.py:445
  53.4 1.3 %collective-permute-start.6 = (bf16[128,512]{1,0:T(8,128)(2,1)S(1)}, bf16[128,512]{1,0:T(8,128)(2,1)S(1)}, u32[]{:S(2)}, u32[]{:S(2)}) collective-permute-start(bf16[128,512]{1,0:T(8,128)(2,1)S(1)} %collective-permute-done.1.rest_1_.refs_3_), channel_id=1, source_target_pairs={{0,16},{16,0},{1,17},{17,1},{2,18},{18,2},{3,19},{19,3},{4,20},{20... | collective-permute-start | bytes 393224 | tf_op jit(solution)/shard_map/ppermute | solution.py:445
  53.4 1.5 %collective-permute-start.4 = (bf16[128,512]{1,0:T(8,128)(2,1)S(1)}, bf16[128,512]{1,0:T(8,128)(2,1)S(1)}, u32[]{:S(2)}, u32[]{:S(2)}) collective-permute-start(bf16[128,512]{1,0:T(8,128)(2,1)S(1)} %collective-permute-done.rest_0_.refs_1_), channel_id=1, source_target_pairs={{0,16},{16,0},{1,17},{17,1},{2,18},{18,2},{3,19},{19,3},{4,20},{20... | collective-permute-start | bytes 393224 | tf_op jit(solution)/shard_map/ppermute | solution.py:445
  61.0 6.5 %collective-permute-start.7 = (f32[32,256]{1,0:T(8,128)S(1)}, f32[32,256]{1,0:T(8,128)S(1)}, u32[]{:S(2)}, u32[]{:S(2)}) collective-permute-start(f32[32,256]{1,0:T(8,128)S(1)} %get-tuple-element.33), channel_id=1, source_target_pairs={{0,96},{32,0},{64,32},{96,64},{16,48},{48,80},{80,112},{112,16},{1... | collective-permute-start | bytes 98312 | tf_op jit(solution)/shard_map/ppermute | solution.py:456
  61.3 6.2 %collective-permute-start.8 = (f32[32,256]{1,0:T(8,128)S(1)}, f32[32,256]{1,0:T(8,128)S(1)}, u32[]{:S(2)}, u32[]{:S(2)}) collective-permute-start(f32[32,256]{1,0:T(8,128)S(1)} %get-tuple-element.34), channel_id=1, source_target_pairs={{0,64},{32,96},{64,0},{96,32},{16,80},{48,112},{80,16},{112,48},{1... | collective-permute-start | bytes 98312 | tf_op jit(solution)/shard_map/ppermute | solution.py:456
  63.2 4.3 %collective-permute-start.9 = (f32[32,256]{1,0:T(8,128)S(1)}, f32[32,256]{1,0:T(8,128)S(1)}, u32[]{:S(2)}, u32[]{:S(2)}) collective-permute-start(f32[32,256]{1,0:T(8,128)S(1)} %get-tuple-element.35), channel_id=1, source_target_pairs={{0,32},{32,64},{64,96},{96,0},{16,112},{48,16},{80,48},{112,80},{1... | collective-permute-start | bytes 98312 | tf_op jit(solution)/shard_map/ppermute | solution.py:456
  64.7 9.6 %collective-permute-start.11 = (bf16[2,224,128]{2,1,0:T(8,128)(2,1)S(1)}, bf16[2,224,128]{2,1,0:T(8,128)(2,1)S(1)}, u32[]{:S(2)}, u32[]{:S(2)}) collective-permute-start(bf16[2,224,128]{2,1,0:T(8,128)(2,1)S(1)} %get-tuple-element.39), channel_id=1, source_target_pairs={{0,2},{1,3},{2,0},{3,1},{16,18},{17,19},{18,16},{19,17},{4,6},{5,7... | collective-permute-start | bytes 344072 | tf_op jit(solution)/shard_map/ppermute | solution.py:456
  68.2 11.2 %all-to-all-start.2 = ((bf16[8,64,128]{2,1,0:T(8,128)(2,1)}), bf16[8,64,128]{2,1,0:T(8,128)(2,1)S(1)}, u32[]{:S(2)}, u32[]{:S(2)}) async-start(bf16[8,64,128]{2,1,0:T(8,128)(2,1)} %get-tuple-element.43), calls=%async_computation.2 | async-start | bytes 262144 | tf_op jit(solution)/shard_map/all_to_all | solution.py:441
  71.6 5.6 %collective-permute-start.10 = (bf16[2,224,128]{2,1,0:T(8,128)(2,1)S(1)}, bf16[2,224,128]{2,1,0:T(8,128)(2,1)S(1)}, u32[]{:S(2)}, u32[]{:S(2)}) collective-permute-start(bf16[2,224,128]{2,1,0:T(8,128)(2,1)S(1)} %get-tuple-element.38), channel_id=1, source_target_pairs={{0,3},{1,0},{2,1},{3,2},{16,17},{17,18},{18,19},{19,16},{4,7},{5,4... | collective-permute-start | bytes 344072 | tf_op jit(solution)/shard_map/ppermute | solution.py:456
  71.6 5.5 %collective-permute-start.12 = (bf16[2,224,128]{2,1,0:T(8,128)(2,1)S(1)}, bf16[2,224,128]{2,1,0:T(8,128)(2,1)S(1)}, u32[]{:S(2)}, u32[]{:S(2)}) collective-permute-start(bf16[2,224,128]{2,1,0:T(8,128)(2,1)S(1)} %get-tuple-element.40), channel_id=1, source_target_pairs={{0,1},{1,2},{2,3},{3,0},{16,19},{17,16},{18,17},{19,18},{4,5},{5,6... | collective-permute-start | bytes 344072 | tf_op jit(solution)/shard_map/ppermute | solution.py:456
  74.3 3.8 %collective-permute-start.15 = (bf16[2,224,128]{2,1,0:T(8,128)(2,1)S(1)}, bf16[2,224,128]{2,1,0:T(8,128)(2,1)S(1)}, u32[]{:S(2)}, u32[]{:S(2)}) collective-permute-start(bf16[2,224,128]{2,1,0:T(8,128)(2,1)S(1)} %collective-permute-done.11.refs_2_), channel_id=1, source_target_pairs={{0,16},{16,0},{1,17},{17,1},{2,18},{18,2},{3,19},{19,3},{4,20},{20... | collective-permute-start | bytes 344072 | tf_op jit(solution)/shard_map/ppermute | solution.py:445
  80.1 13.0 %all-to-all-start.3 = ((bf16[16,64,128]{2,1,0:T(8,128)(2,1)}), bf16[16,64,128]{2,1,0:T(8,128)(2,1)S(1)}, u32[]{:S(2)}, u32[]{:S(2)}) async-start(bf16[16,64,128]{2,1,0:T(8,128)(2,1)} %shard_map.185), calls=%async_computation.3 | async-start | bytes 524288 | tf_op jit(solution)/shard_map/all_to_all | solution.py:441
  85.8 3.8 %collective-permute-start.13 = (bf16[2,224,128]{2,1,0:T(8,128)(2,1)S(1)}, bf16[2,224,128]{2,1,0:T(8,128)(2,1)S(1)}, u32[]{:S(2)}, u32[]{:S(2)}) collective-permute-start(bf16[2,224,128]{2,1,0:T(8,128)(2,1)S(1)} %get-tuple-element.31.refs_0_), channel_id=1, source_target_pairs={{0,16},{16,0},{1,17},{17,1},{2,18},{18,2},{3,19},{19,3},{4,20},{20... | collective-permute-start | bytes 344072 | tf_op jit(solution)/shard_map/ppermute | solution.py:445
  88.6 1.3 %collective-permute-start.14 = (bf16[2,224,128]{2,1,0:T(8,128)(2,1)S(1)}, bf16[2,224,128]{2,1,0:T(8,128)(2,1)S(1)}, u32[]{:S(2)}, u32[]{:S(2)}) collective-permute-start(bf16[2,224,128]{2,1,0:T(8,128)(2,1)S(1)} %collective-permute-done.10.refs_1_.refs_0_), channel_id=1, source_target_pairs={{0,16},{16,0},{1,17},{17,1},{2,18},{18,2},{3,19},{19,3},{4,20},{20... | collective-permute-start | bytes 344072 | tf_op jit(solution)/shard_map/ppermute | solution.py:445
  88.7 1.4 %collective-permute-start.16 = (bf16[2,224,128]{2,1,0:T(8,128)(2,1)S(1)}, bf16[2,224,128]{2,1,0:T(8,128)(2,1)S(1)}, u32[]{:S(2)}, u32[]{:S(2)}) collective-permute-start(bf16[2,224,128]{2,1,0:T(8,128)(2,1)S(1)} %collective-permute-done.12.refs_3_.refs_1_), channel_id=1, source_target_pairs={{0,16},{16,0},{1,17},{17,1},{2,18},{18,2},{3,19},{19,3},{4,20},{20... | collective-permute-start | bytes 344072 | tf_op jit(solution)/shard_map/ppermute | solution.py:445
  93.2 5.0 %collective-permute-start.17 = (bf16[16,64,128]{2,1,0:T(8,128)(2,1)S(1)}, bf16[16,64,128]{2,1,0:T(8,128)(2,1)S(1)}, u32[]{:S(2)}, u32[]{:S(2)}) collective-permute-start(bf16[16,64,128]{2,1,0:T(8,128)(2,1)S(1)} %all-to-all-done.3.own_ref), channel_id=1, source_target_pairs={{0,16},{16,0},{1,17},{17,1},{2,18},{18,2},{3,19},{19,3},{4,20},{20... | collective-permute-start | bytes 786440 | tf_op jit(solution)/shard_map/ppermute | solution.py:445
  (8 other events, 200.5 us)
